TPU v7x, 32 devices: a whole 2x2x4 slice. The times are simulated.
32 devices in a mesh: gx: 8 (over z, x), gy: 2 (over core), gz: 2 (over y).
Axes of the slice: x: 2, y: 2, z: 4, core: 2. Of those that a mesh axis runs over, the one named last changes fastest.
Arguments:
- flow_field: bfloat16 [256, 128, 1024], P('gx', 'gy', 'gz'), may hold values from -96 to 96
- left_x: bfloat16 [256, 128], P('gx'), may hold values from -0.046875 to 0.046875
- last_x: bfloat16 [256, 128], P('gx'), may hold values from -0.375 to 0.375
- last_y: bfloat16 [128, 128], P('gy'), may hold values from -0.0078125 to 0.0078125
- right_y: bfloat16 [128, 256], P('gy'), may hold values from -0.5 to 0.5
- right_m: bfloat16 [1024, 256], P('gz'), may hold values from -0.1875 to 0.1875
- last_m: bfloat16 [1024, 256], P('gz'), may hold values from -0.1875 to 0.1875
Outputs:
- core_first: float32 [256, 128], P('gx')
- core_middle: float32 [128, 128, 128], P(('gx', 'gz'), 'gy')
- core_last: float32 [128, 1024], P(None, 'gz')
All inputs are finite; a program needn't handle non-finite values.
Results may differ from a plain program's by a relative error of at most 0.0053.
Values sent between devices are 32-bit elements; how exact they have to be, the bound alone decides.
No kernel may reach another device: no remote copies, remote signals or barrier semaphores. Data moves between devices by JAX's collectives and lax.ppermute only.
A program may use at most 64 MiB of HBM per device.

v0:
```python
import jax
import jax.numpy as jnp
from jax import lax
from jax.sharding import PartitionSpec as P


def normal_solve(system, right_side):
    gram_matrix = jnp.dot(system, system.T, precision=lax.Precision.HIGHEST)
    factor = jnp.linalg.cholesky(gram_matrix)
    return jax.scipy.linalg.cho_solve((factor, True), right_side)


def per_device(flow_field, left_x, last_x, last_y, right_y, right_m, last_m):
    highest = lax.Precision.HIGHEST
    x_cells, y_cells, m_cells = flow_field.shape
    rank_cols = left_x.shape[1]
    sketch_cols = right_m.shape[1]
    flat_field = flow_field.reshape(x_cells * y_cells, m_cells)
    first_terms = jnp.dot(flat_field, right_m, preferred_element_type=jnp.float32).reshape(
        x_cells, y_cells, sketch_cols
    )
    first_part = jnp.sum(first_terms * right_y.astype(jnp.float32)[None], axis=1)
    first_rows = lax.psum(first_part, ("gy", "gz"))
    left_wide = left_x.astype(jnp.float32)
    first_gram = lax.psum(jnp.dot(left_wide.T, first_rows, precision=highest), "gx")
    core_first = normal_solve(first_gram, jnp.dot(first_gram, first_rows.T, precision=highest)).T
    khatri = (last_x.astype(jnp.float32)[:, None, :] * last_y.astype(jnp.float32)[None]).astype(
        jnp.bfloat16
    )
    khatri = khatri.reshape(x_cells * y_cells, rank_cols)
    last_part = jnp.dot(khatri.T, flat_field, preferred_element_type=jnp.float32)
    core_last = lax.psum(last_part, ("gx", "gy"))
    last_gram = lax.psum(jnp.dot(core_last, last_m.astype(jnp.float32), precision=highest), "gz")
    pinv_last = normal_solve(last_gram, last_gram).T
    flat_terms = jnp.dot(flat_field, last_m, preferred_element_type=jnp.float32)
    last_terms = flat_terms.reshape(x_cells, y_cells * sketch_cols)
    row_share = rank_cols // lax.axis_size(("gx", "gz"))
    sketched = (
        jnp.dot(left_wide.T, last_terms, precision=highest)
        .reshape(row_share * lax.axis_size(("gx", "gz")), y_cells, sketch_cols)
        .reshape(row_share * lax.axis_size(("gx", "gz")) * y_cells, sketch_cols)
    )
    core_middle = lax.psum_scatter(
        jnp.dot(sketched, pinv_last, precision=highest).reshape(
            row_share * lax.axis_size(("gx", "gz")), y_cells, rank_cols
        ),
        ("gx", "gz"),
        scatter_dimension=0,
        tiled=True,
    )
    return (core_first, core_middle, core_last)


def solution(mesh):
    return jax.shard_map(
        per_device,
        mesh=mesh,
        in_specs=(
            P("gx", "gy", "gz"),
            P("gx", None),
            P("gx", None),
            P("gy", None),
            P("gy", None),
            P("gz", None),
            P("gz", None),
        ),
        out_specs=(P("gx", None), P(("gx", "gz"), "gy", None), P(None, "gz")),
        check_vma=False,
    )
```

profile of v0, /device:TPU:0, one launch (start us, length us, event | category | flops | bytes accessed | tf_op | source)
XLA Modules:
  0.0 308.1 jit_solution(2715276260226401153)
XLA Ops:
  7.2 0.0 copy-start
  7.2 0.0 copy-start.4
  7.2 0.0 copy-start.5
  7.2 0.0 all-reduce.6.cloned.1.call-start
  7.2 0.9 convert_element_type.15
  8.1 0.7 convert_element_type.16
  8.8 1.2 convolution_bitcast_fusion
  10.0 0.0 all-reduce.6.cloned.1.call-update
  10.0 0.0 all-reduce.8.cloned.1.call-start
  10.1 0.0 copy-start.2
  10.1 0.0 copy-start.3
  10.1 0.7 multiply_reduce_fusion
  10.9 14.3 %psum.28 = f32[32,256]{1,0:T(8,128)S(1)} all-reduce(f32[32,256]{1,0:T(8,128)S(1)} %multiply_reduce_fusion), channel_id=1, replica_groups=mesh['gx'=8,'gy'=2,'gz'=2] {'gy','gz'}, use_global_device_ids=true, to_apply=%region_1.0 | all-reduce | flops 8192 | bytes 65536 | tf_op jit(solution)/shard_map/psum | solution.py:23
  25.2 78.3 %all-reduce.6.cloned.1.call-done = f32[128,512]{1,0:T(8,128)} async-done(((f32[128,512]{1,0:T(8,128)}), f32[128,512]{1,0:T(8,128)}) %all-reduce.6.cloned.1.call-update) | async-done | bytes 262160 | tf_op jit(solution)/shard_map/psum | solution.py:32
  103.5 1.9 fusion.18
  105.4 0.0 all-reduce.8.cloned.1.call-update
  105.4 0.0 all-reduce.4.cloned.1.call-start
  105.5 0.9 convolution_bitcast_fusion.2
  106.4 0.0 all-reduce.4.cloned.1.call-update
  106.4 0.0 reduce-scatter.2.cloned.1.call-start
  106.5 2.1 fusion.16
  108.5 2.8 reshape.42
  111.4 10.1 %fusion.17 = f32[16384,128]{1,0:T(8,128)} fusion(f32[32,16384]{1,0:T(8,128)} %reshape.42, bf16[32,128]{1,0:T(8,128)(2,1)S(1)} %copy-done.3), kind=kOutput, calls=%fused_computation.32 | convolution fusion | flops 805306368 | bytes 10493952 | tf_op jit(solution)/shard_map/dot_general | solution.py:39
  121.5 6.8 %all-reduce.8.cloned.1.call-done = f32[128,256]{1,0:T(8,128)} async-done(((f32[128,256]{1,0:T(8,128)}), f32[128,256]{1,0:T(8,128)}) %all-reduce.8.cloned.1.call-update) | async-done | bytes 131088 | tf_op jit(solution)/shard_map/psum | solution.py:33
  128.3 1.3 fusion.19
  129.6 0.1 copy.11
  129.7 11.7 %cholesky.55 = f32[128,128]{1,0:T(8,128)S(1)} custom-call(f32[128,128]{1,0:T(8,128)S(1)} %fusion.8), custom_call_target="Cholesky" | custom-call | tf_op jit(solution)/shard_map/jit(cholesky)/cholesky | solution.py:9
  141.4 0.6 compare_reduce_fusion
  142.1 0.7 fusion.4
  142.7 9.8 %custom-call.17 = f32[1,128,128]{1,2,0:T(8,128)S(1)} custom-call(f32[1,128,128]{2,1,0:T(8,128)S(1)} %fusion.4), custom_call_target="InvertDiagBlocksLowerTriangular" | custom-call | tf_op jit(solution)/shard_map/jit(_cho_solve)/triangular_solve | solution.py:10
  152.5 1.2 fusion.6
  153.8 0.3 convolution_bitcast_fusion.1
  154.0 17.1 %fusion.20 = f32[128,64,128]{2,0,1:T(8,128)} fusion(f32[128,64,256]{0,2,1:T(8,128)} %bitcast.58, f32[128,256,1]{1,0,2:T(8,128)S(1)} %convolution_bitcast_fusion.1), kind=kOutput, calls=%fused_computation.35 | convolution fusion | flops 3221225472 | bytes 12713984 | tf_op jit(solution)/shard_map/dot_general | solution.py:44
  171.1 0.0 reduce-scatter.2.cloned.1.call-update
  171.1 31.0 %all-reduce.4.cloned.1.call-done = f32[128,256]{0,1:T(8,128)} async-done(((f32[128,256]{0,1:T(8,128)}), f32[128,256]{0,1:T(8,128)}) %all-reduce.4.cloned.1.call-update) | async-done | bytes 131088 | tf_op jit(solution)/shard_map/psum | solution.py:25
  202.1 1.4 fusion.14
  203.5 0.1 copy.10
  203.6 11.7 %cholesky.44 = f32[128,128]{1,0:T(8,128)S(1)} custom-call(f32[128,128]{1,0:T(8,128)S(1)} %fusion.13), custom_call_target="Cholesky" | custom-call | tf_op jit(solution)/shard_map/jit(cholesky)/cholesky | solution.py:9
  215.3 0.6 compare_reduce_fusion.1
  216.0 0.7 fusion.3
  216.7 9.8 %custom-call.16 = f32[1,128,128]{1,2,0:T(8,128)S(1)} custom-call(f32[1,128,128]{2,1,0:T(8,128)S(1)} %fusion.3), custom_call_target="InvertDiagBlocksLowerTriangular" | custom-call | tf_op jit(solution)/shard_map/jit(_cho_solve)/triangular_solve | solution.py:10
  226.5 1.3 fusion.15
  227.8 0.3 fusion.11
  228.1 0.9 fusion.9
  228.9 70.2 %reduce-scatter.2.cloned.1.call-done = f32[8,64,128]{2,0,1:T(8,128)} async-done(((f32[128,64,128]{2,0,1:T(8,128)}), f32[8,64,128]{2,0,1:T(8,128)}) %reduce-scatter.2.cloned.1.call-update) | async-done | bytes 262160 | tf_op jit(solution)/shard_map/reduce_scatter | solution.py:43
  299.1 1.7 copy.13
  300.9 0.0 copy-done.1
  300.9 0.7 copy.18
  (11 shorter events, 0.1 us)
Async XLA Ops:
  7.2 1.7 copy-start
  7.2 2.9 copy-start.4
  7.2 2.9 copy-start.5
  7.2 96.3 %all-reduce.6.cloned.1.call-start = ((), (), s32[]{:S(2)}) async-start(), calls=%async_computation.2 | async-start | bytes 524288 | tf_op jit(solution)/shard_map/psum | solution.py:32
  10.0 118.3 %all-reduce.8.cloned.1.call-start = ((), (), s32[]{:S(2)}) async-start(), calls=%async_computation.3 | async-start | bytes 262144 | tf_op jit(solution)/shard_map/psum | solution.py:33
  10.1 93.4 %copy-start.2 = (bf16[512,256]{1,0:T(8,128)(2,1)S(1)}, bf16[512,256]{1,0:T(8,128)(2,1)}, u32[]{:S(2)}) copy-start(bf16[512,256]{1,0:T(8,128)(2,1)} %param.14) | copy-start | bytes 786436
  10.1 95.3 %copy-start.3 = (bf16[32,128]{1,0:T(8,128)(2,1)S(1)}, bf16[32,128]{1,0:T(8,128)(2,1)}, u32[]{:S(2)}) copy-start(bf16[32,128]{1,0:T(8,128)(2,1)} %param.9) | copy-start | bytes 24580
  105.4 96.7 %all-reduce.4.cloned.1.call-start = ((), (), s32[]{:S(2)}) async-start(), calls=%async_computation.1 | async-start | bytes 262144 | tf_op jit(solution)/shard_map/psum | solution.py:25
  106.4 192.7 %reduce-scatter.2.cloned.1.call-start = ((), (), s32[]{:S(2)}) async-start(), calls=%async_computation.4 | async-start | bytes 4456448 | tf_op jit(solution)/shard_map/reduce_scatter | solution.py:43
  171.1 129.8 %copy-start.1 = (f32[128,512]{1,0:T(8,128)S(1)}, f32[128,512]{1,0:T(8,128)}, u32[]{:S(2)}) copy-start(f32[128,512]{1,0:T(8,128)} %all-reduce.6.cloned.1.call-done) | copy-start | bytes 786436
Sparse Core Ops, SparseCore 0:
  12.0 91.4 all-reduce.5
  106.3 21.9 all-reduce.7
  132.2 69.8 all-reduce.3
  204.4 94.7 reduce-scatter.1
where the time goes:
time: 308 us
  waiting for transfers between devices  186 us (60%)
  other arithmetic  47.3 us (15%)
  matrix products  40.5 us (13%)
  blocking collectives  14.3 us (5%)
  between operations  14 us (5%)
  local copies, waits for them, and re-layouts  5.42 us (2%)
    psum x1, waiting for transfers between devices, per_device(): core_last = lax.psum(last_part, ('gx', 'gy'))  78.3 us
    reduce_scatter x1, waiting for transfers between devices, per_device(): lax.psum_scatter(jnp.dot(sketched, pinv_last, precision=highest).reshape(...  70.2 us
    psum x1, waiting for transfers between devices, per_device(): lax.psum(jnp.dot(left_wide.T, first_rows, precision=highest), 'gx')  31 us
    another operation x6, other arithmetic, normal_solve(): factor = jnp.linalg.cholesky(gram_matrix)  24.8 us
    another operation x4, other arithmetic, normal_solve(): return jax.scipy.linalg.cho_solve((factor, True), right_side)  20.9 us
    dot_general x1, matrix products, per_device(): jnp.dot(sketched, pinv_last, precision=highest)  17.1 us
    psum x1, blocking collectives, per_device(): first_rows = lax.psum(first_part, ('gy', 'gz'))  14.3 us
    dot_general x1, matrix products, per_device(): jnp.dot(left_wide.T, last_terms, precision=highest)  10.1 us
  transfers between devices with their start and end apart: 4, of which 4 were waited for; matrix products, arithmetic and copies ran while one was open for 28% of the time, Pallas kernels for 0%

commit v1 on v0

v1 whole, which is shorter than its diff:
```python
import jax
import jax.numpy as jnp
from jax import lax
from jax.sharding import PartitionSpec as P

ALL = ("gx", "gy", "gz")


def spread(array, axes):
    count = lax.axis_size(axes)
    copies = jnp.broadcast_to(array[None], (count, *array.shape))
    return lax.all_to_all(copies, axes, 0, 0, tiled=True)


def all_sum(array, axes):
    count = lax.axis_size(axes)
    rows = array.reshape(count, array.shape[0] // count, *array.shape[1:])
    share = jnp.sum(lax.all_to_all(rows, axes, 0, 0, tiled=True), axis=0)
    return spread(share, axes).reshape(array.shape)


def normal_solve(system):
    gram_matrix = jnp.dot(system, system.T, precision=lax.Precision.HIGHEST)
    factor = jnp.linalg.cholesky(gram_matrix)
    return jax.scipy.linalg.cho_solve((factor, True), system).T


def split_dot(left, right):
    high = right.astype(jnp.bfloat16)
    low = (right - high.astype(jnp.float32)).astype(jnp.bfloat16)
    both = jnp.dot(left, jnp.concatenate([high, low], axis=1), preferred_element_type=jnp.float32)
    return both[:, : right.shape[1]] + both[:, right.shape[1] :]


def per_device(flow_field, left_x, last_x, last_y, right_y, right_m, last_m):
    highest = lax.Precision.HIGHEST
    x_cells, y_cells, m_cells = flow_field.shape
    rank_cols = left_x.shape[1]
    sketch_cols = right_m.shape[1]
    flat_field = flow_field.reshape(x_cells * y_cells, m_cells)
    left_wide = left_x.astype(jnp.float32)
    left_all = spread(left_wide, "gx").reshape(-1, rank_cols)

    khatri = (last_x.astype(jnp.float32)[:, None, :] * last_y.astype(jnp.float32)[None]).astype(
        jnp.bfloat16
    )
    khatri = khatri.reshape(x_cells * y_cells, rank_cols)
    last_part = jnp.dot(khatri.T, flat_field, preferred_element_type=jnp.float32)
    first_terms = jnp.dot(flat_field, right_m, preferred_element_type=jnp.float32).reshape(
        x_cells, y_cells, sketch_cols
    )
    first_part = jnp.sum(first_terms * right_y.astype(jnp.float32)[None], axis=1)

    grams = jnp.concatenate(
        [
            jnp.dot(last_part, last_m.astype(jnp.float32), precision=highest),
            jnp.dot(left_wide.T, first_part, precision=highest),
        ],
        axis=0,
    )
    grams = all_sum(grams, ALL)
    pinv_last = normal_solve(grams[:rank_cols])
    pinv_first = normal_solve(grams[rank_cols:])

    projector = jnp.dot(last_m.astype(jnp.float32), pinv_last, precision=highest)
    projected = split_dot(flat_field, projector).reshape(x_cells, y_cells, rank_cols)

    group = ("gx", "gz")
    devices = lax.axis_size(group)
    y_share = y_cells // devices
    pieces = projected.reshape(x_cells, devices, y_share, rank_cols).transpose(1, 0, 2, 3)
    pieces = lax.all_to_all(pieces, group, 0, 0, tiled=True)
    pieces = pieces.reshape(lax.axis_size("gx"), lax.axis_size("gz"), x_cells, y_share * rank_cols)
    column = jnp.sum(pieces, axis=1).reshape(-1, y_share * rank_cols)
    sketched = jnp.dot(left_all.T, column, precision=highest)
    sketched = sketched.reshape(devices, rank_cols // devices, y_share, rank_cols)
    middle = lax.all_to_all(sketched, group, 0, 0, tiled=True)
    core_middle = middle.transpose(1, 0, 2, 3).reshape(rank_cols // devices, y_cells, rank_cols)

    core_last = all_sum(last_part, ("gx", "gy"))
    core_first = all_sum(jnp.dot(first_part, pinv_first, precision=highest), ("gy", "gz"))
    return (core_first, core_middle, core_last)


def solution(mesh):
    return jax.shard_map(
        per_device,
        mesh=mesh,
        in_specs=(
            P("gx", "gy", "gz"),
            P("gx", None),
            P("gx", None),
            P("gy", None),
            P("gy", None),
            P("gz", None),
            P("gz", None),
        ),
        out_specs=(P("gx", None), P(("gx", "gz"), "gy", None), P(None, "gz")),
        check_vma=False,
    )
```

time: 308 us -> 186 us (0.60)
  waiting for transfers between devices: 186 us -> 50.2 us
  matrix products: 40.5 us -> 10.3 us
  starting transfers between devices: 0.16 us -> 29.9 us
  blocking collectives: 14.3 us -> 30.6 us
  between operations: 14 us -> 0.92 us
  local copies, waits for them, and re-layouts: 5.42 us -> 11 us
  other arithmetic: 47.3 us -> 52 us
    psum x3 -> x0, waiting for transfers between devices: 116 us -> none  [the longest x1 78.3 us: per_device(): core_last = lax.psum(last_part, ('gx', 'gy'))]
    reduce_scatter x1 -> x0, waiting for transfers between devices: 70.2 us -> none  [per_device(): lax.psum_scatter(jnp.dot(sketched, pinv_last, precision=highest).reshape(...]
    all_to_all x0 -> x7, waiting for transfers between devices: none -> 50.2 us  [the longest x1 24.6 us: per_device(): pieces = lax.all_to_all(pieces, group, 0, 0, tiled=True)]
    all_to_all x0 -> x2, blocking collectives: none -> 30.6 us  [the longest x1 17.8 us: all_sum(): share = jnp.sum(lax.all_to_all(rows, axes, 0, 0, tiled=True), axis=0)]
    all_to_all x0 -> x7, starting transfers between devices: none -> 29.9 us  [the longest x3 12.6 us: spread(): return lax.all_to_all(copies, axes, 0, 0, tiled=True)]
    dot_general x6, matrix products: 33.3 us -> 5.81 us  [the longest x1 2.09 us: split_dot(): jnp.dot(left, jnp.concatenate([high, low], axis=1), preferred_element_typ...]
    psum x1 -> x0, blocking collectives: 14.3 us -> none  [per_device(): first_rows = lax.psum(first_part, ('gy', 'gz'))]
  transfers between devices with their start and end apart: 4 -> 7, of which waited for: 4 -> 5; matrix products, arithmetic and copies ran while one was open for 28% -> 33% of each run, Pallas kernels for 0% -> 0%
where the time goes in v1:
time: 186 us; the launch traced here: 185 us
  other arithmetic  52 us (28%)
  waiting for transfers between devices  50.2 us (27%)
  blocking collectives  30.6 us (16%)
  starting transfers between devices  29.9 us (16%)
  local copies, waits for them, and re-layouts  11 us (6%)
  matrix products  10.3 us (6%)
    another operation x6, other arithmetic, normal_solve(): factor = jnp.linalg.cholesky(gram_matrix)  24.8 us
    all_to_all x1, waiting for transfers between devices, per_device(): pieces = lax.all_to_all(pieces, group, 0, 0, tiled=True)  24.6 us
    another operation x4, other arithmetic, normal_solve(): return jax.scipy.linalg.cho_solve((factor, True), system).T  21.1 us
    all_to_all x1, blocking collectives, all_sum(): share = jnp.sum(lax.all_to_all(rows, axes, 0, 0, tiled=True), axis=0)  17.8 us
    all_to_all x1, blocking collectives, spread(): return lax.all_to_all(copies, axes, 0, 0, tiled=True)  12.8 us
    all_to_all x3, starting transfers between devices, spread(): return lax.all_to_all(copies, axes, 0, 0, tiled=True)  12.6 us
    all_to_all x1, waiting for transfers between devices, per_device(): middle = lax.all_to_all(sketched, group, 0, 0, tiled=True)  10 us
    all_to_all x2, starting transfers between devices, all_sum(): share = jnp.sum(lax.all_to_all(rows, axes, 0, 0, tiled=True), axis=0)  9.3 us
  transfers between devices with their start and end apart: 7, of which 5 were waited for; matrix products, arithmetic and copies ran while one was open for 33% of the time, Pallas kernels for 0%

profile of v1, /device:TPU:0, one launch (start us, length us, event | category | flops | bytes accessed | tf_op | source)
XLA Modules:
  0.0 185.0 jit_solution(17499939100468273017)
XLA Ops:
  0.6 0.9 convert_element_type.26
  1.6 0.7 convert_element_type.28
  2.3 0.7 convert_element_type.27
  3.0 1.7 multiply_reduce_fusion
  5.0 1.2 fusion
  6.1 1.2 fusion.6
  7.4 17.8 %all_to_all.45 = f32[32,8,256]{2,1,0:T(8,128)S(1)} all-to-all(f32[32,8,256]{2,1,0:T(8,128)S(1)} %maximum_bitcast_fusion), channel_id=1, replica_groups=mesh['gx'=8,'gy'=2,'gz'=2] {'gx','gy','gz'}, dimensions={0} | all-to-all | bytes 524288 | tf_op jit(solution)/shard_map/all_to_all | solution.py:18
  25.3 12.8 %all_to_all.46 = f32[32,8,256]{2,1,0:T(8,128)S(1)} all-to-all(f32[32,8,256]{2,1,0:T(8,128)S(1)} %broadcast_in_dim.8), channel_id=1, replica_groups=mesh['gx'=8,'gy'=2,'gz'=2] {'gx','gy','gz'}, dimensions={0} | all-to-all | bytes 524288 | tf_op jit(solution)/shard_map/all_to_all | solution.py:12
  38.1 0.7 broadcast_in_dim.10
  38.7 3.4 %all-to-all-start.5 = ((f32[8,32,128]{2,1,0:T(8,128)}), f32[8,32,128]{2,1,0:T(8,128)S(1)}, u32[]{:S(2)}, u32[]{:S(2)}) async-start(f32[8,32,128]{2,1,0:T(8,128)} %broadcast_in_dim.10), calls=%async_computation.5 | async-start | bytes 262144 | tf_op jit(solution)/shard_map/all_to_all | solution.py:12
  42.5 11.7 %cholesky.44 = f32[128,128]{1,0:T(8,128)S(1)} custom-call(f32[128,128]{1,0:T(8,128)S(1)} %fusion.21), custom_call_target="Cholesky" | custom-call | tf_op jit(solution)/shard_map/jit(cholesky)/cholesky | solution.py:24
  54.3 0.6 compare_reduce_fusion.1
  54.9 0.7 fusion.13
  55.6 9.8 %custom-call.8 = f32[1,128,128]{1,2,0:T(8,128)S(1)} custom-call(f32[1,128,128]{2,1,0:T(8,128)S(1)} %fusion.13), custom_call_target="InvertDiagBlocksLowerTriangular" | custom-call | tf_op jit(solution)/shard_map/jit(_cho_solve)/triangular_solve | solution.py:25
  65.4 0.3 fusion.9
  66.4 11.7 %cholesky.55 = f32[128,128]{1,0:T(8,128)S(1)} custom-call(f32[128,128]{1,0:T(8,128)S(1)} %fusion.18), custom_call_target="Cholesky" | custom-call | tf_op jit(solution)/shard_map/jit(cholesky)/cholesky | solution.py:24
  78.1 0.6 compare_reduce_fusion
  78.8 0.7 fusion.14
  79.4 10.0 %custom-call.9 = f32[1,128,128]{1,2,0:T(8,128)S(1)} custom-call(f32[1,128,128]{2,1,0:T(8,128)S(1)} %fusion.14), custom_call_target="InvertDiagBlocksLowerTriangular" | custom-call | tf_op jit(solution)/shard_map/jit(_cho_solve)/triangular_solve | solution.py:25
  89.4 0.3 fusion.11
  90.0 0.4 subtract_convert_fusion
  90.4 6.0 %all-to-all-start.7 = ((f32[16,8,512]{2,1,0:T(8,128)}), f32[16,8,512]{2,1,0:T(8,128)S(1)}, u32[]{:S(2)}, u32[]{:S(2)}) async-start(f32[16,8,512]{2,1,0:T(8,128)} %bitcast.25), calls=%async_computation.7 | async-start | bytes 524288 | tf_op jit(solution)/shard_map/all_to_all | solution.py:18
  96.4 0.8 fusion.22
  97.3 2.1 %convolution_bitcast_fusion = f32[2048,256]{0,1:T(8,128)} fusion(bf16[2048,512]{1,0:T(8,128)(2,1)S(1)} %bitcast.78, bf16[512,128]{0,1:T(8,128)(2,1)S(1)} %get-tuple-element.11, bf16[512,128]{0,1:T(8,128)(2,1)S(1)} %get-tuple-element.12), kind=kOutput, calls=%fused_computation | convolution fusion | flops 537395200 | bytes 4456448 | tf_op jit(solution)/shard_map/dot_general | solution.py:31
  99.4 7.1 %all-to-all-done.7 = f32[16,8,512]{2,1,0:T(8,128)S(1)} async-done(((f32[16,8,512]{2,1,0:T(8,128)}), f32[16,8,512]{2,1,0:T(8,128)S(1)}, u32[]{:S(2)}, u32[]{:S(2)}) %all-to-all-start.7) | async-done | bytes 262176 | tf_op jit(solution)/shard_map/all_to_all | solution.py:18
  106.5 3.3 %all-to-all-start.2 = ((f32[4,8,128]{2,1,0:T(8,128)}), f32[4,8,128]{2,1,0:T(8,128)S(1)}, u32[]{:S(2)}, u32[]{:S(2)}) async-start(f32[4,8,128]{2,1,0:T(8,128)} %fusion.22), calls=%async_computation.2 | async-start | bytes 32768 | tf_op jit(solution)/shard_map/all_to_all | solution.py:18
  109.7 1.7 slice_add_fusion
  111.4 1.3 copy.21
  112.7 2.5 %copy.22 = f32[16,32,4,128]{3,2,1,0:T(4,128)} copy(f32[16,32,4,128]{3,2,0,1:T(4,128)} %bitcast.79) | data formatting | bytes 2097152 | tf_op jit(solution)/shard_map/transpose | solution.py:71
  115.3 0.6 copy-done.2
  115.9 4.4 %all-to-all-start.4 = ((f32[16,32,4,128]{3,2,1,0:T(4,128)}), f32[16,32,4,128]{3,2,1,0:T(4,128)S(1)}, u32[]{:S(2)}, u32[]{:S(2)}) async-start(f32[16,32,4,128]{3,2,1,0:T(4,128)} %copy.22), calls=%async_computation.4 | async-start | bytes 2097152 | tf_op jit(solution)/shard_map/all_to_all | solution.py:72
  120.3 24.6 %all-to-all-done.4 = f32[16,32,4,128]{3,2,1,0:T(4,128)S(1)} async-done(((f32[16,32,4,128]{3,2,1,0:T(4,128)}), f32[16,32,4,128]{3,2,1,0:T(4,128)S(1)}, u32[]{:S(2)}, u32[]{:S(2)}) %all-to-all-start.4) | async-done | bytes 1048608 | tf_op jit(solution)/shard_map/all_to_all | solution.py:72
  144.9 0.7 broadcast_in_dim.11
  145.6 6.0 %all-to-all-start.8 = ((f32[16,8,512]{2,1,0:T(8,128)}), f32[16,8,512]{2,1,0:T(8,128)S(1)}, u32[]{:S(2)}, u32[]{:S(2)}) async-start(f32[16,8,512]{2,1,0:T(8,128)} %broadcast_in_dim.11), calls=%async_computation.8 | async-start | bytes 524288 | tf_op jit(solution)/shard_map/all_to_all | solution.py:12
  151.6 0.7 reduce_sum.47
  152.3 1.4 reshape.61
  153.7 1.4 reduce_sum.48
  155.1 6.5 %all-to-all-done.8 = f32[16,8,512]{2,1,0:T(8,128)S(1)} async-done(((f32[16,8,512]{2,1,0:T(8,128)}), f32[16,8,512]{2,1,0:T(8,128)S(1)}, u32[]{:S(2)}, u32[]{:S(2)}) %all-to-all-start.8) | async-done | bytes 262176 | tf_op jit(solution)/shard_map/all_to_all | solution.py:12
  161.6 0.6 broadcast_in_dim.9
  162.2 3.3 %all-to-all-start.3 = ((f32[4,8,128]{2,1,0:T(8,128)}), f32[4,8,128]{2,1,0:T(8,128)S(1)}, u32[]{:S(2)}, u32[]{:S(2)}) async-start(f32[4,8,128]{2,1,0:T(8,128)} %broadcast_in_dim.9), calls=%async_computation.3 | async-start | bytes 32768 | tf_op jit(solution)/shard_map/all_to_all | solution.py:12
  165.5 1.0 convolution_bitcast_fusion.1
  166.5 0.8 copy.23
  167.3 2.0 %all-to-all-done.3 = f32[4,8,128]{2,1,0:T(8,128)S(1)} async-done(((f32[4,8,128]{2,1,0:T(8,128)}), f32[4,8,128]{2,1,0:T(8,128)S(1)}, u32[]{:S(2)}, u32[]{:S(2)}) %all-to-all-start.3) | async-done | bytes 16416 | tf_op jit(solution)/shard_map/all_to_all | solution.py:12
  169.3 3.5 %all-to-all-start.6 = ((f32[16,8,4,128]{3,1,2,0:T(8,128)}), f32[16,8,4,128]{3,1,2,0:T(8,128)S(1)}, u32[]{:S(2)}, u32[]{:S(2)}) async-start(f32[16,8,4,128]{3,1,2,0:T(8,128)} %bitcast.22), calls=%async_computation.6 | async-start | bytes 524288 | tf_op jit(solution)/shard_map/all_to_all | solution.py:77
  172.9 10.0 %all-to-all-done.6 = f32[16,8,4,128]{3,1,2,0:T(8,128)S(1)} async-done(((f32[16,8,4,128]{3,1,2,0:T(8,128)}), f32[16,8,4,128]{3,1,2,0:T(8,128)S(1)}, u32[]{:S(2)}, u32[]{:S(2)}) %all-to-all-start.6) | async-done | bytes 262176 | tf_op jit(solution)/shard_map/all_to_all | solution.py:77
  182.9 0.8 copy.24
  183.7 0.6 copy.27
  184.3 0.7 copy.28
  (24 shorter events, 1.7 us)
Async XLA Ops:
  0.6 2.4 %copy-start = (bf16[32,64,512]{2,1,0:T(8,128)(2,1)S(1)}, bf16[32,64,512]{2,1,0:T(8,128)(2,1)}, u32[]{:S(2)}) copy-start(bf16[32,64,512]{2,1,0:T(8,128)(2,1)} %param.10) | copy-start | bytes 6291460
  1.6 3.1 %copy-start.3 = (bf16[32,128]{1,0:T(8,128)(2,1)S(1)}, bf16[32,128]{1,0:T(8,128)(2,1)}, u32[]{:S(2)}) copy-start(bf16[32,128]{1,0:T(8,128)(2,1)} %param.11) | copy-start | bytes 24580
  4.7 1.5 copy-start.1
  38.7 51.6 %all-to-all-start.5 = ((f32[8,32,128]{2,1,0:T(8,128)}), f32[8,32,128]{2,1,0:T(8,128)S(1)}, u32[]{:S(2)}, u32[]{:S(2)}) async-start(f32[8,32,128]{2,1,0:T(8,128)} %broadcast_in_dim.10), calls=%async_computation.5 | async-start | bytes 262144 | tf_op jit(solution)/shard_map/all_to_all | solution.py:12
  90.4 16.1 %all-to-all-start.7 = ((f32[16,8,512]{2,1,0:T(8,128)}), f32[16,8,512]{2,1,0:T(8,128)S(1)}, u32[]{:S(2)}, u32[]{:S(2)}) async-start(f32[16,8,512]{2,1,0:T(8,128)} %bitcast.25), calls=%async_computation.7 | async-start | bytes 524288 | tf_op jit(solution)/shard_map/all_to_all | solution.py:18
  106.5 8.8 %all-to-all-start.2 = ((f32[4,8,128]{2,1,0:T(8,128)}), f32[4,8,128]{2,1,0:T(8,128)S(1)}, u32[]{:S(2)}, u32[]{:S(2)}) async-start(f32[4,8,128]{2,1,0:T(8,128)} %fusion.22), calls=%async_computation.2 | async-start | bytes 32768 | tf_op jit(solution)/shard_map/all_to_all | solution.py:18
  115.3 0.6 copy-start.2
  115.9 29.0 %all-to-all-start.4 = ((f32[16,32,4,128]{3,2,1,0:T(4,128)}), f32[16,32,4,128]{3,2,1,0:T(4,128)S(1)}, u32[]{:S(2)}, u32[]{:S(2)}) async-start(f32[16,32,4,128]{3,2,1,0:T(4,128)} %copy.22), calls=%async_computation.4 | async-start | bytes 2097152 | tf_op jit(solution)/shard_map/all_to_all | solution.py:72
  145.6 16.1 %all-to-all-start.8 = ((f32[16,8,512]{2,1,0:T(8,128)}), f32[16,8,512]{2,1,0:T(8,128)S(1)}, u32[]{:S(2)}, u32[]{:S(2)}) async-start(f32[16,8,512]{2,1,0:T(8,128)} %broadcast_in_dim.11), calls=%async_computation.8 | async-start | bytes 524288 | tf_op jit(solution)/shard_map/all_to_all | solution.py:12
  162.2 7.1 %all-to-all-start.3 = ((f32[4,8,128]{2,1,0:T(8,128)}), f32[4,8,128]{2,1,0:T(8,128)S(1)}, u32[]{:S(2)}, u32[]{:S(2)}) async-start(f32[4,8,128]{2,1,0:T(8,128)} %broadcast_in_dim.9), calls=%async_computation.3 | async-start | bytes 32768 | tf_op jit(solution)/shard_map/all_to_all | solution.py:12
  169.3 13.6 %all-to-all-start.6 = ((f32[16,8,4,128]{3,1,2,0:T(8,128)}), f32[16,8,4,128]{3,1,2,0:T(8,128)S(1)}, u32[]{:S(2)}, u32[]{:S(2)}) async-start(f32[16,8,4,128]{3,1,2,0:T(8,128)} %bitcast.22), calls=%async_computation.6 | async-start | bytes 524288 | tf_op jit(solution)/shard_map/all_to_all | solution.py:77

commit v2 on v0

v2 whole, which is shorter than its diff:
```python
import functools

import jax
import jax.numpy as jnp
from jax import lax
from jax.experimental import pallas as pl
from jax.experimental.pallas import tpu as pltpu
from jax.sharding import PartitionSpec as P

ALL = ("gx", "gy", "gz")
HIGHEST = lax.Precision.HIGHEST
VMEM_BYTES = 48 * 1024 * 1024
ROWS = 8
LANES = 128
ROW_ROW = (((1,), (1,)), ((), ()))
COL_COL = (((0,), (0,)), ((), ()))


def axis_bits(axis):
    bit = lax.axis_size(axis) // 2
    while bit:
        yield bit
        bit //= 2


def swap(array, axis, bits):
    return lax.ppermute(array, axis, [(s, s ^ bits) for s in range(lax.axis_size(axis))])


def swap_sum(array, axis):
    for bit in axis_bits(axis):
        array = array + swap(array, axis, bit)
    return array


def swap_gather(array, axis):
    held, order = array[None], [0]
    for bit in axis_bits(axis):
        held = jnp.concatenate([held, swap(held, axis, bit)], axis=0)
        order += [o ^ bit for o in order]
    return held, order


def gather_rows(array, outer, inner):
    held = array[None, None]
    for dim, axis in ((0, outer), (1, inner)):
        shape = held.shape
        held = held.reshape(*shape[:dim], 1, 1, *shape[dim + 1 :])
        for bit in axis_bits(axis):
            other = swap(held, axis, bit)
            upper = (lax.axis_index(axis) & bit) != 0
            low = jnp.where(upper, other, held)
            high = jnp.where(upper, held, other)
            held = jnp.concatenate([low, high], axis=dim + 1)
            shape = held.shape
            held = held.reshape(*shape[:dim], shape[dim] * shape[dim + 1], 1, *shape[dim + 2 :])
        shape = held.shape
        held = held.reshape(*shape[: dim + 1], *shape[dim + 2 :])
    return held.reshape(-1, array.shape[-1])


def split_terms(array):
    high = lax.reduce_precision(array, 8, 7)
    return high.astype(jnp.bfloat16), (array - high).astype(jnp.bfloat16)


def invert(system):
    size = system.shape[0]
    lanes = lax.broadcasted_iota(jnp.int32, (ROWS, size), 1)
    subs = lax.broadcasted_iota(jnp.int32, (ROWS, size), 0)
    rows = [system[r : r + ROWS] for r in range(0, size, ROWS)]

    def column(block, at):
        return jnp.broadcast_to(block[:, at : at + 1], (ROWS, size))

    for panel in range(size // ROWS):
        first = panel * ROWS
        inside = (lanes >= first) & (lanes < first + ROWS)
        unit = (lanes - first == subs).astype(jnp.float32)
        pivots = [column(rows[panel], first + c) for c in range(ROWS)]
        solved = jnp.where(inside, unit, rows[panel])
        for k in range(ROWS):
            scale = 1.0 / pivots[k][k : k + 1]
            here = subs == k
            top = solved[k : k + 1] * scale
            solved = jnp.where(here, top, solved - pivots[k] * top)
            for c in range(k + 1, ROWS):
                top = pivots[c][k : k + 1] * scale
                pivots[c] = jnp.where(here, top, pivots[c] - pivots[k] * top)
        for r in range(len(rows)):
            if r == panel:
                continue
            old = rows[r]
            new = jnp.where(inside, 0.0, old)
            for c in range(ROWS):
                new = new - column(old, first + c) * solved[c : c + 1]
            rows[r] = new
        rows[panel] = solved
    return jnp.concatenate(rows, axis=0)


def spd_inverse(system):
    square = lax.dot_general(
        system, system, ROW_ROW, precision=HIGHEST, preferred_element_type=jnp.float32
    )
    return invert(square)


def local_kernel(
    shape, field, last_x, last_y, right_y, right_m, last_m, last_part, first_part, *outs
):
    shares, blocks, halves, y_piece = shape
    *terms, flat = outs
    x_cells, y_cells, m_cells = field.shape
    rows = field[...].reshape(x_cells * y_cells, m_cells)
    here = lax.axis_index("gz")

    term = jnp.dot(rows, last_m[...], preferred_element_type=jnp.float32)
    for c in range(flat.shape[0]):
        flat[c] = term[:, c * LANES : (c + 1) * LANES]
    for s in range(shares):
        start = (here ^ s) * (y_cells // shares)
        for h in range(halves):
            for b in range(blocks):
                for k in range(y_piece):
                    j = start + (b * halves + h) * y_piece + k
                    for c in range(flat.shape[0]):
                        terms[s * halves + h][b, k, :, c * LANES : (c + 1) * LANES] = flat[
                            c, pl.ds(j, x_cells, stride=y_cells), :
                        ]

    khatri = last_x[...].astype(jnp.float32)[:, None, :] * last_y[...].astype(jnp.float32)[None]
    khatri = khatri.astype(jnp.bfloat16).reshape(x_cells * y_cells, -1)
    part = lax.dot_general(khatri, rows, COL_COL, preferred_element_type=jnp.float32)

    @pl.when(pl.program_id(0) == 0)
    def _():
        last_part[...] = part

    @pl.when(pl.program_id(0) != 0)
    def _():
        last_part[...] += part

    first = jnp.dot(rows, right_m[...], preferred_element_type=jnp.float32)
    first = first.reshape(x_cells, y_cells, -1) * right_y[...].astype(jnp.float32)[None]
    first_part[...] = jnp.sum(first, axis=1)


def local_products(shape, field, last_x, last_y, right_y, right_m, last_m):
    shares, blocks, halves, y_piece = shape
    x_cells, y_cells, m_cells = field.shape
    rank, cols = last_x.shape[1], last_m.shape[1]
    whole = lambda *dims: pl.BlockSpec(dims, lambda i: (0,) * len(dims))
    term = jax.ShapeDtypeStruct((blocks, y_piece, x_cells, cols), jnp.float32)
    term_spec = pl.BlockSpec((blocks, y_piece, ROWS, cols), lambda i: (0, 0, i, 0))
    pieces = shares * halves
    return pl.pallas_call(
        functools.partial(local_kernel, shape),
        grid=(x_cells // ROWS,),
        in_specs=[
            pl.BlockSpec((ROWS, y_cells, m_cells), lambda i: (i, 0, 0)),
            pl.BlockSpec((ROWS, rank), lambda i: (i, 0)),
            whole(*last_y.shape),
            whole(*right_y.shape),
            whole(*right_m.shape),
            whole(*last_m.shape),
        ],
        out_specs=[
            whole(rank, m_cells),
            pl.BlockSpec((ROWS, cols), lambda i: (i, 0)),
            *([term_spec] * pieces),
        ],
        out_shape=[
            jax.ShapeDtypeStruct((rank, m_cells), jnp.float32),
            jax.ShapeDtypeStruct((x_cells, cols), jnp.float32),
            *([term] * pieces),
        ],
        scratch_shapes=[pltpu.VMEM((cols // LANES, ROWS * y_cells, LANES), jnp.float32)],
        compiler_params=pltpu.CompilerParams(vmem_limit_bytes=VMEM_BYTES),
        name="local_products",
    )(field, last_x, last_y, right_y, right_m, last_m)


def combine_kernel(shares, *refs):
    terms, outs = refs[:shares], refs[shares:]
    me = lax.axis_index("gx")
    for e, out in enumerate(outs):
        total = terms[0][me ^ e]
        for term in terms[1:]:
            total = total + term[me ^ e]
        out[...] = total


def combine(terms):
    blocks, *piece = terms[0].shape
    return pl.pallas_call(
        functools.partial(combine_kernel, len(terms)),
        out_shape=[jax.ShapeDtypeStruct(tuple(piece), jnp.float32)] * blocks,
        compiler_params=pltpu.CompilerParams(vmem_limit_bytes=VMEM_BYTES),
        name="combine",
    )(*terms)


def last_kernel(halves, shares, left, *refs):
    pieces, out = refs[:-1], refs[-1]
    blocks = len(pieces) // halves
    y_piece = pieces[0].shape[0]
    system = shares[:, 0]
    for k in range(1, shares.shape[1]):
        system = system + shares[:, k]
    system = system.reshape(-1, system.shape[-1])
    pinv = jnp.dot(
        spd_inverse(system), system, precision=HIGHEST, preferred_element_type=jnp.float32
    )
    weights = left[...].astype(jnp.bfloat16)
    for h in range(halves):
        for k in range(y_piece):
            column = jnp.concatenate(
                [piece[k] for piece in pieces[h * blocks : (h + 1) * blocks]], axis=0
            )
            high = column.astype(jnp.bfloat16)
            low = (column - high.astype(jnp.float32)).astype(jnp.bfloat16)
            sketched = lax.dot_general(
                weights, high, COL_COL, preferred_element_type=jnp.float32
            ) + lax.dot_general(weights, low, COL_COL, preferred_element_type=jnp.float32)
            core = lax.dot_general(
                sketched, pinv, ROW_ROW, precision=HIGHEST, preferred_element_type=jnp.float32
            )
            at = h * y_piece + k
            out[:, at] = core.reshape(out.shape[0], out.shape[2], out.shape[3])


def solve_last(halves, own, shares, left, pieces):
    y_own = halves * pieces[0].shape[0]
    rank = left.shape[1]
    return pl.pallas_call(
        functools.partial(last_kernel, halves),
        out_shape=jax.ShapeDtypeStruct((rank // own, y_own, own, rank), jnp.float32),
        compiler_params=pltpu.CompilerParams(vmem_limit_bytes=VMEM_BYTES),
        name="solve_last",
    )(shares, left, *pieces)


def first_kernel(rows, all_rows, left, core_first):
    system = lax.dot_general(
        left[...], all_rows[...], COL_COL, precision=HIGHEST, preferred_element_type=jnp.float32
    )
    inverse = spd_inverse(system)
    scores = lax.dot_general(
        rows[...], system, ROW_ROW, precision=HIGHEST, preferred_element_type=jnp.float32
    )
    core_first[...] = jnp.dot(
        scores, inverse, precision=HIGHEST, preferred_element_type=jnp.float32
    )


def solve_first(rows, all_rows, left):
    return pl.pallas_call(
        first_kernel,
        out_shape=jax.ShapeDtypeStruct((rows.shape[0], left.shape[1]), jnp.float32),
        compiler_params=pltpu.CompilerParams(vmem_limit_bytes=VMEM_BYTES),
        name="solve_first",
    )(rows, all_rows, left)


def per_device(flow_field, left_x, last_x, last_y, right_y, right_m, last_m):
    x_cells, y_cells, m_cells = flow_field.shape
    rank = left_x.shape[1]
    cols = right_m.shape[1]
    blocks, shares = lax.axis_size("gx"), lax.axis_size("gz")
    y_own = y_cells // shares // blocks
    halves = 2 if y_own % 2 == 0 else 1

    last_part, first_part, *terms = local_products(
        (shares, blocks, halves, y_own // halves),
        flow_field,
        last_x,
        last_y,
        right_y,
        right_m,
        last_m,
    )

    for at in range(halves, len(terms)):
        terms[at] = swap(terms[at], "gz", at // halves)
    left_all, order = swap_gather(left_x.astype(jnp.float32), "gx")
    left_all = left_all.reshape(-1, rank)
    pieces = []
    for h in range(halves):
        sent = combine(terms[h::halves])
        pieces += [swap(sent[e], "gx", e) if e else sent[e] for e in order]

    group = ("gx", "gy")
    own = rank // lax.axis_size(group)
    last_rows = lax.all_to_all(last_part.reshape(-1, own, m_cells), group, 0, 0, tiled=True)
    last_rows = jnp.sum(last_rows, axis=0)
    both = jnp.dot(
        jnp.concatenate(split_terms(last_rows), axis=0), last_m, preferred_element_type=jnp.float32
    )
    both = both[:own] + both[own:]
    count = lax.axis_size(ALL)
    copies = jnp.broadcast_to(both[None], (count, own, cols))
    system = lax.all_to_all(copies, ALL, 0, 0, tiled=True).reshape(-1, shares, own, cols)
    if own % ROWS:
        system = jnp.sum(system, axis=1).reshape(-1, 1, ROWS, cols)
    core_last = gather_rows(last_rows, *group)

    group = ("gx", "gz")
    devices = lax.axis_size(group)
    own = rank // devices
    if own % ROWS:
        middle = solve_last(halves, rank, system, left_all, pieces)
        middle = middle.reshape(y_own, devices, own, rank).transpose(1, 0, 2, 3)
    else:
        middle = solve_last(halves, own, system, left_all, pieces)
    received = lax.all_to_all(middle, group, 0, 0, tiled=True)
    received = received.reshape(blocks, shares, y_own, own, rank)
    core_middle = received.transpose(3, 1, 0, 2, 4).reshape(own, y_cells, rank)

    first_rows = swap_sum(swap_sum(first_part, "gy"), "gz")
    first_all = swap_gather(first_rows, "gx")[0].reshape(-1, cols)
    first_rows, _ = lax.optimization_barrier((first_rows, middle))
    core_first = solve_first(first_rows, first_all, left_all)
    return (core_first, core_middle, core_last)


def solution(mesh):
    return jax.shard_map(
        per_device,
        mesh=mesh,
        in_specs=(
            P("gx", "gy", "gz"),
            P("gx", None),
            P("gx", None),
            P("gy", None),
            P("gy", None),
            P("gz", None),
            P("gz", None),
        ),
        out_specs=(P("gx", None), P(("gx", "gz"), "gy", None), P(None, "gz")),
        check_vma=False,
    )
```

time: 308 us -> 102 us (0.33)
  waiting for transfers between devices: 186 us -> 20.1 us
  starting transfers between devices: 0.16 us -> 55.3 us
  other arithmetic: 47.3 us -> 1.52 us
  matrix products: 40.5 us -> 0.15 us
  Pallas kernels: 0 us -> 16.4 us
  blocking collectives: 14.3 us -> 0 us
  between operations: 14 us -> 0.86 us
    psum x3 -> x0, waiting for transfers between devices: 116 us -> none  [the longest x1 78.3 us: per_device(): core_last = lax.psum(last_part, ('gx', 'gy'))]
    reduce_scatter x1 -> x0, waiting for transfers between devices: 70.2 us -> none  [per_device(): lax.psum_scatter(jnp.dot(sketched, pinv_last, precision=highest).reshape(...]
    another operation x10 -> x0, other arithmetic: 45.7 us -> none  [the longest x6 24.8 us: normal_solve(): factor = jnp.linalg.cholesky(gram_matrix)]
    ppermute x0 -> x28, starting transfers between devices: none -> 42.4 us  [swap(): lax.ppermute(array, axis, [(s, s ^ bits) for s in range(lax.axis_size(axi...]
    dot_general x10 -> x1, matrix products: 37.9 us -> 0.15 us  [per_device(): jnp.dot(jnp.concatenate(split_terms(last_rows), axis=0), last_m, preferre...]
    ppermute x0 -> x28, waiting for transfers between devices: none -> 19 us  [swap(): lax.ppermute(array, axis, [(s, s ^ bits) for s in range(lax.axis_size(axi...]
    pallas_call x0 -> x5, Pallas kernels: none -> 16.4 us  [the longest x1 5.71 us: solve_last(): pl.pallas_call(functools.partial(last_kernel, halves), out_shape=jax.Shap...]
    psum x1 -> x0, blocking collectives: 14.3 us -> none  [per_device(): first_rows = lax.psum(first_part, ('gy', 'gz'))]
  transfers between devices with their start and end apart: 4 -> 31, of which waited for: 4 -> 12; matrix products, arithmetic and copies ran while one was open for 28% -> 2% of each run, Pallas kernels for 0% -> 11%
where the time goes in v2:
time: 102 us; the launch traced here: 101 us
  starting transfers between devices  55.3 us (54%)
  waiting for transfers between devices  20.1 us (20%)
  Pallas kernels  16.4 us (16%)
  local copies, waits for them, and re-layouts  7.15 us (7%)
  other arithmetic  1.52 us (1%)
    ppermute x28, starting transfers between devices, swap(): lax.ppermute(array, axis, [(s, s ^ bits) for s in range(lax.axis_size(axi...  42.4 us
    ppermute x28, waiting for transfers between devices, swap(): lax.ppermute(array, axis, [(s, s ^ bits) for s in range(lax.axis_size(axi...  19 us
    pallas_call x1, Pallas kernels, solve_last(): pl.pallas_call(functools.partial(last_kernel, halves), out_shape=jax.Shap...  5.71 us
    unnamed x16, local copies, waits for them, and re-layouts  5.66 us
    pallas_call x1, Pallas kernels, local_products(): pl.pallas_call(functools.partial(local_kernel, shape), grid=(x_cells // R...  5.39 us
    pallas_call x1, Pallas kernels, solve_first(): pl.pallas_call(first_kernel, out_shape=jax.ShapeDtypeStruct((rows.shape[0...  5.19 us
    all_to_all x1, starting transfers between devices, per_device(): lax.all_to_all(copies, ALL, 0, 0, tiled=True).reshape(-1, shares, own, cols)  5 us
    all_to_all x1, starting transfers between devices, per_device(): received = lax.all_to_all(middle, group, 0, 0, tiled=True)  3.97 us
  transfers between devices with their start and end apart: 31, of which 12 were waited for; matrix products, arithmetic and copies ran while one was open for 2% of the time, Pallas kernels for 11%

profile of v2, /device:TPU:0, one launch (start us, length us, event | category | flops | bytes accessed | tf_op | source)
XLA Modules:
  0.0 101.5 jit_solution(1920843586908342840)
XLA Ops:
  0.6 1.6 %copy-done = bf16[32,64,512]{2,1,0:T(8,128)(2,1)S(1)} copy-done((bf16[32,64,512]{2,1,0:T(8,128)(2,1)S(1)}, bf16[32,64,512]{2,1,0:T(8,128)(2,1)}, u32[]{:S(2)}) %copy-start) | copy-done | bytes 2097176
  2.2 0.9 copy-done.1
  3.2 0.9 copy-done.3
  4.1 0.8 copy-done.4
  4.9 0.7 copy-done.5
  5.6 0.7 copy-done.6
  6.3 5.4 %local_products.1 = (f32[128,512]{1,0:T(8,128)}, f32[32,256]{1,0:T(8,128)S(1)}, f32[8,2,32,256]{3,2,1,0:T(8,128)S(1)}, f32[8,2,32,256]{3,2,1,0:T(8,128)S(1)}, f3...) custom-call(bf16[32,64,512]{2,1,0:T(8,128)(2,1)S(1)} %copy-done, bf16[32,128]{1,0:T(8,128)(2,1)S(1)} %copy-done.6, ...), custom_call_target="tpu_custom_call" | custom-call | tf_op jit(solution)/shard_map/local_products/pallas_call | solution.py:157
  12.2 3.7 %collective-permute-start.2 = (f32[1,32,128]{2,1,0:T(8,128)S(1)}, f32[1,32,128]{2,1,0:T(8,128)S(1)}, u32[]{:S(2)}, u32[]{:S(2)}) collective-permute-start(f32[1,32,128]{2,1,0:T(8,128)S(1)} %bitcast_convert_fusion), channel_id=1, source_target_pairs={{0,16},{4,20},{8,24},{12,28},{16,0},{20,4},{24,8},{28,12},{1,17},{... | collective-permute-start | bytes 49160 | tf_op jit(solution)/shard_map/ppermute | solution.py:27
  15.8 3.9 %all-to-all-start = ((f32[16,8,512]{2,1,0:T(8,128)}), f32[16,8,512]{2,1,0:T(8,128)S(1)}, u32[]{:S(2)}, u32[]{:S(2)}) async-start(f32[16,8,512]{2,1,0:T(8,128)} %bitcast), calls=%async_computation | async-start | bytes 524288 | tf_op jit(solution)/shard_map/all_to_all | solution.py:295
  19.7 1.6 %collective-permute-start.1 = (f32[32,256]{1,0:T(8,128)S(1)}, f32[32,256]{1,0:T(8,128)S(1)}, u32[]{:S(2)}, u32[]{:S(2)}) collective-permute-start(f32[32,256]{1,0:T(8,128)S(1)} %add.9), channel_id=1, source_target_pairs={{0,1},{1,0},{2,3},{3,2},{4,5},{5,4},{6,7},{7,6},{8,9},{9,8},{10,11... | collective-permute-start | bytes 98312 | tf_op jit(solution)/shard_map/ppermute | solution.py:27
  21.3 1.9 %collective-permute-start.3 = (f32[2,32,128]{2,1,0:T(8,128)S(1)}, f32[2,32,128]{2,1,0:T(8,128)S(1)}, u32[]{:S(2)}, u32[]{:S(2)}) collective-permute-start(f32[2,32,128]{2,1,0:T(8,128)S(1)} %pad_maximum_fusion.8), channel_id=1, source_target_pairs={{0,8},{4,12},{8,0},{12,4},{16,24},{20,28},{24,16},{28,20},{1,9},{5... | collective-permute-start | bytes 98312 | tf_op jit(solution)/shard_map/ppermute | solution.py:27
  23.2 0.5 collective-permute-start.5
  23.7 1.5 %collective-permute-start.13 = (f32[8,2,32,256]{3,2,1,0:T(8,128)S(1)}, f32[8,2,32,256]{3,2,1,0:T(8,128)S(1)}, u32[]{:S(2)}, u32[]{:S(2)}) collective-permute-start(f32[8,2,32,256]{3,2,1,0:T(8,128)S(1)} %get-tuple-element.39), channel_id=1, source_target_pairs={{0,1},{1,0},{2,3},{3,2},{4,5},{5,4},{6,7},{7,6},{8,9},{9,8},{10,11... | collective-permute-start | bytes 1572872 | tf_op jit(solution)/shard_map/ppermute | solution.py:27
  25.3 2.4 %collective-permute-start.21 = (f32[1,32,256]{2,1,0:T(8,128)S(1)}, f32[1,32,256]{2,1,0:T(8,128)S(1)}, u32[]{:S(2)}, u32[]{:S(2)}) collective-permute-start(f32[1,32,256]{2,1,0:T(8,128)S(1)} %bitcast.31), channel_id=1, source_target_pairs={{0,16},{4,20},{8,24},{12,28},{16,0},{20,4},{24,8},{28,12},{1,17},{... | collective-permute-start | bytes 98312 | tf_op jit(solution)/shard_map/ppermute | solution.py:27
  27.7 1.5 %collective-permute-start.4 = (f32[4,32,128]{2,1,0:T(8,128)S(1)}, f32[4,32,128]{2,1,0:T(8,128)S(1)}, u32[]{:S(2)}, u32[]{:S(2)}) collective-permute-start(f32[4,32,128]{2,1,0:T(8,128)S(1)} %pad_maximum_fusion.5), channel_id=1, source_target_pairs={{0,4},{4,0},{8,12},{12,8},{16,20},{20,16},{24,28},{28,24},{1,5},{5... | collective-permute-start | bytes 196616 | tf_op jit(solution)/shard_map/ppermute | solution.py:27
  29.3 1.5 %collective-permute-done.21 = f32[1,32,256]{2,1,0:T(8,128)S(1)} collective-permute-done((f32[1,32,256]{2,1,0:T(8,128)S(1)}, f32[1,32,256]{2,1,0:T(8,128)S(1)}, u32[]{:S(2)}, u32[]{:S(2)}) %collective-permute-start.21) | collective-permute-done | bytes 32800 | tf_op jit(solution)/shard_map/ppermute | solution.py:27
  30.8 0.6 pad_maximum_fusion.6
  32.1 2.8 %collective-permute-start.24 = (f32[1,1,1,8,512]{4,3,1,2,0:T(8,128)S(1)}, f32[1,1,1,8,512]{4,3,1,2,0:T(8,128)S(1)}, u32[]{:S(2)}, u32[]{:S(2)}) collective-permute-start(f32[1,1,1,8,512]{4,3,1,2,0:T(8,128)S(1)} %bitcast.41), channel_id=1, source_target_pairs={{0,16},{4,20},{8,24},{12,28},{16,0},{20,4},{24,8},{28,12},{1,17},{... | collective-permute-start | bytes 49160 | tf_op jit(solution)/shard_map/ppermute | solution.py:27
  35.0 1.8 %collective-permute-done.24 = f32[1,1,1,8,512]{4,3,1,2,0:T(8,128)S(1)} collective-permute-done((f32[1,1,1,8,512]{4,3,1,2,0:T(8,128)S(1)}, f32[1,1,1,8,512]{4,3,1,2,0:T(8,128)S(1)}, u32[]{:S(2)}, u32[]{:S(2)}) %collective-permute-start.24) | collective-permute-done | bytes 16416 | tf_op jit(solution)/shard_map/ppermute | solution.py:27
  36.8 1.4 %collective-permute-start.25 = (f32[2,1,1,8,512]{4,3,1,0,2:T(8,128)S(1)}, f32[2,1,1,8,512]{4,3,1,0,2:T(8,128)S(1)}, u32[]{:S(2)}, u32[]{:S(2)}) collective-permute-start(f32[2,1,1,8,512]{4,3,1,0,2:T(8,128)S(1)} %maximum_bitcast_fusion), channel_id=1, source_target_pairs={{0,8},{4,12},{8,0},{12,4},{16,24},{20,28},{24,16},{28,20},{1,9},{5... | collective-permute-start | bytes 98312 | tf_op jit(solution)/shard_map/ppermute | solution.py:27
  38.3 0.7 broadcast_in_dim.15
  39.0 5.0 %all-to-all-start.1 = ((f32[32,8,256]{2,1,0:T(8,128)}), f32[32,8,256]{2,1,0:T(8,128)S(1)}, u32[]{:S(2)}, u32[]{:S(2)}) async-start(f32[32,8,256]{2,1,0:T(8,128)} %broadcast_in_dim.15), calls=%async_computation.1 | async-start | bytes 524288 | tf_op jit(solution)/shard_map/all_to_all | solution.py:303
  44.1 2.7 %collective-permute-start.6 = (f32[2,32,256]{2,1,0:T(8,128)S(1)}, f32[2,32,256]{2,1,0:T(8,128)S(1)}, u32[]{:S(2)}, u32[]{:S(2)}) collective-permute-start(f32[2,32,256]{2,1,0:T(8,128)S(1)} %get-tuple-element.31), channel_id=1, source_target_pairs={{0,16},{4,20},{8,24},{12,28},{16,0},{20,4},{24,8},{28,12},{1,17},{... | collective-permute-start | bytes 196616 | tf_op jit(solution)/shard_map/ppermute | solution.py:27
  46.8 1.5 %collective-permute-start.7 = (f32[2,32,256]{2,1,0:T(8,128)S(1)}, f32[2,32,256]{2,1,0:T(8,128)S(1)}, u32[]{:S(2)}, u32[]{:S(2)}) collective-permute-start(f32[2,32,256]{2,1,0:T(8,128)S(1)} %get-tuple-element.32), channel_id=1, source_target_pairs={{0,8},{4,12},{8,0},{12,4},{16,24},{20,28},{24,16},{28,20},{1,9},{5... | collective-permute-start | bytes 196616 | tf_op jit(solution)/shard_map/ppermute | solution.py:27
  48.3 0.7 collective-permute-done.13.refs_1_
  49.0 1.6 %collective-permute-start.8 = (f32[2,32,256]{2,1,0:T(8,128)S(1)}, f32[2,32,256]{2,1,0:T(8,128)S(1)}, u32[]{:S(2)}, u32[]{:S(2)}) collective-permute-start(f32[2,32,256]{2,1,0:T(8,128)S(1)} %get-tuple-element.33), channel_id=1, source_target_pairs={{0,24},{4,28},{8,16},{12,20},{16,8},{20,12},{24,0},{28,4},{1,25},{... | collective-permute-start | bytes 196616 | tf_op jit(solution)/shard_map/ppermute | solution.py:27
  50.7 2.9 %collective-permute-start.9 = (f32[2,32,256]{2,1,0:T(8,128)S(1)}, f32[2,32,256]{2,1,0:T(8,128)S(1)}, u32[]{:S(2)}, u32[]{:S(2)}) collective-permute-start(f32[2,32,256]{2,1,0:T(8,128)S(1)} %get-tuple-element.34), channel_id=1, source_target_pairs={{0,4},{4,0},{8,12},{12,8},{16,20},{20,16},{24,28},{28,24},{1,5},{5... | collective-permute-start | bytes 196616 | tf_op jit(solution)/shard_map/ppermute | solution.py:27
  53.7 5.7 %collective-permute-done.6.refs_1_ = f32[2,32,256]{2,1,0:T(8,128)S(1)} collective-permute-done((f32[2,32,256]{2,1,0:T(8,128)S(1)}, f32[2,32,256]{2,1,0:T(8,128)S(1)}, u32[]{:S(2)}, u32[]{:S(2)}) %collective-permute-start.6) | collective-permute-done | bytes 65568 | tf_op jit(solution)/shard_map/ppermute | solution.py:27
  59.5 2.1 %collective-permute-start.12 = (f32[2,32,256]{2,1,0:T(8,128)S(1)}, f32[2,32,256]{2,1,0:T(8,128)S(1)}, u32[]{:S(2)}, u32[]{:S(2)}) collective-permute-start(f32[2,32,256]{2,1,0:T(8,128)S(1)} %get-tuple-element.37), channel_id=1, source_target_pairs={{0,28},{4,24},{8,20},{12,16},{16,12},{20,8},{24,4},{28,0},{1,29},{... | collective-permute-start | bytes 196616 | tf_op jit(solution)/shard_map/ppermute | solution.py:27
  61.6 2.3 %collective-permute-start.14 = (f32[2,32,256]{2,1,0:T(8,128)S(1)}, f32[2,32,256]{2,1,0:T(8,128)S(1)}, u32[]{:S(2)}, u32[]{:S(2)}) collective-permute-start(f32[2,32,256]{2,1,0:T(8,128)S(1)} %get-tuple-element.41), channel_id=1, source_target_pairs={{0,16},{4,20},{8,24},{12,28},{16,0},{20,4},{24,8},{28,12},{1,17},{... | collective-permute-start | bytes 196616 | tf_op jit(solution)/shard_map/ppermute | solution.py:27
  63.9 0.9 collective-permute-start.15
  64.9 1.2 %collective-permute-start.16 = (f32[2,32,256]{2,1,0:T(8,128)S(1)}, f32[2,32,256]{2,1,0:T(8,128)S(1)}, u32[]{:S(2)}, u32[]{:S(2)}) collective-permute-start(f32[2,32,256]{2,1,0:T(8,128)S(1)} %get-tuple-element.43), channel_id=1, source_target_pairs={{0,24},{4,28},{8,16},{12,20},{16,8},{20,12},{24,0},{28,4},{1,25},{... | collective-permute-start | bytes 196616 | tf_op jit(solution)/shard_map/ppermute | solution.py:27
  66.1 0.8 collective-permute-start.26
  67.3 1.4 %collective-permute-start.23 = (f32[4,32,256]{2,1,0:T(8,128)S(1)}, f32[4,32,256]{2,1,0:T(8,128)S(1)}, u32[]{:S(2)}, u32[]{:S(2)}) collective-permute-start(f32[4,32,256]{2,1,0:T(8,128)S(1)} %pad_maximum_fusion.3), channel_id=1, source_target_pairs={{0,4},{4,0},{8,12},{12,8},{16,20},{20,16},{24,28},{28,24},{1,5},{5... | collective-permute-start | bytes 393224 | tf_op jit(solution)/shard_map/ppermute | solution.py:27
  68.7 1.5 %collective-permute-done.14.refs_9_ = f32[2,32,256]{2,1,0:T(8,128)S(1)} collective-permute-done((f32[2,32,256]{2,1,0:T(8,128)S(1)}, f32[2,32,256]{2,1,0:T(8,128)S(1)}, u32[]{:S(2)}, u32[]{:S(2)}) %collective-permute-start.14) | collective-permute-done | bytes 65568 | tf_op jit(solution)/shard_map/ppermute | solution.py:27
  70.2 1.7 %collective-permute-start.17 = (f32[2,32,256]{2,1,0:T(8,128)S(1)}, f32[2,32,256]{2,1,0:T(8,128)S(1)}, u32[]{:S(2)}, u32[]{:S(2)}) collective-permute-start(f32[2,32,256]{2,1,0:T(8,128)S(1)} %get-tuple-element.44), channel_id=1, source_target_pairs={{0,4},{4,0},{8,12},{12,8},{16,20},{20,16},{24,28},{28,24},{1,5},{5... | collective-permute-start | bytes 196616 | tf_op jit(solution)/shard_map/ppermute | solution.py:27
  72.0 0.9 collective-permute-start.18
  72.9 2.7 %collective-permute-start.19 = (f32[2,32,256]{2,1,0:T(8,128)S(1)}, f32[2,32,256]{2,1,0:T(8,128)S(1)}, u32[]{:S(2)}, u32[]{:S(2)}) collective-permute-start(f32[2,32,256]{2,1,0:T(8,128)S(1)} %get-tuple-element.46), channel_id=1, source_target_pairs={{0,12},{4,8},{8,4},{12,0},{16,28},{20,24},{24,20},{28,16},{1,13},{... | collective-permute-start | bytes 196616 | tf_op jit(solution)/shard_map/ppermute | solution.py:27
  75.6 1.4 %collective-permute-start.20 = (f32[2,32,256]{2,1,0:T(8,128)S(1)}, f32[2,32,256]{2,1,0:T(8,128)S(1)}, u32[]{:S(2)}, u32[]{:S(2)}) collective-permute-start(f32[2,32,256]{2,1,0:T(8,128)S(1)} %get-tuple-element.47), channel_id=1, source_target_pairs={{0,28},{4,24},{8,20},{12,16},{16,12},{20,8},{24,4},{28,0},{1,29},{... | collective-permute-start | bytes 196616 | tf_op jit(solution)/shard_map/ppermute | solution.py:27
  77.0 2.4 %collective-permute-done.18.refs_13_ = f32[2,32,256]{2,1,0:T(8,128)S(1)} collective-permute-done((f32[2,32,256]{2,1,0:T(8,128)S(1)}, f32[2,32,256]{2,1,0:T(8,128)S(1)}, u32[]{:S(2)}, u32[]{:S(2)}) %collective-permute-start.18) | collective-permute-done | bytes 65568 | tf_op jit(solution)/shard_map/ppermute | solution.py:27
  79.4 3.1 %collective-permute-done.20.refs_15_ = f32[2,32,256]{2,1,0:T(8,128)S(1)} collective-permute-done((f32[2,32,256]{2,1,0:T(8,128)S(1)}, f32[2,32,256]{2,1,0:T(8,128)S(1)}, u32[]{:S(2)}, u32[]{:S(2)}) %collective-permute-start.20) | collective-permute-done | bytes 65568 | tf_op jit(solution)/shard_map/ppermute | solution.py:27
  82.5 5.7 %solve_last.1 = f32[16,4,8,128]{3,2,1,0:T(8,128)} custom-call(f32[16,2,8,256]{3,2,1,0:T(8,128)S(1)} %bitcast.30, f32[256,128]{1,0:T(8,128)S(1)} %bitcast.27, f32[2,32,256]{2,1,0:T(8,128)S(1)} %get-tuple-element.30.refs_0_, f32[2,32,256]{2,1,0:T(8,128)S(1)} %collective-permute-done.6.refs_1_, f32[2,32,256]{2,1,0:T(8,128)S(1)} %collective-permute-done.7.refs_2_, ...), custom_call_target="tpu_custom_call" | custom-call | tf_op jit(solution)/shard_map/solve_last/pallas_call | solution.py:236
  88.3 4.0 %all-to-all-start.2 = ((f32[16,4,8,128]{3,2,1,0:T(8,128)}), f32[16,4,8,128]{3,2,1,0:T(8,128)S(1)}, u32[]{:S(2)}, u32[]{:S(2)}) async-start(f32[16,4,8,128]{3,2,1,0:T(8,128)} %solve_last.1), calls=%async_computation.2 | async-start | bytes 524288 | tf_op jit(solution)/shard_map/all_to_all | solution.py:316
  92.4 1.3 %collective-permute-done.27 = f32[8,1,1,8,512]{4,3,2,0,1:T(8,128)S(1)} collective-permute-done((f32[8,1,1,8,512]{4,3,2,0,1:T(8,128)S(1)}, f32[8,1,1,8,512]{4,3,2,0,1:T(8,128)S(1)}, u32[]{:S(2)}, u32[]{:S(2)}) %collective-permute-start.27) | collective-permute-done | bytes 131104 | tf_op jit(solution)/shard_map/ppermute | solution.py:27
  93.7 0.7 pad_maximum_fusion.1
  94.4 5.2 %solve_first.1 = f32[32,128]{1,0:T(8,128)} custom-call(f32[32,256]{1,0:T(8,128)S(1)} %add.10.rows, f32[256,256]{1,0:T(8,128)S(1)} %bitcast.29, f32[256,128]{1,0:T(8,128)S(1)} %bitcast.28), custom_call_target="tpu_custom_call" | custom-call | tf_op jit(solution)/shard_map/solve_first/pallas_call | solution.py:258
  99.6 1.1 %all-to-all-done.2 = f32[16,4,8,128]{3,2,1,0:T(8,128)S(1)} async-done(((f32[16,4,8,128]{3,2,1,0:T(8,128)}), f32[16,4,8,128]{3,2,1,0:T(8,128)S(1)}, u32[]{:S(2)}, u32[]{:S(2)}) %all-to-all-start.2) | async-done | bytes 262176 | tf_op jit(solution)/shard_map/all_to_all | solution.py:316
  100.7 0.8 copy.10
  (58 shorter events, 2.2 us)
Async XLA Ops:
  0.6 1.6 %copy-start = (bf16[32,64,512]{2,1,0:T(8,128)(2,1)S(1)}, bf16[32,64,512]{2,1,0:T(8,128)(2,1)}, u32[]{:S(2)}) copy-start(bf16[32,64,512]{2,1,0:T(8,128)(2,1)} %field.1) | copy-start | bytes 6291460
  2.2 0.9 copy-start.1
  3.2 0.9 copy-start.3
  4.1 0.8 copy-start.4
  4.9 0.7 copy-start.5
  5.6 0.7 copy-start.6
  6.3 5.9 %copy-start.7 = (bf16[32,128]{1,0:T(8,128)(2,1)S(1)}, bf16[32,128]{1,0:T(8,128)(2,1)}, u32[]{:S(2)}) copy-start(bf16[32,128]{1,0:T(8,128)(2,1)} %param.8) | copy-start | bytes 24580
  6.3 28.6 %copy-start.2 = (bf16[512,256]{1,0:T(8,128)(2,1)S(1)}, bf16[512,256]{1,0:T(8,128)(2,1)}, u32[]{:S(2)}) copy-start(bf16[512,256]{1,0:T(8,128)(2,1)} %last_m.1) | copy-start | bytes 786436
  11.7 8.0 %collective-permute-start = (f32[32,256]{1,0:T(8,128)S(1)}, f32[32,256]{1,0:T(8,128)S(1)}, u32[]{:S(2)}, u32[]{:S(2)}) collective-permute-start(f32[32,256]{1,0:T(8,128)S(1)} %get-tuple-element.26), channel_id=1, source_target_pairs={{0,2},{2,0},{1,3},{3,1},{4,6},{6,4},{5,7},{7,5},{8,10},{10,8},{9,1... | collective-permute-start | bytes 98312 | tf_op jit(solution)/shard_map/ppermute | solution.py:27
  12.2 9.2 %collective-permute-start.2 = (f32[1,32,128]{2,1,0:T(8,128)S(1)}, f32[1,32,128]{2,1,0:T(8,128)S(1)}, u32[]{:S(2)}, u32[]{:S(2)}) collective-permute-start(f32[1,32,128]{2,1,0:T(8,128)S(1)} %bitcast_convert_fusion), channel_id=1, source_target_pairs={{0,16},{4,20},{8,24},{12,28},{16,0},{20,4},{24,8},{28,12},{1,17},{... | collective-permute-start | bytes 49160 | tf_op jit(solution)/shard_map/ppermute | solution.py:27
  15.8 16.3 %all-to-all-start = ((f32[16,8,512]{2,1,0:T(8,128)}), f32[16,8,512]{2,1,0:T(8,128)S(1)}, u32[]{:S(2)}, u32[]{:S(2)}) async-start(f32[16,8,512]{2,1,0:T(8,128)} %bitcast), calls=%async_computation | async-start | bytes 524288 | tf_op jit(solution)/shard_map/all_to_all | solution.py:295
  19.7 5.5 %collective-permute-start.1 = (f32[32,256]{1,0:T(8,128)S(1)}, f32[32,256]{1,0:T(8,128)S(1)}, u32[]{:S(2)}, u32[]{:S(2)}) collective-permute-start(f32[32,256]{1,0:T(8,128)S(1)} %add.9), channel_id=1, source_target_pairs={{0,1},{1,0},{2,3},{3,2},{4,5},{5,4},{6,7},{7,6},{8,9},{9,8},{10,11... | collective-permute-start | bytes 98312 | tf_op jit(solution)/shard_map/ppermute | solution.py:27
  21.3 6.4 %collective-permute-start.3 = (f32[2,32,128]{2,1,0:T(8,128)S(1)}, f32[2,32,128]{2,1,0:T(8,128)S(1)}, u32[]{:S(2)}, u32[]{:S(2)}) collective-permute-start(f32[2,32,128]{2,1,0:T(8,128)S(1)} %pad_maximum_fusion.8), channel_id=1, source_target_pairs={{0,8},{4,12},{8,0},{12,4},{16,24},{20,28},{24,16},{28,20},{1,9},{5... | collective-permute-start | bytes 98312 | tf_op jit(solution)/shard_map/ppermute | solution.py:27
  23.2 20.8 %collective-permute-start.5 = (f32[8,2,32,256]{3,2,1,0:T(8,128)}, f32[8,2,32,256]{3,2,1,0:T(8,128)S(1)}, u32[]{:S(2)}, u32[]{:S(2)}) collective-permute-start(f32[8,2,32,256]{3,2,1,0:T(8,128)} %get-tuple-element.29), channel_id=1, source_target_pairs={{0,1},{1,0},{2,3},{3,2},{4,5},{5,4},{6,7},{7,6},{8,9},{9,8},{10,11... | collective-permute-start | bytes 1572872 | tf_op jit(solution)/shard_map/ppermute | solution.py:27
  23.7 25.3 %collective-permute-start.13 = (f32[8,2,32,256]{3,2,1,0:T(8,128)S(1)}, f32[8,2,32,256]{3,2,1,0:T(8,128)S(1)}, u32[]{:S(2)}, u32[]{:S(2)}) collective-permute-start(f32[8,2,32,256]{3,2,1,0:T(8,128)S(1)} %get-tuple-element.39), channel_id=1, source_target_pairs={{0,1},{1,0},{2,3},{3,2},{4,5},{5,4},{6,7},{7,6},{8,9},{9,8},{10,11... | collective-permute-start | bytes 1572872 | tf_op jit(solution)/shard_map/ppermute | solution.py:27
  25.3 5.5 %collective-permute-start.21 = (f32[1,32,256]{2,1,0:T(8,128)S(1)}, f32[1,32,256]{2,1,0:T(8,128)S(1)}, u32[]{:S(2)}, u32[]{:S(2)}) collective-permute-start(f32[1,32,256]{2,1,0:T(8,128)S(1)} %bitcast.31), channel_id=1, source_target_pairs={{0,16},{4,20},{8,24},{12,28},{16,0},{20,4},{24,8},{28,12},{1,17},{... | collective-permute-start | bytes 98312 | tf_op jit(solution)/shard_map/ppermute | solution.py:27
  27.7 4.3 %collective-permute-start.4 = (f32[4,32,128]{2,1,0:T(8,128)S(1)}, f32[4,32,128]{2,1,0:T(8,128)S(1)}, u32[]{:S(2)}, u32[]{:S(2)}) collective-permute-start(f32[4,32,128]{2,1,0:T(8,128)S(1)} %pad_maximum_fusion.5), channel_id=1, source_target_pairs={{0,4},{4,0},{8,12},{12,8},{16,20},{20,16},{24,28},{28,24},{1,5},{5... | collective-permute-start | bytes 196616 | tf_op jit(solution)/shard_map/ppermute | solution.py:27
  31.4 22.3 %collective-permute-start.22 = (f32[2,32,256]{2,1,0:T(8,128)}, f32[2,32,256]{2,1,0:T(8,128)S(1)}, u32[]{:S(2)}, u32[]{:S(2)}) collective-permute-start(f32[2,32,256]{2,1,0:T(8,128)} %pad_maximum_fusion.6), channel_id=1, source_target_pairs={{0,8},{4,12},{8,0},{12,4},{16,24},{20,28},{24,16},{28,20},{1,9},{5... | collective-permute-start | bytes 196616 | tf_op jit(solution)/shard_map/ppermute | solution.py:27
  32.1 4.7 %collective-permute-start.24 = (f32[1,1,1,8,512]{4,3,1,2,0:T(8,128)S(1)}, f32[1,1,1,8,512]{4,3,1,2,0:T(8,128)S(1)}, u32[]{:S(2)}, u32[]{:S(2)}) collective-permute-start(f32[1,1,1,8,512]{4,3,1,2,0:T(8,128)S(1)} %bitcast.41), channel_id=1, source_target_pairs={{0,16},{4,20},{8,24},{12,28},{16,0},{20,4},{24,8},{28,12},{1,17},{... | collective-permute-start | bytes 49160 | tf_op jit(solution)/shard_map/ppermute | solution.py:27
  36.8 13.9 %collective-permute-start.25 = (f32[2,1,1,8,512]{4,3,1,0,2:T(8,128)S(1)}, f32[2,1,1,8,512]{4,3,1,0,2:T(8,128)S(1)}, u32[]{:S(2)}, u32[]{:S(2)}) collective-permute-start(f32[2,1,1,8,512]{4,3,1,0,2:T(8,128)S(1)} %maximum_bitcast_fusion), channel_id=1, source_target_pairs={{0,8},{4,12},{8,0},{12,4},{16,24},{20,28},{24,16},{28,20},{1,9},{5... | collective-permute-start | bytes 98312 | tf_op jit(solution)/shard_map/ppermute | solution.py:27
  39.0 43.5 %all-to-all-start.1 = ((f32[32,8,256]{2,1,0:T(8,128)}), f32[32,8,256]{2,1,0:T(8,128)S(1)}, u32[]{:S(2)}, u32[]{:S(2)}) async-start(f32[32,8,256]{2,1,0:T(8,128)} %broadcast_in_dim.15), calls=%async_computation.1 | async-start | bytes 524288 | tf_op jit(solution)/shard_map/all_to_all | solution.py:303
  44.1 15.4 %collective-permute-start.6 = (f32[2,32,256]{2,1,0:T(8,128)S(1)}, f32[2,32,256]{2,1,0:T(8,128)S(1)}, u32[]{:S(2)}, u32[]{:S(2)}) collective-permute-start(f32[2,32,256]{2,1,0:T(8,128)S(1)} %get-tuple-element.31), channel_id=1, source_target_pairs={{0,16},{4,20},{8,24},{12,28},{16,0},{20,4},{24,8},{28,12},{1,17},{... | collective-permute-start | bytes 196616 | tf_op jit(solution)/shard_map/ppermute | solution.py:27
  46.8 12.7 %collective-permute-start.7 = (f32[2,32,256]{2,1,0:T(8,128)S(1)}, f32[2,32,256]{2,1,0:T(8,128)S(1)}, u32[]{:S(2)}, u32[]{:S(2)}) collective-permute-start(f32[2,32,256]{2,1,0:T(8,128)S(1)} %get-tuple-element.32), channel_id=1, source_target_pairs={{0,8},{4,12},{8,0},{12,4},{16,24},{20,28},{24,16},{28,20},{1,9},{5... | collective-permute-start | bytes 196616 | tf_op jit(solution)/shard_map/ppermute | solution.py:27
  49.0 12.6 %collective-permute-start.8 = (f32[2,32,256]{2,1,0:T(8,128)S(1)}, f32[2,32,256]{2,1,0:T(8,128)S(1)}, u32[]{:S(2)}, u32[]{:S(2)}) collective-permute-start(f32[2,32,256]{2,1,0:T(8,128)S(1)} %get-tuple-element.33), channel_id=1, source_target_pairs={{0,24},{4,28},{8,16},{12,20},{16,8},{20,12},{24,0},{28,4},{1,25},{... | collective-permute-start | bytes 196616 | tf_op jit(solution)/shard_map/ppermute | solution.py:27
  50.7 13.2 %collective-permute-start.9 = (f32[2,32,256]{2,1,0:T(8,128)S(1)}, f32[2,32,256]{2,1,0:T(8,128)S(1)}, u32[]{:S(2)}, u32[]{:S(2)}) collective-permute-start(f32[2,32,256]{2,1,0:T(8,128)S(1)} %get-tuple-element.34), channel_id=1, source_target_pairs={{0,4},{4,0},{8,12},{12,8},{16,20},{20,16},{24,28},{28,24},{1,5},{5... | collective-permute-start | bytes 196616 | tf_op jit(solution)/shard_map/ppermute | solution.py:27
  53.7 11.2 %collective-permute-start.10 = (f32[2,32,256]{2,1,0:T(8,128)S(1)}, f32[2,32,256]{2,1,0:T(8,128)S(1)}, u32[]{:S(2)}, u32[]{:S(2)}) collective-permute-start(f32[2,32,256]{2,1,0:T(8,128)S(1)} %get-tuple-element.35), channel_id=1, source_target_pairs={{0,20},{4,16},{8,28},{12,24},{16,4},{20,0},{24,12},{28,8},{1,21},{... | collective-permute-start | bytes 196616 | tf_op jit(solution)/shard_map/ppermute | solution.py:27
  59.5 6.6 %collective-permute-start.11 = (f32[2,32,256]{2,1,0:T(8,128)S(1)}, f32[2,32,256]{2,1,0:T(8,128)S(1)}, u32[]{:S(2)}, u32[]{:S(2)}) collective-permute-start(f32[2,32,256]{2,1,0:T(8,128)S(1)} %get-tuple-element.36), channel_id=1, source_target_pairs={{0,12},{4,8},{8,4},{12,0},{16,28},{20,24},{24,20},{28,16},{1,13},{... | collective-permute-start | bytes 196616 | tf_op jit(solution)/shard_map/ppermute | solution.py:27
  59.5 7.8 %collective-permute-start.12 = (f32[2,32,256]{2,1,0:T(8,128)S(1)}, f32[2,32,256]{2,1,0:T(8,128)S(1)}, u32[]{:S(2)}, u32[]{:S(2)}) collective-permute-start(f32[2,32,256]{2,1,0:T(8,128)S(1)} %get-tuple-element.37), channel_id=1, source_target_pairs={{0,28},{4,24},{8,20},{12,16},{16,12},{20,8},{24,4},{28,0},{1,29},{... | collective-permute-start | bytes 196616 | tf_op jit(solution)/shard_map/ppermute | solution.py:27
  61.6 8.6 %collective-permute-start.14 = (f32[2,32,256]{2,1,0:T(8,128)S(1)}, f32[2,32,256]{2,1,0:T(8,128)S(1)}, u32[]{:S(2)}, u32[]{:S(2)}) collective-permute-start(f32[2,32,256]{2,1,0:T(8,128)S(1)} %get-tuple-element.41), channel_id=1, source_target_pairs={{0,16},{4,20},{8,24},{12,28},{16,0},{20,4},{24,8},{28,12},{1,17},{... | collective-permute-start | bytes 196616 | tf_op jit(solution)/shard_map/ppermute | solution.py:27
  63.9 8.0 %collective-permute-start.15 = (f32[2,32,256]{2,1,0:T(8,128)S(1)}, f32[2,32,256]{2,1,0:T(8,128)S(1)}, u32[]{:S(2)}, u32[]{:S(2)}) collective-permute-start(f32[2,32,256]{2,1,0:T(8,128)S(1)} %get-tuple-element.42), channel_id=1, source_target_pairs={{0,8},{4,12},{8,0},{12,4},{16,24},{20,28},{24,16},{28,20},{1,9},{5... | collective-permute-start | bytes 196616 | tf_op jit(solution)/shard_map/ppermute | solution.py:27
  64.9 8.0 %collective-permute-start.16 = (f32[2,32,256]{2,1,0:T(8,128)S(1)}, f32[2,32,256]{2,1,0:T(8,128)S(1)}, u32[]{:S(2)}, u32[]{:S(2)}) collective-permute-start(f32[2,32,256]{2,1,0:T(8,128)S(1)} %get-tuple-element.43), channel_id=1, source_target_pairs={{0,24},{4,28},{8,16},{12,20},{16,8},{20,12},{24,0},{28,4},{1,25},{... | collective-permute-start | bytes 196616 | tf_op jit(solution)/shard_map/ppermute | solution.py:27
  66.1 9.5 %collective-permute-start.26 = (f32[4,1,1,8,512]{4,3,1,0,2:T(8,128)S(1)}, f32[4,1,1,8,512]{4,3,1,0,2:T(8,128)S(1)}, u32[]{:S(2)}, u32[]{:S(2)}) collective-permute-start(f32[4,1,1,8,512]{4,3,1,0,2:T(8,128)S(1)} %bitcast.39), channel_id=1, source_target_pairs={{0,4},{4,0},{8,12},{12,8},{16,20},{20,16},{24,28},{28,24},{1,5},{5... | collective-permute-start | bytes 196616 | tf_op jit(solution)/shard_map/ppermute | solution.py:27
  67.3 25.1 %collective-permute-start.23 = (f32[4,32,256]{2,1,0:T(8,128)S(1)}, f32[4,32,256]{2,1,0:T(8,128)S(1)}, u32[]{:S(2)}, u32[]{:S(2)}) collective-permute-start(f32[4,32,256]{2,1,0:T(8,128)S(1)} %pad_maximum_fusion.3), channel_id=1, source_target_pairs={{0,4},{4,0},{8,12},{12,8},{16,20},{20,16},{24,28},{28,24},{1,5},{5... | collective-permute-start | bytes 393224 | tf_op jit(solution)/shard_map/ppermute | solution.py:27
  70.2 6.8 %collective-permute-start.17 = (f32[2,32,256]{2,1,0:T(8,128)S(1)}, f32[2,32,256]{2,1,0:T(8,128)S(1)}, u32[]{:S(2)}, u32[]{:S(2)}) collective-permute-start(f32[2,32,256]{2,1,0:T(8,128)S(1)} %get-tuple-element.44), channel_id=1, source_target_pairs={{0,4},{4,0},{8,12},{12,8},{16,20},{20,16},{24,28},{28,24},{1,5},{5... | collective-permute-start | bytes 196616 | tf_op jit(solution)/shard_map/ppermute | solution.py:27
  72.0 7.5 %collective-permute-start.18 = (f32[2,32,256]{2,1,0:T(8,128)S(1)}, f32[2,32,256]{2,1,0:T(8,128)S(1)}, u32[]{:S(2)}, u32[]{:S(2)}) collective-permute-start(f32[2,32,256]{2,1,0:T(8,128)S(1)} %get-tuple-element.45), channel_id=1, source_target_pairs={{0,20},{4,16},{8,28},{12,24},{16,4},{20,0},{24,12},{28,8},{1,21},{... | collective-permute-start | bytes 196616 | tf_op jit(solution)/shard_map/ppermute | solution.py:27
  72.9 6.5 %collective-permute-start.19 = (f32[2,32,256]{2,1,0:T(8,128)S(1)}, f32[2,32,256]{2,1,0:T(8,128)S(1)}, u32[]{:S(2)}, u32[]{:S(2)}) collective-permute-start(f32[2,32,256]{2,1,0:T(8,128)S(1)} %get-tuple-element.46), channel_id=1, source_target_pairs={{0,12},{4,8},{8,4},{12,0},{16,28},{20,24},{24,20},{28,16},{1,13},{... | collective-permute-start | bytes 196616 | tf_op jit(solution)/shard_map/ppermute | solution.py:27
  75.6 7.0 %collective-permute-start.20 = (f32[2,32,256]{2,1,0:T(8,128)S(1)}, f32[2,32,256]{2,1,0:T(8,128)S(1)}, u32[]{:S(2)}, u32[]{:S(2)}) collective-permute-start(f32[2,32,256]{2,1,0:T(8,128)S(1)} %get-tuple-element.47), channel_id=1, source_target_pairs={{0,28},{4,24},{8,20},{12,16},{16,12},{20,8},{24,4},{28,0},{1,29},{... | collective-permute-start | bytes 196616 | tf_op jit(solution)/shard_map/ppermute | solution.py:27
  88.3 12.4 %all-to-all-start.2 = ((f32[16,4,8,128]{3,2,1,0:T(8,128)}), f32[16,4,8,128]{3,2,1,0:T(8,128)S(1)}, u32[]{:S(2)}, u32[]{:S(2)}) async-start(f32[16,4,8,128]{3,2,1,0:T(8,128)} %solve_last.1), calls=%async_computation.2 | async-start | bytes 524288 | tf_op jit(solution)/shard_map/all_to_all | solution.py:316
  92.3 1.4 %collective-permute-start.27 = (f32[8,1,1,8,512]{4,3,2,0,1:T(8,128)S(1)}, f32[8,1,1,8,512]{4,3,2,0,1:T(8,128)S(1)}, u32[]{:S(2)}, u32[]{:S(2)}) collective-permute-start(f32[8,1,1,8,512]{4,3,2,0,1:T(8,128)S(1)} %bitcast.36), channel_id=1, source_target_pairs={{0,2},{2,0},{1,3},{3,1},{4,6},{6,4},{5,7},{7,5},{8,10},{10,8},{9,1... | collective-permute-start | bytes 393224 | tf_op jit(solution)/shard_map/ppermute | solution.py:27

commit v3 on v2

v3 whole, which is shorter than its diff:
```python
import functools

import jax
import jax.numpy as jnp
from jax import lax
from jax.experimental import pallas as pl
from jax.experimental.pallas import tpu as pltpu
from jax.sharding import PartitionSpec as P

ALL = ("gx", "gy", "gz")
HIGHEST = lax.Precision.HIGHEST
VMEM_BYTES = 48 * 1024 * 1024
LOCAL_VMEM_BYTES = 63 * 1024 * 1024
ROWS = 8
LANES = 128
ROW_ROW = (((1,), (1,)), ((), ()))
COL_COL = (((0,), (0,)), ((), ()))


def axis_bits(axis):
    bit = lax.axis_size(axis) // 2
    while bit:
        yield bit
        bit //= 2


def swap(array, axis, bits):
    return lax.ppermute(array, axis, [(s, s ^ bits) for s in range(lax.axis_size(axis))])


def swap_sum(array, axis):
    for bit in axis_bits(axis):
        array = array + swap(array, axis, bit)
    return array


def swap_gather(array, axis):
    held, order = array[None], [0]
    for bit in axis_bits(axis):
        held = jnp.concatenate([held, swap(held, axis, bit)], axis=0)
        order += [o ^ bit for o in order]
    return held, order


def gather_rows(array, outer, inner):
    held = array[None, None]
    for dim, axis in ((0, outer), (1, inner)):
        shape = held.shape
        held = held.reshape(*shape[:dim], 1, 1, *shape[dim + 1 :])
        for bit in axis_bits(axis):
            other = swap(held, axis, bit)
            upper = (lax.axis_index(axis) & bit) != 0
            low = jnp.where(upper, other, held)
            high = jnp.where(upper, held, other)
            held = jnp.concatenate([low, high], axis=dim + 1)
            shape = held.shape
            held = held.reshape(*shape[:dim], shape[dim] * shape[dim + 1], 1, *shape[dim + 2 :])
        shape = held.shape
        held = held.reshape(*shape[: dim + 1], *shape[dim + 2 :])
    return held.reshape(-1, array.shape[-1])


def split_terms(array):
    high = lax.reduce_precision(array, 8, 7)
    return high.astype(jnp.bfloat16), (array - high).astype(jnp.bfloat16)


def invert(system):
    size = system.shape[0]
    lanes = lax.broadcasted_iota(jnp.int32, (ROWS, size), 1)
    subs = lax.broadcasted_iota(jnp.int32, (ROWS, size), 0)
    rows = [system[r : r + ROWS] for r in range(0, size, ROWS)]

    def column(block, at):
        return jnp.broadcast_to(block[:, at : at + 1], (ROWS, size))

    for panel in range(size // ROWS):
        first = panel * ROWS
        inside = (lanes >= first) & (lanes < first + ROWS)
        unit = (lanes - first == subs).astype(jnp.float32)
        pivots = [column(rows[panel], first + c) for c in range(ROWS)]
        solved = jnp.where(inside, unit, rows[panel])
        for k in range(ROWS):
            scale = 1.0 / pivots[k][k : k + 1]
            here = subs == k
            top = solved[k : k + 1] * scale
            solved = jnp.where(here, top, solved - pivots[k] * top)
            for c in range(k + 1, ROWS):
                top = pivots[c][k : k + 1] * scale
                pivots[c] = jnp.where(here, top, pivots[c] - pivots[k] * top)
        for r in range(len(rows)):
            if r == panel:
                continue
            old = rows[r]
            new = jnp.where(inside, 0.0, old)
            for c in range(ROWS):
                new = new - column(old, first + c) * solved[c : c + 1]
            rows[r] = new
        rows[panel] = solved
    return jnp.concatenate(rows, axis=0)


def spd_inverse(system):
    square = lax.dot_general(
        system, system, ROW_ROW, precision=HIGHEST, preferred_element_type=jnp.float32
    )
    return invert(square)


def local_kernel(
    chunks,
    shares,
    field_hbm,
    last_x_hbm,
    last_y_hbm,
    right_y_hbm,
    right_m_hbm,
    last_m_hbm,
    last_part,
    first_part,
    *refs,
):
    terms = refs[:shares]
    field, last_x, last_y, right_y, right_m, last_m, flat, sems = refs[shares:]
    x_cells, y_cells, m_cells = field.shape
    step = x_cells // chunks
    y_share = y_cells // shares
    parts = [pl.ds(n * step, step) for n in range(chunks)]
    copies = [
        pltpu.make_async_copy(last_m_hbm, last_m, sems.at[0]),
        pltpu.make_async_copy(field_hbm.at[parts[0]], field.at[parts[0]], sems.at[1]),
        pltpu.make_async_copy(last_x_hbm, last_x, sems.at[2]),
        pltpu.make_async_copy(last_y_hbm, last_y, sems.at[3]),
        pltpu.make_async_copy(right_m_hbm, right_m, sems.at[4]),
        pltpu.make_async_copy(right_y_hbm, right_y, sems.at[5]),
    ]
    for n in range(1, chunks):
        copies.append(
            pltpu.make_async_copy(field_hbm.at[parts[n]], field.at[parts[n]], sems.at[5 + n])
        )
    for copy in copies:
        copy.start()
    here = lax.axis_index("gz")
    for n in range(chunks):
        if n == 0:
            copies[0].wait()
            copies[1].wait()
        else:
            copies[5 + n].wait()
        rows = field[parts[n]].reshape(step * y_cells, m_cells)
        term = jnp.dot(rows, last_m[...], preferred_element_type=jnp.float32)
        for c in range(flat.shape[0]):
            flat[c] = term[:, c * LANES : (c + 1) * LANES]
        for s in range(shares):
            start = (here ^ s) * y_share
            for j in range(y_share):
                for c in range(flat.shape[0]):
                    terms[s][j, parts[n], c * LANES : (c + 1) * LANES] = flat[
                        c, pl.ds(start + j, step, stride=y_cells), :
                    ]

        if n == 0:
            copies[2].wait()
            copies[3].wait()
        left = last_x[parts[n]].astype(jnp.float32)[:, None, :]
        khatri = left * last_y[...].astype(jnp.float32)[None]
        khatri = khatri.astype(jnp.bfloat16).reshape(step * y_cells, -1)
        part = lax.dot_general(khatri, rows, COL_COL, preferred_element_type=jnp.float32)
        if n == 0:
            last_part[...] = part
            copies[4].wait()
            copies[5].wait()
        else:
            last_part[...] += part

        first = jnp.dot(rows, right_m[...], preferred_element_type=jnp.float32)
        first = first.reshape(step, y_cells, -1) * right_y[...].astype(jnp.float32)[None]
        first_part[parts[n], :] = jnp.sum(first, axis=1)


def local_products(shares, field, last_x, last_y, right_y, right_m, last_m):
    x_cells, y_cells, m_cells = field.shape
    rank, cols = last_x.shape[1], last_m.shape[1]
    chunks = max(x_cells // 16, 1)
    inputs = (field, last_x, last_y, right_y, right_m, last_m)
    term = jax.ShapeDtypeStruct((y_cells // shares, x_cells, cols), jnp.float32)
    return pl.pallas_call(
        functools.partial(local_kernel, chunks, shares),
        in_specs=[pl.BlockSpec(memory_space=pltpu.HBM)] * len(inputs),
        out_shape=[
            jax.ShapeDtypeStruct((rank, m_cells), jnp.float32),
            jax.ShapeDtypeStruct((x_cells, cols), jnp.float32),
            *([term] * shares),
        ],
        scratch_shapes=[
            *(pltpu.VMEM(x.shape, x.dtype) for x in inputs),
            pltpu.VMEM((cols // LANES, x_cells // chunks * y_cells, LANES), jnp.float32),
            pltpu.SemaphoreType.DMA((5 + chunks,)),
        ],
        compiler_params=pltpu.CompilerParams(vmem_limit_bytes=LOCAL_VMEM_BYTES),
        name="local_products",
    )(*inputs)


def last_kernel(system_shares, *refs):
    terms, projected = refs[:-1], refs[-1]
    system = system_shares[:, 0]
    for k in range(1, system_shares.shape[1]):
        system = system + system_shares[:, k]
    system = system.reshape(-1, system.shape[-1])
    pinv = jnp.dot(
        spd_inverse(system), system, precision=HIGHEST, preferred_element_type=jnp.float32
    )
    total = terms[0][...]
    for term in terms[1:]:
        total = total + term[...]
    core = lax.dot_general(
        total.reshape(-1, total.shape[-1]),
        pinv,
        ROW_ROW,
        precision=HIGHEST,
        preferred_element_type=jnp.float32,
    )
    projected[...] = core.reshape(projected.shape)


def solve_last(system_shares, terms):
    rank = system_shares.shape[0] * system_shares.shape[2]
    return pl.pallas_call(
        last_kernel,
        out_shape=jax.ShapeDtypeStruct((*terms[0].shape[:2], rank), jnp.float32),
        compiler_params=pltpu.CompilerParams(vmem_limit_bytes=VMEM_BYTES),
        name="solve_last",
    )(system_shares, *terms)


def sketch_kernel(order, left_at, pieces, packed, out):
    me = lax.axis_index("gx")
    blocks, y_own, x_cells, cols = pieces.shape
    weights = jnp.concatenate(
        [packed[k, left_at : left_at + x_cells] for k in range(blocks)], axis=0
    ).astype(jnp.bfloat16)
    for j in range(y_own):
        column = jnp.concatenate([pieces[me ^ o, j] for o in order], axis=0)
        high = column.astype(jnp.bfloat16)
        low = (column - high.astype(jnp.float32)).astype(jnp.bfloat16)
        both = lax.dot_general(
            weights,
            jnp.concatenate([high, low], axis=1),
            COL_COL,
            preferred_element_type=jnp.float32,
        )
        both = both[:, :cols] + both[:, cols:]
        out[:, j] = both.reshape(out.shape[0], out.shape[2], cols)


def sketch(order, left_at, own, pieces, packed):
    y_own, cols = pieces.shape[1], pieces.shape[3]
    rank = packed.shape[2]
    return pl.pallas_call(
        functools.partial(sketch_kernel, order, left_at),
        out_shape=jax.ShapeDtypeStruct((rank // own, y_own, own, cols), jnp.float32),
        compiler_params=pltpu.CompilerParams(vmem_limit_bytes=VMEM_BYTES),
        name="sketch",
    )(pieces, packed)


def first_kernel(first_at, left_at, rows, packed, core_first):
    x_cells, cols = rows.shape
    count = cols // LANES
    blocks = range(packed.shape[0])
    left = jnp.concatenate([packed[k, left_at : left_at + x_cells] for k in blocks], axis=0)
    all_rows = jnp.concatenate(
        [
            jnp.concatenate(
                [
                    packed[k, first_at + c * x_cells : first_at + (c + 1) * x_cells]
                    for c in range(count)
                ],
                axis=1,
            )
            for k in blocks
        ],
        axis=0,
    )
    system = lax.dot_general(
        left, all_rows, COL_COL, precision=HIGHEST, preferred_element_type=jnp.float32
    )
    inverse = spd_inverse(system)
    scores = lax.dot_general(
        rows[...], system, ROW_ROW, precision=HIGHEST, preferred_element_type=jnp.float32
    )
    core_first[...] = jnp.dot(
        scores, inverse, precision=HIGHEST, preferred_element_type=jnp.float32
    )


def solve_first(first_at, left_at, rows, packed):
    return pl.pallas_call(
        functools.partial(first_kernel, first_at, left_at),
        out_shape=jax.ShapeDtypeStruct((rows.shape[0], packed.shape[2]), jnp.float32),
        compiler_params=pltpu.CompilerParams(vmem_limit_bytes=VMEM_BYTES),
        name="solve_first",
    )(rows, packed)


def place_kernel(outer_order, inner_order, packed, core_last):
    own = packed.shape[3]
    outer, inner = lax.axis_index("gx"), lax.axis_index("gy")
    for n, i in enumerate(inner_order):
        for k, o in enumerate(outer_order):
            at = ((outer ^ o) * len(inner_order) + (inner ^ i)) * own
            for c in range(packed.shape[2]):
                core_last[pl.ds(pl.multiple_of(at, own), own), c * LANES : (c + 1) * LANES] = (
                    packed[n, k, c]
                )


def place(outer_order, inner_order, packed):
    inner, outer, count, own, lanes = packed.shape
    return pl.pallas_call(
        functools.partial(place_kernel, outer_order, inner_order),
        out_shape=jax.ShapeDtypeStruct((inner * outer * own, count * lanes), jnp.float32),
        compiler_params=pltpu.CompilerParams(vmem_limit_bytes=VMEM_BYTES),
        name="place",
    )(packed)


def per_device(flow_field, left_x, last_x, last_y, right_y, right_m, last_m):
    x_cells, y_cells, m_cells = flow_field.shape
    rank = left_x.shape[1]
    cols = right_m.shape[1]
    blocks, shares = lax.axis_size("gx"), lax.axis_size("gz")
    y_share = y_cells // shares
    y_own = y_share // blocks

    last_part, first_part, *terms = local_products(
        shares, flow_field, last_x, last_y, right_y, right_m, last_m
    )

    for s in range(1, shares):
        terms[s] = swap(terms[s], "gz", s)

    group = ("gx", "gy")
    own = rank // lax.axis_size(group)
    last_rows = lax.all_to_all(last_part.reshape(-1, own, m_cells), group, 0, 0, tiled=True)
    last_rows = jnp.sum(last_rows, axis=0)
    both = jnp.dot(
        jnp.concatenate(split_terms(last_rows), axis=0), last_m, preferred_element_type=jnp.float32
    )
    both = both[:own] + both[own:]
    count = lax.axis_size(ALL)
    copies = jnp.broadcast_to(both[None], (count, own, cols))
    system = lax.all_to_all(copies, ALL, 0, 0, tiled=True).reshape(-1, shares, own, cols)
    if own % ROWS:
        system = jnp.sum(system, axis=1).reshape(-1, 1, ROWS, cols)
    projected = solve_last(system, terms)

    first_rows = swap_sum(swap_sum(first_part, "gy"), "gz")
    packed = jnp.concatenate(
        [
            last_rows.reshape(own, -1, LANES).transpose(1, 0, 2).reshape(-1, LANES),
            first_rows.reshape(x_cells, -1, LANES).transpose(1, 0, 2).reshape(-1, LANES),
            left_x.astype(jnp.float32),
        ],
        axis=0,
    )
    first_at = own * m_cells // LANES
    left_at = first_at + x_cells * cols // LANES
    packed, order = swap_gather(packed, "gx")

    pieces = projected.reshape(blocks, y_own, x_cells, rank)
    pieces = lax.all_to_all(pieces, "gx", 0, 0, tiled=True)
    group = ("gx", "gz")
    devices = lax.axis_size(group)
    rank_own = rank // devices
    if rank_own % ROWS:
        middle = sketch(order, left_at, rank, pieces, packed)
        middle = middle.reshape(y_own, devices, rank_own, rank).transpose(1, 0, 2, 3)
    else:
        middle = sketch(order, left_at, rank_own, pieces, packed)
    received = lax.all_to_all(middle, group, 0, 0, tiled=True)
    received = received.reshape(blocks, shares, y_own, rank_own, rank)
    core_middle = received.transpose(3, 1, 0, 2, 4).reshape(rank_own, y_cells, rank)

    if own % ROWS:
        core_last = gather_rows(last_rows, "gx", "gy")
    else:
        core_last = packed[:, :first_at].reshape(blocks, -1, own, LANES)
        core_last, inner_order = swap_gather(core_last, "gy")
        core_last = place(order, inner_order, core_last)

    first_rows, _ = lax.optimization_barrier((first_rows, middle))
    core_first = solve_first(first_at, left_at, first_rows, packed)
    return (core_first, core_middle, core_last)


def solution(mesh):
    return jax.shard_map(
        per_device,
        mesh=mesh,
        in_specs=(
            P("gx", "gy", "gz"),
            P("gx", None),
            P("gx", None),
            P("gy", None),
            P("gy", None),
            P("gz", None),
            P("gz", None),
        ),
        out_specs=(P("gx", None), P(("gx", "gz"), "gy", None), P(None, "gz")),
        check_vma=False,
    )
```

time: 102 us -> 101 us (level)
  waiting for transfers between devices: 20.1 us -> 47.3 us
  starting transfers between devices: 55.3 us -> 30.3 us
  local copies, waits for them, and re-layouts: 7.15 us -> 1.53 us
  Pallas kernels: 16.4 us -> 19.5 us
    ppermute x28 -> x7, starting transfers between devices: 42.4 us -> 8.28 us  [swap(): lax.ppermute(array, axis, [(s, s ^ bits) for s in range(lax.axis_size(axi...]
    ppermute x28 -> x7, waiting for transfers between devices: 19 us -> 37.7 us  [swap(): lax.ppermute(array, axis, [(s, s ^ bits) for s in range(lax.axis_size(axi...]
    all_to_all x1, waiting for transfers between devices: 0.01 us -> 8.46 us  [per_device(): lax.all_to_all(last_part.reshape(-1, own, m_cells), group, 0, 0, tiled=True)]
    unnamed x16 -> x6, local copies, waits for them, and re-layouts: 5.66 us -> 0.01 us
    all_to_all x0 -> x1, starting transfers between devices: none -> 5.64 us  [per_device(): pieces = lax.all_to_all(pieces, 'gx', 0, 0, tiled=True)]
    all_to_all x1, starting transfers between devices: 3.88 us -> 7.5 us  [per_device(): lax.all_to_all(last_part.reshape(-1, own, m_cells), group, 0, 0, tiled=True)]
    pallas_call x5, Pallas kernels: 16.4 us -> 19.5 us  [the longest x1 6.61 us: local_products(): pl.pallas_call(functools.partial(local_kernel, chunks, shares), in_specs=...]
    all_to_all x1, starting transfers between devices: 5 us -> 2.91 us  [per_device(): lax.all_to_all(copies, ALL, 0, 0, tiled=True).reshape(-1, shares, own, cols)]
  transfers between devices with their start and end apart: 31 -> 11, of which waited for: 12 -> 8; matrix products, arithmetic and copies ran while one was open for 2% -> 2% of each run, Pallas kernels for 11% -> 6%
where the time goes in v3:
time: 101 us; the launch traced here: 100 us
  waiting for transfers between devices  47.3 us (47%)
  starting transfers between devices  30.3 us (30%)
  Pallas kernels  19.5 us (19%)
  local copies, waits for them, and re-layouts  1.53 us (2%)
    ppermute x7, waiting for transfers between devices, swap(): lax.ppermute(array, axis, [(s, s ^ bits) for s in range(lax.axis_size(axi...  37.7 us
    all_to_all x1, waiting for transfers between devices, per_device(): lax.all_to_all(last_part.reshape(-1, own, m_cells), group, 0, 0, tiled=True)  8.46 us
    ppermute x7, starting transfers between devices, swap(): lax.ppermute(array, axis, [(s, s ^ bits) for s in range(lax.axis_size(axi...  8.28 us
    all_to_all x1, starting transfers between devices, per_device(): lax.all_to_all(last_part.reshape(-1, own, m_cells), group, 0, 0, tiled=True)  7.5 us
    pallas_call x1, Pallas kernels, local_products(): pl.pallas_call(functools.partial(local_kernel, chunks, shares), in_specs=...  6.61 us
    pallas_call x1, Pallas kernels, solve_last(): pl.pallas_call(last_kernel, out_shape=jax.ShapeDtypeStruct((*terms[0].sha...  6.02 us
    all_to_all x1, starting transfers between devices, per_device(): received = lax.all_to_all(middle, group, 0, 0, tiled=True)  5.97 us
    all_to_all x1, starting transfers between devices, per_device(): pieces = lax.all_to_all(pieces, 'gx', 0, 0, tiled=True)  5.64 us
  transfers between devices with their start and end apart: 11, of which 8 were waited for; matrix products, arithmetic and copies ran while one was open for 2% of the time, Pallas kernels for 6%

profile of v3, /device:TPU:0, one launch (start us, length us, event | category | flops | bytes accessed | tf_op | source)
XLA Modules:
  0.0 100.5 jit_solution(9538599875972165454)
XLA Ops:
  0.6 0.0 copy-start.1
  0.6 0.0 copy-start.2
  0.7 6.6 %local_products.1 = (f32[128,512]{1,0:T(8,128)}, f32[32,256]{1,0:T(8,128)}, f32[32,32,256]{2,1,0:T(8,128)}, f32[32,32,256]{2,1,0:T(8,128)}) custom-call(bf16[32,64,512]{2,1,0:T(8,128)(2,1)} %field_hbm.1, bf16[32,128]{1,0:T(8,128)(2,1)} %last_x_hbm.1, bf16[64,128]{1,0:T(8,128)(2,1)} %last_y_hbm.1, bf16[64,256]{1,0:T(8,128)(2,1)} %right_y_hbm.1, ...), custom_call_target="tpu_custom_call" | custom-call | tf_op jit(solution)/shard_map/local_products/pallas_call | solution.py:187
  7.3 0.0 copy-start
  7.3 7.5 %all-to-all-start = ((f32[16,8,512]{2,1,0:T(8,128)}), f32[16,8,512]{2,1,0:T(8,128)S(1)}, u32[]{:S(2)}, u32[]{:S(2)}) async-start(f32[16,8,512]{2,1,0:T(8,128)} %bitcast.27), calls=%async_computation | async-start | bytes 524288 | tf_op jit(solution)/shard_map/all_to_all | solution.py:346
  14.8 1.6 %collective-permute-start.2 = (f32[32,32,256]{2,1,0:T(8,128)}, f32[32,32,256]{2,1,0:T(8,128)S(1)}, u32[]{:S(2)}, u32[]{:S(2)}) collective-permute-start(f32[32,32,256]{2,1,0:T(8,128)} %get-tuple-element.11), channel_id=1, source_target_pairs={{0,1},{1,0},{2,3},{3,2},{4,5},{5,4},{6,7},{7,6},{8,9},{9,8},{10,11... | collective-permute-start | bytes 3145736 | tf_op jit(solution)/shard_map/ppermute | solution.py:28
  16.4 8.5 %all-to-all-done = f32[16,8,512]{2,1,0:T(8,128)S(1)} async-done(((f32[16,8,512]{2,1,0:T(8,128)}), f32[16,8,512]{2,1,0:T(8,128)S(1)}, u32[]{:S(2)}, u32[]{:S(2)}) %all-to-all-start) | async-done | bytes 262176 | tf_op jit(solution)/shard_map/all_to_all | solution.py:346
  24.9 0.0 copy-done.1
  24.9 0.1 fusion.1
  25.0 0.7 broadcast_in_dim.4
  25.8 2.9 %all-to-all-start.1 = ((f32[32,8,256]{2,1,0:T(8,128)}), f32[32,8,256]{2,1,0:T(8,128)S(1)}, u32[]{:S(2)}, u32[]{:S(2)}) async-start(f32[32,8,256]{2,1,0:T(8,128)} %broadcast_in_dim.4), calls=%async_computation.1 | async-start | bytes 524288 | tf_op jit(solution)/shard_map/all_to_all | solution.py:354
  28.7 0.3 collective-permute-start
  29.0 1.2 %collective-permute-done = f32[32,256]{1,0:T(8,128)S(1)} collective-permute-done((f32[32,256]{1,0:T(8,128)}, f32[32,256]{1,0:T(8,128)S(1)}, u32[]{:S(2)}, u32[]{:S(2)}) %collective-permute-start) | collective-permute-done | bytes 32800 | tf_op jit(solution)/shard_map/ppermute | solution.py:28
  30.2 0.8 add.9
  30.9 1.8 %collective-permute-start.1 = (f32[32,256]{1,0:T(8,128)S(1)}, f32[32,256]{1,0:T(8,128)S(1)}, u32[]{:S(2)}, u32[]{:S(2)}) collective-permute-start(f32[32,256]{1,0:T(8,128)S(1)} %add.9), channel_id=1, source_target_pairs={{0,1},{1,0},{2,3},{3,2},{4,5},{5,4},{6,7},{7,6},{8,9},{9,8},{10,11... | collective-permute-start | bytes 98312 | tf_op jit(solution)/shard_map/ppermute | solution.py:28
  32.7 0.0 copy-done.2
  32.7 11.3 %collective-permute-done.1 = f32[32,256]{1,0:T(8,128)S(1)} collective-permute-done((f32[32,256]{1,0:T(8,128)S(1)}, f32[32,256]{1,0:T(8,128)S(1)}, u32[]{:S(2)}, u32[]{:S(2)}) %collective-permute-start.1) | collective-permute-done | bytes 32800 | tf_op jit(solution)/shard_map/ppermute | solution.py:28
  44.0 0.0 all-to-all-done.1
  44.0 0.0 collective-permute-done.2.refs_1_
  44.0 0.0 copy-done
  44.0 6.0 %solve_last.1 = f32[32,32,128]{2,1,0:T(8,128)} custom-call(f32[16,2,8,256]{3,2,1,0:T(8,128)S(1)} %bitcast.25, f32[32,32,256]{2,1,0:T(8,128)S(1)} %copy-done, f32[32,32,256]{2,1,0:T(8,128)S(1)} %collective-permute-done.2.refs_1_), custom_call_target="tpu_custom_call" | custom-call | tf_op jit(solution)/shard_map/solve_last/pallas_call | solution.py:229
  50.0 5.6 %all-to-all-start.2 = ((f32[8,4,32,128]{3,2,1,0:T(8,128)}), f32[8,4,32,128]{3,2,1,0:T(8,128)S(1)}, u32[]{:S(2)}, u32[]{:S(2)}) async-start(f32[8,4,32,128]{3,2,1,0:T(8,128)} %bitcast.2), calls=%async_computation.2 | async-start | bytes 1048576 | tf_op jit(solution)/shard_map/all_to_all | solution.py:373
  55.7 3.0 %collective-permute-start.3 = (f32[1,128,128]{2,1,0:T(8,128)S(1)}, f32[1,128,128]{2,1,0:T(8,128)S(1)}, u32[]{:S(2)}, u32[]{:S(2)}) collective-permute-start(f32[1,128,128]{2,1,0:T(8,128)S(1)} %maximum_bitcast_fusion), channel_id=1, source_target_pairs={{0,16},{4,20},{8,24},{12,28},{16,0},{20,4},{24,8},{28,12},{1,17},{... | collective-permute-start | bytes 196616 | tf_op jit(solution)/shard_map/ppermute | solution.py:28
  58.7 14.1 %collective-permute-done.3 = f32[1,128,128]{2,1,0:T(8,128)S(1)} collective-permute-done((f32[1,128,128]{2,1,0:T(8,128)S(1)}, f32[1,128,128]{2,1,0:T(8,128)S(1)}, u32[]{:S(2)}, u32[]{:S(2)}) %collective-permute-start.3) | collective-permute-done | bytes 65568 | tf_op jit(solution)/shard_map/ppermute | solution.py:28
  72.8 0.1 collective-permute-start.4
  72.8 5.0 %collective-permute-done.4 = f32[2,128,128]{2,1,0:T(8,128)S(1)} collective-permute-done((f32[2,128,128]{2,1,0:T(8,128)S(1)}, f32[2,128,128]{2,1,0:T(8,128)S(1)}, u32[]{:S(2)}, u32[]{:S(2)}) %collective-permute-start.4) | collective-permute-done | bytes 131104 | tf_op jit(solution)/shard_map/ppermute | solution.py:28
  77.8 1.5 %collective-permute-start.5 = (f32[4,128,128]{2,1,0:T(8,128)S(1)}, f32[4,128,128]{2,1,0:T(8,128)S(1)}, u32[]{:S(2)}, u32[]{:S(2)}) collective-permute-start(f32[4,128,128]{2,1,0:T(8,128)S(1)} %pad_maximum_fusion.1), channel_id=1, source_target_pairs={{0,4},{4,0},{8,12},{12,8},{16,20},{20,16},{24,28},{28,24},{1,5},{5... | collective-permute-start | bytes 786440 | tf_op jit(solution)/shard_map/ppermute | solution.py:28
  79.3 5.0 %collective-permute-done.5 = f32[4,128,128]{2,1,0:T(8,128)S(1)} collective-permute-done((f32[4,128,128]{2,1,0:T(8,128)S(1)}, f32[4,128,128]{2,1,0:T(8,128)S(1)}, u32[]{:S(2)}, u32[]{:S(2)}) %collective-permute-start.5) | collective-permute-done | bytes 262176 | tf_op jit(solution)/shard_map/ppermute | solution.py:28
  84.3 0.0 all-to-all-done.2.pieces
  84.3 1.0 sketch.1
  85.3 6.0 %all-to-all-start.3 = ((f32[16,4,8,128]{3,2,1,0:T(8,128)}), f32[16,4,8,128]{3,2,1,0:T(8,128)S(1)}, u32[]{:S(2)}, u32[]{:S(2)}) async-start(f32[16,4,8,128]{3,2,1,0:T(8,128)} %sketch.1), calls=%async_computation.3 | async-start | bytes 524288 | tf_op jit(solution)/shard_map/all_to_all | solution.py:382
  91.3 0.1 collective-permute-start.6
  91.3 1.3 %collective-permute-done.6 = f32[1,8,4,8,128]{4,3,2,1,0:T(8,128)S(1)} collective-permute-done((f32[1,8,4,8,128]{4,3,2,1,0:T(8,128)S(1)}, f32[1,8,4,8,128]{4,3,2,1,0:T(8,128)S(1)}, u32[]{:S(2)}, u32[]{:S(2)}) %collective-permute-start.6) | collective-permute-done | bytes 131104 | tf_op jit(solution)/shard_map/ppermute | solution.py:28
  92.7 0.7 place.1
  93.4 5.2 %solve_first.1 = f32[32,128]{1,0:T(8,128)} custom-call(f32[32,256]{1,0:T(8,128)S(1)} %add.10.rows, f32[8,128,128]{2,1,0:T(8,128)S(1)} %pad_maximum_fusion.packed), custom_call_target="tpu_custom_call" | custom-call | tf_op jit(solution)/shard_map/solve_first/pallas_call | solution.py:299
  98.6 1.1 %all-to-all-done.3 = f32[16,4,8,128]{3,2,1,0:T(8,128)S(1)} async-done(((f32[16,4,8,128]{3,2,1,0:T(8,128)}), f32[16,4,8,128]{3,2,1,0:T(8,128)S(1)}, u32[]{:S(2)}, u32[]{:S(2)}) %all-to-all-start.3) | async-done | bytes 262176 | tf_op jit(solution)/shard_map/all_to_all | solution.py:382
  99.7 0.8 copy.11
  (12 shorter events, 0.1 us)
Async XLA Ops:
  0.6 24.2 %copy-start.1 = (bf16[512,256]{1,0:T(8,128)(2,1)S(1)}, bf16[512,256]{1,0:T(8,128)(2,1)}, u32[]{:S(2)}) copy-start(bf16[512,256]{1,0:T(8,128)(2,1)} %last_m_hbm.1) | copy-start | bytes 786436
  0.6 32.1 %copy-start.2 = (bf16[32,128]{1,0:T(8,128)(2,1)S(1)}, bf16[32,128]{1,0:T(8,128)(2,1)}, u32[]{:S(2)}) copy-start(bf16[32,128]{1,0:T(8,128)(2,1)} %param.8) | copy-start | bytes 24580
  7.3 36.8 %copy-start = (f32[32,32,256]{2,1,0:T(8,128)S(1)}, f32[32,32,256]{2,1,0:T(8,128)}, u32[]{:S(2)}) copy-start(f32[32,32,256]{2,1,0:T(8,128)} %get-tuple-element.10.refs_0_) | copy-start | bytes 3145732
  7.3 17.6 %all-to-all-start = ((f32[16,8,512]{2,1,0:T(8,128)}), f32[16,8,512]{2,1,0:T(8,128)S(1)}, u32[]{:S(2)}, u32[]{:S(2)}) async-start(f32[16,8,512]{2,1,0:T(8,128)} %bitcast.27), calls=%async_computation | async-start | bytes 524288 | tf_op jit(solution)/shard_map/all_to_all | solution.py:346
  14.8 29.2 %collective-permute-start.2 = (f32[32,32,256]{2,1,0:T(8,128)}, f32[32,32,256]{2,1,0:T(8,128)S(1)}, u32[]{:S(2)}, u32[]{:S(2)}) collective-permute-start(f32[32,32,256]{2,1,0:T(8,128)} %get-tuple-element.11), channel_id=1, source_target_pairs={{0,1},{1,0},{2,3},{3,2},{4,5},{5,4},{6,7},{7,6},{8,9},{9,8},{10,11... | collective-permute-start | bytes 3145736 | tf_op jit(solution)/shard_map/ppermute | solution.py:28
  25.8 18.2 %all-to-all-start.1 = ((f32[32,8,256]{2,1,0:T(8,128)}), f32[32,8,256]{2,1,0:T(8,128)S(1)}, u32[]{:S(2)}, u32[]{:S(2)}) async-start(f32[32,8,256]{2,1,0:T(8,128)} %broadcast_in_dim.4), calls=%async_computation.1 | async-start | bytes 524288 | tf_op jit(solution)/shard_map/all_to_all | solution.py:354
  28.7 1.5 %collective-permute-start = (f32[32,256]{1,0:T(8,128)}, f32[32,256]{1,0:T(8,128)S(1)}, u32[]{:S(2)}, u32[]{:S(2)}) collective-permute-start(f32[32,256]{1,0:T(8,128)} %get-tuple-element.8), channel_id=1, source_target_pairs={{0,2},{2,0},{1,3},{3,1},{4,6},{6,4},{5,7},{7,5},{8,10},{10,8},{9,1... | collective-permute-start | bytes 98312 | tf_op jit(solution)/shard_map/ppermute | solution.py:28
  30.9 13.0 %collective-permute-start.1 = (f32[32,256]{1,0:T(8,128)S(1)}, f32[32,256]{1,0:T(8,128)S(1)}, u32[]{:S(2)}, u32[]{:S(2)}) collective-permute-start(f32[32,256]{1,0:T(8,128)S(1)} %add.9), channel_id=1, source_target_pairs={{0,1},{1,0},{2,3},{3,2},{4,5},{5,4},{6,7},{7,6},{8,9},{9,8},{10,11... | collective-permute-start | bytes 98312 | tf_op jit(solution)/shard_map/ppermute | solution.py:28
  50.0 34.3 %all-to-all-start.2 = ((f32[8,4,32,128]{3,2,1,0:T(8,128)}), f32[8,4,32,128]{3,2,1,0:T(8,128)S(1)}, u32[]{:S(2)}, u32[]{:S(2)}) async-start(f32[8,4,32,128]{3,2,1,0:T(8,128)} %bitcast.2), calls=%async_computation.2 | async-start | bytes 1048576 | tf_op jit(solution)/shard_map/all_to_all | solution.py:373
  55.7 17.0 %collective-permute-start.3 = (f32[1,128,128]{2,1,0:T(8,128)S(1)}, f32[1,128,128]{2,1,0:T(8,128)S(1)}, u32[]{:S(2)}, u32[]{:S(2)}) collective-permute-start(f32[1,128,128]{2,1,0:T(8,128)S(1)} %maximum_bitcast_fusion), channel_id=1, source_target_pairs={{0,16},{4,20},{8,24},{12,28},{16,0},{20,4},{24,8},{28,12},{1,17},{... | collective-permute-start | bytes 196616 | tf_op jit(solution)/shard_map/ppermute | solution.py:28
  72.8 5.0 %collective-permute-start.4 = (f32[2,128,128]{2,1,0:T(8,128)S(1)}, f32[2,128,128]{2,1,0:T(8,128)S(1)}, u32[]{:S(2)}, u32[]{:S(2)}) collective-permute-start(f32[2,128,128]{2,1,0:T(8,128)S(1)} %pad_maximum_fusion.3), channel_id=1, source_target_pairs={{0,8},{4,12},{8,0},{12,4},{16,24},{20,28},{24,16},{28,20},{1,9},{5... | collective-permute-start | bytes 393224 | tf_op jit(solution)/shard_map/ppermute | solution.py:28
  77.8 6.4 %collective-permute-start.5 = (f32[4,128,128]{2,1,0:T(8,128)S(1)}, f32[4,128,128]{2,1,0:T(8,128)S(1)}, u32[]{:S(2)}, u32[]{:S(2)}) collective-permute-start(f32[4,128,128]{2,1,0:T(8,128)S(1)} %pad_maximum_fusion.1), channel_id=1, source_target_pairs={{0,4},{4,0},{8,12},{12,8},{16,20},{20,16},{24,28},{28,24},{1,5},{5... | collective-permute-start | bytes 786440 | tf_op jit(solution)/shard_map/ppermute | solution.py:28
  85.3 14.5 %all-to-all-start.3 = ((f32[16,4,8,128]{3,2,1,0:T(8,128)}), f32[16,4,8,128]{3,2,1,0:T(8,128)S(1)}, u32[]{:S(2)}, u32[]{:S(2)}) async-start(f32[16,4,8,128]{3,2,1,0:T(8,128)} %sketch.1), calls=%async_computation.3 | async-start | bytes 524288 | tf_op jit(solution)/shard_map/all_to_all | solution.py:382
  91.3 1.4 %collective-permute-start.6 = (f32[1,8,4,8,128]{4,3,2,1,0:T(8,128)S(1)}, f32[1,8,4,8,128]{4,3,2,1,0:T(8,128)S(1)}, u32[]{:S(2)}, u32[]{:S(2)}) collective-permute-start(f32[1,8,4,8,128]{4,3,2,1,0:T(8,128)S(1)} %slice_bitcast_fusion), channel_id=1, source_target_pairs={{0,2},{2,0},{1,3},{3,1},{4,6},{6,4},{5,7},{7,5},{8,10},{10,8},{9,1... | collective-permute-start | bytes 393224 | tf_op jit(solution)/shard_map/ppermute | solution.py:28

commit v4 on v3

--- a/solution.py
+++ b/solution.py
@@ -34,12 +34,14 @@
     return array
 
 
-def swap_gather(array, axis):
+def swap_gather(array, axis, gate=None):
     held, order = array[None], [0]
     for bit in axis_bits(axis):
+        if bit == 1 and gate is not None:
+            held, gate = lax.optimization_barrier((held, gate))
         held = jnp.concatenate([held, swap(held, axis, bit)], axis=0)
         order += [o ^ bit for o in order]
-    return held, order
+    return held, order, gate
 
 
 def gather_rows(array, outer, inner):
@@ -120,8 +122,8 @@
     first_part,
     *refs,
 ):
-    terms = refs[:shares]
-    field, last_x, last_y, right_y, right_m, last_m, flat, sems = refs[shares:]
+    terms_hbm = refs[:shares]
+    field, last_x, last_y, right_y, right_m, last_m, terms, sems, out_sems = refs[shares:]
     x_cells, y_cells, m_cells = field.shape
     step = x_cells // chunks
     y_share = y_cells // shares
@@ -141,61 +143,63 @@
     for copy in copies:
         copy.start()
     here = lax.axis_index("gz")
+    leaving = []
+    copies[0].wait()
     for n in range(chunks):
-        if n == 0:
-            copies[0].wait()
-            copies[1].wait()
-        else:
-            copies[5 + n].wait()
+        copies[5 + n if n else 1].wait()
+        for s in reversed(range(shares)):
+            start = pl.multiple_of((here ^ s) * y_share, y_share)
+            rows = field[parts[n], pl.ds(start, y_share), :].reshape(step * y_share, m_cells)
+            term = jnp.dot(rows, last_m[...], preferred_element_type=jnp.float32)
+            terms[s, parts[n]] = term.reshape(step, y_share, -1)
+            leaving.append(
+                pltpu.make_async_copy(
+                    terms.at[s, parts[n]], terms_hbm[s].at[parts[n]], out_sems.at[s, n]
+                )
+            )
+            leaving[-1].start()
+
+    for copy in copies[2:6]:
+        copy.wait()
+    for n in range(chunks):
         rows = field[parts[n]].reshape(step * y_cells, m_cells)
-        term = jnp.dot(rows, last_m[...], preferred_element_type=jnp.float32)
-        for c in range(flat.shape[0]):
-            flat[c] = term[:, c * LANES : (c + 1) * LANES]
-        for s in range(shares):
-            start = (here ^ s) * y_share
-            for j in range(y_share):
-                for c in range(flat.shape[0]):
-                    terms[s][j, parts[n], c * LANES : (c + 1) * LANES] = flat[
-                        c, pl.ds(start + j, step, stride=y_cells), :
-                    ]
-
-        if n == 0:
-            copies[2].wait()
-            copies[3].wait()
         left = last_x[parts[n]].astype(jnp.float32)[:, None, :]
         khatri = left * last_y[...].astype(jnp.float32)[None]
         khatri = khatri.astype(jnp.bfloat16).reshape(step * y_cells, -1)
         part = lax.dot_general(khatri, rows, COL_COL, preferred_element_type=jnp.float32)
         if n == 0:
             last_part[...] = part
-            copies[4].wait()
-            copies[5].wait()
         else:
             last_part[...] += part
-
         first = jnp.dot(rows, right_m[...], preferred_element_type=jnp.float32)
         first = first.reshape(step, y_cells, -1) * right_y[...].astype(jnp.float32)[None]
         first_part[parts[n], :] = jnp.sum(first, axis=1)
+    for copy in leaving:
+        copy.wait()
 
 
 def local_products(shares, field, last_x, last_y, right_y, right_m, last_m):
     x_cells, y_cells, m_cells = field.shape
     rank, cols = last_x.shape[1], last_m.shape[1]
-    chunks = max(x_cells // 16, 1)
+    chunks = max(x_cells // 8, 1)
     inputs = (field, last_x, last_y, right_y, right_m, last_m)
-    term = jax.ShapeDtypeStruct((y_cells // shares, x_cells, cols), jnp.float32)
+    dims = (x_cells, y_cells // shares, cols)
+    hbm = pl.BlockSpec(memory_space=pltpu.HBM)
+    vmem = pl.BlockSpec(memory_space=pltpu.VMEM)
     return pl.pallas_call(
         functools.partial(local_kernel, chunks, shares),
-        in_specs=[pl.BlockSpec(memory_space=pltpu.HBM)] * len(inputs),
+        in_specs=[hbm] * len(inputs),
+        out_specs=[vmem, vmem, *([hbm] * shares)],
         out_shape=[
             jax.ShapeDtypeStruct((rank, m_cells), jnp.float32),
             jax.ShapeDtypeStruct((x_cells, cols), jnp.float32),
-            *([term] * shares),
+            *([jax.ShapeDtypeStruct(dims, jnp.float32)] * shares),
         ],
         scratch_shapes=[
             *(pltpu.VMEM(x.shape, x.dtype) for x in inputs),
-            pltpu.VMEM((cols // LANES, x_cells // chunks * y_cells, LANES), jnp.float32),
+            pltpu.VMEM((shares, *dims), jnp.float32),
             pltpu.SemaphoreType.DMA((5 + chunks,)),
+            pltpu.SemaphoreType.DMA((shares, chunks)),
         ],
         compiler_params=pltpu.CompilerParams(vmem_limit_bytes=LOCAL_VMEM_BYTES),
         name="local_products",
@@ -203,7 +207,7 @@
 
 
 def last_kernel(system_shares, *refs):
-    terms, projected = refs[:-1], refs[-1]
+    *terms, projected, flat = refs
     system = system_shares[:, 0]
     for k in range(1, system_shares.shape[1]):
         system = system + system_shares[:, k]
@@ -214,21 +218,25 @@
     total = terms[0][...]
     for term in terms[1:]:
         total = total + term[...]
-    core = lax.dot_general(
+    flat[...] = lax.dot_general(
         total.reshape(-1, total.shape[-1]),
         pinv,
         ROW_ROW,
         precision=HIGHEST,
         preferred_element_type=jnp.float32,
     )
-    projected[...] = core.reshape(projected.shape)
+    y_cells, x_cells, _ = projected.shape
+    for j in range(y_cells):
+        projected[j] = flat[pl.ds(j, x_cells, stride=y_cells), :]
 
 
 def solve_last(system_shares, terms):
     rank = system_shares.shape[0] * system_shares.shape[2]
+    x_cells, y_cells, _ = terms[0].shape
     return pl.pallas_call(
         last_kernel,
-        out_shape=jax.ShapeDtypeStruct((*terms[0].shape[:2], rank), jnp.float32),
+        out_shape=jax.ShapeDtypeStruct((y_cells, x_cells, rank), jnp.float32),
+        scratch_shapes=[pltpu.VMEM((x_cells * y_cells, rank), jnp.float32)],
         compiler_params=pltpu.CompilerParams(vmem_limit_bytes=VMEM_BYTES),
         name="solve_last",
     )(system_shares, *terms)
@@ -265,43 +273,56 @@
     )(pieces, packed)
 
 
-def first_kernel(first_at, left_at, rows, packed, core_first):
+def first_sums_kernel(first_at, left_at, rows, packed, sums):
     x_cells, cols = rows.shape
-    count = cols // LANES
     blocks = range(packed.shape[0])
     left = jnp.concatenate([packed[k, left_at : left_at + x_cells] for k in blocks], axis=0)
-    all_rows = jnp.concatenate(
-        [
-            jnp.concatenate(
-                [
-                    packed[k, first_at + c * x_cells : first_at + (c + 1) * x_cells]
-                    for c in range(count)
-                ],
-                axis=1,
-            )
-            for k in blocks
-        ],
-        axis=0,
-    )
-    system = lax.dot_general(
-        left, all_rows, COL_COL, precision=HIGHEST, preferred_element_type=jnp.float32
-    )
+    sums[:x_cells] = rows[...]
+    for c in range(cols // LANES):
+        at = first_at + c * x_cells
+        sums[x_cells:, c * LANES : (c + 1) * LANES] = lax.dot_general(
+            left,
+            jnp.concatenate([packed[k, at : at + x_cells] for k in blocks], axis=0),
+            COL_COL,
+            precision=HIGHEST,
+            preferred_element_type=jnp.float32,
+        )
+
+
+def first_sums(first_at, left_at, rows, packed):
+    return pl.pallas_call(
+        functools.partial(first_sums_kernel, first_at, left_at),
+        out_shape=jax.ShapeDtypeStruct(
+            (rows.shape[0] + packed.shape[2], rows.shape[1]), jnp.float32
+        ),
+        compiler_params=pltpu.CompilerParams(vmem_limit_bytes=VMEM_BYTES),
+        name="first_sums",
+    )(rows, packed)
+
+
+def first_kernel(*refs):
+    *sums, core_first = refs
+    x_cells = core_first.shape[0]
+    total = sums[0][...]
+    for other in sums[1:]:
+        total = total + other[...]
+    system = total[x_cells:]
     inverse = spd_inverse(system)
     scores = lax.dot_general(
-        rows[...], system, ROW_ROW, precision=HIGHEST, preferred_element_type=jnp.float32
+        total[:x_cells], system, ROW_ROW, precision=HIGHEST, preferred_element_type=jnp.float32
     )
     core_first[...] = jnp.dot(
         scores, inverse, precision=HIGHEST, preferred_element_type=jnp.float32
     )
 
 
-def solve_first(first_at, left_at, rows, packed):
-    return pl.pallas_call(
-        functools.partial(first_kernel, first_at, left_at),
-        out_shape=jax.ShapeDtypeStruct((rows.shape[0], packed.shape[2]), jnp.float32),
+def solve_first(x_cells, sums):
+    return pl.pallas_call(
+        first_kernel,
+        out_shape=jax.ShapeDtypeStruct((x_cells, sums[0].shape[0] - x_cells), jnp.float32),
         compiler_params=pltpu.CompilerParams(vmem_limit_bytes=VMEM_BYTES),
         name="solve_first",
-    )(rows, packed)
+    )(*sums)
 
 
 def place_kernel(outer_order, inner_order, packed, core_last):
@@ -354,9 +375,8 @@
     system = lax.all_to_all(copies, ALL, 0, 0, tiled=True).reshape(-1, shares, own, cols)
     if own % ROWS:
         system = jnp.sum(system, axis=1).reshape(-1, 1, ROWS, cols)
-    projected = solve_last(system, terms)
-
-    first_rows = swap_sum(swap_sum(first_part, "gy"), "gz")
+
+    first_rows = swap_sum(first_part, "gy")
     packed = jnp.concatenate(
         [
             last_rows.reshape(own, -1, LANES).transpose(1, 0, 2).reshape(-1, LANES),
@@ -367,7 +387,9 @@
     )
     first_at = own * m_cells // LANES
     left_at = first_at + x_cells * cols // LANES
-    packed, order = swap_gather(packed, "gx")
+    packed, order, system = swap_gather(packed, "gx", system)
+    projected = solve_last(system, terms)
+    projected, packed = lax.optimization_barrier((projected, packed))
 
     pieces = projected.reshape(blocks, y_own, x_cells, rank)
     pieces = lax.all_to_all(pieces, "gx", 0, 0, tiled=True)
@@ -387,11 +409,12 @@
         core_last = gather_rows(last_rows, "gx", "gy")
     else:
         core_last = packed[:, :first_at].reshape(blocks, -1, own, LANES)
-        core_last, inner_order = swap_gather(core_last, "gy")
+        core_last, inner_order, _ = swap_gather(core_last, "gy")
         core_last = place(order, inner_order, core_last)
 
-    first_rows, _ = lax.optimization_barrier((first_rows, middle))
-    core_first = solve_first(first_at, left_at, first_rows, packed)
+    sums = first_sums(first_at, left_at, first_rows, packed)
+    sums = [swap(sums, "gz", z) if z else sums for z in range(shares)]
+    core_first = solve_first(x_cells, sums)
     return (core_first, core_middle, core_last)
 
 

time: 101 us -> 89.5 us (0.89)
  waiting for transfers between devices: 47.3 us -> 27.9 us
  blocking collectives: 0 us -> 17.3 us
  starting transfers between devices: 30.3 us -> 23.7 us
  Pallas kernels: 19.5 us -> 16.8 us
    all_to_all x0 -> x1, blocking collectives: none -> 17.3 us  [per_device(): pieces = lax.all_to_all(pieces, 'gx', 0, 0, tiled=True)]
    ppermute x7, waiting for transfers between devices: 37.7 us -> 20.5 us  [swap(): lax.ppermute(array, axis, [(s, s ^ bits) for s in range(lax.axis_size(axi...]
    all_to_all x1 -> x0, starting transfers between devices: 5.64 us -> none  [per_device(): pieces = lax.all_to_all(pieces, 'gx', 0, 0, tiled=True)]
    pallas_call x1, Pallas kernels: 6.61 us -> 4.35 us  [local_products(): pl.pallas_call(functools.partial(local_kernel, chunks, shares), in_specs=...]
    all_to_all x1, waiting for transfers between devices: 8.46 us -> 7.33 us  [per_device(): lax.all_to_all(last_part.reshape(-1, own, m_cells), group, 0, 0, tiled=True)]
    all_to_all x1, waiting for transfers between devices: 1.08 us -> 0.01 us  [per_device(): received = lax.all_to_all(middle, group, 0, 0, tiled=True)]
    all_to_all x1, starting transfers between devices: 5.97 us -> 4.94 us  [per_device(): received = lax.all_to_all(middle, group, 0, 0, tiled=True)]
    pallas_call x2 -> x3, Pallas kernels: 11.2 us -> 10.7 us  [the longest x1 5.44 us: solve_last(): pl.pallas_call(last_kernel, out_shape=jax.ShapeDtypeStruct((y_cells, x_ce...]
  transfers between devices with their start and end apart: 11 -> 10, of which waited for: 8 -> 4; matrix products, arithmetic and copies ran while one was open for 2% -> 2% of each run, Pallas kernels for 6% -> 13%
where the time goes in v4:
time: 89.5 us; the launch traced here: 89 us
  waiting for transfers between devices  27.9 us (31%)
  starting transfers between devices  23.7 us (26%)
  blocking collectives  17.3 us (19%)
  Pallas kernels  16.8 us (19%)
  local copies, waits for them, and re-layouts  1.53 us (2%)
    ppermute x7, waiting for transfers between devices, swap(): lax.ppermute(array, axis, [(s, s ^ bits) for s in range(lax.axis_size(axi...  20.5 us
    all_to_all x1, blocking collectives, per_device(): pieces = lax.all_to_all(pieces, 'gx', 0, 0, tiled=True)  17.3 us
    ppermute x7, starting transfers between devices, swap(): lax.ppermute(array, axis, [(s, s ^ bits) for s in range(lax.axis_size(axi...  8.32 us
    all_to_all x1, starting transfers between devices, per_device(): lax.all_to_all(last_part.reshape(-1, own, m_cells), group, 0, 0, tiled=True)  7.5 us
    all_to_all x1, waiting for transfers between devices, per_device(): lax.all_to_all(last_part.reshape(-1, own, m_cells), group, 0, 0, tiled=True)  7.33 us
    pallas_call x1, Pallas kernels, solve_last(): pl.pallas_call(last_kernel, out_shape=jax.ShapeDtypeStruct((y_cells, x_ce...  5.44 us
    all_to_all x1, starting transfers between devices, per_device(): received = lax.all_to_all(middle, group, 0, 0, tiled=True)  4.94 us
    pallas_call x1, Pallas kernels, solve_first(): pl.pallas_call(first_kernel, out_shape=jax.ShapeDtypeStruct((x_cells, sum...  4.89 us
  transfers between devices with their start and end apart: 10, of which 4 were waited for; matrix products, arithmetic and copies ran while one was open for 2% of the time, Pallas kernels for 13%

profile of v4, /device:TPU:0, one launch (start us, length us, event | category | flops | bytes accessed | tf_op | source)
XLA Modules:
  0.0 89.0 jit_solution(7036113994663993838)
XLA Ops:
  0.6 0.0 copy-start.1
  0.6 0.0 copy-start.2
  0.7 4.4 %local_products.1 = (f32[128,512]{1,0:T(8,128)}, f32[32,256]{1,0:T(8,128)}, f32[32,32,256]{2,1,0:T(8,128)}, f32[32,32,256]{2,1,0:T(8,128)}) custom-call(bf16[32,64,512]{2,1,0:T(8,128)(2,1)} %field_hbm.1, bf16[32,128]{1,0:T(8,128)(2,1)} %last_x_hbm.1, bf16[64,128]{1,0:T(8,128)(2,1)} %last_y_hbm.1, bf16[64,256]{1,0:T(8,128)(2,1)} %right_y_hbm.1, ...), custom_call_target="tpu_custom_call" | custom-call | tf_op jit(solution)/shard_map/local_products/pallas_call | solution.py:189
  5.0 0.0 copy-start
  5.0 7.5 %all-to-all-start = ((f32[16,8,512]{2,1,0:T(8,128)}), f32[16,8,512]{2,1,0:T(8,128)S(1)}, u32[]{:S(2)}, u32[]{:S(2)}) async-start(f32[16,8,512]{2,1,0:T(8,128)} %bitcast.28), calls=%async_computation | async-start | bytes 524288 | tf_op jit(solution)/shard_map/all_to_all | solution.py:367
  12.5 0.4 collective-permute-start
  12.9 1.5 %collective-permute-start.3 = (f32[32,32,256]{2,1,0:T(8,128)}, f32[32,32,256]{2,1,0:T(8,128)S(1)}, u32[]{:S(2)}, u32[]{:S(2)}) collective-permute-start(f32[32,32,256]{2,1,0:T(8,128)} %get-tuple-element.15), channel_id=1, source_target_pairs={{0,1},{1,0},{2,3},{3,2},{4,5},{5,4},{6,7},{7,6},{8,9},{9,8},{10,11... | collective-permute-start | bytes 3145736 | tf_op jit(solution)/shard_map/ppermute | solution.py:28
  14.5 0.0 copy-done.2
  14.5 0.0 collective-permute-done
  14.5 0.8 add.6.rows
  15.2 7.3 %all-to-all-done = f32[16,8,512]{2,1,0:T(8,128)S(1)} async-done(((f32[16,8,512]{2,1,0:T(8,128)}), f32[16,8,512]{2,1,0:T(8,128)S(1)}, u32[]{:S(2)}, u32[]{:S(2)}) %all-to-all-start) | async-done | bytes 262176 | tf_op jit(solution)/shard_map/all_to_all | solution.py:367
  22.6 0.0 copy-done.1
  22.6 0.1 fusion.1
  22.8 0.7 broadcast_in_dim.10
  23.5 2.9 %all-to-all-start.1 = ((f32[32,8,256]{2,1,0:T(8,128)}), f32[32,8,256]{2,1,0:T(8,128)S(1)}, u32[]{:S(2)}, u32[]{:S(2)}) async-start(f32[32,8,256]{2,1,0:T(8,128)} %broadcast_in_dim.10), calls=%async_computation.1 | async-start | bytes 524288 | tf_op jit(solution)/shard_map/all_to_all | solution.py:375
  26.5 2.7 %collective-permute-start.1 = (f32[1,128,128]{2,1,0:T(8,128)S(1)}, f32[1,128,128]{2,1,0:T(8,128)S(1)}, u32[]{:S(2)}, u32[]{:S(2)}) collective-permute-start(f32[1,128,128]{2,1,0:T(8,128)S(1)} %maximum_bitcast_fusion), channel_id=1, source_target_pairs={{0,16},{4,20},{8,24},{12,28},{16,0},{20,4},{24,8},{28,12},{1,17},{... | collective-permute-start | bytes 196616 | tf_op jit(solution)/shard_map/ppermute | solution.py:28
  29.2 9.4 %collective-permute-done.1 = f32[1,128,128]{2,1,0:T(8,128)S(1)} collective-permute-done((f32[1,128,128]{2,1,0:T(8,128)S(1)}, f32[1,128,128]{2,1,0:T(8,128)S(1)}, u32[]{:S(2)}, u32[]{:S(2)}) %collective-permute-start.1) | collective-permute-done | bytes 65568 | tf_op jit(solution)/shard_map/ppermute | solution.py:28
  38.6 0.1 collective-permute-start.2
  38.7 5.0 %collective-permute-done.2 = f32[2,128,128]{2,1,0:T(8,128)S(1)} collective-permute-done((f32[2,128,128]{2,1,0:T(8,128)S(1)}, f32[2,128,128]{2,1,0:T(8,128)S(1)}, u32[]{:S(2)}, u32[]{:S(2)}) %collective-permute-start.2) | collective-permute-done | bytes 131104 | tf_op jit(solution)/shard_map/ppermute | solution.py:28
  43.8 0.0 all-to-all-done.1
  43.8 1.5 %collective-permute-start.4 = (f32[4,128,128]{2,1,0:T(8,128)S(1)}, f32[4,128,128]{2,1,0:T(8,128)S(1)}, u32[]{:S(2)}, u32[]{:S(2)}) collective-permute-start(f32[4,128,128]{2,1,0:T(8,128)S(1)} %pad_maximum_fusion.1), channel_id=1, source_target_pairs={{0,4},{4,0},{8,12},{12,8},{16,20},{20,16},{24,28},{28,24},{1,5},{5... | collective-permute-start | bytes 786440 | tf_op jit(solution)/shard_map/ppermute | solution.py:28
  45.3 0.0 collective-permute-done.3.refs_1_
  45.3 0.0 copy-done
  45.3 5.4 %solve_last.1 = f32[32,32,128]{2,1,0:T(8,128)S(1)} custom-call(f32[16,2,8,256]{3,2,1,0:T(8,128)S(1)} %bitcast.26, f32[32,32,256]{2,1,0:T(8,128)S(1)} %copy-done, f32[32,32,256]{2,1,0:T(8,128)S(1)} %collective-permute-done.3.refs_1_), custom_call_target="tpu_custom_call" | custom-call | tf_op jit(solution)/shard_map/solve_last/pallas_call | solution.py:236
  50.8 0.0 collective-permute-done.4
  50.8 17.3 %all_to_all.20.pieces = f32[8,4,32,128]{3,2,1,0:T(8,128)S(1)} all-to-all(f32[8,4,32,128]{3,2,1,0:T(8,128)S(1)} %bitcast.25), channel_id=1, replica_groups=mesh['gx'=8,'gy'=2,'gz'=2] {'gx'}, dimensions={0} | all-to-all | bytes 1048576 | tf_op jit(solution)/shard_map/all_to_all | solution.py:395
  68.1 1.0 %sketch.1 = f32[16,4,8,128]{3,2,1,0:T(8,128)} custom-call(f32[8,4,32,128]{3,2,1,0:T(8,128)S(1)} %all_to_all.20.pieces, f32[8,128,128]{2,1,0:T(8,128)S(1)} %pad_maximum_fusion.packed), custom_call_target="tpu_custom_call" | custom-call | tf_op jit(solution)/shard_map/sketch/pallas_call | solution.py:268
  69.1 4.9 %all-to-all-start.3 = ((f32[16,4,8,128]{3,2,1,0:T(8,128)}), f32[16,4,8,128]{3,2,1,0:T(8,128)S(1)}, u32[]{:S(2)}, u32[]{:S(2)}) async-start(f32[16,4,8,128]{3,2,1,0:T(8,128)} %sketch.1), calls=%async_computation.3 | async-start | bytes 524288 | tf_op jit(solution)/shard_map/all_to_all | solution.py:404
  74.0 0.1 collective-permute-start.6
  74.1 0.4 first_sums.1.refs_0_
  74.5 2.0 %collective-permute-start.5 = (f32[160,256]{1,0:T(8,128)S(1)}, f32[160,256]{1,0:T(8,128)S(1)}, u32[]{:S(2)}, u32[]{:S(2)}) collective-permute-start(f32[160,256]{1,0:T(8,128)S(1)} %first_sums.1.refs_0_), channel_id=1, source_target_pairs={{0,1},{1,0},{2,3},{3,2},{4,5},{5,4},{6,7},{7,6},{8,9},{9,8},{10,11... | collective-permute-start | bytes 491528 | tf_op jit(solution)/shard_map/ppermute | solution.py:28
  76.5 0.0 collective-permute-done.6
  76.5 0.7 place.1
  77.3 6.0 %collective-permute-done.5.refs_1_ = f32[160,256]{1,0:T(8,128)S(1)} collective-permute-done((f32[160,256]{1,0:T(8,128)S(1)}, f32[160,256]{1,0:T(8,128)S(1)}, u32[]{:S(2)}, u32[]{:S(2)}) %collective-permute-start.5) | collective-permute-done | bytes 163872 | tf_op jit(solution)/shard_map/ppermute | solution.py:28
  83.3 4.9 %solve_first.1 = f32[32,128]{1,0:T(8,128)} custom-call(f32[160,256]{1,0:T(8,128)S(1)} %first_sums.1.refs_0_, f32[160,256]{1,0:T(8,128)S(1)} %collective-permute-done.5.refs_1_), custom_call_target="tpu_custom_call" | custom-call | tf_op jit(solution)/shard_map/solve_first/pallas_call | solution.py:320
  88.2 0.0 all-to-all-done.3
  88.2 0.8 copy.11
  (11 shorter events, 0.1 us)
Async XLA Ops:
  0.6 22.0 %copy-start.1 = (bf16[512,256]{1,0:T(8,128)(2,1)S(1)}, bf16[512,256]{1,0:T(8,128)(2,1)}, u32[]{:S(2)}) copy-start(bf16[512,256]{1,0:T(8,128)(2,1)} %last_m_hbm.1) | copy-start | bytes 786436
  0.6 13.8 %copy-start.2 = (bf16[32,128]{1,0:T(8,128)(2,1)S(1)}, bf16[32,128]{1,0:T(8,128)(2,1)}, u32[]{:S(2)}) copy-start(bf16[32,128]{1,0:T(8,128)(2,1)} %param.8) | copy-start | bytes 24580
  5.0 40.3 %copy-start = (f32[32,32,256]{2,1,0:T(8,128)S(1)}, f32[32,32,256]{2,1,0:T(8,128)}, u32[]{:S(2)}) copy-start(f32[32,32,256]{2,1,0:T(8,128)} %get-tuple-element.14.refs_0_) | copy-start | bytes 3145732
  5.0 17.6 %all-to-all-start = ((f32[16,8,512]{2,1,0:T(8,128)}), f32[16,8,512]{2,1,0:T(8,128)S(1)}, u32[]{:S(2)}, u32[]{:S(2)}) async-start(f32[16,8,512]{2,1,0:T(8,128)} %bitcast.28), calls=%async_computation | async-start | bytes 524288 | tf_op jit(solution)/shard_map/all_to_all | solution.py:367
  12.5 1.9 %collective-permute-start = (f32[32,256]{1,0:T(8,128)}, f32[32,256]{1,0:T(8,128)S(1)}, u32[]{:S(2)}, u32[]{:S(2)}) collective-permute-start(f32[32,256]{1,0:T(8,128)} %get-tuple-element.11), channel_id=1, source_target_pairs={{0,2},{2,0},{1,3},{3,1},{4,6},{6,4},{5,7},{7,5},{8,10},{10,8},{9,1... | collective-permute-start | bytes 98312 | tf_op jit(solution)/shard_map/ppermute | solution.py:28
  12.9 32.4 %collective-permute-start.3 = (f32[32,32,256]{2,1,0:T(8,128)}, f32[32,32,256]{2,1,0:T(8,128)S(1)}, u32[]{:S(2)}, u32[]{:S(2)}) collective-permute-start(f32[32,32,256]{2,1,0:T(8,128)} %get-tuple-element.15), channel_id=1, source_target_pairs={{0,1},{1,0},{2,3},{3,2},{4,5},{5,4},{6,7},{7,6},{8,9},{9,8},{10,11... | collective-permute-start | bytes 3145736 | tf_op jit(solution)/shard_map/ppermute | solution.py:28
  23.5 20.3 %all-to-all-start.1 = ((f32[32,8,256]{2,1,0:T(8,128)}), f32[32,8,256]{2,1,0:T(8,128)S(1)}, u32[]{:S(2)}, u32[]{:S(2)}) async-start(f32[32,8,256]{2,1,0:T(8,128)} %broadcast_in_dim.10), calls=%async_computation.1 | async-start | bytes 524288 | tf_op jit(solution)/shard_map/all_to_all | solution.py:375
  26.5 12.2 %collective-permute-start.1 = (f32[1,128,128]{2,1,0:T(8,128)S(1)}, f32[1,128,128]{2,1,0:T(8,128)S(1)}, u32[]{:S(2)}, u32[]{:S(2)}) collective-permute-start(f32[1,128,128]{2,1,0:T(8,128)S(1)} %maximum_bitcast_fusion), channel_id=1, source_target_pairs={{0,16},{4,20},{8,24},{12,28},{16,0},{20,4},{24,8},{28,12},{1,17},{... | collective-permute-start | bytes 196616 | tf_op jit(solution)/shard_map/ppermute | solution.py:28
  38.6 5.1 %collective-permute-start.2 = (f32[2,128,128]{2,1,0:T(8,128)S(1)}, f32[2,128,128]{2,1,0:T(8,128)S(1)}, u32[]{:S(2)}, u32[]{:S(2)}) collective-permute-start(f32[2,128,128]{2,1,0:T(8,128)S(1)} %pad_maximum_fusion.3), channel_id=1, source_target_pairs={{0,8},{4,12},{8,0},{12,4},{16,24},{20,28},{24,16},{28,20},{1,9},{5... | collective-permute-start | bytes 393224 | tf_op jit(solution)/shard_map/ppermute | solution.py:28
  43.8 7.0 %collective-permute-start.4 = (f32[4,128,128]{2,1,0:T(8,128)S(1)}, f32[4,128,128]{2,1,0:T(8,128)S(1)}, u32[]{:S(2)}, u32[]{:S(2)}) collective-permute-start(f32[4,128,128]{2,1,0:T(8,128)S(1)} %pad_maximum_fusion.1), channel_id=1, source_target_pairs={{0,4},{4,0},{8,12},{12,8},{16,20},{20,16},{24,28},{28,24},{1,5},{5... | collective-permute-start | bytes 786440 | tf_op jit(solution)/shard_map/ppermute | solution.py:28
  69.1 19.1 %all-to-all-start.3 = ((f32[16,4,8,128]{3,2,1,0:T(8,128)}), f32[16,4,8,128]{3,2,1,0:T(8,128)S(1)}, u32[]{:S(2)}, u32[]{:S(2)}) async-start(f32[16,4,8,128]{3,2,1,0:T(8,128)} %sketch.1), calls=%async_computation.3 | async-start | bytes 524288 | tf_op jit(solution)/shard_map/all_to_all | solution.py:404
  74.0 2.5 %collective-permute-start.6 = (f32[1,8,4,8,128]{4,3,2,1,0:T(8,128)S(1)}, f32[1,8,4,8,128]{4,3,2,1,0:T(8,128)S(1)}, u32[]{:S(2)}, u32[]{:S(2)}) collective-permute-start(f32[1,8,4,8,128]{4,3,2,1,0:T(8,128)S(1)} %slice_bitcast_fusion), channel_id=1, source_target_pairs={{0,2},{2,0},{1,3},{3,1},{4,6},{6,4},{5,7},{7,5},{8,10},{10,8},{9,1... | collective-permute-start | bytes 393224 | tf_op jit(solution)/shard_map/ppermute | solution.py:28
  74.5 8.8 %collective-permute-start.5 = (f32[160,256]{1,0:T(8,128)S(1)}, f32[160,256]{1,0:T(8,128)S(1)}, u32[]{:S(2)}, u32[]{:S(2)}) collective-permute-start(f32[160,256]{1,0:T(8,128)S(1)} %first_sums.1.refs_0_), channel_id=1, source_target_pairs={{0,1},{1,0},{2,3},{3,2},{4,5},{5,4},{6,7},{7,6},{8,9},{9,8},{10,11... | collective-permute-start | bytes 491528 | tf_op jit(solution)/shard_map/ppermute | solution.py:28

commit v5 on v4

--- a/solution.py
+++ b/solution.py
@@ -34,14 +34,27 @@
     return array
 
 
-def swap_gather(array, axis, gate=None):
-    held, order = array[None], [0]
+def after(value, *others):
+    value, *_ = lax.optimization_barrier((value, *others))
+    return value
+
+
+def swap_order(axis):
+    order = [0]
     for bit in axis_bits(axis):
-        if bit == 1 and gate is not None:
-            held, gate = lax.optimization_barrier((held, gate))
-        held = jnp.concatenate([held, swap(held, axis, bit)], axis=0)
         order += [o ^ bit for o in order]
-    return held, order, gate
+    return order
+
+
+def swap_step(held, axis, bit):
+    return jnp.concatenate([held, swap(held, axis, bit)], axis=0)
+
+
+def swap_gather(array, axis):
+    held = array[None]
+    for bit in axis_bits(axis):
+        held = swap_step(held, axis, bit)
+    return held
 
 
 def gather_rows(array, outer, inner):
@@ -273,13 +286,13 @@
     )(pieces, packed)
 
 
-def first_sums_kernel(first_at, left_at, rows, packed, sums):
+def first_sums_kernel(left_at, rows, packed, sums):
     x_cells, cols = rows.shape
     blocks = range(packed.shape[0])
     left = jnp.concatenate([packed[k, left_at : left_at + x_cells] for k in blocks], axis=0)
     sums[:x_cells] = rows[...]
     for c in range(cols // LANES):
-        at = first_at + c * x_cells
+        at = c * x_cells
         sums[x_cells:, c * LANES : (c + 1) * LANES] = lax.dot_general(
             left,
             jnp.concatenate([packed[k, at : at + x_cells] for k in blocks], axis=0),
@@ -289,9 +302,9 @@
         )
 
 
-def first_sums(first_at, left_at, rows, packed):
-    return pl.pallas_call(
-        functools.partial(first_sums_kernel, first_at, left_at),
+def first_sums(left_at, rows, packed):
+    return pl.pallas_call(
+        functools.partial(first_sums_kernel, left_at),
         out_shape=jax.ShapeDtypeStruct(
             (rows.shape[0] + packed.shape[2], rows.shape[1]), jnp.float32
         ),
@@ -316,7 +329,7 @@
     )
 
 
-def solve_first(x_cells, sums):
+def solve_first(x_cells, *sums):
     return pl.pallas_call(
         first_kernel,
         out_shape=jax.ShapeDtypeStruct((x_cells, sums[0].shape[0] - x_cells), jnp.float32),
@@ -362,6 +375,19 @@
     for s in range(1, shares):
         terms[s] = swap(terms[s], "gz", s)
 
+    order = swap_order("gx")
+    first_rows = swap_sum(first_part, "gy")
+    packed = jnp.concatenate(
+        [
+            first_rows.reshape(x_cells, -1, LANES).transpose(1, 0, 2).reshape(-1, LANES),
+            left_x.astype(jnp.float32),
+        ],
+        axis=0,
+    )[None]
+    left_at = x_cells * cols // LANES
+    first_bit, *bits = axis_bits("gx")
+    packed = swap_step(packed, "gx", first_bit)
+
     group = ("gx", "gy")
     own = rank // lax.axis_size(group)
     last_rows = lax.all_to_all(last_part.reshape(-1, own, m_cells), group, 0, 0, tiled=True)
@@ -369,27 +395,19 @@
     both = jnp.dot(
         jnp.concatenate(split_terms(last_rows), axis=0), last_m, preferred_element_type=jnp.float32
     )
-    both = both[:own] + both[own:]
+    both = after(both[:own] + both[own:], packed)
     count = lax.axis_size(ALL)
     copies = jnp.broadcast_to(both[None], (count, own, cols))
     system = lax.all_to_all(copies, ALL, 0, 0, tiled=True).reshape(-1, shares, own, cols)
     if own % ROWS:
         system = jnp.sum(system, axis=1).reshape(-1, 1, ROWS, cols)
 
-    first_rows = swap_sum(first_part, "gy")
-    packed = jnp.concatenate(
-        [
-            last_rows.reshape(own, -1, LANES).transpose(1, 0, 2).reshape(-1, LANES),
-            first_rows.reshape(x_cells, -1, LANES).transpose(1, 0, 2).reshape(-1, LANES),
-            left_x.astype(jnp.float32),
-        ],
-        axis=0,
-    )
-    first_at = own * m_cells // LANES
-    left_at = first_at + x_cells * cols // LANES
-    packed, order, system = swap_gather(packed, "gx", system)
-    projected = solve_last(system, terms)
-    projected, packed = lax.optimization_barrier((projected, packed))
+    for bit in bits:
+        packed = swap_step(packed, "gx", bit)
+    sums = first_sums(left_at, first_rows, packed)
+    projected = solve_last(after(system, sums), terms)
+    sums = [swap(sums, "gz", z) if z else sums for z in range(shares)]
+    projected = after(projected, *sums)
 
     pieces = projected.reshape(blocks, y_own, x_cells, rank)
     pieces = lax.all_to_all(pieces, "gx", 0, 0, tiled=True)
@@ -401,20 +419,20 @@
         middle = middle.reshape(y_own, devices, rank_own, rank).transpose(1, 0, 2, 3)
     else:
         middle = sketch(order, left_at, rank_own, pieces, packed)
+
+    if own % ROWS:
+        core_last = gather_rows(last_rows, "gx", "gy")
+    else:
+        core_last = last_rows.reshape(own, -1, LANES).transpose(1, 0, 2)
+        core_last = swap_gather(core_last, "gx")
+        middle = after(middle, core_last)
+        core_last = swap_gather(core_last, "gy")
+        core_last = place(order, swap_order("gy"), core_last)
+
     received = lax.all_to_all(middle, group, 0, 0, tiled=True)
     received = received.reshape(blocks, shares, y_own, rank_own, rank)
     core_middle = received.transpose(3, 1, 0, 2, 4).reshape(rank_own, y_cells, rank)
-
-    if own % ROWS:
-        core_last = gather_rows(last_rows, "gx", "gy")
-    else:
-        core_last = packed[:, :first_at].reshape(blocks, -1, own, LANES)
-        core_last, inner_order, _ = swap_gather(core_last, "gy")
-        core_last = place(order, inner_order, core_last)
-
-    sums = first_sums(first_at, left_at, first_rows, packed)
-    sums = [swap(sums, "gz", z) if z else sums for z in range(shares)]
-    core_first = solve_first(x_cells, sums)
+    core_first = solve_first(x_cells, after(sums[0], middle), *sums[1:])
     return (core_first, core_middle, core_last)
 
 

time: 89.5 us -> 90.6 us (1.012)
  blocking collectives: 17.3 us -> 0 us
  starting transfers between devices: 23.7 us -> 33.8 us
  waiting for transfers between devices: 27.9 us -> 35.3 us
    all_to_all x1 -> x0, blocking collectives: 17.3 us -> none  [per_device(): pieces = lax.all_to_all(pieces, 'gx', 0, 0, tiled=True)]
    ppermute x7 -> x10, waiting for transfers between devices: 20.5 us -> 31.3 us  [swap(): lax.ppermute(array, axis, [(s, s ^ bits) for s in range(lax.axis_size(axi...]
    all_to_all x1, waiting for transfers between devices: 7.33 us -> 0.01 us  [per_device(): lax.all_to_all(last_part.reshape(-1, own, m_cells), group, 0, 0, tiled=True)]
    ppermute x7 -> x10, starting transfers between devices: 8.32 us -> 13.3 us  [swap(): lax.ppermute(array, axis, [(s, s ^ bits) for s in range(lax.axis_size(axi...]
    all_to_all x1, waiting for transfers between devices: 0.01 us -> 4 us  [per_device(): lax.all_to_all(copies, ALL, 0, 0, tiled=True).reshape(-1, shares, own, cols)]
    all_to_all x0 -> x1, starting transfers between devices: none -> 3.65 us  [per_device(): pieces = lax.all_to_all(pieces, 'gx', 0, 0, tiled=True)]
    all_to_all x1, starting transfers between devices: 2.92 us -> 4.22 us  [per_device(): lax.all_to_all(copies, ALL, 0, 0, tiled=True).reshape(-1, shares, own, cols)]
  transfers between devices with their start and end apart: 10 -> 14, of which waited for: 4 -> 6; matrix products, arithmetic and copies ran while one was open for 2% -> 2% of each run, Pallas kernels for 13% -> 15%
where the time goes in v5:
time: 90.6 us; the launch traced here: 90.1 us
  waiting for transfers between devices  35.3 us (39%)
  starting transfers between devices  33.8 us (37%)
  Pallas kernels  17.6 us (19%)
  local copies, waits for them, and re-layouts  1.52 us (2%)
    ppermute x10, waiting for transfers between devices, swap(): lax.ppermute(array, axis, [(s, s ^ bits) for s in range(lax.axis_size(axi...  31.3 us
    ppermute x10, starting transfers between devices, swap(): lax.ppermute(array, axis, [(s, s ^ bits) for s in range(lax.axis_size(axi...  13.3 us
    all_to_all x1, starting transfers between devices, per_device(): lax.all_to_all(last_part.reshape(-1, own, m_cells), group, 0, 0, tiled=True)  7.15 us
    pallas_call x1, Pallas kernels, solve_last(): pl.pallas_call(last_kernel, out_shape=jax.ShapeDtypeStruct((y_cells, x_ce...  6.24 us
    all_to_all x1, starting transfers between devices, per_device(): received = lax.all_to_all(middle, group, 0, 0, tiled=True)  5.44 us
    pallas_call x1, Pallas kernels, solve_first(): pl.pallas_call(first_kernel, out_shape=jax.ShapeDtypeStruct((x_cells, sum...  4.89 us
    pallas_call x1, Pallas kernels, local_products(): pl.pallas_call(functools.partial(local_kernel, chunks, shares), in_specs=...  4.35 us
    all_to_all x1, starting transfers between devices, per_device(): lax.all_to_all(copies, ALL, 0, 0, tiled=True).reshape(-1, shares, own, cols)  4.22 us
  transfers between devices with their start and end apart: 14, of which 6 were waited for; matrix products, arithmetic and copies ran while one was open for 2% of the time, Pallas kernels for 15%

profile of v5, /device:TPU:0, one launch (start us, length us, event | category | flops | bytes accessed | tf_op | source)
XLA Modules:
  0.0 90.1 jit_solution(6059523982086665825)
XLA Ops:
  0.6 0.0 copy-start.1
  0.6 0.0 copy-start.2
  0.7 4.4 %local_products.1 = (f32[128,512]{1,0:T(8,128)}, f32[32,256]{1,0:T(8,128)}, f32[32,32,256]{2,1,0:T(8,128)}, f32[32,32,256]{2,1,0:T(8,128)}) custom-call(bf16[32,64,512]{2,1,0:T(8,128)(2,1)} %field_hbm.1, bf16[32,128]{1,0:T(8,128)(2,1)} %last_x_hbm.1, bf16[64,128]{1,0:T(8,128)(2,1)} %last_y_hbm.1, bf16[64,256]{1,0:T(8,128)(2,1)} %right_y_hbm.1, ...), custom_call_target="tpu_custom_call" | custom-call | tf_op jit(solution)/shard_map/local_products/pallas_call | solution.py:202
  5.0 0.5 collective-permute-start
  5.5 0.0 copy-start
  5.5 7.1 %all-to-all-start = ((f32[16,8,512]{2,1,0:T(8,128)}), f32[16,8,512]{2,1,0:T(8,128)S(1)}, u32[]{:S(2)}, u32[]{:S(2)}) async-start(f32[16,8,512]{2,1,0:T(8,128)} %bitcast.31), calls=%async_computation | async-start | bytes 524288 | tf_op jit(solution)/shard_map/all_to_all | solution.py:393
  12.7 0.0 copy-done.2
  12.7 0.0 collective-permute-done
  12.7 0.8 add.6.rows
  13.5 2.9 %collective-permute-start.1 = (f32[1,96,128]{2,1,0:T(8,128)S(1)}, f32[1,96,128]{2,1,0:T(8,128)S(1)}, u32[]{:S(2)}, u32[]{:S(2)}) collective-permute-start(f32[1,96,128]{2,1,0:T(8,128)S(1)} %maximum_bitcast_fusion), channel_id=1, source_target_pairs={{0,16},{4,20},{8,24},{12,28},{16,0},{20,4},{24,8},{28,12},{1,17},{... | collective-permute-start | bytes 147464 | tf_op jit(solution)/shard_map/ppermute | solution.py:28
  16.4 1.5 %collective-permute-start.4 = (f32[32,32,256]{2,1,0:T(8,128)}, f32[32,32,256]{2,1,0:T(8,128)S(1)}, u32[]{:S(2)}, u32[]{:S(2)}) collective-permute-start(f32[32,32,256]{2,1,0:T(8,128)} %get-tuple-element.17), channel_id=1, source_target_pairs={{0,1},{1,0},{2,3},{3,2},{4,5},{5,4},{6,7},{7,6},{8,9},{9,8},{10,11... | collective-permute-start | bytes 3145736 | tf_op jit(solution)/shard_map/ppermute | solution.py:28
  17.9 6.5 %collective-permute-done.1 = f32[1,96,128]{2,1,0:T(8,128)S(1)} collective-permute-done((f32[1,96,128]{2,1,0:T(8,128)S(1)}, f32[1,96,128]{2,1,0:T(8,128)S(1)}, u32[]{:S(2)}, u32[]{:S(2)}) %collective-permute-start.1) | collective-permute-done | bytes 49184 | tf_op jit(solution)/shard_map/ppermute | solution.py:28
  24.5 0.1 collective-permute-start.2
  24.5 0.0 all-to-all-done
  24.6 0.0 copy-done.1
  24.6 0.1 fusion.1
  24.8 0.7 broadcast_in_dim.16
  25.5 4.2 %all-to-all-start.1 = ((f32[32,8,256]{2,1,0:T(8,128)}), f32[32,8,256]{2,1,0:T(8,128)S(1)}, u32[]{:S(2)}, u32[]{:S(2)}) async-start(f32[32,8,256]{2,1,0:T(8,128)} %broadcast_in_dim.16), calls=%async_computation.1 | async-start | bytes 524288 | tf_op jit(solution)/shard_map/all_to_all | solution.py:401
  29.7 0.0 collective-permute-done.2
  29.7 1.8 %collective-permute-start.3 = (f32[4,96,128]{2,1,0:T(8,128)S(1)}, f32[4,96,128]{2,1,0:T(8,128)S(1)}, u32[]{:S(2)}, u32[]{:S(2)}) collective-permute-start(f32[4,96,128]{2,1,0:T(8,128)S(1)} %pad_maximum_fusion.2), channel_id=1, source_target_pairs={{0,4},{4,0},{8,12},{12,8},{16,20},{20,16},{24,28},{28,24},{1,5},{5... | collective-permute-start | bytes 589832 | tf_op jit(solution)/shard_map/ppermute | solution.py:28
  31.6 7.9 %collective-permute-done.3 = f32[4,96,128]{2,1,0:T(8,128)S(1)} collective-permute-done((f32[4,96,128]{2,1,0:T(8,128)S(1)}, f32[4,96,128]{2,1,0:T(8,128)S(1)}, u32[]{:S(2)}, u32[]{:S(2)}) %collective-permute-start.3) | collective-permute-done | bytes 196640 | tf_op jit(solution)/shard_map/ppermute | solution.py:28
  39.5 0.4 first_sums.1.refs_0_
  40.0 1.5 %collective-permute-start.5 = (f32[160,256]{1,0:T(8,128)S(1)}, f32[160,256]{1,0:T(8,128)S(1)}, u32[]{:S(2)}, u32[]{:S(2)}) collective-permute-start(f32[160,256]{1,0:T(8,128)S(1)} %first_sums.1.refs_0_), channel_id=1, source_target_pairs={{0,1},{1,0},{2,3},{3,2},{4,5},{5,4},{6,7},{7,6},{8,9},{9,8},{10,11... | collective-permute-start | bytes 491528 | tf_op jit(solution)/shard_map/ppermute | solution.py:28
  41.5 4.0 %all-to-all-done.1 = f32[32,8,256]{2,1,0:T(8,128)S(1)} async-done(((f32[32,8,256]{2,1,0:T(8,128)}), f32[32,8,256]{2,1,0:T(8,128)S(1)}, u32[]{:S(2)}, u32[]{:S(2)}) %all-to-all-start.1) | async-done | bytes 262176 | tf_op jit(solution)/shard_map/all_to_all | solution.py:401
  45.5 0.0 collective-permute-done.4.refs_1_
  45.5 0.0 copy-done
  45.5 6.2 %solve_last.1 = f32[32,32,128]{2,1,0:T(8,128)} custom-call(f32[16,2,8,256]{3,2,1,0:T(8,128)S(1)} %bitcast.25, f32[32,32,256]{2,1,0:T(8,128)S(1)} %copy-done, f32[32,32,256]{2,1,0:T(8,128)S(1)} %collective-permute-done.4.refs_1_), custom_call_target="tpu_custom_call" | custom-call | tf_op jit(solution)/shard_map/solve_last/pallas_call | solution.py:249
  51.7 0.0 collective-permute-done.5.refs_1_
  51.7 3.6 %all-to-all-start.2 = ((f32[8,4,32,128]{3,2,1,0:T(8,128)}), f32[8,4,32,128]{3,2,1,0:T(8,128)S(1)}, u32[]{:S(2)}, u32[]{:S(2)}) async-start(f32[8,4,32,128]{3,2,1,0:T(8,128)} %bitcast.5), calls=%async_computation.2 | async-start | bytes 1048576 | tf_op jit(solution)/shard_map/all_to_all | solution.py:413
  55.3 2.9 %collective-permute-start.6 = (f32[1,4,8,128]{3,2,1,0:T(8,128)S(1)}, f32[1,4,8,128]{3,2,1,0:T(8,128)S(1)}, u32[]{:S(2)}, u32[]{:S(2)}) collective-permute-start(f32[1,4,8,128]{3,2,1,0:T(8,128)S(1)} %bitcast.27), channel_id=1, source_target_pairs={{0,16},{4,20},{8,24},{12,28},{16,0},{20,4},{24,8},{28,12},{1,17},{... | collective-permute-start | bytes 49160 | tf_op jit(solution)/shard_map/ppermute | solution.py:28
  58.3 12.3 %collective-permute-done.6 = f32[1,4,8,128]{3,2,1,0:T(8,128)S(1)} collective-permute-done((f32[1,4,8,128]{3,2,1,0:T(8,128)S(1)}, f32[1,4,8,128]{3,2,1,0:T(8,128)S(1)}, u32[]{:S(2)}, u32[]{:S(2)}) %collective-permute-start.6) | collective-permute-done | bytes 16416 | tf_op jit(solution)/shard_map/ppermute | solution.py:28
  70.5 0.0 collective-permute-start.7
  70.5 0.0 all-to-all-done.2.pieces
  70.5 1.0 %sketch.1 = f32[16,4,8,128]{3,2,1,0:T(8,128)} custom-call(f32[8,4,32,128]{3,2,1,0:T(8,128)S(1)} %all-to-all-done.2.pieces, f32[8,96,128]{2,1,0:T(8,128)S(1)} %pad_maximum_fusion.packed), custom_call_target="tpu_custom_call" | custom-call | tf_op jit(solution)/shard_map/sketch/pallas_call | solution.py:281
  71.5 5.4 %all-to-all-start.3 = ((f32[16,4,8,128]{3,2,1,0:T(8,128)}), f32[16,4,8,128]{3,2,1,0:T(8,128)S(1)}, u32[]{:S(2)}, u32[]{:S(2)}) async-start(f32[16,4,8,128]{3,2,1,0:T(8,128)} %sketch.1), calls=%async_computation.3 | async-start | bytes 524288 | tf_op jit(solution)/shard_map/all_to_all | solution.py:432
  76.9 0.0 collective-permute-done.7
  77.0 2.0 %collective-permute-start.8 = (f32[4,4,8,128]{3,2,1,0:T(8,128)S(1)}, f32[4,4,8,128]{3,2,1,0:T(8,128)S(1)}, u32[]{:S(2)}, u32[]{:S(2)}) collective-permute-start(f32[4,4,8,128]{3,2,1,0:T(8,128)S(1)} %pad_maximum_fusion.5), channel_id=1, source_target_pairs={{0,4},{4,0},{8,12},{12,8},{16,20},{20,16},{24,28},{28,24},{1,5},{5... | collective-permute-start | bytes 196616 | tf_op jit(solution)/shard_map/ppermute | solution.py:28
  79.0 3.2 %collective-permute-done.8 = f32[4,4,8,128]{3,2,1,0:T(8,128)S(1)} collective-permute-done((f32[4,4,8,128]{3,2,1,0:T(8,128)S(1)}, f32[4,4,8,128]{3,2,1,0:T(8,128)S(1)}, u32[]{:S(2)}, u32[]{:S(2)}) %collective-permute-start.8) | collective-permute-done | bytes 65568 | tf_op jit(solution)/shard_map/ppermute | solution.py:28
  82.2 0.1 collective-permute-start.9
  82.3 1.3 %collective-permute-done.9 = f32[1,8,4,8,128]{4,3,2,1,0:T(8,128)S(1)} collective-permute-done((f32[1,8,4,8,128]{4,3,2,1,0:T(8,128)S(1)}, f32[1,8,4,8,128]{4,3,2,1,0:T(8,128)S(1)}, u32[]{:S(2)}, u32[]{:S(2)}) %collective-permute-start.9) | collective-permute-done | bytes 131104 | tf_op jit(solution)/shard_map/ppermute | solution.py:28
  83.6 0.7 place.1
  84.4 4.9 %solve_first.1 = f32[32,128]{1,0:T(8,128)} custom-call(f32[160,256]{1,0:T(8,128)S(1)} %first_sums.1.refs_0_, f32[160,256]{1,0:T(8,128)S(1)} %collective-permute-done.5.refs_1_), custom_call_target="tpu_custom_call" | custom-call | tf_op jit(solution)/shard_map/solve_first/pallas_call | solution.py:333
  89.3 0.0 all-to-all-done.3
  89.3 0.8 copy.11
  (13 shorter events, 0.1 us)
Async XLA Ops:
  0.6 24.0 %copy-start.1 = (bf16[512,256]{1,0:T(8,128)(2,1)S(1)}, bf16[512,256]{1,0:T(8,128)(2,1)}, u32[]{:S(2)}) copy-start(bf16[512,256]{1,0:T(8,128)(2,1)} %last_m_hbm.1) | copy-start | bytes 786436
  0.6 12.0 %copy-start.2 = (bf16[32,128]{1,0:T(8,128)(2,1)S(1)}, bf16[32,128]{1,0:T(8,128)(2,1)}, u32[]{:S(2)}) copy-start(bf16[32,128]{1,0:T(8,128)(2,1)} %param.8) | copy-start | bytes 24580
  5.0 7.7 %collective-permute-start = (f32[32,256]{1,0:T(8,128)}, f32[32,256]{1,0:T(8,128)S(1)}, u32[]{:S(2)}, u32[]{:S(2)}) collective-permute-start(f32[32,256]{1,0:T(8,128)} %get-tuple-element.12), channel_id=1, source_target_pairs={{0,2},{2,0},{1,3},{3,1},{4,6},{6,4},{5,7},{7,5},{8,10},{10,8},{9,1... | collective-permute-start | bytes 98312 | tf_op jit(solution)/shard_map/ppermute | solution.py:28
  5.5 39.9 %copy-start = (f32[32,32,256]{2,1,0:T(8,128)S(1)}, f32[32,32,256]{2,1,0:T(8,128)}, u32[]{:S(2)}) copy-start(f32[32,32,256]{2,1,0:T(8,128)} %get-tuple-element.16.refs_0_) | copy-start | bytes 3145732
  5.5 19.0 %all-to-all-start = ((f32[16,8,512]{2,1,0:T(8,128)}), f32[16,8,512]{2,1,0:T(8,128)S(1)}, u32[]{:S(2)}, u32[]{:S(2)}) async-start(f32[16,8,512]{2,1,0:T(8,128)} %bitcast.31), calls=%async_computation | async-start | bytes 524288 | tf_op jit(solution)/shard_map/all_to_all | solution.py:393
  13.5 10.9 %collective-permute-start.1 = (f32[1,96,128]{2,1,0:T(8,128)S(1)}, f32[1,96,128]{2,1,0:T(8,128)S(1)}, u32[]{:S(2)}, u32[]{:S(2)}) collective-permute-start(f32[1,96,128]{2,1,0:T(8,128)S(1)} %maximum_bitcast_fusion), channel_id=1, source_target_pairs={{0,16},{4,20},{8,24},{12,28},{16,0},{20,4},{24,8},{28,12},{1,17},{... | collective-permute-start | bytes 147464 | tf_op jit(solution)/shard_map/ppermute | solution.py:28
  16.4 29.1 %collective-permute-start.4 = (f32[32,32,256]{2,1,0:T(8,128)}, f32[32,32,256]{2,1,0:T(8,128)S(1)}, u32[]{:S(2)}, u32[]{:S(2)}) collective-permute-start(f32[32,32,256]{2,1,0:T(8,128)} %get-tuple-element.17), channel_id=1, source_target_pairs={{0,1},{1,0},{2,3},{3,2},{4,5},{5,4},{6,7},{7,6},{8,9},{9,8},{10,11... | collective-permute-start | bytes 3145736 | tf_op jit(solution)/shard_map/ppermute | solution.py:28
  24.5 5.3 %collective-permute-start.2 = (f32[2,96,128]{2,1,0:T(8,128)S(1)}, f32[2,96,128]{2,1,0:T(8,128)S(1)}, u32[]{:S(2)}, u32[]{:S(2)}) collective-permute-start(f32[2,96,128]{2,1,0:T(8,128)S(1)} %pad_maximum_fusion.4), channel_id=1, source_target_pairs={{0,8},{4,12},{8,0},{12,4},{16,24},{20,28},{24,16},{28,20},{1,9},{5... | collective-permute-start | bytes 294920 | tf_op jit(solution)/shard_map/ppermute | solution.py:28
  25.5 20.0 %all-to-all-start.1 = ((f32[32,8,256]{2,1,0:T(8,128)}), f32[32,8,256]{2,1,0:T(8,128)S(1)}, u32[]{:S(2)}, u32[]{:S(2)}) async-start(f32[32,8,256]{2,1,0:T(8,128)} %broadcast_in_dim.16), calls=%async_computation.1 | async-start | bytes 524288 | tf_op jit(solution)/shard_map/all_to_all | solution.py:401
  29.7 9.8 %collective-permute-start.3 = (f32[4,96,128]{2,1,0:T(8,128)S(1)}, f32[4,96,128]{2,1,0:T(8,128)S(1)}, u32[]{:S(2)}, u32[]{:S(2)}) collective-permute-start(f32[4,96,128]{2,1,0:T(8,128)S(1)} %pad_maximum_fusion.2), channel_id=1, source_target_pairs={{0,4},{4,0},{8,12},{12,8},{16,20},{20,16},{24,28},{28,24},{1,5},{5... | collective-permute-start | bytes 589832 | tf_op jit(solution)/shard_map/ppermute | solution.py:28
  40.0 11.7 %collective-permute-start.5 = (f32[160,256]{1,0:T(8,128)S(1)}, f32[160,256]{1,0:T(8,128)S(1)}, u32[]{:S(2)}, u32[]{:S(2)}) collective-permute-start(f32[160,256]{1,0:T(8,128)S(1)} %first_sums.1.refs_0_), channel_id=1, source_target_pairs={{0,1},{1,0},{2,3},{3,2},{4,5},{5,4},{6,7},{7,6},{8,9},{9,8},{10,11... | collective-permute-start | bytes 491528 | tf_op jit(solution)/shard_map/ppermute | solution.py:28
  51.7 18.8 %all-to-all-start.2 = ((f32[8,4,32,128]{3,2,1,0:T(8,128)}), f32[8,4,32,128]{3,2,1,0:T(8,128)S(1)}, u32[]{:S(2)}, u32[]{:S(2)}) async-start(f32[8,4,32,128]{3,2,1,0:T(8,128)} %bitcast.5), calls=%async_computation.2 | async-start | bytes 1048576 | tf_op jit(solution)/shard_map/all_to_all | solution.py:413
  55.3 15.2 %collective-permute-start.6 = (f32[1,4,8,128]{3,2,1,0:T(8,128)S(1)}, f32[1,4,8,128]{3,2,1,0:T(8,128)S(1)}, u32[]{:S(2)}, u32[]{:S(2)}) collective-permute-start(f32[1,4,8,128]{3,2,1,0:T(8,128)S(1)} %bitcast.27), channel_id=1, source_target_pairs={{0,16},{4,20},{8,24},{12,28},{16,0},{20,4},{24,8},{28,12},{1,17},{... | collective-permute-start | bytes 49160 | tf_op jit(solution)/shard_map/ppermute | solution.py:28
  70.5 6.4 %collective-permute-start.7 = (f32[2,4,8,128]{3,2,1,0:T(8,128)S(1)}, f32[2,4,8,128]{3,2,1,0:T(8,128)S(1)}, u32[]{:S(2)}, u32[]{:S(2)}) collective-permute-start(f32[2,4,8,128]{3,2,1,0:T(8,128)S(1)} %pad_maximum_fusion.6), channel_id=1, source_target_pairs={{0,8},{4,12},{8,0},{12,4},{16,24},{20,28},{24,16},{28,20},{1,9},{5... | collective-permute-start | bytes 98312 | tf_op jit(solution)/shard_map/ppermute | solution.py:28
  71.5 17.8 %all-to-all-start.3 = ((f32[16,4,8,128]{3,2,1,0:T(8,128)}), f32[16,4,8,128]{3,2,1,0:T(8,128)S(1)}, u32[]{:S(2)}, u32[]{:S(2)}) async-start(f32[16,4,8,128]{3,2,1,0:T(8,128)} %sketch.1), calls=%async_computation.3 | async-start | bytes 524288 | tf_op jit(solution)/shard_map/all_to_all | solution.py:432
  77.0 5.2 %collective-permute-start.8 = (f32[4,4,8,128]{3,2,1,0:T(8,128)S(1)}, f32[4,4,8,128]{3,2,1,0:T(8,128)S(1)}, u32[]{:S(2)}, u32[]{:S(2)}) collective-permute-start(f32[4,4,8,128]{3,2,1,0:T(8,128)S(1)} %pad_maximum_fusion.5), channel_id=1, source_target_pairs={{0,4},{4,0},{8,12},{12,8},{16,20},{20,16},{24,28},{28,24},{1,5},{5... | collective-permute-start | bytes 196616 | tf_op jit(solution)/shard_map/ppermute | solution.py:28
  82.2 1.4 %collective-permute-start.9 = (f32[1,8,4,8,128]{4,3,2,1,0:T(8,128)S(1)}, f32[1,8,4,8,128]{4,3,2,1,0:T(8,128)S(1)}, u32[]{:S(2)}, u32[]{:S(2)}) collective-permute-start(f32[1,8,4,8,128]{4,3,2,1,0:T(8,128)S(1)} %fusion.6), channel_id=1, source_target_pairs={{0,2},{2,0},{1,3},{3,1},{4,6},{6,4},{5,7},{7,5},{8,10},{10,8},{9,1... | collective-permute-start | bytes 393224 | tf_op jit(solution)/shard_map/ppermute | solution.py:28

commit v6 on v5

--- a/solution.py
+++ b/solution.py
@@ -48,13 +48,6 @@
 
 def swap_step(held, axis, bit):
     return jnp.concatenate([held, swap(held, axis, bit)], axis=0)
-
-
-def swap_gather(array, axis):
-    held = array[None]
-    for bit in axis_bits(axis):
-        held = swap_step(held, axis, bit)
-    return held
 
 
 def gather_rows(array, outer, inner):
@@ -219,8 +212,8 @@
     )(*inputs)
 
 
-def last_kernel(system_shares, *refs):
-    *terms, projected, flat = refs
+def last_kernel(y_own, system_shares, *refs):
+    extra, *terms, projected, flat = refs
     system = system_shares[:, 0]
     for k in range(1, system_shares.shape[1]):
         system = system + system_shares[:, k]
@@ -238,31 +231,39 @@
         precision=HIGHEST,
         preferred_element_type=jnp.float32,
     )
-    y_cells, x_cells, _ = projected.shape
-    for j in range(y_cells):
-        projected[j] = flat[pl.ds(j, x_cells, stride=y_cells), :]
-
-
-def solve_last(system_shares, terms):
+    x_cells, y_cells, _ = terms[0].shape
+    for b in range(projected.shape[0]):
+        for j in range(y_own):
+            projected[b, j * x_cells : (j + 1) * x_cells] = flat[
+                pl.ds(b * y_own + j, x_cells, stride=y_cells), :
+            ]
+        projected[b, y_own * x_cells :] = extra[...]
+
+
+def solve_last(blocks, system_shares, extra, terms):
     rank = system_shares.shape[0] * system_shares.shape[2]
     x_cells, y_cells, _ = terms[0].shape
-    return pl.pallas_call(
-        last_kernel,
-        out_shape=jax.ShapeDtypeStruct((y_cells, x_cells, rank), jnp.float32),
+    y_own = y_cells // blocks
+    rows = y_own * x_cells + extra.shape[0]
+    return pl.pallas_call(
+        functools.partial(last_kernel, y_own),
+        out_shape=jax.ShapeDtypeStruct((blocks, rows, rank), jnp.float32),
         scratch_shapes=[pltpu.VMEM((x_cells * y_cells, rank), jnp.float32)],
         compiler_params=pltpu.CompilerParams(vmem_limit_bytes=VMEM_BYTES),
         name="solve_last",
-    )(system_shares, *terms)
-
-
-def sketch_kernel(order, left_at, pieces, packed, out):
+    )(system_shares, extra, *terms)
+
+
+def sketch_kernel(order, left_at, y_own, pieces, packed, out, extra):
     me = lax.axis_index("gx")
-    blocks, y_own, x_cells, cols = pieces.shape
-    weights = jnp.concatenate(
-        [packed[k, left_at : left_at + x_cells] for k in range(blocks)], axis=0
-    ).astype(jnp.bfloat16)
+    blocks, _, cols = pieces.shape
+    x_cells = packed.shape[1] - left_at
+    weights = jnp.concatenate([packed[k, left_at:] for k in range(blocks)], axis=0)
+    weights = weights.astype(jnp.bfloat16)
     for j in range(y_own):
-        column = jnp.concatenate([pieces[me ^ o, j] for o in order], axis=0)
+        column = jnp.concatenate(
+            [pieces[me ^ o, j * x_cells : (j + 1) * x_cells] for o in order], axis=0
+        )
         high = column.astype(jnp.bfloat16)
         low = (column - high.astype(jnp.float32)).astype(jnp.bfloat16)
         both = lax.dot_general(
@@ -273,14 +274,19 @@
         )
         both = both[:, :cols] + both[:, cols:]
         out[:, j] = both.reshape(out.shape[0], out.shape[2], cols)
-
-
-def sketch(order, left_at, own, pieces, packed):
-    y_own, cols = pieces.shape[1], pieces.shape[3]
+    extra[...] = pieces[:, y_own * x_cells :]
+
+
+def sketch(order, left_at, y_own, own, pieces, packed):
+    blocks, rows, cols = pieces.shape
     rank = packed.shape[2]
-    return pl.pallas_call(
-        functools.partial(sketch_kernel, order, left_at),
-        out_shape=jax.ShapeDtypeStruct((rank // own, y_own, own, cols), jnp.float32),
+    extra = rows - y_own * (packed.shape[1] - left_at)
+    return pl.pallas_call(
+        functools.partial(sketch_kernel, order, left_at, y_own),
+        out_shape=(
+            jax.ShapeDtypeStruct((rank // own, y_own, own, cols), jnp.float32),
+            jax.ShapeDtypeStruct((blocks, extra, cols), jnp.float32),
+        ),
         compiler_params=pltpu.CompilerParams(vmem_limit_bytes=VMEM_BYTES),
         name="sketch",
     )(pieces, packed)
@@ -338,26 +344,28 @@
     )(*sums)
 
 
-def place_kernel(outer_order, inner_order, packed, core_last):
-    own = packed.shape[3]
-    outer, inner = lax.axis_index("gx"), lax.axis_index("gy")
-    for n, i in enumerate(inner_order):
-        for k, o in enumerate(outer_order):
-            at = ((outer ^ o) * len(inner_order) + (inner ^ i)) * own
-            for c in range(packed.shape[2]):
-                core_last[pl.ds(pl.multiple_of(at, own), own), c * LANES : (c + 1) * LANES] = (
-                    packed[n, k, c]
-                )
-
-
-def place(outer_order, inner_order, packed):
-    inner, outer, count, own, lanes = packed.shape
-    return pl.pallas_call(
-        functools.partial(place_kernel, outer_order, inner_order),
-        out_shape=jax.ShapeDtypeStruct((inner * outer * own, count * lanes), jnp.float32),
+def place_kernel(own, inner_order, *refs):
+    *parts, core_last = refs
+    inner = lax.axis_index("gy")
+    for part, i in zip(parts, inner_order):
+        for o in range(part.shape[0]):
+            at = pl.multiple_of((o * len(parts) + (inner ^ i)) * own, own)
+            for c in range(part.shape[1] // own):
+                core_last[pl.ds(at, own), c * LANES : (c + 1) * LANES] = part[
+                    o, c * own : (c + 1) * own
+                ]
+
+
+def place(own, inner_order, parts):
+    outer, rows, lanes = parts[0].shape
+    return pl.pallas_call(
+        functools.partial(place_kernel, own, inner_order),
+        out_shape=jax.ShapeDtypeStruct(
+            (len(parts) * outer * own, rows // own * lanes), jnp.float32
+        ),
         compiler_params=pltpu.CompilerParams(vmem_limit_bytes=VMEM_BYTES),
         name="place",
-    )(packed)
+    )(*parts)
 
 
 def per_device(flow_field, left_x, last_x, last_y, right_y, right_m, last_m):
@@ -403,36 +411,38 @@
         system = jnp.sum(system, axis=1).reshape(-1, 1, ROWS, cols)
 
     for bit in bits:
+        if bit == bits[-1]:
+            packed = after(packed, *terms[1:])
         packed = swap_step(packed, "gx", bit)
     sums = first_sums(left_at, first_rows, packed)
-    projected = solve_last(after(system, sums), terms)
+    if own % ROWS:
+        extra = jnp.zeros((ROWS, LANES), jnp.float32)
+    else:
+        extra = last_rows.reshape(own, -1, LANES).transpose(1, 0, 2).reshape(-1, LANES)
+    projected = solve_last(blocks, after(system, sums), extra, terms)
     sums = [swap(sums, "gz", z) if z else sums for z in range(shares)]
     projected = after(projected, *sums)
 
-    pieces = projected.reshape(blocks, y_own, x_cells, rank)
-    pieces = lax.all_to_all(pieces, "gx", 0, 0, tiled=True)
+    pieces = lax.all_to_all(projected, "gx", 0, 0, tiled=True)
+    core_first = solve_first(x_cells, after(sums[0], projected), *sums[1:])
     group = ("gx", "gz")
     devices = lax.axis_size(group)
     rank_own = rank // devices
     if rank_own % ROWS:
-        middle = sketch(order, left_at, rank, pieces, packed)
+        middle, extra = sketch(order, left_at, y_own, rank, pieces, packed)
         middle = middle.reshape(y_own, devices, rank_own, rank).transpose(1, 0, 2, 3)
     else:
-        middle = sketch(order, left_at, rank_own, pieces, packed)
+        middle, extra = sketch(order, left_at, y_own, rank_own, pieces, packed)
+    middle, core_first = lax.optimization_barrier((middle, core_first))
+    received = lax.all_to_all(middle, group, 0, 0, tiled=True)
+    received = received.reshape(blocks, shares, y_own, rank_own, rank)
+    core_middle = received.transpose(3, 1, 0, 2, 4).reshape(rank_own, y_cells, rank)
 
     if own % ROWS:
         core_last = gather_rows(last_rows, "gx", "gy")
     else:
-        core_last = last_rows.reshape(own, -1, LANES).transpose(1, 0, 2)
-        core_last = swap_gather(core_last, "gx")
-        middle = after(middle, core_last)
-        core_last = swap_gather(core_last, "gy")
-        core_last = place(order, swap_order("gy"), core_last)
-
-    received = lax.all_to_all(middle, group, 0, 0, tiled=True)
-    received = received.reshape(blocks, shares, y_own, rank_own, rank)
-    core_middle = received.transpose(3, 1, 0, 2, 4).reshape(rank_own, y_cells, rank)
-    core_first = solve_first(x_cells, after(sums[0], middle), *sums[1:])
+        inner = range(lax.axis_size("gy"))
+        core_last = place(own, inner, [swap(extra, "gy", i) if i else extra for i in inner])
     return (core_first, core_middle, core_last)
 
 

time: 90.6 us -> 91.3 us (level)
  waiting for transfers between devices: 35.3 us -> 40.8 us
  starting transfers between devices: 33.8 us -> 29.1 us
    all_to_all x1, waiting for transfers between devices: 0.01 us -> 10.5 us  [per_device(): pieces = lax.all_to_all(projected, 'gx', 0, 0, tiled=True)]
    ppermute x10 -> x7, waiting for transfers between devices: 31.3 us -> 23.5 us  [swap(): lax.ppermute(array, axis, [(s, s ^ bits) for s in range(lax.axis_size(axi...]
    all_to_all x1, waiting for transfers between devices: 0.01 us -> 6.8 us  [per_device(): received = lax.all_to_all(middle, group, 0, 0, tiled=True)]
    ppermute x10 -> x7, starting transfers between devices: 13.3 us -> 8.51 us  [swap(): lax.ppermute(array, axis, [(s, s ^ bits) for s in range(lax.axis_size(axi...]
    all_to_all x1, waiting for transfers between devices: 4 us -> 0.01 us  [per_device(): lax.all_to_all(copies, ALL, 0, 0, tiled=True).reshape(-1, shares, own, cols)]
    all_to_all x1, starting transfers between devices: 3.65 us -> 5.42 us  [per_device(): pieces = lax.all_to_all(projected, 'gx', 0, 0, tiled=True)]
    all_to_all x1, starting transfers between devices: 5.44 us -> 3.79 us  [per_device(): received = lax.all_to_all(middle, group, 0, 0, tiled=True)]
  transfers between devices with their start and end apart: 14 -> 11, of which waited for: 6 -> 6; matrix products, arithmetic and copies ran while one was open for 2% -> 2% of each run, Pallas kernels for 15% -> 14%
where the time goes in v6:
time: 91.3 us; the launch traced here: 90.8 us
  waiting for transfers between devices  40.8 us (45%)
  starting transfers between devices  29.1 us (32%)
  Pallas kernels  17.6 us (19%)
  local copies, waits for them, and re-layouts  1.54 us (2%)
    ppermute x7, waiting for transfers between devices, swap(): lax.ppermute(array, axis, [(s, s ^ bits) for s in range(lax.axis_size(axi...  23.5 us
    all_to_all x1, waiting for transfers between devices, per_device(): pieces = lax.all_to_all(projected, 'gx', 0, 0, tiled=True)  10.5 us
    ppermute x7, starting transfers between devices, swap(): lax.ppermute(array, axis, [(s, s ^ bits) for s in range(lax.axis_size(axi...  8.51 us
    all_to_all x1, starting transfers between devices, per_device(): lax.all_to_all(last_part.reshape(-1, own, m_cells), group, 0, 0, tiled=True)  7.15 us
    all_to_all x1, waiting for transfers between devices, per_device(): received = lax.all_to_all(middle, group, 0, 0, tiled=True)  6.8 us
    pallas_call x1, Pallas kernels, solve_last(): pl.pallas_call(functools.partial(last_kernel, y_own), out_shape=jax.Shape...  6.29 us
    all_to_all x1, starting transfers between devices, per_device(): pieces = lax.all_to_all(projected, 'gx', 0, 0, tiled=True)  5.42 us
    pallas_call x1, Pallas kernels, solve_first(): pl.pallas_call(first_kernel, out_shape=jax.ShapeDtypeStruct((x_cells, sum...  4.89 us
  transfers between devices with their start and end apart: 11, of which 6 were waited for; matrix products, arithmetic and copies ran while one was open for 2% of the time, Pallas kernels for 14%

profile of v6, /device:TPU:0, one launch (start us, length us, event | category | flops | bytes accessed | tf_op | source)
XLA Modules:
  0.0 90.8 jit_solution(16518192132031036897)
XLA Ops:
  0.6 0.0 copy-start.1
  0.6 0.0 copy-start.2
  0.7 4.4 %local_products.1 = (f32[128,512]{1,0:T(8,128)}, f32[32,256]{1,0:T(8,128)}, f32[32,32,256]{2,1,0:T(8,128)}, f32[32,32,256]{2,1,0:T(8,128)}) custom-call(bf16[32,64,512]{2,1,0:T(8,128)(2,1)} %field_hbm.1, bf16[32,128]{1,0:T(8,128)(2,1)} %last_x_hbm.1, bf16[64,128]{1,0:T(8,128)(2,1)} %last_y_hbm.1, bf16[64,256]{1,0:T(8,128)(2,1)} %right_y_hbm.1, ...), custom_call_target="tpu_custom_call" | custom-call | tf_op jit(solution)/shard_map/local_products/pallas_call | solution.py:195
  5.0 0.5 collective-permute-start
  5.5 0.0 copy-start
  5.5 7.1 %all-to-all-start = ((f32[16,8,512]{2,1,0:T(8,128)}), f32[16,8,512]{2,1,0:T(8,128)S(1)}, u32[]{:S(2)}, u32[]{:S(2)}) async-start(f32[16,8,512]{2,1,0:T(8,128)} %bitcast.25), calls=%async_computation | async-start | bytes 524288 | tf_op jit(solution)/shard_map/all_to_all | solution.py:401
  12.7 1.6 %collective-permute-start.3 = (f32[32,32,256]{2,1,0:T(8,128)}, f32[32,32,256]{2,1,0:T(8,128)S(1)}, u32[]{:S(2)}, u32[]{:S(2)}) collective-permute-start(f32[32,32,256]{2,1,0:T(8,128)} %get-tuple-element.19), channel_id=1, source_target_pairs={{0,1},{1,0},{2,3},{3,2},{4,5},{5,4},{6,7},{7,6},{8,9},{9,8},{10,11... | collective-permute-start | bytes 3145736 | tf_op jit(solution)/shard_map/ppermute | solution.py:28
  14.3 0.0 copy-done.2
  14.3 0.0 collective-permute-done
  14.3 0.8 add.7.rows
  15.1 2.8 %collective-permute-start.1 = (f32[1,96,128]{2,1,0:T(8,128)S(1)}, f32[1,96,128]{2,1,0:T(8,128)S(1)}, u32[]{:S(2)}, u32[]{:S(2)}) collective-permute-start(f32[1,96,128]{2,1,0:T(8,128)S(1)} %maximum_bitcast_fusion), channel_id=1, source_target_pairs={{0,16},{4,20},{8,24},{12,28},{16,0},{20,4},{24,8},{28,12},{1,17},{... | collective-permute-start | bytes 147464 | tf_op jit(solution)/shard_map/ppermute | solution.py:28
  17.9 6.5 %collective-permute-done.1 = f32[1,96,128]{2,1,0:T(8,128)S(1)} collective-permute-done((f32[1,96,128]{2,1,0:T(8,128)S(1)}, f32[1,96,128]{2,1,0:T(8,128)S(1)}, u32[]{:S(2)}, u32[]{:S(2)}) %collective-permute-start.1) | collective-permute-done | bytes 49184 | tf_op jit(solution)/shard_map/ppermute | solution.py:28
  24.5 0.1 collective-permute-start.2
  24.5 0.0 all-to-all-done
  24.6 0.0 copy-done.1
  24.6 0.1 fusion.1
  24.8 0.7 broadcast_in_dim.10
  25.5 4.2 %all-to-all-start.1 = ((f32[32,8,256]{2,1,0:T(8,128)}), f32[32,8,256]{2,1,0:T(8,128)S(1)}, u32[]{:S(2)}, u32[]{:S(2)}) async-start(f32[32,8,256]{2,1,0:T(8,128)} %broadcast_in_dim.10), calls=%async_computation.1 | async-start | bytes 524288 | tf_op jit(solution)/shard_map/all_to_all | solution.py:409
  29.7 0.0 collective-permute-done.2
  29.7 11.3 %collective-permute-done.3.refs_2_ = f32[32,32,256]{2,1,0:T(8,128)S(1)} collective-permute-done((f32[32,32,256]{2,1,0:T(8,128)}, f32[32,32,256]{2,1,0:T(8,128)S(1)}, u32[]{:S(2)}, u32[]{:S(2)}) %collective-permute-start.3) | collective-permute-done | bytes 1048608 | tf_op jit(solution)/shard_map/ppermute | solution.py:28
  41.0 1.7 %collective-permute-start.4 = (f32[4,96,128]{2,1,0:T(8,128)S(1)}, f32[4,96,128]{2,1,0:T(8,128)S(1)}, u32[]{:S(2)}, u32[]{:S(2)}) collective-permute-start(f32[4,96,128]{2,1,0:T(8,128)S(1)} %pad_maximum_fusion), channel_id=1, source_target_pairs={{0,4},{4,0},{8,12},{12,8},{16,20},{20,16},{24,28},{28,24},{1,5},{5... | collective-permute-start | bytes 589832 | tf_op jit(solution)/shard_map/ppermute | solution.py:28
  42.7 4.3 %collective-permute-done.4 = f32[4,96,128]{2,1,0:T(8,128)S(1)} collective-permute-done((f32[4,96,128]{2,1,0:T(8,128)S(1)}, f32[4,96,128]{2,1,0:T(8,128)S(1)}, u32[]{:S(2)}, u32[]{:S(2)}) %collective-permute-start.4) | collective-permute-done | bytes 196640 | tf_op jit(solution)/shard_map/ppermute | solution.py:28
  47.0 0.4 first_sums.1.refs_0_
  47.4 1.8 %collective-permute-start.5 = (f32[160,256]{1,0:T(8,128)S(1)}, f32[160,256]{1,0:T(8,128)S(1)}, u32[]{:S(2)}, u32[]{:S(2)}) collective-permute-start(f32[160,256]{1,0:T(8,128)S(1)} %first_sums.1.refs_0_), channel_id=1, source_target_pairs={{0,1},{1,0},{2,3},{3,2},{4,5},{5,4},{6,7},{7,6},{8,9},{9,8},{10,11... | collective-permute-start | bytes 491528 | tf_op jit(solution)/shard_map/ppermute | solution.py:28
  49.2 0.0 all-to-all-done.1
  49.2 0.0 copy-done
  49.2 6.3 %solve_last.1 = f32[8,160,128]{2,1,0:T(8,128)} custom-call(f32[16,2,8,256]{3,2,1,0:T(8,128)S(1)} %bitcast.22, f32[32,128]{1,0:T(8,128)S(1)} %bitcast.23, f32[32,32,256]{2,1,0:T(8,128)S(1)} %copy-done, f32[32,32,256]{2,1,0:T(8,128)S(1)} %collective-permute-done.3.refs_2_), custom_call_target="tpu_custom_call" | custom-call | tf_op jit(solution)/shard_map/solve_last/pallas_call | solution.py:248
  55.5 0.0 collective-permute-done.5.refs_1_
  55.5 5.4 %all-to-all-start.2 = ((f32[8,160,128]{2,1,0:T(8,128)}), f32[8,160,128]{2,1,0:T(8,128)S(1)}, u32[]{:S(2)}, u32[]{:S(2)}) async-start(f32[8,160,128]{2,1,0:T(8,128)} %solve_last.1), calls=%async_computation.2 | async-start | bytes 1310720 | tf_op jit(solution)/shard_map/all_to_all | solution.py:426
  60.9 4.9 %solve_first.1 = f32[32,128]{1,0:T(8,128)} custom-call(f32[160,256]{1,0:T(8,128)S(1)} %first_sums.1.refs_0_, f32[160,256]{1,0:T(8,128)S(1)} %collective-permute-done.5.refs_1_), custom_call_target="tpu_custom_call" | custom-call | tf_op jit(solution)/shard_map/solve_first/pallas_call | solution.py:339
  65.8 10.5 %all-to-all-done.2.pieces = f32[8,160,128]{2,1,0:T(8,128)S(1)} async-done(((f32[8,160,128]{2,1,0:T(8,128)}), f32[8,160,128]{2,1,0:T(8,128)S(1)}, u32[]{:S(2)}, u32[]{:S(2)}) %all-to-all-start.2) | async-done | bytes 655392 | tf_op jit(solution)/shard_map/all_to_all | solution.py:426
  76.3 1.0 %sketch.1 = (f32[16,4,8,128]{3,2,1,0:T(8,128)}, f32[8,32,128]{2,1,0:T(8,128)S(1)}) custom-call(f32[8,160,128]{2,1,0:T(8,128)S(1)} %all-to-all-done.2.pieces, f32[8,96,128]{2,1,0:T(8,128)S(1)} %constant_dynamic-update-slice_fusion.packed), custom_call_target="tpu_custom_call" | custom-call | tf_op jit(solution)/shard_map/sketch/pallas_call | solution.py:284
  77.3 3.8 %all-to-all-start.3 = ((f32[16,4,8,128]{3,2,1,0:T(8,128)}), f32[16,4,8,128]{3,2,1,0:T(8,128)S(1)}, u32[]{:S(2)}, u32[]{:S(2)}) async-start(f32[16,4,8,128]{3,2,1,0:T(8,128)} %get-tuple-element.27), calls=%async_computation.3 | async-start | bytes 524288 | tf_op jit(solution)/shard_map/all_to_all | solution.py:437
  81.1 0.1 collective-permute-start.6
  81.2 1.3 %collective-permute-done.6.refs_1_ = f32[8,32,128]{2,1,0:T(8,128)S(1)} collective-permute-done((f32[8,32,128]{2,1,0:T(8,128)S(1)}, f32[8,32,128]{2,1,0:T(8,128)S(1)}, u32[]{:S(2)}, u32[]{:S(2)}) %collective-permute-start.6) | collective-permute-done | bytes 131104 | tf_op jit(solution)/shard_map/ppermute | solution.py:28
  82.5 0.7 place.1
  83.2 6.8 %all-to-all-done.3 = f32[16,4,8,128]{3,2,1,0:T(8,128)S(1)} async-done(((f32[16,4,8,128]{3,2,1,0:T(8,128)}), f32[16,4,8,128]{3,2,1,0:T(8,128)S(1)}, u32[]{:S(2)}, u32[]{:S(2)}) %all-to-all-start.3) | async-done | bytes 262176 | tf_op jit(solution)/shard_map/all_to_all | solution.py:437
  90.0 0.8 copy.11
  (10 shorter events, 0.1 us)
Async XLA Ops:
  0.6 24.0 %copy-start.1 = (bf16[512,256]{1,0:T(8,128)(2,1)S(1)}, bf16[512,256]{1,0:T(8,128)(2,1)}, u32[]{:S(2)}) copy-start(bf16[512,256]{1,0:T(8,128)(2,1)} %last_m_hbm.1) | copy-start | bytes 786436
  0.6 13.6 %copy-start.2 = (bf16[32,128]{1,0:T(8,128)(2,1)S(1)}, bf16[32,128]{1,0:T(8,128)(2,1)}, u32[]{:S(2)}) copy-start(bf16[32,128]{1,0:T(8,128)(2,1)} %param.8) | copy-start | bytes 24580
  5.0 9.3 %collective-permute-start = (f32[32,256]{1,0:T(8,128)}, f32[32,256]{1,0:T(8,128)S(1)}, u32[]{:S(2)}, u32[]{:S(2)}) collective-permute-start(f32[32,256]{1,0:T(8,128)} %get-tuple-element.17), channel_id=1, source_target_pairs={{0,2},{2,0},{1,3},{3,1},{4,6},{6,4},{5,7},{7,5},{8,10},{10,8},{9,1... | collective-permute-start | bytes 98312 | tf_op jit(solution)/shard_map/ppermute | solution.py:28
  5.5 43.7 %copy-start = (f32[32,32,256]{2,1,0:T(8,128)S(1)}, f32[32,32,256]{2,1,0:T(8,128)}, u32[]{:S(2)}) copy-start(f32[32,32,256]{2,1,0:T(8,128)} %get-tuple-element.22.refs_1_) | copy-start | bytes 3145732
  5.5 19.0 %all-to-all-start = ((f32[16,8,512]{2,1,0:T(8,128)}), f32[16,8,512]{2,1,0:T(8,128)S(1)}, u32[]{:S(2)}, u32[]{:S(2)}) async-start(f32[16,8,512]{2,1,0:T(8,128)} %bitcast.25), calls=%async_computation | async-start | bytes 524288 | tf_op jit(solution)/shard_map/all_to_all | solution.py:401
  12.7 28.3 %collective-permute-start.3 = (f32[32,32,256]{2,1,0:T(8,128)}, f32[32,32,256]{2,1,0:T(8,128)S(1)}, u32[]{:S(2)}, u32[]{:S(2)}) collective-permute-start(f32[32,32,256]{2,1,0:T(8,128)} %get-tuple-element.19), channel_id=1, source_target_pairs={{0,1},{1,0},{2,3},{3,2},{4,5},{5,4},{6,7},{7,6},{8,9},{9,8},{10,11... | collective-permute-start | bytes 3145736 | tf_op jit(solution)/shard_map/ppermute | solution.py:28
  15.1 9.4 %collective-permute-start.1 = (f32[1,96,128]{2,1,0:T(8,128)S(1)}, f32[1,96,128]{2,1,0:T(8,128)S(1)}, u32[]{:S(2)}, u32[]{:S(2)}) collective-permute-start(f32[1,96,128]{2,1,0:T(8,128)S(1)} %maximum_bitcast_fusion), channel_id=1, source_target_pairs={{0,16},{4,20},{8,24},{12,28},{16,0},{20,4},{24,8},{28,12},{1,17},{... | collective-permute-start | bytes 147464 | tf_op jit(solution)/shard_map/ppermute | solution.py:28
  24.5 5.3 %collective-permute-start.2 = (f32[2,96,128]{2,1,0:T(8,128)S(1)}, f32[2,96,128]{2,1,0:T(8,128)S(1)}, u32[]{:S(2)}, u32[]{:S(2)}) collective-permute-start(f32[2,96,128]{2,1,0:T(8,128)S(1)} %pad_maximum_fusion.1), channel_id=1, source_target_pairs={{0,8},{4,12},{8,0},{12,4},{16,24},{20,28},{24,16},{28,20},{1,9},{5... | collective-permute-start | bytes 294920 | tf_op jit(solution)/shard_map/ppermute | solution.py:28
  25.5 23.7 %all-to-all-start.1 = ((f32[32,8,256]{2,1,0:T(8,128)}), f32[32,8,256]{2,1,0:T(8,128)S(1)}, u32[]{:S(2)}, u32[]{:S(2)}) async-start(f32[32,8,256]{2,1,0:T(8,128)} %broadcast_in_dim.10), calls=%async_computation.1 | async-start | bytes 524288 | tf_op jit(solution)/shard_map/all_to_all | solution.py:409
  41.0 6.0 %collective-permute-start.4 = (f32[4,96,128]{2,1,0:T(8,128)S(1)}, f32[4,96,128]{2,1,0:T(8,128)S(1)}, u32[]{:S(2)}, u32[]{:S(2)}) collective-permute-start(f32[4,96,128]{2,1,0:T(8,128)S(1)} %pad_maximum_fusion), channel_id=1, source_target_pairs={{0,4},{4,0},{8,12},{12,8},{16,20},{20,16},{24,28},{28,24},{1,5},{5... | collective-permute-start | bytes 589832 | tf_op jit(solution)/shard_map/ppermute | solution.py:28
  47.4 8.1 %collective-permute-start.5 = (f32[160,256]{1,0:T(8,128)S(1)}, f32[160,256]{1,0:T(8,128)S(1)}, u32[]{:S(2)}, u32[]{:S(2)}) collective-permute-start(f32[160,256]{1,0:T(8,128)S(1)} %first_sums.1.refs_0_), channel_id=1, source_target_pairs={{0,1},{1,0},{2,3},{3,2},{4,5},{5,4},{6,7},{7,6},{8,9},{9,8},{10,11... | collective-permute-start | bytes 491528 | tf_op jit(solution)/shard_map/ppermute | solution.py:28
  55.5 20.8 %all-to-all-start.2 = ((f32[8,160,128]{2,1,0:T(8,128)}), f32[8,160,128]{2,1,0:T(8,128)S(1)}, u32[]{:S(2)}, u32[]{:S(2)}) async-start(f32[8,160,128]{2,1,0:T(8,128)} %solve_last.1), calls=%async_computation.2 | async-start | bytes 1310720 | tf_op jit(solution)/shard_map/all_to_all | solution.py:426
  77.3 12.7 %all-to-all-start.3 = ((f32[16,4,8,128]{3,2,1,0:T(8,128)}), f32[16,4,8,128]{3,2,1,0:T(8,128)S(1)}, u32[]{:S(2)}, u32[]{:S(2)}) async-start(f32[16,4,8,128]{3,2,1,0:T(8,128)} %get-tuple-element.27), calls=%async_computation.3 | async-start | bytes 524288 | tf_op jit(solution)/shard_map/all_to_all | solution.py:437
  81.1 1.4 %collective-permute-start.6 = (f32[8,32,128]{2,1,0:T(8,128)S(1)}, f32[8,32,128]{2,1,0:T(8,128)S(1)}, u32[]{:S(2)}, u32[]{:S(2)}) collective-permute-start(f32[8,32,128]{2,1,0:T(8,128)S(1)} %get-tuple-element.28.refs_0_), channel_id=1, source_target_pairs={{0,2},{2,0},{1,3},{3,1},{4,6},{6,4},{5,7},{7,5},{8,10},{10,8},{9,1... | collective-permute-start | bytes 393224 | tf_op jit(solution)/shard_map/ppermute | solution.py:28

commit v7 on v6

--- a/solution.py
+++ b/solution.py
@@ -13,6 +13,7 @@
 LOCAL_VMEM_BYTES = 63 * 1024 * 1024
 ROWS = 8
 LANES = 128
+PARTS = 2
 ROW_ROW = (((1,), (1,)), ((), ()))
 COL_COL = (((0,), (0,)), ((), ()))
 
@@ -128,8 +129,8 @@
     first_part,
     *refs,
 ):
-    terms_hbm = refs[:shares]
-    field, last_x, last_y, right_y, right_m, last_m, terms, sems, out_sems = refs[shares:]
+    terms_hbm = refs[: shares * PARTS]
+    field, last_x, last_y, right_y, right_m, last_m, terms, sems, out_sems = refs[shares * PARTS :]
     x_cells, y_cells, m_cells = field.shape
     step = x_cells // chunks
     y_share = y_cells // shares
@@ -158,9 +159,12 @@
             rows = field[parts[n], pl.ds(start, y_share), :].reshape(step * y_share, m_cells)
             term = jnp.dot(rows, last_m[...], preferred_element_type=jnp.float32)
             terms[s, parts[n]] = term.reshape(step, y_share, -1)
+            part, at = divmod(n * step, x_cells // PARTS)
             leaving.append(
                 pltpu.make_async_copy(
-                    terms.at[s, parts[n]], terms_hbm[s].at[parts[n]], out_sems.at[s, n]
+                    terms.at[s, parts[n]],
+                    terms_hbm[s * PARTS + part].at[pl.ds(at, step)],
+                    out_sems.at[s, n],
                 )
             )
             leaving[-1].start()
@@ -190,16 +194,17 @@
     chunks = max(x_cells // 8, 1)
     inputs = (field, last_x, last_y, right_y, right_m, last_m)
     dims = (x_cells, y_cells // shares, cols)
+    part_dims = (x_cells // PARTS, *dims[1:])
     hbm = pl.BlockSpec(memory_space=pltpu.HBM)
     vmem = pl.BlockSpec(memory_space=pltpu.VMEM)
     return pl.pallas_call(
         functools.partial(local_kernel, chunks, shares),
         in_specs=[hbm] * len(inputs),
-        out_specs=[vmem, vmem, *([hbm] * shares)],
+        out_specs=[vmem, vmem, *([hbm] * (shares * PARTS))],
         out_shape=[
             jax.ShapeDtypeStruct((rank, m_cells), jnp.float32),
             jax.ShapeDtypeStruct((x_cells, cols), jnp.float32),
-            *([jax.ShapeDtypeStruct(dims, jnp.float32)] * shares),
+            *([jax.ShapeDtypeStruct(part_dims, jnp.float32)] * (shares * PARTS)),
         ],
         scratch_shapes=[
             *(pltpu.VMEM(x.shape, x.dtype) for x in inputs),
@@ -212,26 +217,47 @@
     )(*inputs)
 
 
-def last_kernel(y_own, system_shares, *refs):
-    extra, *terms, projected, flat = refs
+def inverse_kernel(system_shares, pinv):
     system = system_shares[:, 0]
     for k in range(1, system_shares.shape[1]):
         system = system + system_shares[:, k]
     system = system.reshape(-1, system.shape[-1])
-    pinv = jnp.dot(
+    pinv[...] = jnp.dot(
         spd_inverse(system), system, precision=HIGHEST, preferred_element_type=jnp.float32
     )
-    total = terms[0][...]
-    for term in terms[1:]:
-        total = total + term[...]
-    flat[...] = lax.dot_general(
-        total.reshape(-1, total.shape[-1]),
-        pinv,
-        ROW_ROW,
-        precision=HIGHEST,
-        preferred_element_type=jnp.float32,
-    )
+
+
+def pseudo_inverse(system_shares):
+    rank = system_shares.shape[0] * system_shares.shape[2]
+    return pl.pallas_call(
+        inverse_kernel,
+        out_shape=jax.ShapeDtypeStruct((rank, system_shares.shape[3]), jnp.float32),
+        compiler_params=pltpu.CompilerParams(vmem_limit_bytes=VMEM_BYTES),
+        name="pseudo_inverse",
+    )(system_shares)
+
+
+def two_terms(array):
+    high = array.astype(jnp.bfloat16)
+    return high, (array - high.astype(jnp.float32)).astype(jnp.bfloat16)
+
+
+def project_kernel(y_own, pinv, extra, *refs):
+    *terms, projected, flat = refs
+    rank = pinv.shape[0]
+    pinv_high, pinv_low = two_terms(pinv[...])
+    pinv_both = jnp.concatenate([pinv_high, pinv_low], axis=0)
+    rows = flat.shape[0] // PARTS
+    for part in range(PARTS):
+        total = terms[part][...]
+        for term in terms[part + PARTS :: PARTS]:
+            total = total + term[...]
+        high, low = two_terms(total.reshape(rows, -1))
+        both = lax.dot_general(high, pinv_both, ROW_ROW, preferred_element_type=jnp.float32)
+        rest = lax.dot_general(low, pinv_high, ROW_ROW, preferred_element_type=jnp.float32)
+        flat[part * rows : (part + 1) * rows] = both[:, :rank] + (both[:, rank:] + rest)
     x_cells, y_cells, _ = terms[0].shape
+    x_cells *= PARTS
     for b in range(projected.shape[0]):
         for j in range(y_own):
             projected[b, j * x_cells : (j + 1) * x_cells] = flat[
@@ -240,18 +266,19 @@
         projected[b, y_own * x_cells :] = extra[...]
 
 
-def solve_last(blocks, system_shares, extra, terms):
-    rank = system_shares.shape[0] * system_shares.shape[2]
+def project(blocks, pinv, extra, terms):
+    rank = pinv.shape[0]
     x_cells, y_cells, _ = terms[0].shape
+    x_cells *= PARTS
     y_own = y_cells // blocks
     rows = y_own * x_cells + extra.shape[0]
     return pl.pallas_call(
-        functools.partial(last_kernel, y_own),
+        functools.partial(project_kernel, y_own),
         out_shape=jax.ShapeDtypeStruct((blocks, rows, rank), jnp.float32),
         scratch_shapes=[pltpu.VMEM((x_cells * y_cells, rank), jnp.float32)],
         compiler_params=pltpu.CompilerParams(vmem_limit_bytes=VMEM_BYTES),
-        name="solve_last",
-    )(system_shares, extra, *terms)
+        name="project",
+    )(pinv, extra, *terms)
 
 
 def sketch_kernel(order, left_at, y_own, pieces, packed, out, extra):
@@ -381,7 +408,7 @@
     )
 
     for s in range(1, shares):
-        terms[s] = swap(terms[s], "gz", s)
+        terms[s * PARTS] = swap(terms[s * PARTS], "gz", s)
 
     order = swap_order("gx")
     first_rows = swap_sum(first_part, "gy")
@@ -406,22 +433,24 @@
     both = after(both[:own] + both[own:], packed)
     count = lax.axis_size(ALL)
     copies = jnp.broadcast_to(both[None], (count, own, cols))
+    for s in range(1, shares):
+        for part in range(1, PARTS):
+            at = s * PARTS + part
+            terms[at] = swap(after(terms[at], copies), "gz", s)
     system = lax.all_to_all(copies, ALL, 0, 0, tiled=True).reshape(-1, shares, own, cols)
     if own % ROWS:
         system = jnp.sum(system, axis=1).reshape(-1, 1, ROWS, cols)
 
     for bit in bits:
-        if bit == bits[-1]:
-            packed = after(packed, *terms[1:])
         packed = swap_step(packed, "gx", bit)
     sums = first_sums(left_at, first_rows, packed)
     if own % ROWS:
         extra = jnp.zeros((ROWS, LANES), jnp.float32)
     else:
         extra = last_rows.reshape(own, -1, LANES).transpose(1, 0, 2).reshape(-1, LANES)
-    projected = solve_last(blocks, after(system, sums), extra, terms)
+    pinv = pseudo_inverse(after(system, packed))
+    projected = project(blocks, pinv, extra, terms)
     sums = [swap(sums, "gz", z) if z else sums for z in range(shares)]
-    projected = after(projected, *sums)
 
     pieces = lax.all_to_all(projected, "gx", 0, 0, tiled=True)
     core_first = solve_first(x_cells, after(sums[0], projected), *sums[1:])

time: 91.3 us -> 88.5 us (0.969)
  waiting for transfers between devices: 40.8 us -> 38.7 us
    all_to_all x1, waiting for transfers between devices: 10.5 us -> 6.18 us  [per_device(): pieces = lax.all_to_all(projected, 'gx', 0, 0, tiled=True)]
    all_to_all x1, waiting for transfers between devices: 0.01 us -> 4.25 us  [per_device(): lax.all_to_all(copies, ALL, 0, 0, tiled=True).reshape(-1, shares, own, cols)]
    ppermute x7 -> x8, waiting for transfers between devices: 23.5 us -> 20.3 us  [swap(): lax.ppermute(array, axis, [(s, s ^ bits) for s in range(lax.axis_size(axi...]
    all_to_all x1, starting transfers between devices: 5.42 us -> 3.63 us  [per_device(): pieces = lax.all_to_all(projected, 'gx', 0, 0, tiled=True)]
    ppermute x7 -> x8, starting transfers between devices: 8.51 us -> 9.95 us  [swap(): lax.ppermute(array, axis, [(s, s ^ bits) for s in range(lax.axis_size(axi...]
    all_to_all x1, waiting for transfers between devices: 6.8 us -> 7.91 us  [per_device(): received = lax.all_to_all(middle, group, 0, 0, tiled=True)]
    all_to_all x1, starting transfers between devices: 4.22 us -> 3.26 us  [per_device(): lax.all_to_all(copies, ALL, 0, 0, tiled=True).reshape(-1, shares, own, cols)]
    all_to_all x1, starting transfers between devices: 3.79 us -> 4.73 us  [per_device(): received = lax.all_to_all(middle, group, 0, 0, tiled=True)]
  transfers between devices with their start and end apart: 11 -> 12, of which waited for: 6 -> 7; matrix products, arithmetic and copies ran while one was open for 2% -> 2% of each run, Pallas kernels for 14% -> 12%
where the time goes in v7:
time: 88.5 us; the launch traced here: 87.9 us
  waiting for transfers between devices  38.7 us (44%)
  starting transfers between devices  28.6 us (32%)
  Pallas kernels  17.3 us (20%)
  local copies, waits for them, and re-layouts  1.52 us (2%)
    ppermute x8, waiting for transfers between devices, swap(): lax.ppermute(array, axis, [(s, s ^ bits) for s in range(lax.axis_size(axi...  20.3 us
    ppermute x8, starting transfers between devices, swap(): lax.ppermute(array, axis, [(s, s ^ bits) for s in range(lax.axis_size(axi...  9.95 us
    all_to_all x1, waiting for transfers between devices, per_device(): received = lax.all_to_all(middle, group, 0, 0, tiled=True)  7.91 us
    all_to_all x1, starting transfers between devices, per_device(): lax.all_to_all(last_part.reshape(-1, own, m_cells), group, 0, 0, tiled=True)  7.06 us
    all_to_all x1, waiting for transfers between devices, per_device(): pieces = lax.all_to_all(projected, 'gx', 0, 0, tiled=True)  6.18 us
    pallas_call x1, Pallas kernels, solve_first(): pl.pallas_call(first_kernel, out_shape=jax.ShapeDtypeStruct((x_cells, sum...  4.89 us
    all_to_all x1, starting transfers between devices, per_device(): received = lax.all_to_all(middle, group, 0, 0, tiled=True)  4.73 us
    pallas_call x1, Pallas kernels, pseudo_inverse(): pl.pallas_call(inverse_kernel, out_shape=jax.ShapeDtypeStruct((rank, syst...  4.35 us
  transfers between devices with their start and end apart: 12, of which 7 were waited for; matrix products, arithmetic and copies ran while one was open for 2% of the time, Pallas kernels for 12%

profile of v7, /device:TPU:0, one launch (start us, length us, event | category | flops | bytes accessed | tf_op | source)
XLA Modules:
  0.0 87.9 jit_solution(8305322143756883124)
XLA Ops:
  0.6 0.0 copy-start.2
  0.6 0.0 copy-start.3
  0.7 4.3 %local_products.1 = (f32[128,512]{1,0:T(8,128)}, f32[32,256]{1,0:T(8,128)}, f32[16,32,256]{2,1,0:T(8,128)}, f32[16,32,256]{2,1,0:T(8,128)}, f32[16,32,256]{2,1,0:T(8,128)}, /*index=5*/f32[16,32,256]{2,1,0:T(8,128)}) custom-call(bf16[32,64,512]{2,1,0:T(8,128)(2,1)} %field_hbm.1, bf16[32,128]{1,0:T(8,128)(2,1)} %last_x_hbm.1, bf16[64,128]{1,0:T(8,128)(2,1)} %last_y_hbm.1, ...), custom_call_target="tpu_custom_call" | custom-call | tf_op jit(solution)/shard_map/local_products/pallas_call | solution.py:200
  5.0 0.0 copy-start
  5.0 0.0 copy-start.1
  5.0 0.5 collective-permute-start
  5.5 7.1 %all-to-all-start = ((f32[16,8,512]{2,1,0:T(8,128)}), f32[16,8,512]{2,1,0:T(8,128)S(1)}, u32[]{:S(2)}, u32[]{:S(2)}) async-start(f32[16,8,512]{2,1,0:T(8,128)} %bitcast.25), calls=%async_computation | async-start | bytes 524288 | tf_op jit(solution)/shard_map/all_to_all | solution.py:428
  12.6 0.0 copy-done.3
  12.6 0.0 collective-permute-done
  12.6 0.8 add.7.rows
  13.4 2.9 %collective-permute-start.1 = (f32[1,96,128]{2,1,0:T(8,128)S(1)}, f32[1,96,128]{2,1,0:T(8,128)S(1)}, u32[]{:S(2)}, u32[]{:S(2)}) collective-permute-start(f32[1,96,128]{2,1,0:T(8,128)S(1)} %maximum_bitcast_fusion), channel_id=1, source_target_pairs={{0,16},{4,20},{8,24},{12,28},{16,0},{20,4},{24,8},{28,12},{1,17},{... | collective-permute-start | bytes 147464 | tf_op jit(solution)/shard_map/ppermute | solution.py:29
  16.3 1.5 %collective-permute-start.4 = (f32[16,32,256]{2,1,0:T(8,128)}, f32[16,32,256]{2,1,0:T(8,128)S(1)}, u32[]{:S(2)}, u32[]{:S(2)}) collective-permute-start(f32[16,32,256]{2,1,0:T(8,128)} %get-tuple-element.23), channel_id=1, source_target_pairs={{0,1},{1,0},{2,3},{3,2},{4,5},{5,4},{6,7},{7,6},{8,9},{9,8},{10,11... | collective-permute-start | bytes 1572872 | tf_op jit(solution)/shard_map/ppermute | solution.py:29
  17.8 6.5 %collective-permute-done.1 = f32[1,96,128]{2,1,0:T(8,128)S(1)} collective-permute-done((f32[1,96,128]{2,1,0:T(8,128)S(1)}, f32[1,96,128]{2,1,0:T(8,128)S(1)}, u32[]{:S(2)}, u32[]{:S(2)}) %collective-permute-start.1) | collective-permute-done | bytes 49184 | tf_op jit(solution)/shard_map/ppermute | solution.py:29
  24.4 0.1 collective-permute-start.2
  24.5 0.0 all-to-all-done
  24.5 0.0 copy-done.2
  24.5 0.1 fusion.1
  24.7 0.7 broadcast_in_dim.10
  25.4 1.5 %collective-permute-start.5 = (f32[16,32,256]{2,1,0:T(8,128)}, f32[16,32,256]{2,1,0:T(8,128)S(1)}, u32[]{:S(2)}, u32[]{:S(2)}) collective-permute-start(f32[16,32,256]{2,1,0:T(8,128)} %get-tuple-element.25), channel_id=1, source_target_pairs={{0,1},{1,0},{2,3},{3,2},{4,5},{5,4},{6,7},{7,6},{8,9},{9,8},{10,11... | collective-permute-start | bytes 1572872 | tf_op jit(solution)/shard_map/ppermute | solution.py:29
  26.9 3.3 %all-to-all-start.1 = ((f32[32,8,256]{2,1,0:T(8,128)}), f32[32,8,256]{2,1,0:T(8,128)S(1)}, u32[]{:S(2)}, u32[]{:S(2)}) async-start(f32[32,8,256]{2,1,0:T(8,128)} %broadcast_in_dim.10), calls=%async_computation.1 | async-start | bytes 524288 | tf_op jit(solution)/shard_map/all_to_all | solution.py:440
  30.2 0.0 collective-permute-done.2
  30.2 1.8 %collective-permute-start.3 = (f32[4,96,128]{2,1,0:T(8,128)S(1)}, f32[4,96,128]{2,1,0:T(8,128)S(1)}, u32[]{:S(2)}, u32[]{:S(2)}) collective-permute-start(f32[4,96,128]{2,1,0:T(8,128)S(1)} %pad_maximum_fusion.1), channel_id=1, source_target_pairs={{0,4},{4,0},{8,12},{12,8},{16,20},{20,16},{24,28},{28,24},{1,5},{5... | collective-permute-start | bytes 589832 | tf_op jit(solution)/shard_map/ppermute | solution.py:29
  32.1 7.9 %collective-permute-done.3 = f32[4,96,128]{2,1,0:T(8,128)S(1)} collective-permute-done((f32[4,96,128]{2,1,0:T(8,128)S(1)}, f32[4,96,128]{2,1,0:T(8,128)S(1)}, u32[]{:S(2)}, u32[]{:S(2)}) %collective-permute-start.3) | collective-permute-done | bytes 196640 | tf_op jit(solution)/shard_map/ppermute | solution.py:29
  40.0 4.2 %all-to-all-done.1 = f32[32,8,256]{2,1,0:T(8,128)S(1)} async-done(((f32[32,8,256]{2,1,0:T(8,128)}), f32[32,8,256]{2,1,0:T(8,128)S(1)}, u32[]{:S(2)}, u32[]{:S(2)}) %all-to-all-start.1) | async-done | bytes 262176 | tf_op jit(solution)/shard_map/all_to_all | solution.py:440
  44.3 4.4 %pseudo_inverse.1.pinv = f32[128,256]{1,0:T(8,128)S(1)} custom-call(f32[16,2,8,256]{3,2,1,0:T(8,128)S(1)} %bitcast.22), custom_call_target="tpu_custom_call" | custom-call | tf_op jit(solution)/shard_map/pseudo_inverse/pallas_call | solution.py:232
  48.6 0.0 collective-permute-done.4.refs_2_
  48.6 0.0 collective-permute-done.5.refs_3_
  48.7 0.0 copy-done
  48.7 0.0 copy-done.1
  48.7 1.6 %project.1 = f32[8,160,128]{2,1,0:T(8,128)} custom-call(f32[128,256]{1,0:T(8,128)S(1)} %pseudo_inverse.1.pinv, f32[32,128]{1,0:T(8,128)S(1)} %bitcast.23, f32[16,32,256]{2,1,0:T(8,128)S(1)} %copy-done, f32[16,32,256]{2,1,0:T(8,128)S(1)} %copy-done.1, f32[16,32,256]{2,1,0:T(8,128)S(1)} %collective-permute-done.4.refs_2_, ...), custom_call_target="tpu_custom_call" | custom-call | tf_op jit(solution)/shard_map/project/pallas_call | solution.py:275
  50.2 3.6 %all-to-all-start.2 = ((f32[8,160,128]{2,1,0:T(8,128)}), f32[8,160,128]{2,1,0:T(8,128)S(1)}, u32[]{:S(2)}, u32[]{:S(2)}) async-start(f32[8,160,128]{2,1,0:T(8,128)} %project.1), calls=%async_computation.2 | async-start | bytes 1310720 | tf_op jit(solution)/shard_map/all_to_all | solution.py:455
  53.9 0.4 first_sums.1.refs_0_
  54.3 1.5 %collective-permute-start.6 = (f32[160,256]{1,0:T(8,128)S(1)}, f32[160,256]{1,0:T(8,128)S(1)}, u32[]{:S(2)}, u32[]{:S(2)}) collective-permute-start(f32[160,256]{1,0:T(8,128)S(1)} %first_sums.1.refs_0_), channel_id=1, source_target_pairs={{0,1},{1,0},{2,3},{3,2},{4,5},{5,4},{6,7},{7,6},{8,9},{9,8},{10,11... | collective-permute-start | bytes 491528 | tf_op jit(solution)/shard_map/ppermute | solution.py:29
  55.8 4.5 %collective-permute-done.6.refs_1_ = f32[160,256]{1,0:T(8,128)S(1)} collective-permute-done((f32[160,256]{1,0:T(8,128)S(1)}, f32[160,256]{1,0:T(8,128)S(1)}, u32[]{:S(2)}, u32[]{:S(2)}) %collective-permute-start.6) | collective-permute-done | bytes 163872 | tf_op jit(solution)/shard_map/ppermute | solution.py:29
  60.3 4.9 %solve_first.1 = f32[32,128]{1,0:T(8,128)} custom-call(f32[160,256]{1,0:T(8,128)S(1)} %first_sums.1.refs_0_, f32[160,256]{1,0:T(8,128)S(1)} %collective-permute-done.6.refs_1_), custom_call_target="tpu_custom_call" | custom-call | tf_op jit(solution)/shard_map/solve_first/pallas_call | solution.py:366
  65.2 6.2 %all-to-all-done.2.pieces = f32[8,160,128]{2,1,0:T(8,128)S(1)} async-done(((f32[8,160,128]{2,1,0:T(8,128)}), f32[8,160,128]{2,1,0:T(8,128)S(1)}, u32[]{:S(2)}, u32[]{:S(2)}) %all-to-all-start.2) | async-done | bytes 655392 | tf_op jit(solution)/shard_map/all_to_all | solution.py:455
  71.4 1.0 %sketch.1 = (f32[16,4,8,128]{3,2,1,0:T(8,128)}, f32[8,32,128]{2,1,0:T(8,128)S(1)}) custom-call(f32[8,160,128]{2,1,0:T(8,128)S(1)} %all-to-all-done.2.pieces, f32[8,96,128]{2,1,0:T(8,128)S(1)} %pad_maximum_fusion.packed), custom_call_target="tpu_custom_call" | custom-call | tf_op jit(solution)/shard_map/sketch/pallas_call | solution.py:311
  72.4 4.7 %all-to-all-start.3 = ((f32[16,4,8,128]{3,2,1,0:T(8,128)}), f32[16,4,8,128]{3,2,1,0:T(8,128)S(1)}, u32[]{:S(2)}, u32[]{:S(2)}) async-start(f32[16,4,8,128]{3,2,1,0:T(8,128)} %get-tuple-element.29), calls=%async_computation.3 | async-start | bytes 524288 | tf_op jit(solution)/shard_map/all_to_all | solution.py:466
  77.1 0.1 collective-permute-start.7
  77.2 1.3 %collective-permute-done.7.refs_1_ = f32[8,32,128]{2,1,0:T(8,128)S(1)} collective-permute-done((f32[8,32,128]{2,1,0:T(8,128)S(1)}, f32[8,32,128]{2,1,0:T(8,128)S(1)}, u32[]{:S(2)}, u32[]{:S(2)}) %collective-permute-start.7) | collective-permute-done | bytes 131104 | tf_op jit(solution)/shard_map/ppermute | solution.py:29
  78.5 0.7 place.1
  79.3 7.9 %all-to-all-done.3 = f32[16,4,8,128]{3,2,1,0:T(8,128)S(1)} async-done(((f32[16,4,8,128]{3,2,1,0:T(8,128)}), f32[16,4,8,128]{3,2,1,0:T(8,128)S(1)}, u32[]{:S(2)}, u32[]{:S(2)}) %all-to-all-start.3) | async-done | bytes 262176 | tf_op jit(solution)/shard_map/all_to_all | solution.py:466
  87.2 0.8 copy.11
  (9 shorter events, 0.1 us)
Async XLA Ops:
  0.6 23.9 %copy-start.2 = (bf16[512,256]{1,0:T(8,128)(2,1)S(1)}, bf16[512,256]{1,0:T(8,128)(2,1)}, u32[]{:S(2)}) copy-start(bf16[512,256]{1,0:T(8,128)(2,1)} %last_m_hbm.1) | copy-start | bytes 786436
  0.6 12.0 %copy-start.3 = (bf16[32,128]{1,0:T(8,128)(2,1)S(1)}, bf16[32,128]{1,0:T(8,128)(2,1)}, u32[]{:S(2)}) copy-start(bf16[32,128]{1,0:T(8,128)(2,1)} %param.8) | copy-start | bytes 24580
  5.0 43.7 %copy-start = (f32[16,32,256]{2,1,0:T(8,128)S(1)}, f32[16,32,256]{2,1,0:T(8,128)}, u32[]{:S(2)}) copy-start(f32[16,32,256]{2,1,0:T(8,128)} %get-tuple-element.21.refs_0_) | copy-start | bytes 1572868
  5.0 43.7 %copy-start.1 = (f32[16,32,256]{2,1,0:T(8,128)S(1)}, f32[16,32,256]{2,1,0:T(8,128)}, u32[]{:S(2)}) copy-start(f32[16,32,256]{2,1,0:T(8,128)} %get-tuple-element.22.refs_1_) | copy-start | bytes 1572868
  5.0 7.6 %collective-permute-start = (f32[32,256]{1,0:T(8,128)}, f32[32,256]{1,0:T(8,128)S(1)}, u32[]{:S(2)}, u32[]{:S(2)}) collective-permute-start(f32[32,256]{1,0:T(8,128)} %get-tuple-element.18), channel_id=1, source_target_pairs={{0,2},{2,0},{1,3},{3,1},{4,6},{6,4},{5,7},{7,5},{8,10},{10,8},{9,1... | collective-permute-start | bytes 98312 | tf_op jit(solution)/shard_map/ppermute | solution.py:29
  5.5 18.9 %all-to-all-start = ((f32[16,8,512]{2,1,0:T(8,128)}), f32[16,8,512]{2,1,0:T(8,128)S(1)}, u32[]{:S(2)}, u32[]{:S(2)}) async-start(f32[16,8,512]{2,1,0:T(8,128)} %bitcast.25), calls=%async_computation | async-start | bytes 524288 | tf_op jit(solution)/shard_map/all_to_all | solution.py:428
  13.4 10.9 %collective-permute-start.1 = (f32[1,96,128]{2,1,0:T(8,128)S(1)}, f32[1,96,128]{2,1,0:T(8,128)S(1)}, u32[]{:S(2)}, u32[]{:S(2)}) collective-permute-start(f32[1,96,128]{2,1,0:T(8,128)S(1)} %maximum_bitcast_fusion), channel_id=1, source_target_pairs={{0,16},{4,20},{8,24},{12,28},{16,0},{20,4},{24,8},{28,12},{1,17},{... | collective-permute-start | bytes 147464 | tf_op jit(solution)/shard_map/ppermute | solution.py:29
  16.3 32.3 %collective-permute-start.4 = (f32[16,32,256]{2,1,0:T(8,128)}, f32[16,32,256]{2,1,0:T(8,128)S(1)}, u32[]{:S(2)}, u32[]{:S(2)}) collective-permute-start(f32[16,32,256]{2,1,0:T(8,128)} %get-tuple-element.23), channel_id=1, source_target_pairs={{0,1},{1,0},{2,3},{3,2},{4,5},{5,4},{6,7},{7,6},{8,9},{9,8},{10,11... | collective-permute-start | bytes 1572872 | tf_op jit(solution)/shard_map/ppermute | solution.py:29
  24.4 5.8 %collective-permute-start.2 = (f32[2,96,128]{2,1,0:T(8,128)S(1)}, f32[2,96,128]{2,1,0:T(8,128)S(1)}, u32[]{:S(2)}, u32[]{:S(2)}) collective-permute-start(f32[2,96,128]{2,1,0:T(8,128)S(1)} %pad_maximum_fusion.2), channel_id=1, source_target_pairs={{0,8},{4,12},{8,0},{12,4},{16,24},{20,28},{24,16},{28,20},{1,9},{5... | collective-permute-start | bytes 294920 | tf_op jit(solution)/shard_map/ppermute | solution.py:29
  25.4 23.2 %collective-permute-start.5 = (f32[16,32,256]{2,1,0:T(8,128)}, f32[16,32,256]{2,1,0:T(8,128)S(1)}, u32[]{:S(2)}, u32[]{:S(2)}) collective-permute-start(f32[16,32,256]{2,1,0:T(8,128)} %get-tuple-element.25), channel_id=1, source_target_pairs={{0,1},{1,0},{2,3},{3,2},{4,5},{5,4},{6,7},{7,6},{8,9},{9,8},{10,11... | collective-permute-start | bytes 1572872 | tf_op jit(solution)/shard_map/ppermute | solution.py:29
  26.9 17.3 %all-to-all-start.1 = ((f32[32,8,256]{2,1,0:T(8,128)}), f32[32,8,256]{2,1,0:T(8,128)S(1)}, u32[]{:S(2)}, u32[]{:S(2)}) async-start(f32[32,8,256]{2,1,0:T(8,128)} %broadcast_in_dim.10), calls=%async_computation.1 | async-start | bytes 524288 | tf_op jit(solution)/shard_map/all_to_all | solution.py:440
  30.2 9.8 %collective-permute-start.3 = (f32[4,96,128]{2,1,0:T(8,128)S(1)}, f32[4,96,128]{2,1,0:T(8,128)S(1)}, u32[]{:S(2)}, u32[]{:S(2)}) collective-permute-start(f32[4,96,128]{2,1,0:T(8,128)S(1)} %pad_maximum_fusion.1), channel_id=1, source_target_pairs={{0,4},{4,0},{8,12},{12,8},{16,20},{20,16},{24,28},{28,24},{1,5},{5... | collective-permute-start | bytes 589832 | tf_op jit(solution)/shard_map/ppermute | solution.py:29
  50.2 21.2 %all-to-all-start.2 = ((f32[8,160,128]{2,1,0:T(8,128)}), f32[8,160,128]{2,1,0:T(8,128)S(1)}, u32[]{:S(2)}, u32[]{:S(2)}) async-start(f32[8,160,128]{2,1,0:T(8,128)} %project.1), calls=%async_computation.2 | async-start | bytes 1310720 | tf_op jit(solution)/shard_map/all_to_all | solution.py:455
  54.3 6.1 %collective-permute-start.6 = (f32[160,256]{1,0:T(8,128)S(1)}, f32[160,256]{1,0:T(8,128)S(1)}, u32[]{:S(2)}, u32[]{:S(2)}) collective-permute-start(f32[160,256]{1,0:T(8,128)S(1)} %first_sums.1.refs_0_), channel_id=1, source_target_pairs={{0,1},{1,0},{2,3},{3,2},{4,5},{5,4},{6,7},{7,6},{8,9},{9,8},{10,11... | collective-permute-start | bytes 491528 | tf_op jit(solution)/shard_map/ppermute | solution.py:29
  72.4 14.8 %all-to-all-start.3 = ((f32[16,4,8,128]{3,2,1,0:T(8,128)}), f32[16,4,8,128]{3,2,1,0:T(8,128)S(1)}, u32[]{:S(2)}, u32[]{:S(2)}) async-start(f32[16,4,8,128]{3,2,1,0:T(8,128)} %get-tuple-element.29), calls=%async_computation.3 | async-start | bytes 524288 | tf_op jit(solution)/shard_map/all_to_all | solution.py:466
  77.1 1.4 %collective-permute-start.7 = (f32[8,32,128]{2,1,0:T(8,128)S(1)}, f32[8,32,128]{2,1,0:T(8,128)S(1)}, u32[]{:S(2)}, u32[]{:S(2)}) collective-permute-start(f32[8,32,128]{2,1,0:T(8,128)S(1)} %get-tuple-element.30.refs_0_), channel_id=1, source_target_pairs={{0,2},{2,0},{1,3},{3,1},{4,6},{6,4},{5,7},{7,5},{8,10},{10,8},{9,1... | collective-permute-start | bytes 393224 | tf_op jit(solution)/shard_map/ppermute | solution.py:29

commit v8 on v7

--- a/solution.py
+++ b/solution.py
@@ -408,7 +408,8 @@
     )
 
     for s in range(1, shares):
-        terms[s * PARTS] = swap(terms[s * PARTS], "gz", s)
+        for part in range(PARTS):
+            terms[s * PARTS + part] = swap(terms[s * PARTS + part], "gz", s)
 
     order = swap_order("gx")
     first_rows = swap_sum(first_part, "gy")
@@ -426,17 +427,13 @@
     group = ("gx", "gy")
     own = rank // lax.axis_size(group)
     last_rows = lax.all_to_all(last_part.reshape(-1, own, m_cells), group, 0, 0, tiled=True)
-    last_rows = jnp.sum(last_rows, axis=0)
+    last_rows = jnp.sum(after(last_rows, *terms[PARTS::PARTS]), axis=0)
     both = jnp.dot(
         jnp.concatenate(split_terms(last_rows), axis=0), last_m, preferred_element_type=jnp.float32
     )
     both = after(both[:own] + both[own:], packed)
     count = lax.axis_size(ALL)
     copies = jnp.broadcast_to(both[None], (count, own, cols))
-    for s in range(1, shares):
-        for part in range(1, PARTS):
-            at = s * PARTS + part
-            terms[at] = swap(after(terms[at], copies), "gz", s)
     system = lax.all_to_all(copies, ALL, 0, 0, tiled=True).reshape(-1, shares, own, cols)
     if own % ROWS:
         system = jnp.sum(system, axis=1).reshape(-1, 1, ROWS, cols)
@@ -448,7 +445,7 @@
         extra = jnp.zeros((ROWS, LANES), jnp.float32)
     else:
         extra = last_rows.reshape(own, -1, LANES).transpose(1, 0, 2).reshape(-1, LANES)
-    pinv = pseudo_inverse(after(system, packed))
+    pinv = pseudo_inverse(after(system, packed, *terms[PARTS:]))
     projected = project(blocks, pinv, extra, terms)
     sums = [swap(sums, "gz", z) if z else sums for z in range(shares)]
 

time: 88.5 us -> 85 us (0.960)
  waiting for transfers between devices: 38.7 us -> 36.5 us
  starting transfers between devices: 28.6 us -> 27.4 us
    all_to_all x1, waiting for transfers between devices: 4.25 us -> 0.86 us  [per_device(): lax.all_to_all(copies, ALL, 0, 0, tiled=True).reshape(-1, shares, own, cols)]
    ppermute x8, waiting for transfers between devices: 20.3 us -> 21.5 us  [swap(): lax.ppermute(array, axis, [(s, s ^ bits) for s in range(lax.axis_size(axi...]
    all_to_all x1, starting transfers between devices: 7.06 us -> 5.91 us  [per_device(): lax.all_to_all(last_part.reshape(-1, own, m_cells), group, 0, 0, tiled=True)]
  transfers between devices with their start and end apart: 12 -> 12, of which waited for: 7 -> 8; matrix products, arithmetic and copies ran while one was open for 2% -> 2% of each run, Pallas kernels for 12% -> 7%
where the time goes in v8:
time: 85 us; the launch traced here: 84.5 us
  waiting for transfers between devices  36.5 us (43%)
  starting transfers between devices  27.4 us (32%)
  Pallas kernels  17.2 us (20%)
  local copies, waits for them, and re-layouts  1.52 us (2%)
  other arithmetic  0.87 us (1%)
    ppermute x8, waiting for transfers between devices, swap(): lax.ppermute(array, axis, [(s, s ^ bits) for s in range(lax.axis_size(axi...  21.5 us
    ppermute x8, starting transfers between devices, swap(): lax.ppermute(array, axis, [(s, s ^ bits) for s in range(lax.axis_size(axi...  9.75 us
    all_to_all x1, waiting for transfers between devices, per_device(): received = lax.all_to_all(middle, group, 0, 0, tiled=True)  7.91 us
    all_to_all x1, waiting for transfers between devices, per_device(): pieces = lax.all_to_all(projected, 'gx', 0, 0, tiled=True)  6.18 us
    all_to_all x1, starting transfers between devices, per_device(): lax.all_to_all(last_part.reshape(-1, own, m_cells), group, 0, 0, tiled=True)  5.91 us
    pallas_call x1, Pallas kernels, solve_first(): pl.pallas_call(first_kernel, out_shape=jax.ShapeDtypeStruct((x_cells, sum...  4.89 us
    all_to_all x1, starting transfers between devices, per_device(): received = lax.all_to_all(middle, group, 0, 0, tiled=True)  4.63 us
    pallas_call x1, Pallas kernels, pseudo_inverse(): pl.pallas_call(inverse_kernel, out_shape=jax.ShapeDtypeStruct((rank, syst...  4.35 us
  transfers between devices with their start and end apart: 12, of which 8 were waited for; matrix products, arithmetic and copies ran while one was open for 2% of the time, Pallas kernels for 7%

profile of v8, /device:TPU:0, one launch (start us, length us, event | category | flops | bytes accessed | tf_op | source)
XLA Modules:
  0.0 84.5 jit_solution(1062934199729875674)
XLA Ops:
  0.6 0.0 copy-start.2
  0.6 0.0 copy-start.3
  0.7 4.3 %local_products.1 = (f32[128,512]{1,0:T(8,128)}, f32[32,256]{1,0:T(8,128)}, f32[16,32,256]{2,1,0:T(8,128)}, f32[16,32,256]{2,1,0:T(8,128)}, f32[16,32,256]{2,1,0:T(8,128)}, /*index=5*/f32[16,32,256]{2,1,0:T(8,128)}) custom-call(bf16[32,64,512]{2,1,0:T(8,128)(2,1)} %field_hbm.1, bf16[32,128]{1,0:T(8,128)(2,1)} %last_x_hbm.1, bf16[64,128]{1,0:T(8,128)(2,1)} %last_y_hbm.1, ...), custom_call_target="tpu_custom_call" | custom-call | tf_op jit(solution)/shard_map/local_products/pallas_call | solution.py:200
  5.0 0.0 copy-start
  5.0 0.0 copy-start.1
  5.0 0.5 collective-permute-start.1
  5.5 2.6 %collective-permute-start = (f32[16,32,256]{2,1,0:T(8,128)}, f32[16,32,256]{2,1,0:T(8,128)S(1)}, u32[]{:S(2)}, u32[]{:S(2)}) collective-permute-start(f32[16,32,256]{2,1,0:T(8,128)} %get-tuple-element.18), channel_id=1, source_target_pairs={{0,1},{1,0},{2,3},{3,2},{4,5},{5,4},{6,7},{7,6},{8,9},{9,8},{10,11... | collective-permute-start | bytes 1572872 | tf_op jit(solution)/shard_map/ppermute | solution.py:29
  8.1 5.9 %all-to-all-start = ((f32[16,8,512]{2,1,0:T(8,128)}), f32[16,8,512]{2,1,0:T(8,128)S(1)}, u32[]{:S(2)}, u32[]{:S(2)}) async-start(f32[16,8,512]{2,1,0:T(8,128)} %bitcast.25), calls=%async_computation | async-start | bytes 524288 | tf_op jit(solution)/shard_map/all_to_all | solution.py:429
  14.1 0.0 copy-done.3
  14.1 0.0 collective-permute-done.1
  14.1 0.8 add.7.rows
  14.9 2.9 %collective-permute-start.2 = (f32[1,96,128]{2,1,0:T(8,128)S(1)}, f32[1,96,128]{2,1,0:T(8,128)S(1)}, u32[]{:S(2)}, u32[]{:S(2)}) collective-permute-start(f32[1,96,128]{2,1,0:T(8,128)S(1)} %maximum_bitcast_fusion), channel_id=1, source_target_pairs={{0,16},{4,20},{8,24},{12,28},{16,0},{20,4},{24,8},{28,12},{1,17},{... | collective-permute-start | bytes 147464 | tf_op jit(solution)/shard_map/ppermute | solution.py:29
  17.8 0.5 collective-permute-start.5
  18.3 7.5 %collective-permute-done.2 = f32[1,96,128]{2,1,0:T(8,128)S(1)} collective-permute-done((f32[1,96,128]{2,1,0:T(8,128)S(1)}, f32[1,96,128]{2,1,0:T(8,128)S(1)}, u32[]{:S(2)}, u32[]{:S(2)}) %collective-permute-start.2) | collective-permute-done | bytes 49184 | tf_op jit(solution)/shard_map/ppermute | solution.py:29
  25.8 0.1 collective-permute-start.3
  25.9 0.0 all-to-all-done
  25.9 0.0 collective-permute-done.refs_2_
  26.0 0.0 copy-done.2
  26.0 0.1 fusion.1
  26.1 0.7 broadcast_in_dim.10
  26.9 3.3 %all-to-all-start.1 = ((f32[32,8,256]{2,1,0:T(8,128)}), f32[32,8,256]{2,1,0:T(8,128)S(1)}, u32[]{:S(2)}, u32[]{:S(2)}) async-start(f32[32,8,256]{2,1,0:T(8,128)} %broadcast_in_dim.10), calls=%async_computation.1 | async-start | bytes 524288 | tf_op jit(solution)/shard_map/all_to_all | solution.py:437
  30.1 0.4 collective-permute-done.3
  30.5 1.5 %collective-permute-start.4 = (f32[4,96,128]{2,1,0:T(8,128)S(1)}, f32[4,96,128]{2,1,0:T(8,128)S(1)}, u32[]{:S(2)}, u32[]{:S(2)}) collective-permute-start(f32[4,96,128]{2,1,0:T(8,128)S(1)} %pad_maximum_fusion.1), channel_id=1, source_target_pairs={{0,4},{4,0},{8,12},{12,8},{16,20},{20,16},{24,28},{28,24},{1,5},{5... | collective-permute-start | bytes 589832 | tf_op jit(solution)/shard_map/ppermute | solution.py:29
  32.0 7.9 %collective-permute-done.4 = f32[4,96,128]{2,1,0:T(8,128)S(1)} collective-permute-done((f32[4,96,128]{2,1,0:T(8,128)S(1)}, f32[4,96,128]{2,1,0:T(8,128)S(1)}, u32[]{:S(2)}, u32[]{:S(2)}) %collective-permute-start.4) | collective-permute-done | bytes 196640 | tf_op jit(solution)/shard_map/ppermute | solution.py:29
  40.0 0.0 collective-permute-done.5.refs_3_
  40.0 0.9 %all-to-all-done.1 = f32[32,8,256]{2,1,0:T(8,128)S(1)} async-done(((f32[32,8,256]{2,1,0:T(8,128)}), f32[32,8,256]{2,1,0:T(8,128)S(1)}, u32[]{:S(2)}, u32[]{:S(2)}) %all-to-all-start.1) | async-done | bytes 262176 | tf_op jit(solution)/shard_map/all_to_all | solution.py:437
  40.8 4.4 %pseudo_inverse.1.pinv = f32[128,256]{1,0:T(8,128)S(1)} custom-call(f32[16,2,8,256]{3,2,1,0:T(8,128)S(1)} %bitcast.22), custom_call_target="tpu_custom_call" | custom-call | tf_op jit(solution)/shard_map/pseudo_inverse/pallas_call | solution.py:232
  45.2 0.0 copy-done
  45.2 0.0 copy-done.1
  45.2 1.6 %project.1 = f32[8,160,128]{2,1,0:T(8,128)} custom-call(f32[128,256]{1,0:T(8,128)S(1)} %pseudo_inverse.1.pinv, f32[32,128]{1,0:T(8,128)S(1)} %bitcast.23, f32[16,32,256]{2,1,0:T(8,128)S(1)} %copy-done, f32[16,32,256]{2,1,0:T(8,128)S(1)} %copy-done.1, f32[16,32,256]{2,1,0:T(8,128)S(1)} %collective-permute-done.refs_2_, ...), custom_call_target="tpu_custom_call" | custom-call | tf_op jit(solution)/shard_map/project/pallas_call | solution.py:275
  46.8 3.8 %all-to-all-start.2 = ((f32[8,160,128]{2,1,0:T(8,128)}), f32[8,160,128]{2,1,0:T(8,128)S(1)}, u32[]{:S(2)}, u32[]{:S(2)}) async-start(f32[8,160,128]{2,1,0:T(8,128)} %project.1), calls=%async_computation.2 | async-start | bytes 1310720 | tf_op jit(solution)/shard_map/all_to_all | solution.py:452
  50.6 0.4 first_sums.1.refs_0_
  51.0 1.6 %collective-permute-start.6 = (f32[160,256]{1,0:T(8,128)S(1)}, f32[160,256]{1,0:T(8,128)S(1)}, u32[]{:S(2)}, u32[]{:S(2)}) collective-permute-start(f32[160,256]{1,0:T(8,128)S(1)} %first_sums.1.refs_0_), channel_id=1, source_target_pairs={{0,1},{1,0},{2,3},{3,2},{4,5},{5,4},{6,7},{7,6},{8,9},{9,8},{10,11... | collective-permute-start | bytes 491528 | tf_op jit(solution)/shard_map/ppermute | solution.py:29
  52.6 4.4 %collective-permute-done.6.refs_1_ = f32[160,256]{1,0:T(8,128)S(1)} collective-permute-done((f32[160,256]{1,0:T(8,128)S(1)}, f32[160,256]{1,0:T(8,128)S(1)}, u32[]{:S(2)}, u32[]{:S(2)}) %collective-permute-start.6) | collective-permute-done | bytes 163872 | tf_op jit(solution)/shard_map/ppermute | solution.py:29
  57.0 4.9 %solve_first.1 = f32[32,128]{1,0:T(8,128)} custom-call(f32[160,256]{1,0:T(8,128)S(1)} %first_sums.1.refs_0_, f32[160,256]{1,0:T(8,128)S(1)} %collective-permute-done.6.refs_1_), custom_call_target="tpu_custom_call" | custom-call | tf_op jit(solution)/shard_map/solve_first/pallas_call | solution.py:366
  61.9 6.2 %all-to-all-done.2.pieces = f32[8,160,128]{2,1,0:T(8,128)S(1)} async-done(((f32[8,160,128]{2,1,0:T(8,128)}), f32[8,160,128]{2,1,0:T(8,128)S(1)}, u32[]{:S(2)}, u32[]{:S(2)}) %all-to-all-start.2) | async-done | bytes 655392 | tf_op jit(solution)/shard_map/all_to_all | solution.py:452
  68.1 1.0 %sketch.1 = (f32[16,4,8,128]{3,2,1,0:T(8,128)}, f32[8,32,128]{2,1,0:T(8,128)S(1)}) custom-call(f32[8,160,128]{2,1,0:T(8,128)S(1)} %all-to-all-done.2.pieces, f32[8,96,128]{2,1,0:T(8,128)S(1)} %pad_maximum_fusion.packed), custom_call_target="tpu_custom_call" | custom-call | tf_op jit(solution)/shard_map/sketch/pallas_call | solution.py:311
  69.0 4.6 %all-to-all-start.3 = ((f32[16,4,8,128]{3,2,1,0:T(8,128)}), f32[16,4,8,128]{3,2,1,0:T(8,128)S(1)}, u32[]{:S(2)}, u32[]{:S(2)}) async-start(f32[16,4,8,128]{3,2,1,0:T(8,128)} %get-tuple-element.29), calls=%async_computation.3 | async-start | bytes 524288 | tf_op jit(solution)/shard_map/all_to_all | solution.py:463
  73.7 0.1 collective-permute-start.7
  73.8 1.3 %collective-permute-done.7.refs_1_ = f32[8,32,128]{2,1,0:T(8,128)S(1)} collective-permute-done((f32[8,32,128]{2,1,0:T(8,128)S(1)}, f32[8,32,128]{2,1,0:T(8,128)S(1)}, u32[]{:S(2)}, u32[]{:S(2)}) %collective-permute-start.7) | collective-permute-done | bytes 131104 | tf_op jit(solution)/shard_map/ppermute | solution.py:29
  75.1 0.7 place.1
  75.8 7.9 %all-to-all-done.3 = f32[16,4,8,128]{3,2,1,0:T(8,128)S(1)} async-done(((f32[16,4,8,128]{3,2,1,0:T(8,128)}), f32[16,4,8,128]{3,2,1,0:T(8,128)S(1)}, u32[]{:S(2)}, u32[]{:S(2)}) %all-to-all-start.3) | async-done | bytes 262176 | tf_op jit(solution)/shard_map/all_to_all | solution.py:463
  83.7 0.8 copy.11
  (9 shorter events, 0.1 us)
Async XLA Ops:
  0.6 25.3 %copy-start.2 = (bf16[512,256]{1,0:T(8,128)(2,1)S(1)}, bf16[512,256]{1,0:T(8,128)(2,1)}, u32[]{:S(2)}) copy-start(bf16[512,256]{1,0:T(8,128)(2,1)} %last_m_hbm.1) | copy-start | bytes 786436
  0.6 13.4 %copy-start.3 = (bf16[32,128]{1,0:T(8,128)(2,1)S(1)}, bf16[32,128]{1,0:T(8,128)(2,1)}, u32[]{:S(2)}) copy-start(bf16[32,128]{1,0:T(8,128)(2,1)} %param.8) | copy-start | bytes 24580
  5.0 40.2 %copy-start = (f32[16,32,256]{2,1,0:T(8,128)S(1)}, f32[16,32,256]{2,1,0:T(8,128)}, u32[]{:S(2)}) copy-start(f32[16,32,256]{2,1,0:T(8,128)} %get-tuple-element.24.refs_0_) | copy-start | bytes 1572868
  5.0 40.2 %copy-start.1 = (f32[16,32,256]{2,1,0:T(8,128)S(1)}, f32[16,32,256]{2,1,0:T(8,128)}, u32[]{:S(2)}) copy-start(f32[16,32,256]{2,1,0:T(8,128)} %get-tuple-element.25.refs_1_) | copy-start | bytes 1572868
  5.0 9.1 %collective-permute-start.1 = (f32[32,256]{1,0:T(8,128)}, f32[32,256]{1,0:T(8,128)S(1)}, u32[]{:S(2)}, u32[]{:S(2)}) collective-permute-start(f32[32,256]{1,0:T(8,128)} %get-tuple-element.20), channel_id=1, source_target_pairs={{0,2},{2,0},{1,3},{3,1},{4,6},{6,4},{5,7},{7,5},{8,10},{10,8},{9,1... | collective-permute-start | bytes 98312 | tf_op jit(solution)/shard_map/ppermute | solution.py:29
  5.5 20.4 %collective-permute-start = (f32[16,32,256]{2,1,0:T(8,128)}, f32[16,32,256]{2,1,0:T(8,128)S(1)}, u32[]{:S(2)}, u32[]{:S(2)}) collective-permute-start(f32[16,32,256]{2,1,0:T(8,128)} %get-tuple-element.18), channel_id=1, source_target_pairs={{0,1},{1,0},{2,3},{3,2},{4,5},{5,4},{6,7},{7,6},{8,9},{9,8},{10,11... | collective-permute-start | bytes 1572872 | tf_op jit(solution)/shard_map/ppermute | solution.py:29
  8.1 17.8 %all-to-all-start = ((f32[16,8,512]{2,1,0:T(8,128)}), f32[16,8,512]{2,1,0:T(8,128)S(1)}, u32[]{:S(2)}, u32[]{:S(2)}) async-start(f32[16,8,512]{2,1,0:T(8,128)} %bitcast.25), calls=%async_computation | async-start | bytes 524288 | tf_op jit(solution)/shard_map/all_to_all | solution.py:429
  14.9 10.9 %collective-permute-start.2 = (f32[1,96,128]{2,1,0:T(8,128)S(1)}, f32[1,96,128]{2,1,0:T(8,128)S(1)}, u32[]{:S(2)}, u32[]{:S(2)}) collective-permute-start(f32[1,96,128]{2,1,0:T(8,128)S(1)} %maximum_bitcast_fusion), channel_id=1, source_target_pairs={{0,16},{4,20},{8,24},{12,28},{16,0},{20,4},{24,8},{28,12},{1,17},{... | collective-permute-start | bytes 147464 | tf_op jit(solution)/shard_map/ppermute | solution.py:29
  17.8 22.2 %collective-permute-start.5 = (f32[16,32,256]{2,1,0:T(8,128)}, f32[16,32,256]{2,1,0:T(8,128)S(1)}, u32[]{:S(2)}, u32[]{:S(2)}) collective-permute-start(f32[16,32,256]{2,1,0:T(8,128)} %get-tuple-element.22), channel_id=1, source_target_pairs={{0,1},{1,0},{2,3},{3,2},{4,5},{5,4},{6,7},{7,6},{8,9},{9,8},{10,11... | collective-permute-start | bytes 1572872 | tf_op jit(solution)/shard_map/ppermute | solution.py:29
  25.8 4.7 %collective-permute-start.3 = (f32[2,96,128]{2,1,0:T(8,128)S(1)}, f32[2,96,128]{2,1,0:T(8,128)S(1)}, u32[]{:S(2)}, u32[]{:S(2)}) collective-permute-start(f32[2,96,128]{2,1,0:T(8,128)S(1)} %pad_maximum_fusion.2), channel_id=1, source_target_pairs={{0,8},{4,12},{8,0},{12,4},{16,24},{20,28},{24,16},{28,20},{1,9},{5... | collective-permute-start | bytes 294920 | tf_op jit(solution)/shard_map/ppermute | solution.py:29
  26.9 14.0 %all-to-all-start.1 = ((f32[32,8,256]{2,1,0:T(8,128)}), f32[32,8,256]{2,1,0:T(8,128)S(1)}, u32[]{:S(2)}, u32[]{:S(2)}) async-start(f32[32,8,256]{2,1,0:T(8,128)} %broadcast_in_dim.10), calls=%async_computation.1 | async-start | bytes 524288 | tf_op jit(solution)/shard_map/all_to_all | solution.py:437
  30.5 9.4 %collective-permute-start.4 = (f32[4,96,128]{2,1,0:T(8,128)S(1)}, f32[4,96,128]{2,1,0:T(8,128)S(1)}, u32[]{:S(2)}, u32[]{:S(2)}) collective-permute-start(f32[4,96,128]{2,1,0:T(8,128)S(1)} %pad_maximum_fusion.1), channel_id=1, source_target_pairs={{0,4},{4,0},{8,12},{12,8},{16,20},{20,16},{24,28},{28,24},{1,5},{5... | collective-permute-start | bytes 589832 | tf_op jit(solution)/shard_map/ppermute | solution.py:29
  46.8 21.3 %all-to-all-start.2 = ((f32[8,160,128]{2,1,0:T(8,128)}), f32[8,160,128]{2,1,0:T(8,128)S(1)}, u32[]{:S(2)}, u32[]{:S(2)}) async-start(f32[8,160,128]{2,1,0:T(8,128)} %project.1), calls=%async_computation.2 | async-start | bytes 1310720 | tf_op jit(solution)/shard_map/all_to_all | solution.py:452
  51.0 6.0 %collective-permute-start.6 = (f32[160,256]{1,0:T(8,128)S(1)}, f32[160,256]{1,0:T(8,128)S(1)}, u32[]{:S(2)}, u32[]{:S(2)}) collective-permute-start(f32[160,256]{1,0:T(8,128)S(1)} %first_sums.1.refs_0_), channel_id=1, source_target_pairs={{0,1},{1,0},{2,3},{3,2},{4,5},{5,4},{6,7},{7,6},{8,9},{9,8},{10,11... | collective-permute-start | bytes 491528 | tf_op jit(solution)/shard_map/ppermute | solution.py:29
  69.0 14.7 %all-to-all-start.3 = ((f32[16,4,8,128]{3,2,1,0:T(8,128)}), f32[16,4,8,128]{3,2,1,0:T(8,128)S(1)}, u32[]{:S(2)}, u32[]{:S(2)}) async-start(f32[16,4,8,128]{3,2,1,0:T(8,128)} %get-tuple-element.29), calls=%async_computation.3 | async-start | bytes 524288 | tf_op jit(solution)/shard_map/all_to_all | solution.py:463
  73.7 1.4 %collective-permute-start.7 = (f32[8,32,128]{2,1,0:T(8,128)S(1)}, f32[8,32,128]{2,1,0:T(8,128)S(1)}, u32[]{:S(2)}, u32[]{:S(2)}) collective-permute-start(f32[8,32,128]{2,1,0:T(8,128)S(1)} %get-tuple-element.30.refs_0_), channel_id=1, source_target_pairs={{0,2},{2,0},{1,3},{3,1},{4,6},{6,4},{5,7},{7,5},{8,10},{10,8},{9,1... | collective-permute-start | bytes 393224 | tf_op jit(solution)/shard_map/ppermute | solution.py:29

commit v9 on v8

--- a/solution.py
+++ b/solution.py
@@ -87,16 +87,20 @@
         first = panel * ROWS
         inside = (lanes >= first) & (lanes < first + ROWS)
         unit = (lanes - first == subs).astype(jnp.float32)
-        pivots = [column(rows[panel], first + c) for c in range(ROWS)]
-        solved = jnp.where(inside, unit, rows[panel])
-        for k in range(ROWS):
-            scale = 1.0 / pivots[k][k : k + 1]
-            here = subs == k
-            top = solved[k : k + 1] * scale
-            solved = jnp.where(here, top, solved - pivots[k] * top)
-            for c in range(k + 1, ROWS):
-                top = pivots[c][k : k + 1] * scale
-                pivots[c] = jnp.where(here, top, pivots[c] - pivots[k] * top)
+        work = [column(rows[panel], first + c) for c in range(ROWS)]
+        work.append(jnp.where(inside, unit, rows[panel]))
+        for k in range(0, ROWS, 2):
+            p, q = work[k], work[k + 1]
+            a, b, d = p[k : k + 1], q[k : k + 1], q[k + 1 : k + 2]
+            scale = 1.0 / (a * d - b * b)
+            a, b, d = a * scale, b * scale, d * scale
+            for c in range(k + 2, ROWS + 1):
+                upper, lower = work[c][k : k + 1], work[c][k + 1 : k + 2]
+                top = d * upper - b * lower
+                low = a * lower - b * upper
+                rest = work[c] - p * top - q * low
+                work[c] = jnp.where(subs == k, top, jnp.where(subs == k + 1, low, rest))
+        solved = work[ROWS]
         for r in range(len(rows)):
             if r == panel:
                 continue
@@ -129,8 +133,9 @@
     first_part,
     *refs,
 ):
-    terms_hbm = refs[: shares * PARTS]
-    field, last_x, last_y, right_y, right_m, last_m, terms, sems, out_sems = refs[shares * PARTS :]
+    count = (shares - 1) * PARTS
+    terms_hbm = refs[:count]
+    field, last_x, last_y, right_y, right_m, last_m, terms, sems, out_sems = refs[count:]
     x_cells, y_cells, m_cells = field.shape
     step = x_cells // chunks
     y_share = y_cells // shares
@@ -154,17 +159,17 @@
     copies[0].wait()
     for n in range(chunks):
         copies[5 + n if n else 1].wait()
-        for s in reversed(range(shares)):
+        for s in range(1, shares):
             start = pl.multiple_of((here ^ s) * y_share, y_share)
             rows = field[parts[n], pl.ds(start, y_share), :].reshape(step * y_share, m_cells)
             term = jnp.dot(rows, last_m[...], preferred_element_type=jnp.float32)
-            terms[s, parts[n]] = term.reshape(step, y_share, -1)
+            terms[s - 1, parts[n]] = term.reshape(step, y_share, -1)
             part, at = divmod(n * step, x_cells // PARTS)
             leaving.append(
                 pltpu.make_async_copy(
-                    terms.at[s, parts[n]],
-                    terms_hbm[s * PARTS + part].at[pl.ds(at, step)],
-                    out_sems.at[s, n],
+                    terms.at[s - 1, parts[n]],
+                    terms_hbm[(s - 1) * PARTS + part].at[pl.ds(at, step)],
+                    out_sems.at[s - 1, n],
                 )
             )
             leaving[-1].start()
@@ -200,21 +205,26 @@
     return pl.pallas_call(
         functools.partial(local_kernel, chunks, shares),
         in_specs=[hbm] * len(inputs),
-        out_specs=[vmem, vmem, *([hbm] * (shares * PARTS))],
+        out_specs=[vmem, vmem, *([hbm] * ((shares - 1) * PARTS))],
         out_shape=[
             jax.ShapeDtypeStruct((rank, m_cells), jnp.float32),
             jax.ShapeDtypeStruct((x_cells, cols), jnp.float32),
-            *([jax.ShapeDtypeStruct(part_dims, jnp.float32)] * (shares * PARTS)),
+            *([jax.ShapeDtypeStruct(part_dims, jnp.float32)] * ((shares - 1) * PARTS)),
         ],
         scratch_shapes=[
             *(pltpu.VMEM(x.shape, x.dtype) for x in inputs),
-            pltpu.VMEM((shares, *dims), jnp.float32),
+            pltpu.VMEM((shares - 1, *dims), jnp.float32),
             pltpu.SemaphoreType.DMA((5 + chunks,)),
-            pltpu.SemaphoreType.DMA((shares, chunks)),
+            pltpu.SemaphoreType.DMA((shares - 1, chunks)),
         ],
         compiler_params=pltpu.CompilerParams(vmem_limit_bytes=LOCAL_VMEM_BYTES),
         name="local_products",
     )(*inputs)
+
+
+def two_terms(array):
+    high = array.astype(jnp.bfloat16)
+    return high, (array - high.astype(jnp.float32)).astype(jnp.bfloat16)
 
 
 def inverse_kernel(system_shares, pinv):
@@ -222,9 +232,16 @@
     for k in range(1, system_shares.shape[1]):
         system = system + system_shares[:, k]
     system = system.reshape(-1, system.shape[-1])
-    pinv[...] = jnp.dot(
-        spd_inverse(system), system, precision=HIGHEST, preferred_element_type=jnp.float32
-    )
+    cols = system.shape[1]
+    high, low = two_terms(spd_inverse(system))
+    system_high, system_low = two_terms(system)
+    both = jnp.dot(
+        high,
+        jnp.concatenate([system_high, system_low], axis=1),
+        preferred_element_type=jnp.float32,
+    )
+    rest = jnp.dot(low, system_high, preferred_element_type=jnp.float32)
+    pinv[...] = both[:, :cols] + (both[:, cols:] + rest)
 
 
 def pseudo_inverse(system_shares):
@@ -237,27 +254,22 @@
     )(system_shares)
 
 
-def two_terms(array):
-    high = array.astype(jnp.bfloat16)
-    return high, (array - high.astype(jnp.float32)).astype(jnp.bfloat16)
-
-
-def project_kernel(y_own, pinv, extra, *refs):
+def project_kernel(y_own, pinv, extra, kept, *refs):
     *terms, projected, flat = refs
     rank = pinv.shape[0]
     pinv_high, pinv_low = two_terms(pinv[...])
     pinv_both = jnp.concatenate([pinv_high, pinv_low], axis=0)
     rows = flat.shape[0] // PARTS
+    x_cells, y_cells, _ = kept.shape
+    x_part = x_cells // PARTS
     for part in range(PARTS):
-        total = terms[part][...]
-        for term in terms[part + PARTS :: PARTS]:
+        total = kept[part * x_part : (part + 1) * x_part]
+        for term in terms[part::PARTS]:
             total = total + term[...]
         high, low = two_terms(total.reshape(rows, -1))
         both = lax.dot_general(high, pinv_both, ROW_ROW, preferred_element_type=jnp.float32)
         rest = lax.dot_general(low, pinv_high, ROW_ROW, preferred_element_type=jnp.float32)
         flat[part * rows : (part + 1) * rows] = both[:, :rank] + (both[:, rank:] + rest)
-    x_cells, y_cells, _ = terms[0].shape
-    x_cells *= PARTS
     for b in range(projected.shape[0]):
         for j in range(y_own):
             projected[b, j * x_cells : (j + 1) * x_cells] = flat[
@@ -266,10 +278,9 @@
         projected[b, y_own * x_cells :] = extra[...]
 
 
-def project(blocks, pinv, extra, terms):
+def project(blocks, pinv, extra, kept, terms):
     rank = pinv.shape[0]
-    x_cells, y_cells, _ = terms[0].shape
-    x_cells *= PARTS
+    x_cells, y_cells, _ = kept.shape
     y_own = y_cells // blocks
     rows = y_own * x_cells + extra.shape[0]
     return pl.pallas_call(
@@ -278,7 +289,7 @@
         scratch_shapes=[pltpu.VMEM((x_cells * y_cells, rank), jnp.float32)],
         compiler_params=pltpu.CompilerParams(vmem_limit_bytes=VMEM_BYTES),
         name="project",
-    )(pinv, extra, *terms)
+    )(pinv, extra, kept, *terms)
 
 
 def sketch_kernel(order, left_at, y_own, pieces, packed, out, extra):
@@ -407,15 +418,17 @@
         shares, flow_field, last_x, last_y, right_y, right_m, last_m
     )
 
-    for s in range(1, shares):
-        for part in range(PARTS):
-            terms[s * PARTS + part] = swap(terms[s * PARTS + part], "gz", s)
+    terms = [swap(term, "gz", 1 + at // PARTS) for at, term in enumerate(terms)]
+    here = lax.axis_index("gz")
+    kept = flow_field.reshape(x_cells, shares, y_share, m_cells)
+    kept = lax.dynamic_index_in_dim(kept, here, 1, False).reshape(-1, m_cells)
+    kept = jnp.dot(kept, last_m, preferred_element_type=jnp.float32)
+    kept = kept.reshape(x_cells, y_share, cols)
 
     order = swap_order("gx")
-    first_rows = swap_sum(first_part, "gy")
     packed = jnp.concatenate(
         [
-            first_rows.reshape(x_cells, -1, LANES).transpose(1, 0, 2).reshape(-1, LANES),
+            first_part.reshape(x_cells, -1, LANES).transpose(1, 0, 2).reshape(-1, LANES),
             left_x.astype(jnp.float32),
         ],
         axis=0,
@@ -427,11 +440,11 @@
     group = ("gx", "gy")
     own = rank // lax.axis_size(group)
     last_rows = lax.all_to_all(last_part.reshape(-1, own, m_cells), group, 0, 0, tiled=True)
-    last_rows = jnp.sum(after(last_rows, *terms[PARTS::PARTS]), axis=0)
+    last_rows = jnp.sum(after(last_rows, *terms[::PARTS]), axis=0)
     both = jnp.dot(
         jnp.concatenate(split_terms(last_rows), axis=0), last_m, preferred_element_type=jnp.float32
     )
-    both = after(both[:own] + both[own:], packed)
+    both = after(both[:own] + both[own:], packed, kept)
     count = lax.axis_size(ALL)
     copies = jnp.broadcast_to(both[None], (count, own, cols))
     system = lax.all_to_all(copies, ALL, 0, 0, tiled=True).reshape(-1, shares, own, cols)
@@ -440,14 +453,15 @@
 
     for bit in bits:
         packed = swap_step(packed, "gx", bit)
-    sums = first_sums(left_at, first_rows, packed)
+    sums = first_sums(left_at, first_part, packed)
     if own % ROWS:
         extra = jnp.zeros((ROWS, LANES), jnp.float32)
     else:
         extra = last_rows.reshape(own, -1, LANES).transpose(1, 0, 2).reshape(-1, LANES)
-    pinv = pseudo_inverse(after(system, packed, *terms[PARTS:]))
-    projected = project(blocks, pinv, extra, terms)
-    sums = [swap(sums, "gz", z) if z else sums for z in range(shares)]
+    pinv = pseudo_inverse(after(system, packed, *terms))
+    projected = project(blocks, pinv, extra, kept, terms)
+    sums = swap_sum(sums, "gz")
+    sums = [swap(sums, "gy", y) if y else sums for y in range(lax.axis_size("gy"))]
 
     pieces = lax.all_to_all(projected, "gx", 0, 0, tiled=True)
     core_first = solve_first(x_cells, after(sums[0], projected), *sums[1:])

time: 85 us -> 84.7 us (level)
  waiting for transfers between devices: 36.5 us -> 34.7 us
  matrix products: 0.15 us -> 1.8 us
    all_to_all x1, waiting for transfers between devices: 6.18 us -> 4.41 us  [per_device(): pieces = lax.all_to_all(projected, 'gx', 0, 0, tiled=True)]
    dot_general x0 -> x1, matrix products: none -> 1.65 us  [per_device(): kept = jnp.dot(kept, last_m, preferred_element_type=jnp.float32)]
  transfers between devices with their start and end apart: 12 -> 12, of which waited for: 8 -> 9; matrix products, arithmetic and copies ran while one was open for 2% -> 4% of each run, Pallas kernels for 7% -> 7%
where the time goes in v9:
time: 84.7 us; the launch traced here: 84.2 us
  waiting for transfers between devices  34.7 us (41%)
  starting transfers between devices  27.3 us (32%)
  Pallas kernels  17.2 us (20%)
  local copies, waits for them, and re-layouts  2.28 us (3%)
  matrix products  1.8 us (2%)
    ppermute x8, waiting for transfers between devices, swap(): lax.ppermute(array, axis, [(s, s ^ bits) for s in range(lax.axis_size(axi...  21.5 us
    ppermute x8, starting transfers between devices, swap(): lax.ppermute(array, axis, [(s, s ^ bits) for s in range(lax.axis_size(axi...  9.74 us
    all_to_all x1, waiting for transfers between devices, per_device(): received = lax.all_to_all(middle, group, 0, 0, tiled=True)  7.91 us
    all_to_all x1, starting transfers between devices, per_device(): lax.all_to_all(last_part.reshape(-1, own, m_cells), group, 0, 0, tiled=True)  5.91 us
    pallas_call x1, Pallas kernels, solve_first(): pl.pallas_call(first_kernel, out_shape=jax.ShapeDtypeStruct((x_cells, sum...  4.98 us
    all_to_all x1, starting transfers between devices, per_device(): received = lax.all_to_all(middle, group, 0, 0, tiled=True)  4.62 us
    all_to_all x1, waiting for transfers between devices, per_device(): pieces = lax.all_to_all(projected, 'gx', 0, 0, tiled=True)  4.41 us
    pallas_call x1, Pallas kernels, pseudo_inverse(): pl.pallas_call(inverse_kernel, out_shape=jax.ShapeDtypeStruct((rank, syst...  4.34 us
  transfers between devices with their start and end apart: 12, of which 9 were waited for; matrix products, arithmetic and copies ran while one was open for 4% of the time, Pallas kernels for 7%

profile of v9, /device:TPU:0, one launch (start us, length us, event | category | flops | bytes accessed | tf_op | source)
XLA Modules:
  0.0 84.2 jit_solution(3549500791909904944)
XLA Ops:
  0.6 0.0 copy-start.1
  0.6 0.0 copy-start.2
  0.7 4.2 %local_products.1 = (f32[128,512]{1,0:T(8,128)}, f32[32,256]{1,0:T(8,128)}, f32[16,32,256]{2,1,0:T(8,128)}, f32[16,32,256]{2,1,0:T(8,128)}) custom-call(bf16[32,64,512]{2,1,0:T(8,128)(2,1)} %field_hbm.1, bf16[32,128]{1,0:T(8,128)(2,1)} %last_x_hbm.1, bf16[64,128]{1,0:T(8,128)(2,1)} %last_y_hbm.1, bf16[64,256]{1,0:T(8,128)(2,1)} %right_y_hbm.1, ...), custom_call_target="tpu_custom_call" | custom-call | tf_op jit(solution)/shard_map/local_products/pallas_call | solution.py:205
  4.8 3.0 %collective-permute-start = (f32[16,32,256]{2,1,0:T(8,128)}, f32[16,32,256]{2,1,0:T(8,128)S(1)}, u32[]{:S(2)}, u32[]{:S(2)}) collective-permute-start(f32[16,32,256]{2,1,0:T(8,128)} %get-tuple-element.16), channel_id=1, source_target_pairs={{0,1},{1,0},{2,3},{3,2},{4,5},{5,4},{6,7},{7,6},{8,9},{9,8},{10,11... | collective-permute-start | bytes 1572872 | tf_op jit(solution)/shard_map/ppermute | solution.py:29
  7.9 5.9 %all-to-all-start = ((f32[16,8,512]{2,1,0:T(8,128)}), f32[16,8,512]{2,1,0:T(8,128)S(1)}, u32[]{:S(2)}, u32[]{:S(2)}) async-start(f32[16,8,512]{2,1,0:T(8,128)} %bitcast.35), calls=%async_computation | async-start | bytes 524288 | tf_op jit(solution)/shard_map/all_to_all | solution.py:442
  13.8 0.8 copy_bitcast_fusion
  14.5 0.0 copy-done.2
  14.6 2.9 %collective-permute-start.1 = (f32[1,96,128]{2,1,0:T(8,128)S(1)}, f32[1,96,128]{2,1,0:T(8,128)S(1)}, u32[]{:S(2)}, u32[]{:S(2)}) collective-permute-start(f32[1,96,128]{2,1,0:T(8,128)S(1)} %maximum_bitcast_fusion), channel_id=1, source_target_pairs={{0,16},{4,20},{8,24},{12,28},{16,0},{20,4},{24,8},{28,12},{1,17},{... | collective-permute-start | bytes 147464 | tf_op jit(solution)/shard_map/ppermute | solution.py:29
  17.4 0.5 collective-permute-start.4
  18.0 0.0 copy-done.1
  18.0 1.7 %fusion.kept = f32[32,32,256]{2,1,0:T(8,128)S(1)} fusion(bf16[32,2,32,512]{3,2,1,0:T(8,128)(2,1)} %bitcast.33, s32[]{:T(128)S(6)} %select_n.4, bf16[512,256]{1,0:T(8,128)(2,1)S(1)} %copy-done.1), kind=kOutput, calls=%fused_computation | convolution fusion | flops 268435456 | bytes 2359300 | tf_op jit(solution)/shard_map/dot_general | solution.py:425
  19.6 5.9 %collective-permute-done.1 = f32[1,96,128]{2,1,0:T(8,128)S(1)} collective-permute-done((f32[1,96,128]{2,1,0:T(8,128)S(1)}, f32[1,96,128]{2,1,0:T(8,128)S(1)}, u32[]{:S(2)}, u32[]{:S(2)}) %collective-permute-start.1) | collective-permute-done | bytes 49184 | tf_op jit(solution)/shard_map/ppermute | solution.py:29
  25.5 0.1 collective-permute-start.2
  25.6 0.0 all-to-all-done
  25.6 0.0 collective-permute-done.refs_0_
  25.7 0.1 fusion.5
  25.8 0.7 broadcast_in_dim.10
  26.6 3.3 %all-to-all-start.1 = ((f32[32,8,256]{2,1,0:T(8,128)}), f32[32,8,256]{2,1,0:T(8,128)S(1)}, u32[]{:S(2)}, u32[]{:S(2)}) async-start(f32[32,8,256]{2,1,0:T(8,128)} %broadcast_in_dim.10), calls=%async_computation.1 | async-start | bytes 524288 | tf_op jit(solution)/shard_map/all_to_all | solution.py:450
  29.8 0.4 collective-permute-done.2
  30.2 1.5 %collective-permute-start.3 = (f32[4,96,128]{2,1,0:T(8,128)S(1)}, f32[4,96,128]{2,1,0:T(8,128)S(1)}, u32[]{:S(2)}, u32[]{:S(2)}) collective-permute-start(f32[4,96,128]{2,1,0:T(8,128)S(1)} %pad_maximum_fusion.1), channel_id=1, source_target_pairs={{0,4},{4,0},{8,12},{12,8},{16,20},{20,16},{24,28},{28,24},{1,5},{5... | collective-permute-start | bytes 589832 | tf_op jit(solution)/shard_map/ppermute | solution.py:29
  31.8 7.9 %collective-permute-done.3 = f32[4,96,128]{2,1,0:T(8,128)S(1)} collective-permute-done((f32[4,96,128]{2,1,0:T(8,128)S(1)}, f32[4,96,128]{2,1,0:T(8,128)S(1)}, u32[]{:S(2)}, u32[]{:S(2)}) %collective-permute-start.3) | collective-permute-done | bytes 196640 | tf_op jit(solution)/shard_map/ppermute | solution.py:29
  39.7 0.0 collective-permute-done.4.refs_1_
  39.7 0.9 %all-to-all-done.1 = f32[32,8,256]{2,1,0:T(8,128)S(1)} async-done(((f32[32,8,256]{2,1,0:T(8,128)}), f32[32,8,256]{2,1,0:T(8,128)S(1)}, u32[]{:S(2)}, u32[]{:S(2)}) %all-to-all-start.1) | async-done | bytes 262176 | tf_op jit(solution)/shard_map/all_to_all | solution.py:450
  40.5 4.3 %pseudo_inverse.1.pinv = f32[128,256]{1,0:T(8,128)S(1)} custom-call(f32[16,2,8,256]{3,2,1,0:T(8,128)S(1)} %bitcast.31), custom_call_target="tpu_custom_call" | custom-call | tf_op jit(solution)/shard_map/pseudo_inverse/pallas_call | solution.py:249
  44.9 0.0 copy-start
  44.9 1.6 %project.1 = f32[8,160,128]{2,1,0:T(8,128)} custom-call(f32[128,256]{1,0:T(8,128)S(1)} %pseudo_inverse.1.pinv, f32[32,128]{1,0:T(8,128)S(1)} %bitcast.32, f32[32,32,256]{2,1,0:T(8,128)S(1)} %fusion.kept, f32[16,32,256]{2,1,0:T(8,128)S(1)} %collective-permute-done.refs_0_, f32[16,32,256]{2,1,0:T(8,128)S(1)} %collective-permute-done.4.refs_1_), custom_call_target="tpu_custom_call" | custom-call | tf_op jit(solution)/shard_map/project/pallas_call | solution.py:286
  46.5 3.8 %all-to-all-start.2 = ((f32[8,160,128]{2,1,0:T(8,128)}), f32[8,160,128]{2,1,0:T(8,128)S(1)}, u32[]{:S(2)}, u32[]{:S(2)}) async-start(f32[8,160,128]{2,1,0:T(8,128)} %project.1), calls=%async_computation.2 | async-start | bytes 1310720 | tf_op jit(solution)/shard_map/all_to_all | solution.py:466
  50.3 0.0 copy-done
  50.3 0.4 first_sums.1
  50.7 1.6 %collective-permute-start.5 = (f32[160,256]{1,0:T(8,128)S(1)}, f32[160,256]{1,0:T(8,128)S(1)}, u32[]{:S(2)}, u32[]{:S(2)}) collective-permute-start(f32[160,256]{1,0:T(8,128)S(1)} %first_sums.1), channel_id=1, source_target_pairs={{0,1},{1,0},{2,3},{3,2},{4,5},{5,4},{6,7},{7,6},{8,9},{9,8},{10,11... | collective-permute-start | bytes 491528 | tf_op jit(solution)/shard_map/ppermute | solution.py:29
  52.3 4.6 %collective-permute-done.5 = f32[160,256]{1,0:T(8,128)S(1)} collective-permute-done((f32[160,256]{1,0:T(8,128)S(1)}, f32[160,256]{1,0:T(8,128)S(1)}, u32[]{:S(2)}, u32[]{:S(2)}) %collective-permute-start.5) | collective-permute-done | bytes 163872 | tf_op jit(solution)/shard_map/ppermute | solution.py:29
  56.9 0.1 collective-permute-start.6
  57.0 1.4 %collective-permute-done.6.refs_1_ = f32[160,256]{1,0:T(8,128)S(1)} collective-permute-done((f32[160,256]{1,0:T(8,128)S(1)}, f32[160,256]{1,0:T(8,128)S(1)}, u32[]{:S(2)}, u32[]{:S(2)}) %collective-permute-start.6) | collective-permute-done | bytes 163872 | tf_op jit(solution)/shard_map/ppermute | solution.py:29
  58.4 5.0 %solve_first.1 = f32[32,128]{1,0:T(8,128)} custom-call(f32[160,256]{1,0:T(8,128)S(1)} %add.12.refs_0_, f32[160,256]{1,0:T(8,128)S(1)} %collective-permute-done.6.refs_1_), custom_call_target="tpu_custom_call" | custom-call | tf_op jit(solution)/shard_map/solve_first/pallas_call | solution.py:377
  63.4 4.4 %all-to-all-done.2.pieces = f32[8,160,128]{2,1,0:T(8,128)S(1)} async-done(((f32[8,160,128]{2,1,0:T(8,128)}), f32[8,160,128]{2,1,0:T(8,128)S(1)}, u32[]{:S(2)}, u32[]{:S(2)}) %all-to-all-start.2) | async-done | bytes 655392 | tf_op jit(solution)/shard_map/all_to_all | solution.py:466
  67.8 1.0 %sketch.1 = (f32[16,4,8,128]{3,2,1,0:T(8,128)}, f32[8,32,128]{2,1,0:T(8,128)S(1)}) custom-call(f32[8,160,128]{2,1,0:T(8,128)S(1)} %all-to-all-done.2.pieces, f32[8,96,128]{2,1,0:T(8,128)S(1)} %pad_maximum_fusion.packed), custom_call_target="tpu_custom_call" | custom-call | tf_op jit(solution)/shard_map/sketch/pallas_call | solution.py:322
  68.7 4.6 %all-to-all-start.3 = ((f32[16,4,8,128]{3,2,1,0:T(8,128)}), f32[16,4,8,128]{3,2,1,0:T(8,128)S(1)}, u32[]{:S(2)}, u32[]{:S(2)}) async-start(f32[16,4,8,128]{3,2,1,0:T(8,128)} %get-tuple-element.25), calls=%async_computation.3 | async-start | bytes 524288 | tf_op jit(solution)/shard_map/all_to_all | solution.py:477
  73.4 0.1 collective-permute-start.7
  73.4 1.3 %collective-permute-done.7.refs_1_ = f32[8,32,128]{2,1,0:T(8,128)S(1)} collective-permute-done((f32[8,32,128]{2,1,0:T(8,128)S(1)}, f32[8,32,128]{2,1,0:T(8,128)S(1)}, u32[]{:S(2)}, u32[]{:S(2)}) %collective-permute-start.7) | collective-permute-done | bytes 131104 | tf_op jit(solution)/shard_map/ppermute | solution.py:29
  74.8 0.7 place.1
  75.5 7.9 %all-to-all-done.3 = f32[16,4,8,128]{3,2,1,0:T(8,128)S(1)} async-done(((f32[16,4,8,128]{3,2,1,0:T(8,128)}), f32[16,4,8,128]{3,2,1,0:T(8,128)S(1)}, u32[]{:S(2)}, u32[]{:S(2)}) %all-to-all-start.3) | async-done | bytes 262176 | tf_op jit(solution)/shard_map/all_to_all | solution.py:477
  83.4 0.8 copy.12
  (9 shorter events, 0.1 us)
Async XLA Ops:
  0.6 17.3 %copy-start.1 = (bf16[512,256]{1,0:T(8,128)(2,1)S(1)}, bf16[512,256]{1,0:T(8,128)(2,1)}, u32[]{:S(2)}) copy-start(bf16[512,256]{1,0:T(8,128)(2,1)} %last_m_hbm.1) | copy-start | bytes 786436
  0.6 13.9 %copy-start.2 = (bf16[32,128]{1,0:T(8,128)(2,1)S(1)}, bf16[32,128]{1,0:T(8,128)(2,1)}, u32[]{:S(2)}) copy-start(bf16[32,128]{1,0:T(8,128)(2,1)} %param.8) | copy-start | bytes 24580
  4.8 20.8 %collective-permute-start = (f32[16,32,256]{2,1,0:T(8,128)}, f32[16,32,256]{2,1,0:T(8,128)S(1)}, u32[]{:S(2)}, u32[]{:S(2)}) collective-permute-start(f32[16,32,256]{2,1,0:T(8,128)} %get-tuple-element.16), channel_id=1, source_target_pairs={{0,1},{1,0},{2,3},{3,2},{4,5},{5,4},{6,7},{7,6},{8,9},{9,8},{10,11... | collective-permute-start | bytes 1572872 | tf_op jit(solution)/shard_map/ppermute | solution.py:29
  7.9 17.8 %all-to-all-start = ((f32[16,8,512]{2,1,0:T(8,128)}), f32[16,8,512]{2,1,0:T(8,128)S(1)}, u32[]{:S(2)}, u32[]{:S(2)}) async-start(f32[16,8,512]{2,1,0:T(8,128)} %bitcast.35), calls=%async_computation | async-start | bytes 524288 | tf_op jit(solution)/shard_map/all_to_all | solution.py:442
  14.6 11.0 %collective-permute-start.1 = (f32[1,96,128]{2,1,0:T(8,128)S(1)}, f32[1,96,128]{2,1,0:T(8,128)S(1)}, u32[]{:S(2)}, u32[]{:S(2)}) collective-permute-start(f32[1,96,128]{2,1,0:T(8,128)S(1)} %maximum_bitcast_fusion), channel_id=1, source_target_pairs={{0,16},{4,20},{8,24},{12,28},{16,0},{20,4},{24,8},{28,12},{1,17},{... | collective-permute-start | bytes 147464 | tf_op jit(solution)/shard_map/ppermute | solution.py:29
  17.4 22.2 %collective-permute-start.4 = (f32[16,32,256]{2,1,0:T(8,128)}, f32[16,32,256]{2,1,0:T(8,128)S(1)}, u32[]{:S(2)}, u32[]{:S(2)}) collective-permute-start(f32[16,32,256]{2,1,0:T(8,128)} %get-tuple-element.20), channel_id=1, source_target_pairs={{0,1},{1,0},{2,3},{3,2},{4,5},{5,4},{6,7},{7,6},{8,9},{9,8},{10,11... | collective-permute-start | bytes 1572872 | tf_op jit(solution)/shard_map/ppermute | solution.py:29
  25.5 4.7 %collective-permute-start.2 = (f32[2,96,128]{2,1,0:T(8,128)S(1)}, f32[2,96,128]{2,1,0:T(8,128)S(1)}, u32[]{:S(2)}, u32[]{:S(2)}) collective-permute-start(f32[2,96,128]{2,1,0:T(8,128)S(1)} %pad_maximum_fusion.2), channel_id=1, source_target_pairs={{0,8},{4,12},{8,0},{12,4},{16,24},{20,28},{24,16},{28,20},{1,9},{5... | collective-permute-start | bytes 294920 | tf_op jit(solution)/shard_map/ppermute | solution.py:29
  26.6 14.0 %all-to-all-start.1 = ((f32[32,8,256]{2,1,0:T(8,128)}), f32[32,8,256]{2,1,0:T(8,128)S(1)}, u32[]{:S(2)}, u32[]{:S(2)}) async-start(f32[32,8,256]{2,1,0:T(8,128)} %broadcast_in_dim.10), calls=%async_computation.1 | async-start | bytes 524288 | tf_op jit(solution)/shard_map/all_to_all | solution.py:450
  30.2 9.4 %collective-permute-start.3 = (f32[4,96,128]{2,1,0:T(8,128)S(1)}, f32[4,96,128]{2,1,0:T(8,128)S(1)}, u32[]{:S(2)}, u32[]{:S(2)}) collective-permute-start(f32[4,96,128]{2,1,0:T(8,128)S(1)} %pad_maximum_fusion.1), channel_id=1, source_target_pairs={{0,4},{4,0},{8,12},{12,8},{16,20},{20,16},{24,28},{28,24},{1,5},{5... | collective-permute-start | bytes 589832 | tf_op jit(solution)/shard_map/ppermute | solution.py:29
  44.9 5.4 %copy-start = (f32[32,256]{1,0:T(8,128)S(1)}, f32[32,256]{1,0:T(8,128)}, u32[]{:S(2)}) copy-start(f32[32,256]{1,0:T(8,128)} %get-tuple-element.18.rows) | copy-start | bytes 98308
  46.5 21.3 %all-to-all-start.2 = ((f32[8,160,128]{2,1,0:T(8,128)}), f32[8,160,128]{2,1,0:T(8,128)S(1)}, u32[]{:S(2)}, u32[]{:S(2)}) async-start(f32[8,160,128]{2,1,0:T(8,128)} %project.1), calls=%async_computation.2 | async-start | bytes 1310720 | tf_op jit(solution)/shard_map/all_to_all | solution.py:466
  50.7 6.2 %collective-permute-start.5 = (f32[160,256]{1,0:T(8,128)S(1)}, f32[160,256]{1,0:T(8,128)S(1)}, u32[]{:S(2)}, u32[]{:S(2)}) collective-permute-start(f32[160,256]{1,0:T(8,128)S(1)} %first_sums.1), channel_id=1, source_target_pairs={{0,1},{1,0},{2,3},{3,2},{4,5},{5,4},{6,7},{7,6},{8,9},{9,8},{10,11... | collective-permute-start | bytes 491528 | tf_op jit(solution)/shard_map/ppermute | solution.py:29
  56.9 1.5 %collective-permute-start.6 = (f32[160,256]{1,0:T(8,128)S(1)}, f32[160,256]{1,0:T(8,128)S(1)}, u32[]{:S(2)}, u32[]{:S(2)}) collective-permute-start(f32[160,256]{1,0:T(8,128)S(1)} %add.12.refs_0_), channel_id=1, source_target_pairs={{0,2},{2,0},{1,3},{3,1},{4,6},{6,4},{5,7},{7,5},{8,10},{10,8},{9,1... | collective-permute-start | bytes 491528 | tf_op jit(solution)/shard_map/ppermute | solution.py:29
  68.7 14.7 %all-to-all-start.3 = ((f32[16,4,8,128]{3,2,1,0:T(8,128)}), f32[16,4,8,128]{3,2,1,0:T(8,128)S(1)}, u32[]{:S(2)}, u32[]{:S(2)}) async-start(f32[16,4,8,128]{3,2,1,0:T(8,128)} %get-tuple-element.25), calls=%async_computation.3 | async-start | bytes 524288 | tf_op jit(solution)/shard_map/all_to_all | solution.py:477
  73.4 1.4 %collective-permute-start.7 = (f32[8,32,128]{2,1,0:T(8,128)S(1)}, f32[8,32,128]{2,1,0:T(8,128)S(1)}, u32[]{:S(2)}, u32[]{:S(2)}) collective-permute-start(f32[8,32,128]{2,1,0:T(8,128)S(1)} %get-tuple-element.26.refs_0_), channel_id=1, source_target_pairs={{0,2},{2,0},{1,3},{3,1},{4,6},{6,4},{5,7},{7,5},{8,10},{10,8},{9,1... | collective-permute-start | bytes 393224 | tf_op jit(solution)/shard_map/ppermute | solution.py:29

commit v10 on v9

--- a/solution.py
+++ b/solution.py
@@ -254,7 +254,7 @@
     )(system_shares)
 
 
-def project_kernel(y_own, pinv, extra, kept, *refs):
+def project_kernel(y_own, pinv, kept, *refs):
     *terms, projected, flat = refs
     rank = pinv.shape[0]
     pinv_high, pinv_low = two_terms(pinv[...])
@@ -275,82 +275,86 @@
             projected[b, j * x_cells : (j + 1) * x_cells] = flat[
                 pl.ds(b * y_own + j, x_cells, stride=y_cells), :
             ]
-        projected[b, y_own * x_cells :] = extra[...]
-
-
-def project(blocks, pinv, extra, kept, terms):
+
+
+def project(blocks, pinv, kept, terms):
     rank = pinv.shape[0]
     x_cells, y_cells, _ = kept.shape
     y_own = y_cells // blocks
-    rows = y_own * x_cells + extra.shape[0]
+    rows = y_own * x_cells
     return pl.pallas_call(
         functools.partial(project_kernel, y_own),
         out_shape=jax.ShapeDtypeStruct((blocks, rows, rank), jnp.float32),
         scratch_shapes=[pltpu.VMEM((x_cells * y_cells, rank), jnp.float32)],
         compiler_params=pltpu.CompilerParams(vmem_limit_bytes=VMEM_BYTES),
         name="project",
-    )(pinv, extra, kept, *terms)
-
-
-def sketch_kernel(order, left_at, y_own, pieces, packed, out, extra):
+    )(pinv, kept, *terms)
+
+
+def packed_units(packed, unit):
+    return [(k, n * unit) for k in range(packed.shape[0]) for n in range(2)]
+
+
+def sketch_kernel(order, left_at, unit, pieces, packed, out):
     me = lax.axis_index("gx")
-    blocks, _, cols = pieces.shape
-    x_cells = packed.shape[1] - left_at
-    weights = jnp.concatenate([packed[k, left_at:] for k in range(blocks)], axis=0)
+    _, rows, cols = pieces.shape
+    x_cells = unit - left_at
+    weights = jnp.concatenate(
+        [packed[k, at + left_at : at + unit] for k, at in packed_units(packed, unit)], axis=0
+    )
     weights = weights.astype(jnp.bfloat16)
-    for j in range(y_own):
+    for j in range(rows // x_cells):
         column = jnp.concatenate(
             [pieces[me ^ o, j * x_cells : (j + 1) * x_cells] for o in order], axis=0
         )
-        high = column.astype(jnp.bfloat16)
-        low = (column - high.astype(jnp.float32)).astype(jnp.bfloat16)
         both = lax.dot_general(
             weights,
-            jnp.concatenate([high, low], axis=1),
+            jnp.concatenate(two_terms(column), axis=1),
             COL_COL,
             preferred_element_type=jnp.float32,
         )
         both = both[:, :cols] + both[:, cols:]
         out[:, j] = both.reshape(out.shape[0], out.shape[2], cols)
-    extra[...] = pieces[:, y_own * x_cells :]
-
-
-def sketch(order, left_at, y_own, own, pieces, packed):
-    blocks, rows, cols = pieces.shape
+
+
+def sketch(order, left_at, unit, own, pieces, packed):
+    _, rows, cols = pieces.shape
     rank = packed.shape[2]
-    extra = rows - y_own * (packed.shape[1] - left_at)
-    return pl.pallas_call(
-        functools.partial(sketch_kernel, order, left_at, y_own),
-        out_shape=(
-            jax.ShapeDtypeStruct((rank // own, y_own, own, cols), jnp.float32),
-            jax.ShapeDtypeStruct((blocks, extra, cols), jnp.float32),
-        ),
+    y_own = rows // (unit - left_at)
+    return pl.pallas_call(
+        functools.partial(sketch_kernel, order, left_at, unit),
+        out_shape=jax.ShapeDtypeStruct((rank // own, y_own, own, cols), jnp.float32),
         compiler_params=pltpu.CompilerParams(vmem_limit_bytes=VMEM_BYTES),
         name="sketch",
     )(pieces, packed)
 
 
-def first_sums_kernel(left_at, rows, packed, sums):
+def first_sums_kernel(left_at, unit, rows, packed, sums, extra):
     x_cells, cols = rows.shape
-    blocks = range(packed.shape[0])
-    left = jnp.concatenate([packed[k, left_at : left_at + x_cells] for k in blocks], axis=0)
+    units = packed_units(packed, unit)
+    left = jnp.concatenate([packed[k, at + left_at : at + unit] for k, at in units], axis=0)
     sums[:x_cells] = rows[...]
     for c in range(cols // LANES):
-        at = c * x_cells
+        first = c * x_cells
         sums[x_cells:, c * LANES : (c + 1) * LANES] = lax.dot_general(
             left,
-            jnp.concatenate([packed[k, at : at + x_cells] for k in blocks], axis=0),
+            jnp.concatenate(
+                [packed[k, at + first : at + first + x_cells] for k, at in units], axis=0
+            ),
             COL_COL,
             precision=HIGHEST,
             preferred_element_type=jnp.float32,
         )
-
-
-def first_sums(left_at, rows, packed):
-    return pl.pallas_call(
-        functools.partial(first_sums_kernel, left_at),
-        out_shape=jax.ShapeDtypeStruct(
-            (rows.shape[0] + packed.shape[2], rows.shape[1]), jnp.float32
+    extra[...] = packed[:, 2 * unit :]
+
+
+def first_sums(left_at, unit, rows, packed):
+    entries, height, rank = packed.shape
+    return pl.pallas_call(
+        functools.partial(first_sums_kernel, left_at, unit),
+        out_shape=(
+            jax.ShapeDtypeStruct((rows.shape[0] + rank, rows.shape[1]), jnp.float32),
+            jax.ShapeDtypeStruct((entries, height - 2 * unit, rank), jnp.float32),
         ),
         compiler_params=pltpu.CompilerParams(vmem_limit_bytes=VMEM_BYTES),
         name="first_sums",
@@ -382,22 +386,23 @@
     )(*sums)
 
 
-def place_kernel(own, inner_order, *refs):
+def place_kernel(own, outer_order, *refs):
     *parts, core_last = refs
-    inner = lax.axis_index("gy")
-    for part, i in zip(parts, inner_order):
-        for o in range(part.shape[0]):
-            at = pl.multiple_of((o * len(parts) + (inner ^ i)) * own, own)
+    outer, inner = lax.axis_index("gx"), lax.axis_index("gy")
+    for i, part in enumerate(parts):
+        for k, o in enumerate(outer_order):
+            at = ((outer ^ o) * len(parts) + (inner ^ i)) * own
+            at = pl.multiple_of(at, own)
             for c in range(part.shape[1] // own):
                 core_last[pl.ds(at, own), c * LANES : (c + 1) * LANES] = part[
-                    o, c * own : (c + 1) * own
+                    k, c * own : (c + 1) * own
                 ]
 
 
-def place(own, inner_order, parts):
+def place(own, outer_order, parts):
     outer, rows, lanes = parts[0].shape
     return pl.pallas_call(
-        functools.partial(place_kernel, own, inner_order),
+        functools.partial(place_kernel, own, outer_order),
         out_shape=jax.ShapeDtypeStruct(
             (len(parts) * outer * own, rows // own * lanes), jnp.float32
         ),
@@ -425,17 +430,16 @@
     kept = jnp.dot(kept, last_m, preferred_element_type=jnp.float32)
     kept = kept.reshape(x_cells, y_share, cols)
 
-    order = swap_order("gx")
     packed = jnp.concatenate(
         [
             first_part.reshape(x_cells, -1, LANES).transpose(1, 0, 2).reshape(-1, LANES),
             left_x.astype(jnp.float32),
         ],
         axis=0,
-    )[None]
-    left_at = x_cells * cols // LANES
-    first_bit, *bits = axis_bits("gx")
-    packed = swap_step(packed, "gx", first_bit)
+    )
+    unit = packed.shape[0]
+    left_at = unit - x_cells
+    packed = jnp.concatenate([packed, swap(packed, "gx", 1)], axis=0)
 
     group = ("gx", "gy")
     own = rank // lax.axis_size(group)
@@ -451,29 +455,37 @@
     if own % ROWS:
         system = jnp.sum(system, axis=1).reshape(-1, 1, ROWS, cols)
 
-    for bit in bits:
-        packed = swap_step(packed, "gx", bit)
-    sums = first_sums(left_at, first_part, packed)
     if own % ROWS:
         extra = jnp.zeros((ROWS, LANES), jnp.float32)
     else:
         extra = last_rows.reshape(own, -1, LANES).transpose(1, 0, 2).reshape(-1, LANES)
-    pinv = pseudo_inverse(after(system, packed, *terms))
-    projected = project(blocks, pinv, extra, kept, terms)
+    packed = jnp.concatenate([packed, extra], axis=0)[None]
+    *bits, _ = axis_bits("gx")
+    others = [0]
+    for bit in bits:
+        if bit == bits[-1]:
+            system = after(system, packed)
+        packed = swap_step(packed, "gx", bit)
+        others += [o ^ bit for o in others]
+    order = [o ^ n for o in others for n in range(2)]
+
+    pinv = pseudo_inverse(after(system, *terms))
+    projected = after(project(blocks, pinv, kept, terms), packed)
+    sums, extra = first_sums(left_at, unit, first_part, packed)
     sums = swap_sum(sums, "gz")
     sums = [swap(sums, "gy", y) if y else sums for y in range(lax.axis_size("gy"))]
 
     pieces = lax.all_to_all(projected, "gx", 0, 0, tiled=True)
-    core_first = solve_first(x_cells, after(sums[0], projected), *sums[1:])
     group = ("gx", "gz")
     devices = lax.axis_size(group)
     rank_own = rank // devices
     if rank_own % ROWS:
-        middle, extra = sketch(order, left_at, y_own, rank, pieces, packed)
+        middle = sketch(order, left_at, unit, rank, pieces, packed)
         middle = middle.reshape(y_own, devices, rank_own, rank).transpose(1, 0, 2, 3)
     else:
-        middle, extra = sketch(order, left_at, y_own, rank_own, pieces, packed)
-    middle, core_first = lax.optimization_barrier((middle, core_first))
+        middle = sketch(order, left_at, unit, rank_own, pieces, packed)
+    extra = jnp.concatenate([extra, swap(extra, "gx", 1)], axis=0)
+    middle = after(middle, extra, *sums)
     received = lax.all_to_all(middle, group, 0, 0, tiled=True)
     received = received.reshape(blocks, shares, y_own, rank_own, rank)
     core_middle = received.transpose(3, 1, 0, 2, 4).reshape(rank_own, y_cells, rank)
@@ -481,8 +493,10 @@
     if own % ROWS:
         core_last = gather_rows(last_rows, "gx", "gy")
     else:
+        outer = [o ^ n for n in range(2) for o in others]
         inner = range(lax.axis_size("gy"))
-        core_last = place(own, inner, [swap(extra, "gy", i) if i else extra for i in inner])
+        core_last = place(own, outer, [swap(extra, "gy", i) if i else extra for i in inner])
+    core_first = solve_first(x_cells, after(sums[0], middle), *sums[1:])
     return (core_first, core_middle, core_last)
 
 

time: 84.7 us -> 88.7 us (1.047)
  starting transfers between devices: 27.3 us -> 32.7 us
  waiting for transfers between devices: 34.7 us -> 33.3 us
    all_to_all x1, waiting for transfers between devices: 7.91 us -> 2.92 us  [per_device(): received = lax.all_to_all(middle, group, 0, 0, tiled=True)]
    all_to_all x1, waiting for transfers between devices: 0.01 us -> 3.65 us  [per_device(): lax.all_to_all(last_part.reshape(-1, own, m_cells), group, 0, 0, tiled=True)]
    ppermute x8 -> x9, starting transfers between devices: 9.74 us -> 12.3 us  [swap(): lax.ppermute(array, axis, [(s, s ^ bits) for s in range(lax.axis_size(axi...]
    all_to_all x1, starting transfers between devices: 5.91 us -> 7.37 us  [per_device(): lax.all_to_all(last_part.reshape(-1, own, m_cells), group, 0, 0, tiled=True)]
    all_to_all x1, waiting for transfers between devices: 4.41 us -> 5.76 us  [per_device(): pieces = lax.all_to_all(projected, 'gx', 0, 0, tiled=True)]
    ppermute x8 -> x9, waiting for transfers between devices: 21.5 us -> 21 us  [swap(): lax.ppermute(array, axis, [(s, s ^ bits) for s in range(lax.axis_size(axi...]
  transfers between devices with their start and end apart: 12 -> 13, of which waited for: 9 -> 8; matrix products, arithmetic and copies ran while one was open for 4% -> 4% of each run, Pallas kernels for 7% -> 8%
where the time goes in v10:
time: 88.7 us; the launch traced here: 88.1 us
  waiting for transfers between devices  33.3 us (38%)
  starting transfers between devices  32.7 us (37%)
  Pallas kernels  17.1 us (19%)
  local copies, waits for them, and re-layouts  2.29 us (3%)
  matrix products  1.8 us (2%)
    ppermute x9, waiting for transfers between devices, swap(): lax.ppermute(array, axis, [(s, s ^ bits) for s in range(lax.axis_size(axi...  21 us
    ppermute x9, starting transfers between devices, swap(): lax.ppermute(array, axis, [(s, s ^ bits) for s in range(lax.axis_size(axi...  12.3 us
    all_to_all x1, starting transfers between devices, per_device(): lax.all_to_all(last_part.reshape(-1, own, m_cells), group, 0, 0, tiled=True)  7.37 us
    all_to_all x1, waiting for transfers between devices, per_device(): pieces = lax.all_to_all(projected, 'gx', 0, 0, tiled=True)  5.76 us
    pallas_call x1, Pallas kernels, solve_first(): pl.pallas_call(first_kernel, out_shape=jax.ShapeDtypeStruct((x_cells, sum...  4.98 us
    all_to_all x1, starting transfers between devices, per_device(): received = lax.all_to_all(middle, group, 0, 0, tiled=True)  4.66 us
    all_to_all x1, starting transfers between devices, per_device(): pieces = lax.all_to_all(projected, 'gx', 0, 0, tiled=True)  4.62 us
    pallas_call x1, Pallas kernels, pseudo_inverse(): pl.pallas_call(inverse_kernel, out_shape=jax.ShapeDtypeStruct((rank, syst...  4.34 us
  transfers between devices with their start and end apart: 13, of which 8 were waited for; matrix products, arithmetic and copies ran while one was open for 4% of the time, Pallas kernels for 8%

profile of v10, /device:TPU:0, one launch (start us, length us, event | category | flops | bytes accessed | tf_op | source)
XLA Modules:
  0.0 88.1 jit_solution(13184597945016446113)
XLA Ops:
  0.6 0.0 copy-start.1
  0.6 0.0 copy-start.2
  0.7 4.2 %local_products.1 = (f32[128,512]{1,0:T(8,128)}, f32[32,256]{1,0:T(8,128)}, f32[16,32,256]{2,1,0:T(8,128)}, f32[16,32,256]{2,1,0:T(8,128)}) custom-call(bf16[32,64,512]{2,1,0:T(8,128)(2,1)} %field_hbm.1, bf16[32,128]{1,0:T(8,128)(2,1)} %last_x_hbm.1, bf16[64,128]{1,0:T(8,128)(2,1)} %last_y_hbm.1, bf16[64,256]{1,0:T(8,128)(2,1)} %right_y_hbm.1, ...), custom_call_target="tpu_custom_call" | custom-call | tf_op jit(solution)/shard_map/local_products/pallas_call | solution.py:205
  4.8 7.4 %all-to-all-start = ((f32[16,8,512]{2,1,0:T(8,128)}), f32[16,8,512]{2,1,0:T(8,128)S(1)}, u32[]{:S(2)}, u32[]{:S(2)}) async-start(f32[16,8,512]{2,1,0:T(8,128)} %bitcast.36), calls=%async_computation | async-start | bytes 524288 | tf_op jit(solution)/shard_map/all_to_all | solution.py:446
  12.2 1.6 %collective-permute-start.1 = (f32[16,32,256]{2,1,0:T(8,128)}, f32[16,32,256]{2,1,0:T(8,128)S(1)}, u32[]{:S(2)}, u32[]{:S(2)}) collective-permute-start(f32[16,32,256]{2,1,0:T(8,128)} %get-tuple-element.18), channel_id=1, source_target_pairs={{0,1},{1,0},{2,3},{3,2},{4,5},{5,4},{6,7},{7,6},{8,9},{9,8},{10,11... | collective-permute-start | bytes 1572872 | tf_op jit(solution)/shard_map/ppermute | solution.py:29
  13.8 0.0 copy-done.2
  13.8 0.8 copy_bitcast_fusion
  14.6 1.9 %collective-permute-start = (f32[96,128]{1,0:T(8,128)S(1)}, f32[96,128]{1,0:T(8,128)S(1)}, u32[]{:S(2)}, u32[]{:S(2)}) collective-permute-start(f32[96,128]{1,0:T(8,128)S(1)} %pad_maximum_fusion.2), channel_id=1, source_target_pairs={{0,4},{4,0},{8,12},{12,8},{16,20},{20,16},{24,28},{28,24},{1,5},{5... | collective-permute-start | bytes 147464 | tf_op jit(solution)/shard_map/ppermute | solution.py:29
  16.4 0.5 collective-permute-start.5
  16.9 0.0 copy-done.1
  16.9 1.7 %fusion.kept = f32[32,32,256]{2,1,0:T(8,128)S(1)} fusion(bf16[32,2,32,512]{3,2,1,0:T(8,128)(2,1)} %bitcast.32, s32[]{:T(128)S(6)} %select_n.4, bf16[512,256]{1,0:T(8,128)(2,1)S(1)} %copy-done.1), kind=kOutput, calls=%fused_computation | convolution fusion | flops 268435456 | bytes 2359300 | tf_op jit(solution)/shard_map/dot_general | solution.py:430
  18.6 3.7 %all-to-all-done = f32[16,8,512]{2,1,0:T(8,128)S(1)} async-done(((f32[16,8,512]{2,1,0:T(8,128)}), f32[16,8,512]{2,1,0:T(8,128)S(1)}, u32[]{:S(2)}, u32[]{:S(2)}) %all-to-all-start) | async-done | bytes 262176 | tf_op jit(solution)/shard_map/all_to_all | solution.py:446
  22.3 5.0 %collective-permute-done.1.refs_0_ = f32[16,32,256]{2,1,0:T(8,128)S(1)} collective-permute-done((f32[16,32,256]{2,1,0:T(8,128)}, f32[16,32,256]{2,1,0:T(8,128)S(1)}, u32[]{:S(2)}, u32[]{:S(2)}) %collective-permute-start.1) | collective-permute-done | bytes 524320 | tf_op jit(solution)/shard_map/ppermute | solution.py:29
  27.3 0.0 collective-permute-done
  27.3 2.9 %collective-permute-start.2 = (f32[1,224,128]{2,1,0:T(8,128)S(1)}, f32[1,224,128]{2,1,0:T(8,128)S(1)}, u32[]{:S(2)}, u32[]{:S(2)}) collective-permute-start(f32[1,224,128]{2,1,0:T(8,128)S(1)} %maximum_bitcast_fusion), channel_id=1, source_target_pairs={{0,16},{4,20},{8,24},{12,28},{16,0},{20,4},{24,8},{28,12},{1,17},{... | collective-permute-start | bytes 344072 | tf_op jit(solution)/shard_map/ppermute | solution.py:29
  30.1 0.1 fusion.5
  30.3 0.7 broadcast_in_dim.10
  31.0 3.7 %all-to-all-start.1 = ((f32[32,8,256]{2,1,0:T(8,128)}), f32[32,8,256]{2,1,0:T(8,128)S(1)}, u32[]{:S(2)}, u32[]{:S(2)}) async-start(f32[32,8,256]{2,1,0:T(8,128)} %broadcast_in_dim.10), calls=%async_computation.1 | async-start | bytes 524288 | tf_op jit(solution)/shard_map/all_to_all | solution.py:454
  34.7 0.0 collective-permute-done.2
  34.8 1.8 %collective-permute-start.3 = (f32[2,224,128]{2,1,0:T(8,128)S(1)}, f32[2,224,128]{2,1,0:T(8,128)S(1)}, u32[]{:S(2)}, u32[]{:S(2)}) collective-permute-start(f32[2,224,128]{2,1,0:T(8,128)S(1)} %pad_maximum_fusion.1), channel_id=1, source_target_pairs={{0,8},{4,12},{8,0},{12,4},{16,24},{20,28},{24,16},{28,20},{1,9},{5... | collective-permute-start | bytes 688136 | tf_op jit(solution)/shard_map/ppermute | solution.py:29
  36.6 10.1 %collective-permute-done.3 = f32[2,224,128]{2,1,0:T(8,128)S(1)} collective-permute-done((f32[2,224,128]{2,1,0:T(8,128)S(1)}, f32[2,224,128]{2,1,0:T(8,128)S(1)}, u32[]{:S(2)}, u32[]{:S(2)}) %collective-permute-start.3) | collective-permute-done | bytes 229408 | tf_op jit(solution)/shard_map/ppermute | solution.py:29
  46.8 0.0 all-to-all-done.1
  46.8 0.0 copy-start
  46.8 0.0 collective-permute-done.5.refs_1_
  46.8 4.3 %pseudo_inverse.1.pinv = f32[128,256]{1,0:T(8,128)S(1)} custom-call(f32[16,2,8,256]{3,2,1,0:T(8,128)S(1)} %bitcast.31), custom_call_target="tpu_custom_call" | custom-call | tf_op jit(solution)/shard_map/pseudo_inverse/pallas_call | solution.py:249
  51.1 1.5 %project.1 = f32[8,128,128]{2,1,0:T(8,128)} custom-call(f32[128,256]{1,0:T(8,128)S(1)} %pseudo_inverse.1.pinv, f32[32,32,256]{2,1,0:T(8,128)S(1)} %fusion.kept, f32[16,32,256]{2,1,0:T(8,128)S(1)} %collective-permute-done.1.refs_0_, f32[16,32,256]{2,1,0:T(8,128)S(1)} %collective-permute-done.5.refs_1_), custom_call_target="tpu_custom_call" | custom-call | tf_op jit(solution)/shard_map/project/pallas_call | solution.py:285
  52.6 4.6 %all-to-all-start.2 = ((f32[8,128,128]{2,1,0:T(8,128)}), f32[8,128,128]{2,1,0:T(8,128)S(1)}, u32[]{:S(2)}, u32[]{:S(2)}) async-start(f32[8,128,128]{2,1,0:T(8,128)} %project.1), calls=%async_computation.2 | async-start | bytes 1048576 | tf_op jit(solution)/shard_map/all_to_all | solution.py:478
  57.3 0.0 copy-done
  57.3 0.4 first_sums.1
  57.7 1.6 %collective-permute-start.4 = (f32[160,256]{1,0:T(8,128)S(1)}, f32[160,256]{1,0:T(8,128)S(1)}, u32[]{:S(2)}, u32[]{:S(2)}) collective-permute-start(f32[160,256]{1,0:T(8,128)S(1)} %get-tuple-element.20), channel_id=1, source_target_pairs={{0,1},{1,0},{2,3},{3,2},{4,5},{5,4},{6,7},{7,6},{8,9},{9,8},{10,11... | collective-permute-start | bytes 491528 | tf_op jit(solution)/shard_map/ppermute | solution.py:29
  59.2 2.0 %collective-permute-start.6 = (f32[4,32,128]{2,1,0:T(8,128)S(1)}, f32[4,32,128]{2,1,0:T(8,128)S(1)}, u32[]{:S(2)}, u32[]{:S(2)}) collective-permute-start(f32[4,32,128]{2,1,0:T(8,128)S(1)} %get-tuple-element.26), channel_id=1, source_target_pairs={{0,4},{4,0},{8,12},{12,8},{16,20},{20,16},{24,28},{28,24},{1,5},{5... | collective-permute-start | bytes 196616 | tf_op jit(solution)/shard_map/ppermute | solution.py:29
  61.2 2.1 %collective-permute-done.4 = f32[160,256]{1,0:T(8,128)S(1)} collective-permute-done((f32[160,256]{1,0:T(8,128)S(1)}, f32[160,256]{1,0:T(8,128)S(1)}, u32[]{:S(2)}, u32[]{:S(2)}) %collective-permute-start.4) | collective-permute-done | bytes 163872 | tf_op jit(solution)/shard_map/ppermute | solution.py:29
  63.4 0.1 collective-permute-start.7
  63.5 2.5 %collective-permute-done.6 = f32[4,32,128]{2,1,0:T(8,128)S(1)} collective-permute-done((f32[4,32,128]{2,1,0:T(8,128)S(1)}, f32[4,32,128]{2,1,0:T(8,128)S(1)}, u32[]{:S(2)}, u32[]{:S(2)}) %collective-permute-start.6) | collective-permute-done | bytes 65568 | tf_op jit(solution)/shard_map/ppermute | solution.py:29
  65.9 5.8 %all-to-all-done.2.pieces = f32[8,128,128]{2,1,0:T(8,128)S(1)} async-done(((f32[8,128,128]{2,1,0:T(8,128)}), f32[8,128,128]{2,1,0:T(8,128)S(1)}, u32[]{:S(2)}, u32[]{:S(2)}) %all-to-all-start.2) | async-done | bytes 524320 | tf_op jit(solution)/shard_map/all_to_all | solution.py:478
  71.7 1.0 %sketch.1 = f32[16,4,8,128]{3,2,1,0:T(8,128)} custom-call(f32[8,128,128]{2,1,0:T(8,128)S(1)} %all-to-all-done.2.pieces, f32[4,224,128]{2,1,0:T(8,128)S(1)} %pad_maximum_fusion.packed), custom_call_target="tpu_custom_call" | custom-call | tf_op jit(solution)/shard_map/sketch/pallas_call | solution.py:324
  72.7 0.0 collective-permute-done.7.refs_1_
  72.7 4.7 %all-to-all-start.3 = ((f32[16,4,8,128]{3,2,1,0:T(8,128)}), f32[16,4,8,128]{3,2,1,0:T(8,128)S(1)}, u32[]{:S(2)}, u32[]{:S(2)}) async-start(f32[16,4,8,128]{3,2,1,0:T(8,128)} %sketch.1), calls=%async_computation.3 | async-start | bytes 524288 | tf_op jit(solution)/shard_map/all_to_all | solution.py:489
  77.3 0.1 collective-permute-start.8
  77.4 1.3 %collective-permute-done.8.refs_1_ = f32[8,32,128]{2,1,0:T(8,128)S(1)} collective-permute-done((f32[8,32,128]{2,1,0:T(8,128)S(1)}, f32[8,32,128]{2,1,0:T(8,128)S(1)}, u32[]{:S(2)}, u32[]{:S(2)}) %collective-permute-start.8) | collective-permute-done | bytes 131104 | tf_op jit(solution)/shard_map/ppermute | solution.py:29
  78.7 0.7 place.1
  79.5 5.0 %solve_first.1 = f32[32,128]{1,0:T(8,128)} custom-call(f32[160,256]{1,0:T(8,128)S(1)} %add.10.refs_0_, f32[160,256]{1,0:T(8,128)S(1)} %collective-permute-done.7.refs_1_), custom_call_target="tpu_custom_call" | custom-call | tf_op jit(solution)/shard_map/solve_first/pallas_call | solution.py:381
  84.5 2.9 %all-to-all-done.3 = f32[16,4,8,128]{3,2,1,0:T(8,128)S(1)} async-done(((f32[16,4,8,128]{3,2,1,0:T(8,128)}), f32[16,4,8,128]{3,2,1,0:T(8,128)S(1)}, u32[]{:S(2)}, u32[]{:S(2)}) %all-to-all-start.3) | async-done | bytes 262176 | tf_op jit(solution)/shard_map/all_to_all | solution.py:489
  87.4 0.8 copy.12
  (11 shorter events, 0.1 us)
Async XLA Ops:
  0.6 16.3 %copy-start.1 = (bf16[512,256]{1,0:T(8,128)(2,1)S(1)}, bf16[512,256]{1,0:T(8,128)(2,1)}, u32[]{:S(2)}) copy-start(bf16[512,256]{1,0:T(8,128)(2,1)} %last_m_hbm.1) | copy-start | bytes 786436
  0.6 13.1 %copy-start.2 = (bf16[32,128]{1,0:T(8,128)(2,1)S(1)}, bf16[32,128]{1,0:T(8,128)(2,1)}, u32[]{:S(2)}) copy-start(bf16[32,128]{1,0:T(8,128)(2,1)} %param.8) | copy-start | bytes 24580
  4.8 17.4 %all-to-all-start = ((f32[16,8,512]{2,1,0:T(8,128)}), f32[16,8,512]{2,1,0:T(8,128)S(1)}, u32[]{:S(2)}, u32[]{:S(2)}) async-start(f32[16,8,512]{2,1,0:T(8,128)} %bitcast.36), calls=%async_computation | async-start | bytes 524288 | tf_op jit(solution)/shard_map/all_to_all | solution.py:446
  12.2 15.0 %collective-permute-start.1 = (f32[16,32,256]{2,1,0:T(8,128)}, f32[16,32,256]{2,1,0:T(8,128)S(1)}, u32[]{:S(2)}, u32[]{:S(2)}) collective-permute-start(f32[16,32,256]{2,1,0:T(8,128)} %get-tuple-element.18), channel_id=1, source_target_pairs={{0,1},{1,0},{2,3},{3,2},{4,5},{5,4},{6,7},{7,6},{8,9},{9,8},{10,11... | collective-permute-start | bytes 1572872 | tf_op jit(solution)/shard_map/ppermute | solution.py:29
  14.6 12.7 %collective-permute-start = (f32[96,128]{1,0:T(8,128)S(1)}, f32[96,128]{1,0:T(8,128)S(1)}, u32[]{:S(2)}, u32[]{:S(2)}) collective-permute-start(f32[96,128]{1,0:T(8,128)S(1)} %pad_maximum_fusion.2), channel_id=1, source_target_pairs={{0,4},{4,0},{8,12},{12,8},{16,20},{20,16},{24,28},{28,24},{1,5},{5... | collective-permute-start | bytes 147464 | tf_op jit(solution)/shard_map/ppermute | solution.py:29
  16.4 30.4 %collective-permute-start.5 = (f32[16,32,256]{2,1,0:T(8,128)}, f32[16,32,256]{2,1,0:T(8,128)S(1)}, u32[]{:S(2)}, u32[]{:S(2)}) collective-permute-start(f32[16,32,256]{2,1,0:T(8,128)} %get-tuple-element.23), channel_id=1, source_target_pairs={{0,1},{1,0},{2,3},{3,2},{4,5},{5,4},{6,7},{7,6},{8,9},{9,8},{10,11... | collective-permute-start | bytes 1572872 | tf_op jit(solution)/shard_map/ppermute | solution.py:29
  27.3 7.5 %collective-permute-start.2 = (f32[1,224,128]{2,1,0:T(8,128)S(1)}, f32[1,224,128]{2,1,0:T(8,128)S(1)}, u32[]{:S(2)}, u32[]{:S(2)}) collective-permute-start(f32[1,224,128]{2,1,0:T(8,128)S(1)} %maximum_bitcast_fusion), channel_id=1, source_target_pairs={{0,16},{4,20},{8,24},{12,28},{16,0},{20,4},{24,8},{28,12},{1,17},{... | collective-permute-start | bytes 344072 | tf_op jit(solution)/shard_map/ppermute | solution.py:29
  31.0 15.7 %all-to-all-start.1 = ((f32[32,8,256]{2,1,0:T(8,128)}), f32[32,8,256]{2,1,0:T(8,128)S(1)}, u32[]{:S(2)}, u32[]{:S(2)}) async-start(f32[32,8,256]{2,1,0:T(8,128)} %broadcast_in_dim.10), calls=%async_computation.1 | async-start | bytes 524288 | tf_op jit(solution)/shard_map/all_to_all | solution.py:454
  34.8 11.9 %collective-permute-start.3 = (f32[2,224,128]{2,1,0:T(8,128)S(1)}, f32[2,224,128]{2,1,0:T(8,128)S(1)}, u32[]{:S(2)}, u32[]{:S(2)}) collective-permute-start(f32[2,224,128]{2,1,0:T(8,128)S(1)} %pad_maximum_fusion.1), channel_id=1, source_target_pairs={{0,8},{4,12},{8,0},{12,4},{16,24},{20,28},{24,16},{28,20},{1,9},{5... | collective-permute-start | bytes 688136 | tf_op jit(solution)/shard_map/ppermute | solution.py:29
  46.8 10.5 %copy-start = (f32[32,256]{1,0:T(8,128)S(1)}, f32[32,256]{1,0:T(8,128)}, u32[]{:S(2)}) copy-start(f32[32,256]{1,0:T(8,128)} %get-tuple-element.16.rows) | copy-start | bytes 98308
  52.6 19.1 %all-to-all-start.2 = ((f32[8,128,128]{2,1,0:T(8,128)}), f32[8,128,128]{2,1,0:T(8,128)S(1)}, u32[]{:S(2)}, u32[]{:S(2)}) async-start(f32[8,128,128]{2,1,0:T(8,128)} %project.1), calls=%async_computation.2 | async-start | bytes 1048576 | tf_op jit(solution)/shard_map/all_to_all | solution.py:478
  57.7 5.7 %collective-permute-start.4 = (f32[160,256]{1,0:T(8,128)S(1)}, f32[160,256]{1,0:T(8,128)S(1)}, u32[]{:S(2)}, u32[]{:S(2)}) collective-permute-start(f32[160,256]{1,0:T(8,128)S(1)} %get-tuple-element.20), channel_id=1, source_target_pairs={{0,1},{1,0},{2,3},{3,2},{4,5},{5,4},{6,7},{7,6},{8,9},{9,8},{10,11... | collective-permute-start | bytes 491528 | tf_op jit(solution)/shard_map/ppermute | solution.py:29
  59.2 6.7 %collective-permute-start.6 = (f32[4,32,128]{2,1,0:T(8,128)S(1)}, f32[4,32,128]{2,1,0:T(8,128)S(1)}, u32[]{:S(2)}, u32[]{:S(2)}) collective-permute-start(f32[4,32,128]{2,1,0:T(8,128)S(1)} %get-tuple-element.26), channel_id=1, source_target_pairs={{0,4},{4,0},{8,12},{12,8},{16,20},{20,16},{24,28},{28,24},{1,5},{5... | collective-permute-start | bytes 196616 | tf_op jit(solution)/shard_map/ppermute | solution.py:29
  63.4 9.3 %collective-permute-start.7 = (f32[160,256]{1,0:T(8,128)S(1)}, f32[160,256]{1,0:T(8,128)S(1)}, u32[]{:S(2)}, u32[]{:S(2)}) collective-permute-start(f32[160,256]{1,0:T(8,128)S(1)} %add.10.refs_0_), channel_id=1, source_target_pairs={{0,2},{2,0},{1,3},{3,1},{4,6},{6,4},{5,7},{7,5},{8,10},{10,8},{9,1... | collective-permute-start | bytes 491528 | tf_op jit(solution)/shard_map/ppermute | solution.py:29
  72.7 14.7 %all-to-all-start.3 = ((f32[16,4,8,128]{3,2,1,0:T(8,128)}), f32[16,4,8,128]{3,2,1,0:T(8,128)S(1)}, u32[]{:S(2)}, u32[]{:S(2)}) async-start(f32[16,4,8,128]{3,2,1,0:T(8,128)} %sketch.1), calls=%async_computation.3 | async-start | bytes 524288 | tf_op jit(solution)/shard_map/all_to_all | solution.py:489
  77.3 1.4 %collective-permute-start.8 = (f32[8,32,128]{2,1,0:T(8,128)S(1)}, f32[8,32,128]{2,1,0:T(8,128)S(1)}, u32[]{:S(2)}, u32[]{:S(2)}) collective-permute-start(f32[8,32,128]{2,1,0:T(8,128)S(1)} %constant_dynamic-update-slice_fusion.refs_0_), channel_id=1, source_target_pairs={{0,2},{2,0},{1,3},{3,1},{4,6},{6,4},{5,7},{7,5},{8,10},{10,8},{9,1... | collective-permute-start | bytes 393224 | tf_op jit(solution)/shard_map/ppermute | solution.py:29

commit v11 on v9

--- a/solution.py
+++ b/solution.py
@@ -18,6 +18,11 @@
 COL_COL = (((0,), (0,)), ((), ()))
 
 
+def gather_bits(axis):
+    *bits, last = axis_bits(axis)
+    return [last, *bits]
+
+
 def axis_bits(axis):
     bit = lax.axis_size(axis) // 2
     while bit:
@@ -42,7 +47,7 @@
 
 def swap_order(axis):
     order = [0]
-    for bit in axis_bits(axis):
+    for bit in gather_bits(axis):
         order += [o ^ bit for o in order]
     return order
 
@@ -101,15 +106,26 @@
                 rest = work[c] - p * top - q * low
                 work[c] = jnp.where(subs == k, top, jnp.where(subs == k + 1, low, rest))
         solved = work[ROWS]
+        signs = jnp.where(inside, 0.0, jnp.where(lanes < first, -1.0, 1.0))
+        update = lax.dot_general(
+            signs * rows[panel],
+            solved,
+            COL_COL,
+            precision=HIGHEST,
+            preferred_element_type=jnp.float32,
+        )
         for r in range(len(rows)):
             if r == panel:
+                rows[r] = solved
                 continue
             old = rows[r]
             new = jnp.where(inside, 0.0, old)
-            for c in range(ROWS):
-                new = new - column(old, first + c) * solved[c : c + 1]
+            if r == panel + 1:
+                for c in range(ROWS):
+                    new = new - column(old, first + c) * solved[c : c + 1]
+            else:
+                new = new - update[r * ROWS : (r + 1) * ROWS]
             rows[r] = new
-        rows[panel] = solved
     return jnp.concatenate(rows, axis=0)
 
 
@@ -434,7 +450,7 @@
         axis=0,
     )[None]
     left_at = x_cells * cols // LANES
-    first_bit, *bits = axis_bits("gx")
+    first_bit, *bits = gather_bits("gx")
     packed = swap_step(packed, "gx", first_bit)
 
     group = ("gx", "gy")

time: 84.7 us -> 84.9 us (level)
  waiting for transfers between devices: 34.7 us -> 31.7 us
  starting transfers between devices: 27.3 us -> 30 us
    ppermute x8, waiting for transfers between devices: 21.5 us -> 17.5 us  [swap(): lax.ppermute(array, axis, [(s, s ^ bits) for s in range(lax.axis_size(axi...]
    all_to_all x1, waiting for transfers between devices: 0.01 us -> 1.79 us  [per_device(): lax.all_to_all(last_part.reshape(-1, own, m_cells), group, 0, 0, tiled=True)]
    ppermute x8, starting transfers between devices: 9.74 us -> 11.1 us  [swap(): lax.ppermute(array, axis, [(s, s ^ bits) for s in range(lax.axis_size(axi...]
    all_to_all x1, waiting for transfers between devices: 0.86 us -> 0.01 us  [per_device(): lax.all_to_all(copies, ALL, 0, 0, tiled=True).reshape(-1, shares, own, cols)]
  transfers between devices with their start and end apart: 12 -> 12, of which waited for: 9 -> 8; matrix products, arithmetic and copies ran while one was open for 4% -> 4% of each run, Pallas kernels for 7% -> 8%
where the time goes in v11:
time: 84.9 us; the launch traced here: 84.3 us
  waiting for transfers between devices  31.7 us (37%)
  starting transfers between devices  30 us (35%)
  Pallas kernels  17.6 us (21%)
  local copies, waits for them, and re-layouts  2.28 us (3%)
  matrix products  1.8 us (2%)
    ppermute x8, waiting for transfers between devices, swap(): lax.ppermute(array, axis, [(s, s ^ bits) for s in range(lax.axis_size(axi...  17.5 us
    ppermute x8, starting transfers between devices, swap(): lax.ppermute(array, axis, [(s, s ^ bits) for s in range(lax.axis_size(axi...  11.1 us
    all_to_all x1, waiting for transfers between devices, per_device(): received = lax.all_to_all(middle, group, 0, 0, tiled=True)  7.91 us
    all_to_all x1, starting transfers between devices, per_device(): lax.all_to_all(last_part.reshape(-1, own, m_cells), group, 0, 0, tiled=True)  5.9 us
    pallas_call x1, Pallas kernels, solve_first(): pl.pallas_call(first_kernel, out_shape=jax.ShapeDtypeStruct((x_cells, sum...  5.19 us
    all_to_all x1, starting transfers between devices, per_device(): received = lax.all_to_all(middle, group, 0, 0, tiled=True)  4.65 us
    all_to_all x1, starting transfers between devices, per_device(): pieces = lax.all_to_all(projected, 'gx', 0, 0, tiled=True)  4.61 us
    pallas_call x1, Pallas kernels, pseudo_inverse(): pl.pallas_call(inverse_kernel, out_shape=jax.ShapeDtypeStruct((rank, syst...  4.59 us
  transfers between devices with their start and end apart: 12, of which 8 were waited for; matrix products, arithmetic and copies ran while one was open for 4% of the time, Pallas kernels for 8%

profile of v11, /device:TPU:0, one launch (start us, length us, event | category | flops | bytes accessed | tf_op | source)
XLA Modules:
  0.0 84.3 jit_solution(6207930425822934438)
XLA Ops:
  0.6 0.0 copy-start.1
  0.6 0.0 copy-start.2
  0.7 4.2 %local_products.1 = (f32[128,512]{1,0:T(8,128)}, f32[32,256]{1,0:T(8,128)}, f32[16,32,256]{2,1,0:T(8,128)}, f32[16,32,256]{2,1,0:T(8,128)}) custom-call(bf16[32,64,512]{2,1,0:T(8,128)(2,1)} %field_hbm.1, bf16[32,128]{1,0:T(8,128)(2,1)} %last_x_hbm.1, bf16[64,128]{1,0:T(8,128)(2,1)} %last_y_hbm.1, bf16[64,256]{1,0:T(8,128)(2,1)} %right_y_hbm.1, ...), custom_call_target="tpu_custom_call" | custom-call | tf_op jit(solution)/shard_map/local_products/pallas_call | solution.py:221
  4.8 3.0 %collective-permute-start = (f32[16,32,256]{2,1,0:T(8,128)}, f32[16,32,256]{2,1,0:T(8,128)S(1)}, u32[]{:S(2)}, u32[]{:S(2)}) collective-permute-start(f32[16,32,256]{2,1,0:T(8,128)} %get-tuple-element.16), channel_id=1, source_target_pairs={{0,1},{1,0},{2,3},{3,2},{4,5},{5,4},{6,7},{7,6},{8,9},{9,8},{10,11... | collective-permute-start | bytes 1572872 | tf_op jit(solution)/shard_map/ppermute | solution.py:34
  7.9 5.9 %all-to-all-start = ((f32[16,8,512]{2,1,0:T(8,128)}), f32[16,8,512]{2,1,0:T(8,128)S(1)}, u32[]{:S(2)}, u32[]{:S(2)}) async-start(f32[16,8,512]{2,1,0:T(8,128)} %bitcast.35), calls=%async_computation | async-start | bytes 524288 | tf_op jit(solution)/shard_map/all_to_all | solution.py:458
  13.8 0.8 copy_bitcast_fusion
  14.5 0.0 copy-done.2
  14.6 2.0 %collective-permute-start.1 = (f32[1,96,128]{2,1,0:T(8,128)S(1)}, f32[1,96,128]{2,1,0:T(8,128)S(1)}, u32[]{:S(2)}, u32[]{:S(2)}) collective-permute-start(f32[1,96,128]{2,1,0:T(8,128)S(1)} %maximum_bitcast_fusion), channel_id=1, source_target_pairs={{0,4},{4,0},{8,12},{12,8},{16,20},{20,16},{24,28},{28,24},{1,5},{5... | collective-permute-start | bytes 147464 | tf_op jit(solution)/shard_map/ppermute | solution.py:34
  16.5 0.5 collective-permute-start.4
  17.0 0.0 copy-done.1
  17.1 1.7 %fusion.kept = f32[32,32,256]{2,1,0:T(8,128)S(1)} fusion(bf16[32,2,32,512]{3,2,1,0:T(8,128)(2,1)} %bitcast.33, s32[]{:T(128)S(6)} %select_n.4, bf16[512,256]{1,0:T(8,128)(2,1)S(1)} %copy-done.1), kind=kOutput, calls=%fused_computation | convolution fusion | flops 268435456 | bytes 2359300 | tf_op jit(solution)/shard_map/dot_general | solution.py:441
  18.7 1.2 %collective-permute-done.1 = f32[1,96,128]{2,1,0:T(8,128)S(1)} collective-permute-done((f32[1,96,128]{2,1,0:T(8,128)S(1)}, f32[1,96,128]{2,1,0:T(8,128)S(1)}, u32[]{:S(2)}, u32[]{:S(2)}) %collective-permute-start.1) | collective-permute-done | bytes 49184 | tf_op jit(solution)/shard_map/ppermute | solution.py:34
  19.9 2.1 %collective-permute-start.2 = (f32[2,96,128]{2,1,0:T(8,128)S(1)}, f32[2,96,128]{2,1,0:T(8,128)S(1)}, u32[]{:S(2)}, u32[]{:S(2)}) collective-permute-start(f32[2,96,128]{2,1,0:T(8,128)S(1)} %pad_maximum_fusion.2), channel_id=1, source_target_pairs={{0,16},{4,20},{8,24},{12,28},{16,0},{20,4},{24,8},{28,12},{1,17},{... | collective-permute-start | bytes 294920 | tf_op jit(solution)/shard_map/ppermute | solution.py:34
  22.0 1.8 %all-to-all-done = f32[16,8,512]{2,1,0:T(8,128)S(1)} async-done(((f32[16,8,512]{2,1,0:T(8,128)}), f32[16,8,512]{2,1,0:T(8,128)S(1)}, u32[]{:S(2)}, u32[]{:S(2)}) %all-to-all-start) | async-done | bytes 262176 | tf_op jit(solution)/shard_map/all_to_all | solution.py:458
  23.8 0.0 collective-permute-done.refs_0_
  23.9 0.1 fusion.5
  24.0 0.7 broadcast_in_dim.10
  24.7 3.7 %all-to-all-start.1 = ((f32[32,8,256]{2,1,0:T(8,128)}), f32[32,8,256]{2,1,0:T(8,128)S(1)}, u32[]{:S(2)}, u32[]{:S(2)}) async-start(f32[32,8,256]{2,1,0:T(8,128)} %broadcast_in_dim.10), calls=%async_computation.1 | async-start | bytes 524288 | tf_op jit(solution)/shard_map/all_to_all | solution.py:466
  28.5 0.0 collective-permute-done.2
  28.5 1.8 %collective-permute-start.3 = (f32[4,96,128]{2,1,0:T(8,128)S(1)}, f32[4,96,128]{2,1,0:T(8,128)S(1)}, u32[]{:S(2)}, u32[]{:S(2)}) collective-permute-start(f32[4,96,128]{2,1,0:T(8,128)S(1)} %pad_maximum_fusion.1), channel_id=1, source_target_pairs={{0,8},{4,12},{8,0},{12,4},{16,24},{20,28},{24,16},{28,20},{1,9},{5... | collective-permute-start | bytes 589832 | tf_op jit(solution)/shard_map/ppermute | solution.py:34
  30.4 9.4 %collective-permute-done.3 = f32[4,96,128]{2,1,0:T(8,128)S(1)} collective-permute-done((f32[4,96,128]{2,1,0:T(8,128)S(1)}, f32[4,96,128]{2,1,0:T(8,128)S(1)}, u32[]{:S(2)}, u32[]{:S(2)}) %collective-permute-start.3) | collective-permute-done | bytes 196640 | tf_op jit(solution)/shard_map/ppermute | solution.py:34
  39.8 0.0 collective-permute-done.4.refs_1_
  39.8 0.0 all-to-all-done.1
  39.8 4.6 %pseudo_inverse.1.pinv = f32[128,256]{1,0:T(8,128)S(1)} custom-call(f32[16,2,8,256]{3,2,1,0:T(8,128)S(1)} %bitcast.31), custom_call_target="tpu_custom_call" | custom-call | tf_op jit(solution)/shard_map/pseudo_inverse/pallas_call | solution.py:265
  44.4 0.0 copy-start
  44.4 1.6 %project.1 = f32[8,160,128]{2,1,0:T(8,128)} custom-call(f32[128,256]{1,0:T(8,128)S(1)} %pseudo_inverse.1.pinv, f32[32,128]{1,0:T(8,128)S(1)} %bitcast.32, f32[32,32,256]{2,1,0:T(8,128)S(1)} %fusion.kept, f32[16,32,256]{2,1,0:T(8,128)S(1)} %collective-permute-done.refs_0_, f32[16,32,256]{2,1,0:T(8,128)S(1)} %collective-permute-done.4.refs_1_), custom_call_target="tpu_custom_call" | custom-call | tf_op jit(solution)/shard_map/project/pallas_call | solution.py:302
  46.0 4.6 %all-to-all-start.2 = ((f32[8,160,128]{2,1,0:T(8,128)}), f32[8,160,128]{2,1,0:T(8,128)S(1)}, u32[]{:S(2)}, u32[]{:S(2)}) async-start(f32[8,160,128]{2,1,0:T(8,128)} %project.1), calls=%async_computation.2 | async-start | bytes 1310720 | tf_op jit(solution)/shard_map/all_to_all | solution.py:482
  50.6 0.0 copy-done
  50.6 0.4 first_sums.1
  51.0 1.6 %collective-permute-start.5 = (f32[160,256]{1,0:T(8,128)S(1)}, f32[160,256]{1,0:T(8,128)S(1)}, u32[]{:S(2)}, u32[]{:S(2)}) collective-permute-start(f32[160,256]{1,0:T(8,128)S(1)} %first_sums.1), channel_id=1, source_target_pairs={{0,1},{1,0},{2,3},{3,2},{4,5},{5,4},{6,7},{7,6},{8,9},{9,8},{10,11... | collective-permute-start | bytes 491528 | tf_op jit(solution)/shard_map/ppermute | solution.py:34
  52.6 4.1 %collective-permute-done.5 = f32[160,256]{1,0:T(8,128)S(1)} collective-permute-done((f32[160,256]{1,0:T(8,128)S(1)}, f32[160,256]{1,0:T(8,128)S(1)}, u32[]{:S(2)}, u32[]{:S(2)}) %collective-permute-start.5) | collective-permute-done | bytes 163872 | tf_op jit(solution)/shard_map/ppermute | solution.py:34
  56.7 0.1 collective-permute-start.6
  56.8 1.4 %collective-permute-done.6.refs_1_ = f32[160,256]{1,0:T(8,128)S(1)} collective-permute-done((f32[160,256]{1,0:T(8,128)S(1)}, f32[160,256]{1,0:T(8,128)S(1)}, u32[]{:S(2)}, u32[]{:S(2)}) %collective-permute-start.6) | collective-permute-done | bytes 163872 | tf_op jit(solution)/shard_map/ppermute | solution.py:34
  58.2 5.2 %solve_first.1 = f32[32,128]{1,0:T(8,128)} custom-call(f32[160,256]{1,0:T(8,128)S(1)} %add.12.refs_0_, f32[160,256]{1,0:T(8,128)S(1)} %collective-permute-done.6.refs_1_), custom_call_target="tpu_custom_call" | custom-call | tf_op jit(solution)/shard_map/solve_first/pallas_call | solution.py:393
  63.4 4.5 %all-to-all-done.2.pieces = f32[8,160,128]{2,1,0:T(8,128)S(1)} async-done(((f32[8,160,128]{2,1,0:T(8,128)}), f32[8,160,128]{2,1,0:T(8,128)S(1)}, u32[]{:S(2)}, u32[]{:S(2)}) %all-to-all-start.2) | async-done | bytes 655392 | tf_op jit(solution)/shard_map/all_to_all | solution.py:482
  67.9 1.0 %sketch.1 = (f32[16,4,8,128]{3,2,1,0:T(8,128)}, f32[8,32,128]{2,1,0:T(8,128)S(1)}) custom-call(f32[8,160,128]{2,1,0:T(8,128)S(1)} %all-to-all-done.2.pieces, f32[8,96,128]{2,1,0:T(8,128)S(1)} %pad_maximum_fusion.packed), custom_call_target="tpu_custom_call" | custom-call | tf_op jit(solution)/shard_map/sketch/pallas_call | solution.py:338
  68.8 4.7 %all-to-all-start.3 = ((f32[16,4,8,128]{3,2,1,0:T(8,128)}), f32[16,4,8,128]{3,2,1,0:T(8,128)S(1)}, u32[]{:S(2)}, u32[]{:S(2)}) async-start(f32[16,4,8,128]{3,2,1,0:T(8,128)} %get-tuple-element.25), calls=%async_computation.3 | async-start | bytes 524288 | tf_op jit(solution)/shard_map/all_to_all | solution.py:493
  73.5 0.1 collective-permute-start.7
  73.6 1.3 %collective-permute-done.7.refs_1_ = f32[8,32,128]{2,1,0:T(8,128)S(1)} collective-permute-done((f32[8,32,128]{2,1,0:T(8,128)S(1)}, f32[8,32,128]{2,1,0:T(8,128)S(1)}, u32[]{:S(2)}, u32[]{:S(2)}) %collective-permute-start.7) | collective-permute-done | bytes 131104 | tf_op jit(solution)/shard_map/ppermute | solution.py:34
  74.9 0.7 place.1
  75.6 7.9 %all-to-all-done.3 = f32[16,4,8,128]{3,2,1,0:T(8,128)S(1)} async-done(((f32[16,4,8,128]{3,2,1,0:T(8,128)}), f32[16,4,8,128]{3,2,1,0:T(8,128)S(1)}, u32[]{:S(2)}, u32[]{:S(2)}) %all-to-all-start.3) | async-done | bytes 262176 | tf_op jit(solution)/shard_map/all_to_all | solution.py:493
  83.5 0.8 copy.12
  (9 shorter events, 0.1 us)
Async XLA Ops:
  0.6 16.4 %copy-start.1 = (bf16[512,256]{1,0:T(8,128)(2,1)S(1)}, bf16[512,256]{1,0:T(8,128)(2,1)}, u32[]{:S(2)}) copy-start(bf16[512,256]{1,0:T(8,128)(2,1)} %last_m_hbm.1) | copy-start | bytes 786436
  0.6 13.9 %copy-start.2 = (bf16[32,128]{1,0:T(8,128)(2,1)S(1)}, bf16[32,128]{1,0:T(8,128)(2,1)}, u32[]{:S(2)}) copy-start(bf16[32,128]{1,0:T(8,128)(2,1)} %param.8) | copy-start | bytes 24580
  4.8 19.0 %collective-permute-start = (f32[16,32,256]{2,1,0:T(8,128)}, f32[16,32,256]{2,1,0:T(8,128)S(1)}, u32[]{:S(2)}, u32[]{:S(2)}) collective-permute-start(f32[16,32,256]{2,1,0:T(8,128)} %get-tuple-element.16), channel_id=1, source_target_pairs={{0,1},{1,0},{2,3},{3,2},{4,5},{5,4},{6,7},{7,6},{8,9},{9,8},{10,11... | collective-permute-start | bytes 1572872 | tf_op jit(solution)/shard_map/ppermute | solution.py:34
  7.9 16.0 %all-to-all-start = ((f32[16,8,512]{2,1,0:T(8,128)}), f32[16,8,512]{2,1,0:T(8,128)S(1)}, u32[]{:S(2)}, u32[]{:S(2)}) async-start(f32[16,8,512]{2,1,0:T(8,128)} %bitcast.35), calls=%async_computation | async-start | bytes 524288 | tf_op jit(solution)/shard_map/all_to_all | solution.py:458
  14.6 5.4 %collective-permute-start.1 = (f32[1,96,128]{2,1,0:T(8,128)S(1)}, f32[1,96,128]{2,1,0:T(8,128)S(1)}, u32[]{:S(2)}, u32[]{:S(2)}) collective-permute-start(f32[1,96,128]{2,1,0:T(8,128)S(1)} %maximum_bitcast_fusion), channel_id=1, source_target_pairs={{0,4},{4,0},{8,12},{12,8},{16,20},{20,16},{24,28},{28,24},{1,5},{5... | collective-permute-start | bytes 147464 | tf_op jit(solution)/shard_map/ppermute | solution.py:34
  16.5 23.3 %collective-permute-start.4 = (f32[16,32,256]{2,1,0:T(8,128)}, f32[16,32,256]{2,1,0:T(8,128)S(1)}, u32[]{:S(2)}, u32[]{:S(2)}) collective-permute-start(f32[16,32,256]{2,1,0:T(8,128)} %get-tuple-element.20), channel_id=1, source_target_pairs={{0,1},{1,0},{2,3},{3,2},{4,5},{5,4},{6,7},{7,6},{8,9},{9,8},{10,11... | collective-permute-start | bytes 1572872 | tf_op jit(solution)/shard_map/ppermute | solution.py:34
  19.9 8.5 %collective-permute-start.2 = (f32[2,96,128]{2,1,0:T(8,128)S(1)}, f32[2,96,128]{2,1,0:T(8,128)S(1)}, u32[]{:S(2)}, u32[]{:S(2)}) collective-permute-start(f32[2,96,128]{2,1,0:T(8,128)S(1)} %pad_maximum_fusion.2), channel_id=1, source_target_pairs={{0,16},{4,20},{8,24},{12,28},{16,0},{20,4},{24,8},{28,12},{1,17},{... | collective-permute-start | bytes 294920 | tf_op jit(solution)/shard_map/ppermute | solution.py:34
  24.7 15.1 %all-to-all-start.1 = ((f32[32,8,256]{2,1,0:T(8,128)}), f32[32,8,256]{2,1,0:T(8,128)S(1)}, u32[]{:S(2)}, u32[]{:S(2)}) async-start(f32[32,8,256]{2,1,0:T(8,128)} %broadcast_in_dim.10), calls=%async_computation.1 | async-start | bytes 524288 | tf_op jit(solution)/shard_map/all_to_all | solution.py:466
  28.5 11.3 %collective-permute-start.3 = (f32[4,96,128]{2,1,0:T(8,128)S(1)}, f32[4,96,128]{2,1,0:T(8,128)S(1)}, u32[]{:S(2)}, u32[]{:S(2)}) collective-permute-start(f32[4,96,128]{2,1,0:T(8,128)S(1)} %pad_maximum_fusion.1), channel_id=1, source_target_pairs={{0,8},{4,12},{8,0},{12,4},{16,24},{20,28},{24,16},{28,20},{1,9},{5... | collective-permute-start | bytes 589832 | tf_op jit(solution)/shard_map/ppermute | solution.py:34
  44.4 6.2 %copy-start = (f32[32,256]{1,0:T(8,128)S(1)}, f32[32,256]{1,0:T(8,128)}, u32[]{:S(2)}) copy-start(f32[32,256]{1,0:T(8,128)} %get-tuple-element.18.rows) | copy-start | bytes 98308
  46.0 21.9 %all-to-all-start.2 = ((f32[8,160,128]{2,1,0:T(8,128)}), f32[8,160,128]{2,1,0:T(8,128)S(1)}, u32[]{:S(2)}, u32[]{:S(2)}) async-start(f32[8,160,128]{2,1,0:T(8,128)} %project.1), calls=%async_computation.2 | async-start | bytes 1310720 | tf_op jit(solution)/shard_map/all_to_all | solution.py:482
  51.0 5.7 %collective-permute-start.5 = (f32[160,256]{1,0:T(8,128)S(1)}, f32[160,256]{1,0:T(8,128)S(1)}, u32[]{:S(2)}, u32[]{:S(2)}) collective-permute-start(f32[160,256]{1,0:T(8,128)S(1)} %first_sums.1), channel_id=1, source_target_pairs={{0,1},{1,0},{2,3},{3,2},{4,5},{5,4},{6,7},{7,6},{8,9},{9,8},{10,11... | collective-permute-start | bytes 491528 | tf_op jit(solution)/shard_map/ppermute | solution.py:34
  56.7 1.5 %collective-permute-start.6 = (f32[160,256]{1,0:T(8,128)S(1)}, f32[160,256]{1,0:T(8,128)S(1)}, u32[]{:S(2)}, u32[]{:S(2)}) collective-permute-start(f32[160,256]{1,0:T(8,128)S(1)} %add.12.refs_0_), channel_id=1, source_target_pairs={{0,2},{2,0},{1,3},{3,1},{4,6},{6,4},{5,7},{7,5},{8,10},{10,8},{9,1... | collective-permute-start | bytes 491528 | tf_op jit(solution)/shard_map/ppermute | solution.py:34
  68.8 14.7 %all-to-all-start.3 = ((f32[16,4,8,128]{3,2,1,0:T(8,128)}), f32[16,4,8,128]{3,2,1,0:T(8,128)S(1)}, u32[]{:S(2)}, u32[]{:S(2)}) async-start(f32[16,4,8,128]{3,2,1,0:T(8,128)} %get-tuple-element.25), calls=%async_computation.3 | async-start | bytes 524288 | tf_op jit(solution)/shard_map/all_to_all | solution.py:493
  73.5 1.4 %collective-permute-start.7 = (f32[8,32,128]{2,1,0:T(8,128)S(1)}, f32[8,32,128]{2,1,0:T(8,128)S(1)}, u32[]{:S(2)}, u32[]{:S(2)}) collective-permute-start(f32[8,32,128]{2,1,0:T(8,128)S(1)} %get-tuple-element.26.refs_0_), channel_id=1, source_target_pairs={{0,2},{2,0},{1,3},{3,1},{4,6},{6,4},{5,7},{7,5},{8,10},{10,8},{9,1... | collective-permute-start | bytes 393224 | tf_op jit(solution)/shard_map/ppermute | solution.py:34

commit v12 on v9

--- a/solution.py
+++ b/solution.py
@@ -18,6 +18,11 @@
 COL_COL = (((0,), (0,)), ((), ()))
 
 
+def gather_bits(axis):
+    *bits, last = axis_bits(axis)
+    return [last, *bits]
+
+
 def axis_bits(axis):
     bit = lax.axis_size(axis) // 2
     while bit:
@@ -42,7 +47,7 @@
 
 def swap_order(axis):
     order = [0]
-    for bit in axis_bits(axis):
+    for bit in gather_bits(axis):
         order += [o ^ bit for o in order]
     return order
 
@@ -249,6 +254,7 @@
     return pl.pallas_call(
         inverse_kernel,
         out_shape=jax.ShapeDtypeStruct((rank, system_shares.shape[3]), jnp.float32),
+        cost_estimate=pl.CostEstimate(flops=5 * 10**9, bytes_accessed=0, transcendentals=0),
         compiler_params=pltpu.CompilerParams(vmem_limit_bytes=VMEM_BYTES),
         name="pseudo_inverse",
     )(system_shares)
@@ -287,6 +293,7 @@
         functools.partial(project_kernel, y_own),
         out_shape=jax.ShapeDtypeStruct((blocks, rows, rank), jnp.float32),
         scratch_shapes=[pltpu.VMEM((x_cells * y_cells, rank), jnp.float32)],
+        cost_estimate=pl.CostEstimate(flops=2 * 10**9, bytes_accessed=0, transcendentals=0),
         compiler_params=pltpu.CompilerParams(vmem_limit_bytes=VMEM_BYTES),
         name="project",
     )(pinv, extra, kept, *terms)
@@ -434,7 +441,7 @@
         axis=0,
     )[None]
     left_at = x_cells * cols // LANES
-    first_bit, *bits = axis_bits("gx")
+    first_bit, *bits = gather_bits("gx")
     packed = swap_step(packed, "gx", first_bit)
 
     group = ("gx", "gy")
@@ -452,14 +459,16 @@
         system = jnp.sum(system, axis=1).reshape(-1, 1, ROWS, cols)
 
     for bit in bits:
+        if bit == bits[-1]:
+            system = after(system, packed)
         packed = swap_step(packed, "gx", bit)
     sums = first_sums(left_at, first_part, packed)
     if own % ROWS:
         extra = jnp.zeros((ROWS, LANES), jnp.float32)
     else:
         extra = last_rows.reshape(own, -1, LANES).transpose(1, 0, 2).reshape(-1, LANES)
-    pinv = pseudo_inverse(after(system, packed, *terms))
-    projected = project(blocks, pinv, extra, kept, terms)
+    pinv = pseudo_inverse(after(system, *terms))
+    projected = after(project(blocks, pinv, extra, kept, terms), packed)
     sums = swap_sum(sums, "gz")
     sums = [swap(sums, "gy", y) if y else sums for y in range(lax.axis_size("gy"))]
 

time: 84.7 us -> 84.7 us (level)
  waiting for transfers between devices: 34.7 us -> 31.9 us
  starting transfers between devices: 27.3 us -> 30.1 us
    ppermute x8, waiting for transfers between devices: 21.5 us -> 17.5 us  [swap(): lax.ppermute(array, axis, [(s, s ^ bits) for s in range(lax.axis_size(axi...]
    all_to_all x1, waiting for transfers between devices: 0.01 us -> 1.79 us  [per_device(): lax.all_to_all(last_part.reshape(-1, own, m_cells), group, 0, 0, tiled=True)]
    ppermute x8, starting transfers between devices: 9.74 us -> 11.1 us  [swap(): lax.ppermute(array, axis, [(s, s ^ bits) for s in range(lax.axis_size(axi...]
    all_to_all x1, waiting for transfers between devices: 0.86 us -> 0.01 us  [per_device(): lax.all_to_all(copies, ALL, 0, 0, tiled=True).reshape(-1, shares, own, cols)]
  transfers between devices with their start and end apart: 12 -> 12, of which waited for: 9 -> 8; matrix products, arithmetic and copies ran while one was open for 4% -> 4% of each run, Pallas kernels for 7% -> 7%
where the time goes in v12:
time: 84.7 us; the launch traced here: 84.1 us
  waiting for transfers between devices  31.9 us (38%)
  starting transfers between devices  30.1 us (36%)
  Pallas kernels  17.2 us (20%)
  local copies, waits for them, and re-layouts  2.28 us (3%)
  matrix products  1.8 us (2%)
    ppermute x8, waiting for transfers between devices, swap(): lax.ppermute(array, axis, [(s, s ^ bits) for s in range(lax.axis_size(axi...  17.5 us
    ppermute x8, starting transfers between devices, swap(): lax.ppermute(array, axis, [(s, s ^ bits) for s in range(lax.axis_size(axi...  11.1 us
    all_to_all x1, waiting for transfers between devices, per_device(): received = lax.all_to_all(middle, group, 0, 0, tiled=True)  7.91 us
    all_to_all x1, starting transfers between devices, per_device(): lax.all_to_all(last_part.reshape(-1, own, m_cells), group, 0, 0, tiled=True)  5.91 us
    pallas_call x1, Pallas kernels, solve_first(): pl.pallas_call(first_kernel, out_shape=jax.ShapeDtypeStruct((x_cells, sum...  4.98 us
    all_to_all x1, waiting for transfers between devices, per_device(): pieces = lax.all_to_all(projected, 'gx', 0, 0, tiled=True)  4.68 us
    all_to_all x1, starting transfers between devices, per_device(): received = lax.all_to_all(middle, group, 0, 0, tiled=True)  4.67 us
    all_to_all x1, starting transfers between devices, per_device(): pieces = lax.all_to_all(projected, 'gx', 0, 0, tiled=True)  4.64 us
  transfers between devices with their start and end apart: 12, of which 8 were waited for; matrix products, arithmetic and copies ran while one was open for 4% of the time, Pallas kernels for 7%

profile of v12, /device:TPU:0, one launch (start us, length us, event | category | flops | bytes accessed | tf_op | source)
XLA Modules:
  0.0 84.1 jit_solution(10988363378614817312)
XLA Ops:
  0.6 0.0 copy-start.1
  0.6 0.0 copy-start.2
  0.7 4.2 %local_products.1 = (f32[128,512]{1,0:T(8,128)}, f32[32,256]{1,0:T(8,128)}, f32[16,32,256]{2,1,0:T(8,128)}, f32[16,32,256]{2,1,0:T(8,128)}) custom-call(bf16[32,64,512]{2,1,0:T(8,128)(2,1)} %field_hbm.1, bf16[32,128]{1,0:T(8,128)(2,1)} %last_x_hbm.1, bf16[64,128]{1,0:T(8,128)(2,1)} %last_y_hbm.1, bf16[64,256]{1,0:T(8,128)(2,1)} %right_y_hbm.1, ...), custom_call_target="tpu_custom_call" | custom-call | tf_op jit(solution)/shard_map/local_products/pallas_call | solution.py:210
  4.8 3.0 %collective-permute-start = (f32[16,32,256]{2,1,0:T(8,128)}, f32[16,32,256]{2,1,0:T(8,128)S(1)}, u32[]{:S(2)}, u32[]{:S(2)}) collective-permute-start(f32[16,32,256]{2,1,0:T(8,128)} %get-tuple-element.18), channel_id=1, source_target_pairs={{0,1},{1,0},{2,3},{3,2},{4,5},{5,4},{6,7},{7,6},{8,9},{9,8},{10,11... | collective-permute-start | bytes 1572872 | tf_op jit(solution)/shard_map/ppermute | solution.py:34
  7.9 5.9 %all-to-all-start = ((f32[16,8,512]{2,1,0:T(8,128)}), f32[16,8,512]{2,1,0:T(8,128)S(1)}, u32[]{:S(2)}, u32[]{:S(2)}) async-start(f32[16,8,512]{2,1,0:T(8,128)} %bitcast.35), calls=%async_computation | async-start | bytes 524288 | tf_op jit(solution)/shard_map/all_to_all | solution.py:449
  13.8 0.8 copy_bitcast_fusion
  14.5 0.0 copy-done.2
  14.6 2.0 %collective-permute-start.1 = (f32[1,96,128]{2,1,0:T(8,128)S(1)}, f32[1,96,128]{2,1,0:T(8,128)S(1)}, u32[]{:S(2)}, u32[]{:S(2)}) collective-permute-start(f32[1,96,128]{2,1,0:T(8,128)S(1)} %maximum_bitcast_fusion), channel_id=1, source_target_pairs={{0,4},{4,0},{8,12},{12,8},{16,20},{20,16},{24,28},{28,24},{1,5},{5... | collective-permute-start | bytes 147464 | tf_op jit(solution)/shard_map/ppermute | solution.py:34
  16.5 0.5 collective-permute-start.3
  17.1 0.0 copy-done.1
  17.1 1.7 %fusion.kept = f32[32,32,256]{2,1,0:T(8,128)S(1)} fusion(bf16[32,2,32,512]{3,2,1,0:T(8,128)(2,1)} %bitcast.33, s32[]{:T(128)S(6)} %select_n.4, bf16[512,256]{1,0:T(8,128)(2,1)S(1)} %copy-done.1), kind=kOutput, calls=%fused_computation | convolution fusion | flops 268435456 | bytes 2359300 | tf_op jit(solution)/shard_map/dot_general | solution.py:432
  18.7 1.2 %collective-permute-done.1 = f32[1,96,128]{2,1,0:T(8,128)S(1)} collective-permute-done((f32[1,96,128]{2,1,0:T(8,128)S(1)}, f32[1,96,128]{2,1,0:T(8,128)S(1)}, u32[]{:S(2)}, u32[]{:S(2)}) %collective-permute-start.1) | collective-permute-done | bytes 49184 | tf_op jit(solution)/shard_map/ppermute | solution.py:34
  20.0 2.1 %collective-permute-start.2 = (f32[2,96,128]{2,1,0:T(8,128)S(1)}, f32[2,96,128]{2,1,0:T(8,128)S(1)}, u32[]{:S(2)}, u32[]{:S(2)}) collective-permute-start(f32[2,96,128]{2,1,0:T(8,128)S(1)} %pad_maximum_fusion.2), channel_id=1, source_target_pairs={{0,16},{4,20},{8,24},{12,28},{16,0},{20,4},{24,8},{28,12},{1,17},{... | collective-permute-start | bytes 294920 | tf_op jit(solution)/shard_map/ppermute | solution.py:34
  22.0 1.8 %all-to-all-done = f32[16,8,512]{2,1,0:T(8,128)S(1)} async-done(((f32[16,8,512]{2,1,0:T(8,128)}), f32[16,8,512]{2,1,0:T(8,128)S(1)}, u32[]{:S(2)}, u32[]{:S(2)}) %all-to-all-start) | async-done | bytes 262176 | tf_op jit(solution)/shard_map/all_to_all | solution.py:449
  23.8 0.0 collective-permute-done.refs_0_
  23.9 0.1 fusion.5
  24.0 0.7 broadcast_in_dim.10
  24.8 3.7 %all-to-all-start.1 = ((f32[32,8,256]{2,1,0:T(8,128)}), f32[32,8,256]{2,1,0:T(8,128)S(1)}, u32[]{:S(2)}, u32[]{:S(2)}) async-start(f32[32,8,256]{2,1,0:T(8,128)} %broadcast_in_dim.10), calls=%async_computation.1 | async-start | bytes 524288 | tf_op jit(solution)/shard_map/all_to_all | solution.py:457
  28.5 0.0 collective-permute-done.2
  28.5 1.8 %collective-permute-start.4 = (f32[4,96,128]{2,1,0:T(8,128)S(1)}, f32[4,96,128]{2,1,0:T(8,128)S(1)}, u32[]{:S(2)}, u32[]{:S(2)}) collective-permute-start(f32[4,96,128]{2,1,0:T(8,128)S(1)} %pad_maximum_fusion.1), channel_id=1, source_target_pairs={{0,8},{4,12},{8,0},{12,4},{16,24},{20,28},{24,16},{28,20},{1,9},{5... | collective-permute-start | bytes 589832 | tf_op jit(solution)/shard_map/ppermute | solution.py:34
  30.4 9.4 %collective-permute-done.4 = f32[4,96,128]{2,1,0:T(8,128)S(1)} collective-permute-done((f32[4,96,128]{2,1,0:T(8,128)S(1)}, f32[4,96,128]{2,1,0:T(8,128)S(1)}, u32[]{:S(2)}, u32[]{:S(2)}) %collective-permute-start.4) | collective-permute-done | bytes 196640 | tf_op jit(solution)/shard_map/ppermute | solution.py:34
  39.8 0.0 all-to-all-done.1
  39.8 0.0 collective-permute-done.3.refs_1_
  39.8 4.3 %pseudo_inverse.1.pinv = f32[128,256]{1,0:T(8,128)S(1)} custom-call(f32[16,2,8,256]{3,2,1,0:T(8,128)S(1)} %bitcast.31), custom_call_target="tpu_custom_call" | custom-call | flops 5000000000 | tf_op jit(solution)/shard_map/pseudo_inverse/pallas_call | solution.py:254
  44.2 0.0 copy-start
  44.2 1.6 %project.1 = f32[8,160,128]{2,1,0:T(8,128)} custom-call(f32[128,256]{1,0:T(8,128)S(1)} %pseudo_inverse.1.pinv, f32[32,128]{1,0:T(8,128)S(1)} %bitcast.32, f32[32,32,256]{2,1,0:T(8,128)S(1)} %fusion.kept, f32[16,32,256]{2,1,0:T(8,128)S(1)} %collective-permute-done.refs_0_, f32[16,32,256]{2,1,0:T(8,128)S(1)} %collective-permute-done.3.refs_1_), custom_call_target="tpu_custom_call" | custom-call | flops 2000000000 | tf_op jit(solution)/shard_map/project/pallas_call | solution.py:292
  45.8 4.6 %all-to-all-start.2 = ((f32[8,160,128]{2,1,0:T(8,128)}), f32[8,160,128]{2,1,0:T(8,128)S(1)}, u32[]{:S(2)}, u32[]{:S(2)}) async-start(f32[8,160,128]{2,1,0:T(8,128)} %project.1), calls=%async_computation.2 | async-start | bytes 1310720 | tf_op jit(solution)/shard_map/all_to_all | solution.py:475
  50.4 0.0 copy-done
  50.4 0.4 first_sums.1
  50.8 1.5 %collective-permute-start.5 = (f32[160,256]{1,0:T(8,128)S(1)}, f32[160,256]{1,0:T(8,128)S(1)}, u32[]{:S(2)}, u32[]{:S(2)}) collective-permute-start(f32[160,256]{1,0:T(8,128)S(1)} %first_sums.1), channel_id=1, source_target_pairs={{0,1},{1,0},{2,3},{3,2},{4,5},{5,4},{6,7},{7,6},{8,9},{9,8},{10,11... | collective-permute-start | bytes 491528 | tf_op jit(solution)/shard_map/ppermute | solution.py:34
  52.3 4.1 %collective-permute-done.5 = f32[160,256]{1,0:T(8,128)S(1)} collective-permute-done((f32[160,256]{1,0:T(8,128)S(1)}, f32[160,256]{1,0:T(8,128)S(1)}, u32[]{:S(2)}, u32[]{:S(2)}) %collective-permute-start.5) | collective-permute-done | bytes 163872 | tf_op jit(solution)/shard_map/ppermute | solution.py:34
  56.5 0.1 collective-permute-start.6
  56.6 1.4 %collective-permute-done.6.refs_1_ = f32[160,256]{1,0:T(8,128)S(1)} collective-permute-done((f32[160,256]{1,0:T(8,128)S(1)}, f32[160,256]{1,0:T(8,128)S(1)}, u32[]{:S(2)}, u32[]{:S(2)}) %collective-permute-start.6) | collective-permute-done | bytes 163872 | tf_op jit(solution)/shard_map/ppermute | solution.py:34
  58.0 5.0 %solve_first.1 = f32[32,128]{1,0:T(8,128)} custom-call(f32[160,256]{1,0:T(8,128)S(1)} %add.12.refs_0_, f32[160,256]{1,0:T(8,128)S(1)} %collective-permute-done.6.refs_1_), custom_call_target="tpu_custom_call" | custom-call | tf_op jit(solution)/shard_map/solve_first/pallas_call | solution.py:384
  62.9 4.7 %all-to-all-done.2.pieces = f32[8,160,128]{2,1,0:T(8,128)S(1)} async-done(((f32[8,160,128]{2,1,0:T(8,128)}), f32[8,160,128]{2,1,0:T(8,128)S(1)}, u32[]{:S(2)}, u32[]{:S(2)}) %all-to-all-start.2) | async-done | bytes 655392 | tf_op jit(solution)/shard_map/all_to_all | solution.py:475
  67.6 1.0 %sketch.1 = (f32[16,4,8,128]{3,2,1,0:T(8,128)}, f32[8,32,128]{2,1,0:T(8,128)S(1)}) custom-call(f32[8,160,128]{2,1,0:T(8,128)S(1)} %all-to-all-done.2.pieces, f32[8,96,128]{2,1,0:T(8,128)S(1)} %pad_maximum_fusion.packed), custom_call_target="tpu_custom_call" | custom-call | tf_op jit(solution)/shard_map/sketch/pallas_call | solution.py:329
  68.6 4.7 %all-to-all-start.3 = ((f32[16,4,8,128]{3,2,1,0:T(8,128)}), f32[16,4,8,128]{3,2,1,0:T(8,128)S(1)}, u32[]{:S(2)}, u32[]{:S(2)}) async-start(f32[16,4,8,128]{3,2,1,0:T(8,128)} %get-tuple-element.29), calls=%async_computation.3 | async-start | bytes 524288 | tf_op jit(solution)/shard_map/all_to_all | solution.py:486
  73.3 0.1 collective-permute-start.7
  73.3 1.3 %collective-permute-done.7.refs_1_ = f32[8,32,128]{2,1,0:T(8,128)S(1)} collective-permute-done((f32[8,32,128]{2,1,0:T(8,128)S(1)}, f32[8,32,128]{2,1,0:T(8,128)S(1)}, u32[]{:S(2)}, u32[]{:S(2)}) %collective-permute-start.7) | collective-permute-done | bytes 131104 | tf_op jit(solution)/shard_map/ppermute | solution.py:34
  74.7 0.7 place.1
  75.4 7.9 %all-to-all-done.3 = f32[16,4,8,128]{3,2,1,0:T(8,128)S(1)} async-done(((f32[16,4,8,128]{3,2,1,0:T(8,128)}), f32[16,4,8,128]{3,2,1,0:T(8,128)S(1)}, u32[]{:S(2)}, u32[]{:S(2)}) %all-to-all-start.3) | async-done | bytes 262176 | tf_op jit(solution)/shard_map/all_to_all | solution.py:486
  83.3 0.8 copy.12
  (9 shorter events, 0.1 us)
Async XLA Ops:
  0.6 16.4 %copy-start.1 = (bf16[512,256]{1,0:T(8,128)(2,1)S(1)}, bf16[512,256]{1,0:T(8,128)(2,1)}, u32[]{:S(2)}) copy-start(bf16[512,256]{1,0:T(8,128)(2,1)} %last_m_hbm.1) | copy-start | bytes 786436
  0.6 13.9 %copy-start.2 = (bf16[32,128]{1,0:T(8,128)(2,1)S(1)}, bf16[32,128]{1,0:T(8,128)(2,1)}, u32[]{:S(2)}) copy-start(bf16[32,128]{1,0:T(8,128)(2,1)} %param.8) | copy-start | bytes 24580
  4.8 19.0 %collective-permute-start = (f32[16,32,256]{2,1,0:T(8,128)}, f32[16,32,256]{2,1,0:T(8,128)S(1)}, u32[]{:S(2)}, u32[]{:S(2)}) collective-permute-start(f32[16,32,256]{2,1,0:T(8,128)} %get-tuple-element.18), channel_id=1, source_target_pairs={{0,1},{1,0},{2,3},{3,2},{4,5},{5,4},{6,7},{7,6},{8,9},{9,8},{10,11... | collective-permute-start | bytes 1572872 | tf_op jit(solution)/shard_map/ppermute | solution.py:34
  7.9 16.0 %all-to-all-start = ((f32[16,8,512]{2,1,0:T(8,128)}), f32[16,8,512]{2,1,0:T(8,128)S(1)}, u32[]{:S(2)}, u32[]{:S(2)}) async-start(f32[16,8,512]{2,1,0:T(8,128)} %bitcast.35), calls=%async_computation | async-start | bytes 524288 | tf_op jit(solution)/shard_map/all_to_all | solution.py:449
  14.6 5.4 %collective-permute-start.1 = (f32[1,96,128]{2,1,0:T(8,128)S(1)}, f32[1,96,128]{2,1,0:T(8,128)S(1)}, u32[]{:S(2)}, u32[]{:S(2)}) collective-permute-start(f32[1,96,128]{2,1,0:T(8,128)S(1)} %maximum_bitcast_fusion), channel_id=1, source_target_pairs={{0,4},{4,0},{8,12},{12,8},{16,20},{20,16},{24,28},{28,24},{1,5},{5... | collective-permute-start | bytes 147464 | tf_op jit(solution)/shard_map/ppermute | solution.py:34
  16.5 23.3 %collective-permute-start.3 = (f32[16,32,256]{2,1,0:T(8,128)}, f32[16,32,256]{2,1,0:T(8,128)S(1)}, u32[]{:S(2)}, u32[]{:S(2)}) collective-permute-start(f32[16,32,256]{2,1,0:T(8,128)} %get-tuple-element.23), channel_id=1, source_target_pairs={{0,1},{1,0},{2,3},{3,2},{4,5},{5,4},{6,7},{7,6},{8,9},{9,8},{10,11... | collective-permute-start | bytes 1572872 | tf_op jit(solution)/shard_map/ppermute | solution.py:34
  20.0 8.5 %collective-permute-start.2 = (f32[2,96,128]{2,1,0:T(8,128)S(1)}, f32[2,96,128]{2,1,0:T(8,128)S(1)}, u32[]{:S(2)}, u32[]{:S(2)}) collective-permute-start(f32[2,96,128]{2,1,0:T(8,128)S(1)} %pad_maximum_fusion.2), channel_id=1, source_target_pairs={{0,16},{4,20},{8,24},{12,28},{16,0},{20,4},{24,8},{28,12},{1,17},{... | collective-permute-start | bytes 294920 | tf_op jit(solution)/shard_map/ppermute | solution.py:34
  24.8 15.1 %all-to-all-start.1 = ((f32[32,8,256]{2,1,0:T(8,128)}), f32[32,8,256]{2,1,0:T(8,128)S(1)}, u32[]{:S(2)}, u32[]{:S(2)}) async-start(f32[32,8,256]{2,1,0:T(8,128)} %broadcast_in_dim.10), calls=%async_computation.1 | async-start | bytes 524288 | tf_op jit(solution)/shard_map/all_to_all | solution.py:457
  28.5 11.3 %collective-permute-start.4 = (f32[4,96,128]{2,1,0:T(8,128)S(1)}, f32[4,96,128]{2,1,0:T(8,128)S(1)}, u32[]{:S(2)}, u32[]{:S(2)}) collective-permute-start(f32[4,96,128]{2,1,0:T(8,128)S(1)} %pad_maximum_fusion.1), channel_id=1, source_target_pairs={{0,8},{4,12},{8,0},{12,4},{16,24},{20,28},{24,16},{28,20},{1,9},{5... | collective-permute-start | bytes 589832 | tf_op jit(solution)/shard_map/ppermute | solution.py:34
  44.2 6.2 %copy-start = (f32[32,256]{1,0:T(8,128)S(1)}, f32[32,256]{1,0:T(8,128)}, u32[]{:S(2)}) copy-start(f32[32,256]{1,0:T(8,128)} %get-tuple-element.20.rows) | copy-start | bytes 98308
  45.8 21.9 %all-to-all-start.2 = ((f32[8,160,128]{2,1,0:T(8,128)}), f32[8,160,128]{2,1,0:T(8,128)S(1)}, u32[]{:S(2)}, u32[]{:S(2)}) async-start(f32[8,160,128]{2,1,0:T(8,128)} %project.1), calls=%async_computation.2 | async-start | bytes 1310720 | tf_op jit(solution)/shard_map/all_to_all | solution.py:475
  50.8 5.7 %collective-permute-start.5 = (f32[160,256]{1,0:T(8,128)S(1)}, f32[160,256]{1,0:T(8,128)S(1)}, u32[]{:S(2)}, u32[]{:S(2)}) collective-permute-start(f32[160,256]{1,0:T(8,128)S(1)} %first_sums.1), channel_id=1, source_target_pairs={{0,1},{1,0},{2,3},{3,2},{4,5},{5,4},{6,7},{7,6},{8,9},{9,8},{10,11... | collective-permute-start | bytes 491528 | tf_op jit(solution)/shard_map/ppermute | solution.py:34
  56.5 1.5 %collective-permute-start.6 = (f32[160,256]{1,0:T(8,128)S(1)}, f32[160,256]{1,0:T(8,128)S(1)}, u32[]{:S(2)}, u32[]{:S(2)}) collective-permute-start(f32[160,256]{1,0:T(8,128)S(1)} %add.12.refs_0_), channel_id=1, source_target_pairs={{0,2},{2,0},{1,3},{3,1},{4,6},{6,4},{5,7},{7,5},{8,10},{10,8},{9,1... | collective-permute-start | bytes 491528 | tf_op jit(solution)/shard_map/ppermute | solution.py:34
  68.6 14.7 %all-to-all-start.3 = ((f32[16,4,8,128]{3,2,1,0:T(8,128)}), f32[16,4,8,128]{3,2,1,0:T(8,128)S(1)}, u32[]{:S(2)}, u32[]{:S(2)}) async-start(f32[16,4,8,128]{3,2,1,0:T(8,128)} %get-tuple-element.29), calls=%async_computation.3 | async-start | bytes 524288 | tf_op jit(solution)/shard_map/all_to_all | solution.py:486
  73.3 1.4 %collective-permute-start.7 = (f32[8,32,128]{2,1,0:T(8,128)S(1)}, f32[8,32,128]{2,1,0:T(8,128)S(1)}, u32[]{:S(2)}, u32[]{:S(2)}) collective-permute-start(f32[8,32,128]{2,1,0:T(8,128)S(1)} %get-tuple-element.30.refs_0_), channel_id=1, source_target_pairs={{0,2},{2,0},{1,3},{3,1},{4,6},{6,4},{5,7},{7,5},{8,10},{10,8},{9,1... | collective-permute-start | bytes 393224 | tf_op jit(solution)/shard_map/ppermute | solution.py:34

commit v13 on v10

--- a/solution.py
+++ b/solution.py
@@ -18,6 +18,11 @@
 COL_COL = (((0,), (0,)), ((), ()))
 
 
+def gather_bits(axis):
+    *bits, last = axis_bits(axis)
+    return [last, *bits]
+
+
 def axis_bits(axis):
     bit = lax.axis_size(axis) // 2
     while bit:
@@ -42,7 +47,7 @@
 
 def swap_order(axis):
     order = [0]
-    for bit in axis_bits(axis):
+    for bit in gather_bits(axis):
         order += [o ^ bit for o in order]
     return order
 
@@ -249,6 +254,7 @@
     return pl.pallas_call(
         inverse_kernel,
         out_shape=jax.ShapeDtypeStruct((rank, system_shares.shape[3]), jnp.float32),
+        cost_estimate=pl.CostEstimate(flops=5 * 10**9, bytes_accessed=0, transcendentals=0),
         compiler_params=pltpu.CompilerParams(vmem_limit_bytes=VMEM_BYTES),
         name="pseudo_inverse",
     )(system_shares)
@@ -286,23 +292,17 @@
         functools.partial(project_kernel, y_own),
         out_shape=jax.ShapeDtypeStruct((blocks, rows, rank), jnp.float32),
         scratch_shapes=[pltpu.VMEM((x_cells * y_cells, rank), jnp.float32)],
+        cost_estimate=pl.CostEstimate(flops=2 * 10**9, bytes_accessed=0, transcendentals=0),
         compiler_params=pltpu.CompilerParams(vmem_limit_bytes=VMEM_BYTES),
         name="project",
     )(pinv, kept, *terms)
 
 
-def packed_units(packed, unit):
-    return [(k, n * unit) for k in range(packed.shape[0]) for n in range(2)]
-
-
-def sketch_kernel(order, left_at, unit, pieces, packed, out):
+def sketch_kernel(order, pieces, left, out):
     me = lax.axis_index("gx")
     _, rows, cols = pieces.shape
-    x_cells = unit - left_at
-    weights = jnp.concatenate(
-        [packed[k, at + left_at : at + unit] for k, at in packed_units(packed, unit)], axis=0
-    )
-    weights = weights.astype(jnp.bfloat16)
+    blocks, x_cells, _ = left.shape
+    weights = jnp.concatenate([left[k] for k in range(blocks)], axis=0).astype(jnp.bfloat16)
     for j in range(rows // x_cells):
         column = jnp.concatenate(
             [pieces[me ^ o, j * x_cells : (j + 1) * x_cells] for o in order], axis=0
@@ -317,48 +317,52 @@
         out[:, j] = both.reshape(out.shape[0], out.shape[2], cols)
 
 
-def sketch(order, left_at, unit, own, pieces, packed):
+def sketch(order, own, pieces, left):
     _, rows, cols = pieces.shape
-    rank = packed.shape[2]
-    y_own = rows // (unit - left_at)
-    return pl.pallas_call(
-        functools.partial(sketch_kernel, order, left_at, unit),
-        out_shape=jax.ShapeDtypeStruct((rank // own, y_own, own, cols), jnp.float32),
+    _, x_cells, rank = left.shape
+    return pl.pallas_call(
+        functools.partial(sketch_kernel, order),
+        out_shape=jax.ShapeDtypeStruct((rank // own, rows // x_cells, own, cols), jnp.float32),
         compiler_params=pltpu.CompilerParams(vmem_limit_bytes=VMEM_BYTES),
         name="sketch",
-    )(pieces, packed)
-
-
-def first_sums_kernel(left_at, unit, rows, packed, sums, extra):
+    )(pieces, left)
+
+
+def first_sums_kernel(rows, left, mine, other, sums, extra):
     x_cells, cols = rows.shape
-    units = packed_units(packed, unit)
-    left = jnp.concatenate([packed[k, at + left_at : at + unit] for k, at in units], axis=0)
+    blocks = left.shape[0]
+    height = x_cells * cols // LANES
+    left_all = jnp.concatenate([left[k] for k in range(blocks)], axis=0)
     sums[:x_cells] = rows[...]
     for c in range(cols // LANES):
-        first = c * x_cells
+        at = [k * height + c * x_cells for k in range(blocks // 2)]
         sums[x_cells:, c * LANES : (c + 1) * LANES] = lax.dot_general(
-            left,
-            jnp.concatenate(
-                [packed[k, at + first : at + first + x_cells] for k, at in units], axis=0
-            ),
+            left_all,
+            jnp.concatenate([part[a : a + x_cells] for part in (mine, other) for a in at], axis=0),
             COL_COL,
             precision=HIGHEST,
             preferred_element_type=jnp.float32,
         )
-    extra[...] = packed[:, 2 * unit :]
-
-
-def first_sums(left_at, unit, rows, packed):
-    entries, height, rank = packed.shape
-    return pl.pallas_call(
-        functools.partial(first_sums_kernel, left_at, unit),
+    count = blocks // 4
+    deep = extra.shape[1]
+    for n, part in enumerate((mine, other)):
+        for k in range(count):
+            at = blocks // 2 * height + k * deep
+            extra[n * count + k] = part[at : at + deep]
+
+
+def first_sums(rows, left, mine, other):
+    blocks, x_cells, rank = left.shape
+    deep = (mine.shape[0] - blocks // 2 * x_cells * rows.shape[1] // LANES) // (blocks // 4)
+    return pl.pallas_call(
+        first_sums_kernel,
         out_shape=(
             jax.ShapeDtypeStruct((rows.shape[0] + rank, rows.shape[1]), jnp.float32),
-            jax.ShapeDtypeStruct((entries, height - 2 * unit, rank), jnp.float32),
+            jax.ShapeDtypeStruct((blocks // 2, deep, rank), jnp.float32),
         ),
         compiler_params=pltpu.CompilerParams(vmem_limit_bytes=VMEM_BYTES),
         name="first_sums",
-    )(rows, packed)
+    )(rows, left, mine, other)
 
 
 def first_kernel(*refs):
@@ -430,16 +434,17 @@
     kept = jnp.dot(kept, last_m, preferred_element_type=jnp.float32)
     kept = kept.reshape(x_cells, y_share, cols)
 
+    order = swap_order("gx")
     packed = jnp.concatenate(
         [
             first_part.reshape(x_cells, -1, LANES).transpose(1, 0, 2).reshape(-1, LANES),
             left_x.astype(jnp.float32),
         ],
         axis=0,
-    )
-    unit = packed.shape[0]
-    left_at = unit - x_cells
-    packed = jnp.concatenate([packed, swap(packed, "gx", 1)], axis=0)
+    )[None]
+    left_at = x_cells * cols // LANES
+    first_bit, *bits = gather_bits("gx")
+    packed = swap_step(packed, "gx", first_bit)
 
     group = ("gx", "gy")
     own = rank // lax.axis_size(group)
@@ -455,23 +460,29 @@
     if own % ROWS:
         system = jnp.sum(system, axis=1).reshape(-1, 1, ROWS, cols)
 
+    *middle_bits, last_bit = bits
+    for bit in middle_bits:
+        packed = swap_step(packed, "gx", bit)
+    left_all = swap_step(packed[:, left_at:], "gx", last_bit)
+
     if own % ROWS:
         extra = jnp.zeros((ROWS, LANES), jnp.float32)
     else:
         extra = last_rows.reshape(own, -1, LANES).transpose(1, 0, 2).reshape(-1, LANES)
-    packed = jnp.concatenate([packed, extra], axis=0)[None]
-    *bits, _ = axis_bits("gx")
+    extra = extra[None]
     others = [0]
-    for bit in bits:
-        if bit == bits[-1]:
-            system = after(system, packed)
-        packed = swap_step(packed, "gx", bit)
+    for bit in middle_bits:
+        extra = swap_step(extra, "gx", bit)
         others += [o ^ bit for o in others]
-    order = [o ^ n for o in others for n in range(2)]
-
-    pinv = pseudo_inverse(after(system, *terms))
-    projected = after(project(blocks, pinv, kept, terms), packed)
-    sums, extra = first_sums(left_at, unit, first_part, packed)
+    others += [o ^ last_bit for o in others]
+    mine = jnp.concatenate(
+        [packed[:, :left_at].reshape(-1, LANES), extra.reshape(-1, LANES)], axis=0
+    )
+    system = after(system, left_all, *terms)
+    other = swap(after(mine, system), "gx", last_bit)
+    pinv = pseudo_inverse(system)
+    projected = project(blocks, pinv, kept, terms)
+    sums, extra = first_sums(first_part, left_all, mine, other)
     sums = swap_sum(sums, "gz")
     sums = [swap(sums, "gy", y) if y else sums for y in range(lax.axis_size("gy"))]
 
@@ -480,10 +491,10 @@
     devices = lax.axis_size(group)
     rank_own = rank // devices
     if rank_own % ROWS:
-        middle = sketch(order, left_at, unit, rank, pieces, packed)
+        middle = sketch(order, rank, pieces, left_all)
         middle = middle.reshape(y_own, devices, rank_own, rank).transpose(1, 0, 2, 3)
     else:
-        middle = sketch(order, left_at, unit, rank_own, pieces, packed)
+        middle = sketch(order, rank_own, pieces, left_all)
     extra = jnp.concatenate([extra, swap(extra, "gx", 1)], axis=0)
     middle = after(middle, extra, *sums)
     received = lax.all_to_all(middle, group, 0, 0, tiled=True)

time: 88.7 us -> 105 us (1.18)
  waiting for transfers between devices: 33.3 us -> 47.3 us
  starting transfers between devices: 32.7 us -> 34.6 us
    ppermute x9 -> x11, waiting for transfers between devices: 21 us -> 40.9 us  [swap(): lax.ppermute(array, axis, [(s, s ^ bits) for s in range(lax.axis_size(axi...]
    all_to_all x1, waiting for transfers between devices: 5.76 us -> 0.01 us  [per_device(): pieces = lax.all_to_all(projected, 'gx', 0, 0, tiled=True)]
    all_to_all x1, starting transfers between devices: 3.68 us -> 5.91 us  [per_device(): lax.all_to_all(copies, ALL, 0, 0, tiled=True).reshape(-1, shares, own, cols)]
    ppermute x9 -> x11, starting transfers between devices: 12.3 us -> 12.9 us  [swap(): lax.ppermute(array, axis, [(s, s ^ bits) for s in range(lax.axis_size(axi...]
  transfers between devices with their start and end apart: 13 -> 15, of which waited for: 8 -> 12; matrix products, arithmetic and copies ran while one was open for 4% -> 3% of each run, Pallas kernels for 8% -> 7%
where the time goes in v13:
time: 105 us; the launch traced here: 104 us
  waiting for transfers between devices  47.3 us (45%)
  starting transfers between devices  34.6 us (33%)
  Pallas kernels  17.1 us (16%)
  local copies, waits for them, and re-layouts  2.29 us (2%)
  matrix products  1.81 us (2%)
    ppermute x11, waiting for transfers between devices, swap(): lax.ppermute(array, axis, [(s, s ^ bits) for s in range(lax.axis_size(axi...  40.9 us
    ppermute x11, starting transfers between devices, swap(): lax.ppermute(array, axis, [(s, s ^ bits) for s in range(lax.axis_size(axi...  12.9 us
    all_to_all x1, starting transfers between devices, per_device(): lax.all_to_all(last_part.reshape(-1, own, m_cells), group, 0, 0, tiled=True)  7.37 us
    all_to_all x1, starting transfers between devices, per_device(): lax.all_to_all(copies, ALL, 0, 0, tiled=True).reshape(-1, shares, own, cols)  5.91 us
    pallas_call x1, Pallas kernels, solve_first(): pl.pallas_call(first_kernel, out_shape=jax.ShapeDtypeStruct((x_cells, sum...  4.98 us
    all_to_all x1, starting transfers between devices, per_device(): received = lax.all_to_all(middle, group, 0, 0, tiled=True)  4.79 us
    pallas_call x1, Pallas kernels, pseudo_inverse(): pl.pallas_call(inverse_kernel, out_shape=jax.ShapeDtypeStruct((rank, syst...  4.34 us
    pallas_call x1, Pallas kernels, local_products(): pl.pallas_call(functools.partial(local_kernel, chunks, shares), in_specs=...  4.17 us
  transfers between devices with their start and end apart: 15, of which 12 were waited for; matrix products, arithmetic and copies ran while one was open for 3% of the time, Pallas kernels for 7%

profile of v13, /device:TPU:0, one launch (start us, length us, event | category | flops | bytes accessed | tf_op | source)
XLA Modules:
  0.0 104.1 jit_solution(7017111483581326505)
XLA Ops:
  0.6 0.0 copy-start.1
  0.6 0.0 copy-start.2
  0.7 4.2 %local_products.1 = (f32[128,512]{1,0:T(8,128)}, f32[32,256]{1,0:T(8,128)}, f32[16,32,256]{2,1,0:T(8,128)}, f32[16,32,256]{2,1,0:T(8,128)}) custom-call(bf16[32,64,512]{2,1,0:T(8,128)(2,1)} %field_hbm.1, bf16[32,128]{1,0:T(8,128)(2,1)} %last_x_hbm.1, bf16[64,128]{1,0:T(8,128)(2,1)} %last_y_hbm.1, bf16[64,256]{1,0:T(8,128)(2,1)} %right_y_hbm.1, ...), custom_call_target="tpu_custom_call" | custom-call | tf_op jit(solution)/shard_map/local_products/pallas_call | solution.py:210
  4.8 7.4 %all-to-all-start = ((f32[16,8,512]{2,1,0:T(8,128)}), f32[16,8,512]{2,1,0:T(8,128)S(1)}, u32[]{:S(2)}, u32[]{:S(2)}) async-start(f32[16,8,512]{2,1,0:T(8,128)} %bitcast.37), calls=%async_computation | async-start | bytes 524288 | tf_op jit(solution)/shard_map/all_to_all | solution.py:451
  12.2 1.6 %collective-permute-start.3 = (f32[16,32,256]{2,1,0:T(8,128)}, f32[16,32,256]{2,1,0:T(8,128)S(1)}, u32[]{:S(2)}, u32[]{:S(2)}) collective-permute-start(f32[16,32,256]{2,1,0:T(8,128)} %get-tuple-element.17), channel_id=1, source_target_pairs={{0,1},{1,0},{2,3},{3,2},{4,5},{5,4},{6,7},{7,6},{8,9},{9,8},{10,11... | collective-permute-start | bytes 1572872 | tf_op jit(solution)/shard_map/ppermute | solution.py:34
  13.8 0.8 copy_bitcast_fusion
  14.5 0.0 copy-done.2
  14.6 1.9 %collective-permute-start = (f32[1,96,128]{2,1,0:T(8,128)S(1)}, f32[1,96,128]{2,1,0:T(8,128)S(1)}, u32[]{:S(2)}, u32[]{:S(2)}) collective-permute-start(f32[1,96,128]{2,1,0:T(8,128)S(1)} %maximum_bitcast_fusion), channel_id=1, source_target_pairs={{0,4},{4,0},{8,12},{12,8},{16,20},{20,16},{24,28},{28,24},{1,5},{5... | collective-permute-start | bytes 147464 | tf_op jit(solution)/shard_map/ppermute | solution.py:34
  16.5 0.5 collective-permute-start.5
  17.0 0.0 copy-done.1
  17.0 1.7 %fusion.kept = f32[32,32,256]{2,1,0:T(8,128)S(1)} fusion(bf16[32,2,32,512]{3,2,1,0:T(8,128)(2,1)} %bitcast.34, s32[]{:T(128)S(6)} %select_n.4, bf16[512,256]{1,0:T(8,128)(2,1)S(1)} %copy-done.1), kind=kOutput, calls=%fused_computation | convolution fusion | flops 268435456 | bytes 2359300 | tf_op jit(solution)/shard_map/dot_general | solution.py:434
  18.7 0.2 collective-permute-done
  18.9 3.4 %all-to-all-done = f32[16,8,512]{2,1,0:T(8,128)S(1)} async-done(((f32[16,8,512]{2,1,0:T(8,128)}), f32[16,8,512]{2,1,0:T(8,128)S(1)}, u32[]{:S(2)}, u32[]{:S(2)}) %all-to-all-start) | async-done | bytes 262176 | tf_op jit(solution)/shard_map/all_to_all | solution.py:451
  22.3 5.0 %collective-permute-done.3.refs_0_ = f32[16,32,256]{2,1,0:T(8,128)S(1)} collective-permute-done((f32[16,32,256]{2,1,0:T(8,128)}, f32[16,32,256]{2,1,0:T(8,128)S(1)}, u32[]{:S(2)}, u32[]{:S(2)}) %collective-permute-start.3) | collective-permute-done | bytes 524320 | tf_op jit(solution)/shard_map/ppermute | solution.py:34
  27.3 0.1 fusion.5
  27.4 0.7 broadcast_in_dim.10
  28.1 5.9 %all-to-all-start.1 = ((f32[32,8,256]{2,1,0:T(8,128)}), f32[32,8,256]{2,1,0:T(8,128)S(1)}, u32[]{:S(2)}, u32[]{:S(2)}) async-start(f32[32,8,256]{2,1,0:T(8,128)} %broadcast_in_dim.10), calls=%async_computation.1 | async-start | bytes 524288 | tf_op jit(solution)/shard_map/all_to_all | solution.py:459
  34.1 2.7 %collective-permute-start.1 = (f32[2,96,128]{2,1,0:T(8,128)S(1)}, f32[2,96,128]{2,1,0:T(8,128)S(1)}, u32[]{:S(2)}, u32[]{:S(2)}) collective-permute-start(f32[2,96,128]{2,1,0:T(8,128)S(1)} %pad_maximum_fusion.4), channel_id=1, source_target_pairs={{0,16},{4,20},{8,24},{12,28},{16,0},{20,4},{24,8},{28,12},{1,17},{... | collective-permute-start | bytes 294920 | tf_op jit(solution)/shard_map/ppermute | solution.py:34
  36.8 10.9 %collective-permute-done.1 = f32[2,96,128]{2,1,0:T(8,128)S(1)} collective-permute-done((f32[2,96,128]{2,1,0:T(8,128)S(1)}, f32[2,96,128]{2,1,0:T(8,128)S(1)}, u32[]{:S(2)}, u32[]{:S(2)}) %collective-permute-start.1) | collective-permute-done | bytes 98336 | tf_op jit(solution)/shard_map/ppermute | solution.py:34
  47.7 0.0 collective-permute-start.2
  47.7 4.3 %collective-permute-done.2 = f32[4,32,128]{2,1,0:T(8,128)S(1)} collective-permute-done((f32[4,32,128]{2,1,0:T(8,128)S(1)}, f32[4,32,128]{2,1,0:T(8,128)S(1)}, u32[]{:S(2)}, u32[]{:S(2)}) %collective-permute-start.2) | collective-permute-done | bytes 65568 | tf_op jit(solution)/shard_map/ppermute | solution.py:34
  51.9 0.0 collective-permute-done.5.refs_1_
  52.0 0.0 all-to-all-done.1
  52.0 4.3 %pseudo_inverse.1.pinv = f32[128,256]{1,0:T(8,128)S(1)} custom-call(f32[16,2,8,256]{3,2,1,0:T(8,128)S(1)} %bitcast.33), custom_call_target="tpu_custom_call" | custom-call | flops 5000000000 | tf_op jit(solution)/shard_map/pseudo_inverse/pallas_call | solution.py:254
  56.3 0.0 copy-start
  56.3 1.5 %project.1 = f32[8,128,128]{2,1,0:T(8,128)} custom-call(f32[128,256]{1,0:T(8,128)S(1)} %pseudo_inverse.1.pinv, f32[32,32,256]{2,1,0:T(8,128)S(1)} %fusion.kept, f32[16,32,256]{2,1,0:T(8,128)S(1)} %collective-permute-done.3.refs_0_, f32[16,32,256]{2,1,0:T(8,128)S(1)} %collective-permute-done.5.refs_1_), custom_call_target="tpu_custom_call" | custom-call | flops 2000000000 | tf_op jit(solution)/shard_map/project/pallas_call | solution.py:291
  57.8 3.6 %all-to-all-start.2 = ((f32[8,128,128]{2,1,0:T(8,128)}), f32[8,128,128]{2,1,0:T(8,128)S(1)}, u32[]{:S(2)}, u32[]{:S(2)}) async-start(f32[8,128,128]{2,1,0:T(8,128)} %project.1), calls=%async_computation.2 | async-start | bytes 1048576 | tf_op jit(solution)/shard_map/all_to_all | solution.py:489
  61.5 2.9 %collective-permute-start.4 = (f32[1,32,128]{2,1,0:T(8,128)S(1)}, f32[1,32,128]{2,1,0:T(8,128)S(1)}, u32[]{:S(2)}, u32[]{:S(2)}) collective-permute-start(f32[1,32,128]{2,1,0:T(8,128)S(1)} %bitcast.39), channel_id=1, source_target_pairs={{0,16},{4,20},{8,24},{12,28},{16,0},{20,4},{24,8},{28,12},{1,17},{... | collective-permute-start | bytes 49160 | tf_op jit(solution)/shard_map/ppermute | solution.py:34
  64.4 11.2 %collective-permute-done.4 = f32[1,32,128]{2,1,0:T(8,128)S(1)} collective-permute-done((f32[1,32,128]{2,1,0:T(8,128)S(1)}, f32[1,32,128]{2,1,0:T(8,128)S(1)}, u32[]{:S(2)}, u32[]{:S(2)}) %collective-permute-start.4) | collective-permute-done | bytes 16416 | tf_op jit(solution)/shard_map/ppermute | solution.py:34
  75.6 0.1 collective-permute-start.6
  75.7 5.3 %collective-permute-done.6.other = f32[320,128]{1,0:T(8,128)S(1)} collective-permute-done((f32[320,128]{1,0:T(8,128)S(1)}, f32[320,128]{1,0:T(8,128)S(1)}, u32[]{:S(2)}, u32[]{:S(2)}) %collective-permute-start.6) | collective-permute-done | bytes 163872 | tf_op jit(solution)/shard_map/ppermute | solution.py:34
  81.0 0.0 copy-done
  81.0 0.4 first_sums.1
  81.4 1.5 %collective-permute-start.7 = (f32[160,256]{1,0:T(8,128)S(1)}, f32[160,256]{1,0:T(8,128)S(1)}, u32[]{:S(2)}, u32[]{:S(2)}) collective-permute-start(f32[160,256]{1,0:T(8,128)S(1)} %get-tuple-element.23), channel_id=1, source_target_pairs={{0,1},{1,0},{2,3},{3,2},{4,5},{5,4},{6,7},{7,6},{8,9},{9,8},{10,11... | collective-permute-start | bytes 491528 | tf_op jit(solution)/shard_map/ppermute | solution.py:34
  83.0 1.5 %collective-permute-start.8 = (f32[4,32,128]{2,1,0:T(8,128)S(1)}, f32[4,32,128]{2,1,0:T(8,128)S(1)}, u32[]{:S(2)}, u32[]{:S(2)}) collective-permute-start(f32[4,32,128]{2,1,0:T(8,128)S(1)} %get-tuple-element.24), channel_id=1, source_target_pairs={{0,4},{4,0},{8,12},{12,8},{16,20},{20,16},{24,28},{28,24},{1,5},{5... | collective-permute-start | bytes 196616 | tf_op jit(solution)/shard_map/ppermute | solution.py:34
  84.5 2.4 %collective-permute-done.7 = f32[160,256]{1,0:T(8,128)S(1)} collective-permute-done((f32[160,256]{1,0:T(8,128)S(1)}, f32[160,256]{1,0:T(8,128)S(1)}, u32[]{:S(2)}, u32[]{:S(2)}) %collective-permute-start.7) | collective-permute-done | bytes 163872 | tf_op jit(solution)/shard_map/ppermute | solution.py:34
  86.8 0.1 collective-permute-start.9
  86.9 0.3 collective-permute-done.8
  87.3 0.0 all-to-all-done.2.pieces
  87.3 1.0 sketch.1
  88.2 0.1 collective-permute-done.9.refs_1_
  88.3 4.8 %all-to-all-start.3 = ((f32[16,4,8,128]{3,2,1,0:T(8,128)}), f32[16,4,8,128]{3,2,1,0:T(8,128)S(1)}, u32[]{:S(2)}, u32[]{:S(2)}) async-start(f32[16,4,8,128]{3,2,1,0:T(8,128)} %sketch.1), calls=%async_computation.3 | async-start | bytes 524288 | tf_op jit(solution)/shard_map/all_to_all | solution.py:500
  93.1 0.1 collective-permute-start.10
  93.2 1.3 %collective-permute-done.10.refs_1_ = f32[8,32,128]{2,1,0:T(8,128)S(1)} collective-permute-done((f32[8,32,128]{2,1,0:T(8,128)S(1)}, f32[8,32,128]{2,1,0:T(8,128)S(1)}, u32[]{:S(2)}, u32[]{:S(2)}) %collective-permute-start.10) | collective-permute-done | bytes 131104 | tf_op jit(solution)/shard_map/ppermute | solution.py:34
  94.5 0.7 place.1
  95.3 5.0 %solve_first.1 = f32[32,128]{1,0:T(8,128)} custom-call(f32[160,256]{1,0:T(8,128)S(1)} %add.12.refs_0_, f32[160,256]{1,0:T(8,128)S(1)} %collective-permute-done.9.refs_1_), custom_call_target="tpu_custom_call" | custom-call | tf_op jit(solution)/shard_map/solve_first/pallas_call | solution.py:385
  100.2 3.0 %all-to-all-done.3 = f32[16,4,8,128]{3,2,1,0:T(8,128)S(1)} async-done(((f32[16,4,8,128]{3,2,1,0:T(8,128)}), f32[16,4,8,128]{3,2,1,0:T(8,128)S(1)}, u32[]{:S(2)}, u32[]{:S(2)}) %all-to-all-start.3) | async-done | bytes 262176 | tf_op jit(solution)/shard_map/all_to_all | solution.py:500
  103.3 0.8 copy.12
  (14 shorter events, 0.1 us)
Async XLA Ops:
  0.6 16.4 %copy-start.1 = (bf16[512,256]{1,0:T(8,128)(2,1)S(1)}, bf16[512,256]{1,0:T(8,128)(2,1)}, u32[]{:S(2)}) copy-start(bf16[512,256]{1,0:T(8,128)(2,1)} %last_m_hbm.1) | copy-start | bytes 786436
  0.6 13.9 %copy-start.2 = (bf16[32,128]{1,0:T(8,128)(2,1)S(1)}, bf16[32,128]{1,0:T(8,128)(2,1)}, u32[]{:S(2)}) copy-start(bf16[32,128]{1,0:T(8,128)(2,1)} %param.8) | copy-start | bytes 24580
  4.8 17.4 %all-to-all-start = ((f32[16,8,512]{2,1,0:T(8,128)}), f32[16,8,512]{2,1,0:T(8,128)S(1)}, u32[]{:S(2)}, u32[]{:S(2)}) async-start(f32[16,8,512]{2,1,0:T(8,128)} %bitcast.37), calls=%async_computation | async-start | bytes 524288 | tf_op jit(solution)/shard_map/all_to_all | solution.py:451
  12.2 15.0 %collective-permute-start.3 = (f32[16,32,256]{2,1,0:T(8,128)}, f32[16,32,256]{2,1,0:T(8,128)S(1)}, u32[]{:S(2)}, u32[]{:S(2)}) collective-permute-start(f32[16,32,256]{2,1,0:T(8,128)} %get-tuple-element.17), channel_id=1, source_target_pairs={{0,1},{1,0},{2,3},{3,2},{4,5},{5,4},{6,7},{7,6},{8,9},{9,8},{10,11... | collective-permute-start | bytes 1572872 | tf_op jit(solution)/shard_map/ppermute | solution.py:34
  14.6 4.3 %collective-permute-start = (f32[1,96,128]{2,1,0:T(8,128)S(1)}, f32[1,96,128]{2,1,0:T(8,128)S(1)}, u32[]{:S(2)}, u32[]{:S(2)}) collective-permute-start(f32[1,96,128]{2,1,0:T(8,128)S(1)} %maximum_bitcast_fusion), channel_id=1, source_target_pairs={{0,4},{4,0},{8,12},{12,8},{16,20},{20,16},{24,28},{28,24},{1,5},{5... | collective-permute-start | bytes 147464 | tf_op jit(solution)/shard_map/ppermute | solution.py:34
  16.5 35.5 %collective-permute-start.5 = (f32[16,32,256]{2,1,0:T(8,128)}, f32[16,32,256]{2,1,0:T(8,128)S(1)}, u32[]{:S(2)}, u32[]{:S(2)}) collective-permute-start(f32[16,32,256]{2,1,0:T(8,128)} %get-tuple-element.20), channel_id=1, source_target_pairs={{0,1},{1,0},{2,3},{3,2},{4,5},{5,4},{6,7},{7,6},{8,9},{9,8},{10,11... | collective-permute-start | bytes 1572872 | tf_op jit(solution)/shard_map/ppermute | solution.py:34
  28.1 23.8 %all-to-all-start.1 = ((f32[32,8,256]{2,1,0:T(8,128)}), f32[32,8,256]{2,1,0:T(8,128)S(1)}, u32[]{:S(2)}, u32[]{:S(2)}) async-start(f32[32,8,256]{2,1,0:T(8,128)} %broadcast_in_dim.10), calls=%async_computation.1 | async-start | bytes 524288 | tf_op jit(solution)/shard_map/all_to_all | solution.py:459
  34.1 13.6 %collective-permute-start.1 = (f32[2,96,128]{2,1,0:T(8,128)S(1)}, f32[2,96,128]{2,1,0:T(8,128)S(1)}, u32[]{:S(2)}, u32[]{:S(2)}) collective-permute-start(f32[2,96,128]{2,1,0:T(8,128)S(1)} %pad_maximum_fusion.4), channel_id=1, source_target_pairs={{0,16},{4,20},{8,24},{12,28},{16,0},{20,4},{24,8},{28,12},{1,17},{... | collective-permute-start | bytes 294920 | tf_op jit(solution)/shard_map/ppermute | solution.py:34
  47.7 4.3 %collective-permute-start.2 = (f32[4,32,128]{2,1,0:T(8,128)S(1)}, f32[4,32,128]{2,1,0:T(8,128)S(1)}, u32[]{:S(2)}, u32[]{:S(2)}) collective-permute-start(f32[4,32,128]{2,1,0:T(8,128)S(1)} %pad_maximum_fusion.5), channel_id=1, source_target_pairs={{0,8},{4,12},{8,0},{12,4},{16,24},{20,28},{24,16},{28,20},{1,9},{5... | collective-permute-start | bytes 196616 | tf_op jit(solution)/shard_map/ppermute | solution.py:34
  56.3 24.7 %copy-start = (f32[32,256]{1,0:T(8,128)S(1)}, f32[32,256]{1,0:T(8,128)}, u32[]{:S(2)}) copy-start(f32[32,256]{1,0:T(8,128)} %get-tuple-element.15.rows) | copy-start | bytes 98308
  57.8 29.4 %all-to-all-start.2 = ((f32[8,128,128]{2,1,0:T(8,128)}), f32[8,128,128]{2,1,0:T(8,128)S(1)}, u32[]{:S(2)}, u32[]{:S(2)}) async-start(f32[8,128,128]{2,1,0:T(8,128)} %project.1), calls=%async_computation.2 | async-start | bytes 1048576 | tf_op jit(solution)/shard_map/all_to_all | solution.py:489
  61.5 14.1 %collective-permute-start.4 = (f32[1,32,128]{2,1,0:T(8,128)S(1)}, f32[1,32,128]{2,1,0:T(8,128)S(1)}, u32[]{:S(2)}, u32[]{:S(2)}) collective-permute-start(f32[1,32,128]{2,1,0:T(8,128)S(1)} %bitcast.39), channel_id=1, source_target_pairs={{0,16},{4,20},{8,24},{12,28},{16,0},{20,4},{24,8},{28,12},{1,17},{... | collective-permute-start | bytes 49160 | tf_op jit(solution)/shard_map/ppermute | solution.py:34
  75.6 5.4 %collective-permute-start.6 = (f32[320,128]{1,0:T(8,128)S(1)}, f32[320,128]{1,0:T(8,128)S(1)}, u32[]{:S(2)}, u32[]{:S(2)}) collective-permute-start(f32[320,128]{1,0:T(8,128)S(1)} %pad_maximum_fusion.mine), channel_id=1, source_target_pairs={{0,8},{4,12},{8,0},{12,4},{16,24},{20,28},{24,16},{28,20},{1,9},{5... | collective-permute-start | bytes 491528 | tf_op jit(solution)/shard_map/ppermute | solution.py:34
  81.4 5.4 %collective-permute-start.7 = (f32[160,256]{1,0:T(8,128)S(1)}, f32[160,256]{1,0:T(8,128)S(1)}, u32[]{:S(2)}, u32[]{:S(2)}) collective-permute-start(f32[160,256]{1,0:T(8,128)S(1)} %get-tuple-element.23), channel_id=1, source_target_pairs={{0,1},{1,0},{2,3},{3,2},{4,5},{5,4},{6,7},{7,6},{8,9},{9,8},{10,11... | collective-permute-start | bytes 491528 | tf_op jit(solution)/shard_map/ppermute | solution.py:34
  83.0 4.3 %collective-permute-start.8 = (f32[4,32,128]{2,1,0:T(8,128)S(1)}, f32[4,32,128]{2,1,0:T(8,128)S(1)}, u32[]{:S(2)}, u32[]{:S(2)}) collective-permute-start(f32[4,32,128]{2,1,0:T(8,128)S(1)} %get-tuple-element.24), channel_id=1, source_target_pairs={{0,4},{4,0},{8,12},{12,8},{16,20},{20,16},{24,28},{28,24},{1,5},{5... | collective-permute-start | bytes 196616 | tf_op jit(solution)/shard_map/ppermute | solution.py:34
  86.8 1.5 %collective-permute-start.9 = (f32[160,256]{1,0:T(8,128)S(1)}, f32[160,256]{1,0:T(8,128)S(1)}, u32[]{:S(2)}, u32[]{:S(2)}) collective-permute-start(f32[160,256]{1,0:T(8,128)S(1)} %add.12.refs_0_), channel_id=1, source_target_pairs={{0,2},{2,0},{1,3},{3,1},{4,6},{6,4},{5,7},{7,5},{8,10},{10,8},{9,1... | collective-permute-start | bytes 491528 | tf_op jit(solution)/shard_map/ppermute | solution.py:34
  88.3 15.0 %all-to-all-start.3 = ((f32[16,4,8,128]{3,2,1,0:T(8,128)}), f32[16,4,8,128]{3,2,1,0:T(8,128)S(1)}, u32[]{:S(2)}, u32[]{:S(2)}) async-start(f32[16,4,8,128]{3,2,1,0:T(8,128)} %sketch.1), calls=%async_computation.3 | async-start | bytes 524288 | tf_op jit(solution)/shard_map/all_to_all | solution.py:500
  93.1 1.4 %collective-permute-start.10 = (f32[8,32,128]{2,1,0:T(8,128)S(1)}, f32[8,32,128]{2,1,0:T(8,128)S(1)}, u32[]{:S(2)}, u32[]{:S(2)}) collective-permute-start(f32[8,32,128]{2,1,0:T(8,128)S(1)} %constant_dynamic-update-slice_fusion.refs_0_), channel_id=1, source_target_pairs={{0,2},{2,0},{1,3},{3,1},{4,6},{6,4},{5,7},{7,5},{8,10},{10,8},{9,1... | collective-permute-start | bytes 393224 | tf_op jit(solution)/shard_map/ppermute | solution.py:34

commit v14 on v9

--- a/solution.py
+++ b/solution.py
@@ -18,6 +18,11 @@
 COL_COL = (((0,), (0,)), ((), ()))
 
 
+def gather_bits(axis):
+    *bits, low, last = axis_bits(axis)
+    return [low, *bits, last]
+
+
 def axis_bits(axis):
     bit = lax.axis_size(axis) // 2
     while bit:
@@ -42,7 +47,7 @@
 
 def swap_order(axis):
     order = [0]
-    for bit in axis_bits(axis):
+    for bit in gather_bits(axis):
         order += [o ^ bit for o in order]
     return order
 
@@ -227,46 +232,35 @@
     return high, (array - high.astype(jnp.float32)).astype(jnp.bfloat16)
 
 
-def inverse_kernel(system_shares, pinv):
+def last_kernel(y_own, system_shares, extra, kept, *refs):
+    *terms, projected, flat = refs
+    x_cells, y_cells, cols = kept.shape
+    x_part = x_cells // PARTS
+    totals = []
+    for part in range(PARTS):
+        total = kept[part * x_part : (part + 1) * x_part]
+        for term in terms[part::PARTS]:
+            total = total + term[...]
+        totals.append(two_terms(total.reshape(x_part * y_cells, cols)))
+
     system = system_shares[:, 0]
     for k in range(1, system_shares.shape[1]):
         system = system + system_shares[:, k]
-    system = system.reshape(-1, system.shape[-1])
-    cols = system.shape[1]
+    system = system.reshape(-1, cols)
+    rank = system.shape[0]
+    system_high, system_low = two_terms(system)
     high, low = two_terms(spd_inverse(system))
-    system_high, system_low = two_terms(system)
     both = jnp.dot(
         high,
         jnp.concatenate([system_high, system_low], axis=1),
         preferred_element_type=jnp.float32,
     )
     rest = jnp.dot(low, system_high, preferred_element_type=jnp.float32)
-    pinv[...] = both[:, :cols] + (both[:, cols:] + rest)
-
-
-def pseudo_inverse(system_shares):
-    rank = system_shares.shape[0] * system_shares.shape[2]
-    return pl.pallas_call(
-        inverse_kernel,
-        out_shape=jax.ShapeDtypeStruct((rank, system_shares.shape[3]), jnp.float32),
-        compiler_params=pltpu.CompilerParams(vmem_limit_bytes=VMEM_BYTES),
-        name="pseudo_inverse",
-    )(system_shares)
-
-
-def project_kernel(y_own, pinv, extra, kept, *refs):
-    *terms, projected, flat = refs
-    rank = pinv.shape[0]
-    pinv_high, pinv_low = two_terms(pinv[...])
+    pinv_high, pinv_low = two_terms(both[:, :cols] + (both[:, cols:] + rest))
     pinv_both = jnp.concatenate([pinv_high, pinv_low], axis=0)
+
     rows = flat.shape[0] // PARTS
-    x_cells, y_cells, _ = kept.shape
-    x_part = x_cells // PARTS
-    for part in range(PARTS):
-        total = kept[part * x_part : (part + 1) * x_part]
-        for term in terms[part::PARTS]:
-            total = total + term[...]
-        high, low = two_terms(total.reshape(rows, -1))
+    for part, (high, low) in enumerate(totals):
         both = lax.dot_general(high, pinv_both, ROW_ROW, preferred_element_type=jnp.float32)
         rest = lax.dot_general(low, pinv_high, ROW_ROW, preferred_element_type=jnp.float32)
         flat[part * rows : (part + 1) * rows] = both[:, :rank] + (both[:, rank:] + rest)
@@ -278,18 +272,19 @@
         projected[b, y_own * x_cells :] = extra[...]
 
 
-def project(blocks, pinv, extra, kept, terms):
-    rank = pinv.shape[0]
+def solve_last(blocks, system_shares, extra, kept, terms):
+    rank = system_shares.shape[0] * system_shares.shape[2]
     x_cells, y_cells, _ = kept.shape
     y_own = y_cells // blocks
     rows = y_own * x_cells + extra.shape[0]
     return pl.pallas_call(
-        functools.partial(project_kernel, y_own),
+        functools.partial(last_kernel, y_own),
         out_shape=jax.ShapeDtypeStruct((blocks, rows, rank), jnp.float32),
         scratch_shapes=[pltpu.VMEM((x_cells * y_cells, rank), jnp.float32)],
+        cost_estimate=pl.CostEstimate(flops=6 * 10**9, bytes_accessed=0, transcendentals=0),
         compiler_params=pltpu.CompilerParams(vmem_limit_bytes=VMEM_BYTES),
-        name="project",
-    )(pinv, extra, kept, *terms)
+        name="solve_last",
+    )(system_shares, extra, kept, *terms)
 
 
 def sketch_kernel(order, left_at, y_own, pieces, packed, out, extra):
@@ -434,7 +429,7 @@
         axis=0,
     )[None]
     left_at = x_cells * cols // LANES
-    first_bit, *bits = axis_bits("gx")
+    first_bit, *bits = gather_bits("gx")
     packed = swap_step(packed, "gx", first_bit)
 
     group = ("gx", "gy")
@@ -458,8 +453,7 @@
         extra = jnp.zeros((ROWS, LANES), jnp.float32)
     else:
         extra = last_rows.reshape(own, -1, LANES).transpose(1, 0, 2).reshape(-1, LANES)
-    pinv = pseudo_inverse(after(system, packed, *terms))
-    projected = project(blocks, pinv, extra, kept, terms)
+    projected = solve_last(blocks, after(system, packed), extra, kept, terms)
     sums = swap_sum(sums, "gz")
     sums = [swap(sums, "gy", y) if y else sums for y in range(lax.axis_size("gy"))]
 

time: 84.7 us -> 82.9 us (0.979)
  waiting for transfers between devices: 34.7 us -> 31.7 us
  starting transfers between devices: 27.3 us -> 28.7 us
    ppermute x8, waiting for transfers between devices: 21.5 us -> 18.7 us  [swap(): lax.ppermute(array, axis, [(s, s ^ bits) for s in range(lax.axis_size(axi...]
    ppermute x8, starting transfers between devices: 9.74 us -> 11.8 us  [swap(): lax.ppermute(array, axis, [(s, s ^ bits) for s in range(lax.axis_size(axi...]
    pallas_call x2 -> x1, Pallas kernels: 5.94 us -> 5.8 us  [solve_last(): pl.pallas_call(functools.partial(last_kernel, y_own), out_shape=jax.Shape...]
where the time goes in v14:
time: 82.9 us; the launch traced here: 82.4 us
  waiting for transfers between devices  31.7 us (38%)
  starting transfers between devices  28.7 us (35%)
  Pallas kernels  17 us (21%)
  local copies, waits for them, and re-layouts  2.28 us (3%)
  matrix products  1.8 us (2%)
    ppermute x8, waiting for transfers between devices, swap(): lax.ppermute(array, axis, [(s, s ^ bits) for s in range(lax.axis_size(axi...  18.7 us
    ppermute x8, starting transfers between devices, swap(): lax.ppermute(array, axis, [(s, s ^ bits) for s in range(lax.axis_size(axi...  11.8 us
    all_to_all x1, waiting for transfers between devices, per_device(): received = lax.all_to_all(middle, group, 0, 0, tiled=True)  7.91 us
    all_to_all x1, starting transfers between devices, per_device(): lax.all_to_all(last_part.reshape(-1, own, m_cells), group, 0, 0, tiled=True)  5.91 us
    pallas_call x1, Pallas kernels, solve_last(): pl.pallas_call(functools.partial(last_kernel, y_own), out_shape=jax.Shape...  5.8 us
    pallas_call x1, Pallas kernels, solve_first(): pl.pallas_call(first_kernel, out_shape=jax.ShapeDtypeStruct((x_cells, sum...  4.98 us
    all_to_all x1, starting transfers between devices, per_device(): received = lax.all_to_all(middle, group, 0, 0, tiled=True)  4.63 us
    all_to_all x1, waiting for transfers between devices, per_device(): pieces = lax.all_to_all(projected, 'gx', 0, 0, tiled=True)  4.41 us
  transfers between devices with their start and end apart: 12, of which 9 were waited for; matrix products, arithmetic and copies ran while one was open for 4% of the time, Pallas kernels for 7%

profile of v14, /device:TPU:0, one launch (start us, length us, event | category | flops | bytes accessed | tf_op | source)
XLA Modules:
  0.0 82.4 jit_solution(6114580581446343839)
XLA Ops:
  0.6 0.0 copy-start.1
  0.6 0.0 copy-start.2
  0.7 4.2 %local_products.1 = (f32[128,512]{1,0:T(8,128)}, f32[32,256]{1,0:T(8,128)}, f32[16,32,256]{2,1,0:T(8,128)}, f32[16,32,256]{2,1,0:T(8,128)}) custom-call(bf16[32,64,512]{2,1,0:T(8,128)(2,1)} %field_hbm.1, bf16[32,128]{1,0:T(8,128)(2,1)} %last_x_hbm.1, bf16[64,128]{1,0:T(8,128)(2,1)} %last_y_hbm.1, bf16[64,256]{1,0:T(8,128)(2,1)} %right_y_hbm.1, ...), custom_call_target="tpu_custom_call" | custom-call | tf_op jit(solution)/shard_map/local_products/pallas_call | solution.py:210
  4.8 3.0 %collective-permute-start = (f32[16,32,256]{2,1,0:T(8,128)}, f32[16,32,256]{2,1,0:T(8,128)S(1)}, u32[]{:S(2)}, u32[]{:S(2)}) collective-permute-start(f32[16,32,256]{2,1,0:T(8,128)} %get-tuple-element.16), channel_id=1, source_target_pairs={{0,1},{1,0},{2,3},{3,2},{4,5},{5,4},{6,7},{7,6},{8,9},{9,8},{10,11... | collective-permute-start | bytes 1572872 | tf_op jit(solution)/shard_map/ppermute | solution.py:34
  7.9 5.9 %all-to-all-start = ((f32[16,8,512]{2,1,0:T(8,128)}), f32[16,8,512]{2,1,0:T(8,128)S(1)}, u32[]{:S(2)}, u32[]{:S(2)}) async-start(f32[16,8,512]{2,1,0:T(8,128)} %bitcast.35), calls=%async_computation | async-start | bytes 524288 | tf_op jit(solution)/shard_map/all_to_all | solution.py:437
  13.8 0.8 copy_bitcast_fusion
  14.5 0.0 copy-done.2
  14.6 2.0 %collective-permute-start.1 = (f32[1,96,128]{2,1,0:T(8,128)S(1)}, f32[1,96,128]{2,1,0:T(8,128)S(1)}, u32[]{:S(2)}, u32[]{:S(2)}) collective-permute-start(f32[1,96,128]{2,1,0:T(8,128)S(1)} %maximum_bitcast_fusion), channel_id=1, source_target_pairs={{0,8},{4,12},{8,0},{12,4},{16,24},{20,28},{24,16},{28,20},{1,9},{5... | collective-permute-start | bytes 147464 | tf_op jit(solution)/shard_map/ppermute | solution.py:34
  16.5 0.5 collective-permute-start.4
  17.1 0.0 copy-done.1
  17.1 1.7 %fusion.kept = f32[32,32,256]{2,1,0:T(8,128)S(1)} fusion(bf16[32,2,32,512]{3,2,1,0:T(8,128)(2,1)} %bitcast.33, s32[]{:T(128)S(6)} %select_n.4, bf16[512,256]{1,0:T(8,128)(2,1)S(1)} %copy-done.1), kind=kOutput, calls=%fused_computation | convolution fusion | flops 268435456 | bytes 2359300 | tf_op jit(solution)/shard_map/dot_general | solution.py:420
  18.7 2.9 %collective-permute-done.1 = f32[1,96,128]{2,1,0:T(8,128)S(1)} collective-permute-done((f32[1,96,128]{2,1,0:T(8,128)S(1)}, f32[1,96,128]{2,1,0:T(8,128)S(1)}, u32[]{:S(2)}, u32[]{:S(2)}) %collective-permute-start.1) | collective-permute-done | bytes 49184 | tf_op jit(solution)/shard_map/ppermute | solution.py:34
  21.6 3.0 %collective-permute-start.2 = (f32[2,96,128]{2,1,0:T(8,128)S(1)}, f32[2,96,128]{2,1,0:T(8,128)S(1)}, u32[]{:S(2)}, u32[]{:S(2)}) collective-permute-start(f32[2,96,128]{2,1,0:T(8,128)S(1)} %pad_maximum_fusion.2), channel_id=1, source_target_pairs={{0,16},{4,20},{8,24},{12,28},{16,0},{20,4},{24,8},{28,12},{1,17},{... | collective-permute-start | bytes 294920 | tf_op jit(solution)/shard_map/ppermute | solution.py:34
  24.6 0.0 all-to-all-done
  24.6 0.0 collective-permute-done.refs_0_
  24.7 0.1 fusion.5
  24.8 0.7 broadcast_in_dim.10
  25.6 2.6 %all-to-all-start.1 = ((f32[32,8,256]{2,1,0:T(8,128)}), f32[32,8,256]{2,1,0:T(8,128)S(1)}, u32[]{:S(2)}, u32[]{:S(2)}) async-start(f32[32,8,256]{2,1,0:T(8,128)} %broadcast_in_dim.10), calls=%async_computation.1 | async-start | bytes 524288 | tf_op jit(solution)/shard_map/all_to_all | solution.py:445
  28.2 1.2 %collective-permute-done.2 = f32[2,96,128]{2,1,0:T(8,128)S(1)} collective-permute-done((f32[2,96,128]{2,1,0:T(8,128)S(1)}, f32[2,96,128]{2,1,0:T(8,128)S(1)}, u32[]{:S(2)}, u32[]{:S(2)}) %collective-permute-start.2) | collective-permute-done | bytes 98336 | tf_op jit(solution)/shard_map/ppermute | solution.py:34
  29.3 1.5 %collective-permute-start.3 = (f32[4,96,128]{2,1,0:T(8,128)S(1)}, f32[4,96,128]{2,1,0:T(8,128)S(1)}, u32[]{:S(2)}, u32[]{:S(2)}) collective-permute-start(f32[4,96,128]{2,1,0:T(8,128)S(1)} %pad_maximum_fusion.1), channel_id=1, source_target_pairs={{0,4},{4,0},{8,12},{12,8},{16,20},{20,16},{24,28},{28,24},{1,5},{5... | collective-permute-start | bytes 589832 | tf_op jit(solution)/shard_map/ppermute | solution.py:34
  30.9 7.4 %collective-permute-done.3 = f32[4,96,128]{2,1,0:T(8,128)S(1)} collective-permute-done((f32[4,96,128]{2,1,0:T(8,128)S(1)}, f32[4,96,128]{2,1,0:T(8,128)S(1)}, u32[]{:S(2)}, u32[]{:S(2)}) %collective-permute-start.3) | collective-permute-done | bytes 196640 | tf_op jit(solution)/shard_map/ppermute | solution.py:34
  38.2 0.6 all-to-all-done.1
  38.8 0.0 collective-permute-done.4.refs_1_
  38.8 0.0 copy-start
  38.9 5.8 %solve_last.1 = f32[8,160,128]{2,1,0:T(8,128)} custom-call(f32[16,2,8,256]{3,2,1,0:T(8,128)S(1)} %bitcast.31, f32[32,128]{1,0:T(8,128)S(1)} %bitcast.32, f32[32,32,256]{2,1,0:T(8,128)S(1)} %fusion.kept, f32[16,32,256]{2,1,0:T(8,128)S(1)} %collective-permute-done.refs_0_, f32[16,32,256]{2,1,0:T(8,128)S(1)} %collective-permute-done.4.refs_1_), custom_call_target="tpu_custom_call" | custom-call | flops 6000000000 | tf_op jit(solution)/shard_map/solve_last/pallas_call | solution.py:280
  44.7 3.8 %all-to-all-start.2 = ((f32[8,160,128]{2,1,0:T(8,128)}), f32[8,160,128]{2,1,0:T(8,128)S(1)}, u32[]{:S(2)}, u32[]{:S(2)}) async-start(f32[8,160,128]{2,1,0:T(8,128)} %solve_last.1), calls=%async_computation.2 | async-start | bytes 1310720 | tf_op jit(solution)/shard_map/all_to_all | solution.py:460
  48.5 0.0 copy-done
  48.5 0.4 first_sums.1
  48.9 1.6 %collective-permute-start.5 = (f32[160,256]{1,0:T(8,128)S(1)}, f32[160,256]{1,0:T(8,128)S(1)}, u32[]{:S(2)}, u32[]{:S(2)}) collective-permute-start(f32[160,256]{1,0:T(8,128)S(1)} %first_sums.1), channel_id=1, source_target_pairs={{0,1},{1,0},{2,3},{3,2},{4,5},{5,4},{6,7},{7,6},{8,9},{9,8},{10,11... | collective-permute-start | bytes 491528 | tf_op jit(solution)/shard_map/ppermute | solution.py:34
  50.5 4.6 %collective-permute-done.5 = f32[160,256]{1,0:T(8,128)S(1)} collective-permute-done((f32[160,256]{1,0:T(8,128)S(1)}, f32[160,256]{1,0:T(8,128)S(1)}, u32[]{:S(2)}, u32[]{:S(2)}) %collective-permute-start.5) | collective-permute-done | bytes 163872 | tf_op jit(solution)/shard_map/ppermute | solution.py:34
  55.1 0.1 collective-permute-start.6
  55.2 1.4 %collective-permute-done.6.refs_1_ = f32[160,256]{1,0:T(8,128)S(1)} collective-permute-done((f32[160,256]{1,0:T(8,128)S(1)}, f32[160,256]{1,0:T(8,128)S(1)}, u32[]{:S(2)}, u32[]{:S(2)}) %collective-permute-start.6) | collective-permute-done | bytes 163872 | tf_op jit(solution)/shard_map/ppermute | solution.py:34
  56.6 5.0 %solve_first.1 = f32[32,128]{1,0:T(8,128)} custom-call(f32[160,256]{1,0:T(8,128)S(1)} %add.12.refs_0_, f32[160,256]{1,0:T(8,128)S(1)} %collective-permute-done.6.refs_1_), custom_call_target="tpu_custom_call" | custom-call | tf_op jit(solution)/shard_map/solve_first/pallas_call | solution.py:372
  61.6 4.4 %all-to-all-done.2.pieces = f32[8,160,128]{2,1,0:T(8,128)S(1)} async-done(((f32[8,160,128]{2,1,0:T(8,128)}), f32[8,160,128]{2,1,0:T(8,128)S(1)}, u32[]{:S(2)}, u32[]{:S(2)}) %all-to-all-start.2) | async-done | bytes 655392 | tf_op jit(solution)/shard_map/all_to_all | solution.py:460
  66.0 1.0 %sketch.1 = (f32[16,4,8,128]{3,2,1,0:T(8,128)}, f32[8,32,128]{2,1,0:T(8,128)S(1)}) custom-call(f32[8,160,128]{2,1,0:T(8,128)S(1)} %all-to-all-done.2.pieces, f32[8,96,128]{2,1,0:T(8,128)S(1)} %pad_maximum_fusion.packed), custom_call_target="tpu_custom_call" | custom-call | tf_op jit(solution)/shard_map/sketch/pallas_call | solution.py:317
  66.9 4.6 %all-to-all-start.3 = ((f32[16,4,8,128]{3,2,1,0:T(8,128)}), f32[16,4,8,128]{3,2,1,0:T(8,128)S(1)}, u32[]{:S(2)}, u32[]{:S(2)}) async-start(f32[16,4,8,128]{3,2,1,0:T(8,128)} %get-tuple-element.25), calls=%async_computation.3 | async-start | bytes 524288 | tf_op jit(solution)/shard_map/all_to_all | solution.py:471
  71.6 0.1 collective-permute-start.7
  71.6 1.3 %collective-permute-done.7.refs_1_ = f32[8,32,128]{2,1,0:T(8,128)S(1)} collective-permute-done((f32[8,32,128]{2,1,0:T(8,128)S(1)}, f32[8,32,128]{2,1,0:T(8,128)S(1)}, u32[]{:S(2)}, u32[]{:S(2)}) %collective-permute-start.7) | collective-permute-done | bytes 131104 | tf_op jit(solution)/shard_map/ppermute | solution.py:34
  73.0 0.7 place.1
  73.7 7.9 %all-to-all-done.3 = f32[16,4,8,128]{3,2,1,0:T(8,128)S(1)} async-done(((f32[16,4,8,128]{3,2,1,0:T(8,128)}), f32[16,4,8,128]{3,2,1,0:T(8,128)S(1)}, u32[]{:S(2)}, u32[]{:S(2)}) %all-to-all-start.3) | async-done | bytes 262176 | tf_op jit(solution)/shard_map/all_to_all | solution.py:471
  81.6 0.8 copy.12
  (9 shorter events, 0.1 us)
Async XLA Ops:
  0.6 16.4 %copy-start.1 = (bf16[512,256]{1,0:T(8,128)(2,1)S(1)}, bf16[512,256]{1,0:T(8,128)(2,1)}, u32[]{:S(2)}) copy-start(bf16[512,256]{1,0:T(8,128)(2,1)} %last_m_hbm.1) | copy-start | bytes 786436
  0.6 13.9 %copy-start.2 = (bf16[32,128]{1,0:T(8,128)(2,1)S(1)}, bf16[32,128]{1,0:T(8,128)(2,1)}, u32[]{:S(2)}) copy-start(bf16[32,128]{1,0:T(8,128)(2,1)} %param.8) | copy-start | bytes 24580
  4.8 19.8 %collective-permute-start = (f32[16,32,256]{2,1,0:T(8,128)}, f32[16,32,256]{2,1,0:T(8,128)S(1)}, u32[]{:S(2)}, u32[]{:S(2)}) collective-permute-start(f32[16,32,256]{2,1,0:T(8,128)} %get-tuple-element.16), channel_id=1, source_target_pairs={{0,1},{1,0},{2,3},{3,2},{4,5},{5,4},{6,7},{7,6},{8,9},{9,8},{10,11... | collective-permute-start | bytes 1572872 | tf_op jit(solution)/shard_map/ppermute | solution.py:34
  7.9 16.8 %all-to-all-start = ((f32[16,8,512]{2,1,0:T(8,128)}), f32[16,8,512]{2,1,0:T(8,128)S(1)}, u32[]{:S(2)}, u32[]{:S(2)}) async-start(f32[16,8,512]{2,1,0:T(8,128)} %bitcast.35), calls=%async_computation | async-start | bytes 524288 | tf_op jit(solution)/shard_map/all_to_all | solution.py:437
  14.6 7.1 %collective-permute-start.1 = (f32[1,96,128]{2,1,0:T(8,128)S(1)}, f32[1,96,128]{2,1,0:T(8,128)S(1)}, u32[]{:S(2)}, u32[]{:S(2)}) collective-permute-start(f32[1,96,128]{2,1,0:T(8,128)S(1)} %maximum_bitcast_fusion), channel_id=1, source_target_pairs={{0,8},{4,12},{8,0},{12,4},{16,24},{20,28},{24,16},{28,20},{1,9},{5... | collective-permute-start | bytes 147464 | tf_op jit(solution)/shard_map/ppermute | solution.py:34
  16.5 22.3 %collective-permute-start.4 = (f32[16,32,256]{2,1,0:T(8,128)}, f32[16,32,256]{2,1,0:T(8,128)S(1)}, u32[]{:S(2)}, u32[]{:S(2)}) collective-permute-start(f32[16,32,256]{2,1,0:T(8,128)} %get-tuple-element.21), channel_id=1, source_target_pairs={{0,1},{1,0},{2,3},{3,2},{4,5},{5,4},{6,7},{7,6},{8,9},{9,8},{10,11... | collective-permute-start | bytes 1572872 | tf_op jit(solution)/shard_map/ppermute | solution.py:34
  21.6 7.7 %collective-permute-start.2 = (f32[2,96,128]{2,1,0:T(8,128)S(1)}, f32[2,96,128]{2,1,0:T(8,128)S(1)}, u32[]{:S(2)}, u32[]{:S(2)}) collective-permute-start(f32[2,96,128]{2,1,0:T(8,128)S(1)} %pad_maximum_fusion.2), channel_id=1, source_target_pairs={{0,16},{4,20},{8,24},{12,28},{16,0},{20,4},{24,8},{28,12},{1,17},{... | collective-permute-start | bytes 294920 | tf_op jit(solution)/shard_map/ppermute | solution.py:34
  25.6 13.3 %all-to-all-start.1 = ((f32[32,8,256]{2,1,0:T(8,128)}), f32[32,8,256]{2,1,0:T(8,128)S(1)}, u32[]{:S(2)}, u32[]{:S(2)}) async-start(f32[32,8,256]{2,1,0:T(8,128)} %broadcast_in_dim.10), calls=%async_computation.1 | async-start | bytes 524288 | tf_op jit(solution)/shard_map/all_to_all | solution.py:445
  29.3 8.9 %collective-permute-start.3 = (f32[4,96,128]{2,1,0:T(8,128)S(1)}, f32[4,96,128]{2,1,0:T(8,128)S(1)}, u32[]{:S(2)}, u32[]{:S(2)}) collective-permute-start(f32[4,96,128]{2,1,0:T(8,128)S(1)} %pad_maximum_fusion.1), channel_id=1, source_target_pairs={{0,4},{4,0},{8,12},{12,8},{16,20},{20,16},{24,28},{28,24},{1,5},{5... | collective-permute-start | bytes 589832 | tf_op jit(solution)/shard_map/ppermute | solution.py:34
  38.8 9.7 %copy-start = (f32[32,256]{1,0:T(8,128)S(1)}, f32[32,256]{1,0:T(8,128)}, u32[]{:S(2)}) copy-start(f32[32,256]{1,0:T(8,128)} %get-tuple-element.18.rows) | copy-start | bytes 98308
  44.7 21.3 %all-to-all-start.2 = ((f32[8,160,128]{2,1,0:T(8,128)}), f32[8,160,128]{2,1,0:T(8,128)S(1)}, u32[]{:S(2)}, u32[]{:S(2)}) async-start(f32[8,160,128]{2,1,0:T(8,128)} %solve_last.1), calls=%async_computation.2 | async-start | bytes 1310720 | tf_op jit(solution)/shard_map/all_to_all | solution.py:460
  48.9 6.2 %collective-permute-start.5 = (f32[160,256]{1,0:T(8,128)S(1)}, f32[160,256]{1,0:T(8,128)S(1)}, u32[]{:S(2)}, u32[]{:S(2)}) collective-permute-start(f32[160,256]{1,0:T(8,128)S(1)} %first_sums.1), channel_id=1, source_target_pairs={{0,1},{1,0},{2,3},{3,2},{4,5},{5,4},{6,7},{7,6},{8,9},{9,8},{10,11... | collective-permute-start | bytes 491528 | tf_op jit(solution)/shard_map/ppermute | solution.py:34
  55.1 1.5 %collective-permute-start.6 = (f32[160,256]{1,0:T(8,128)S(1)}, f32[160,256]{1,0:T(8,128)S(1)}, u32[]{:S(2)}, u32[]{:S(2)}) collective-permute-start(f32[160,256]{1,0:T(8,128)S(1)} %add.12.refs_0_), channel_id=1, source_target_pairs={{0,2},{2,0},{1,3},{3,1},{4,6},{6,4},{5,7},{7,5},{8,10},{10,8},{9,1... | collective-permute-start | bytes 491528 | tf_op jit(solution)/shard_map/ppermute | solution.py:34
  66.9 14.7 %all-to-all-start.3 = ((f32[16,4,8,128]{3,2,1,0:T(8,128)}), f32[16,4,8,128]{3,2,1,0:T(8,128)S(1)}, u32[]{:S(2)}, u32[]{:S(2)}) async-start(f32[16,4,8,128]{3,2,1,0:T(8,128)} %get-tuple-element.25), calls=%async_computation.3 | async-start | bytes 524288 | tf_op jit(solution)/shard_map/all_to_all | solution.py:471
  71.6 1.4 %collective-permute-start.7 = (f32[8,32,128]{2,1,0:T(8,128)S(1)}, f32[8,32,128]{2,1,0:T(8,128)S(1)}, u32[]{:S(2)}, u32[]{:S(2)}) collective-permute-start(f32[8,32,128]{2,1,0:T(8,128)S(1)} %get-tuple-element.26.refs_0_), channel_id=1, source_target_pairs={{0,2},{2,0},{1,3},{3,1},{4,6},{6,4},{5,7},{7,5},{8,10},{10,8},{9,1... | collective-permute-start | bytes 393224 | tf_op jit(solution)/shard_map/ppermute | solution.py:34

commit v15 on v14

--- a/solution.py
+++ b/solution.py
@@ -232,7 +232,7 @@
     return high, (array - high.astype(jnp.float32)).astype(jnp.bfloat16)
 
 
-def last_kernel(y_own, system_shares, extra, kept, *refs):
+def last_kernel(y_own, system_shares, kept, *refs):
     *terms, projected, flat = refs
     x_cells, y_cells, cols = kept.shape
     x_part = x_cells // PARTS
@@ -269,14 +269,13 @@
             projected[b, j * x_cells : (j + 1) * x_cells] = flat[
                 pl.ds(b * y_own + j, x_cells, stride=y_cells), :
             ]
-        projected[b, y_own * x_cells :] = extra[...]
-
-
-def solve_last(blocks, system_shares, extra, kept, terms):
+
+
+def solve_last(blocks, system_shares, kept, terms):
     rank = system_shares.shape[0] * system_shares.shape[2]
     x_cells, y_cells, _ = kept.shape
     y_own = y_cells // blocks
-    rows = y_own * x_cells + extra.shape[0]
+    rows = y_own * x_cells
     return pl.pallas_call(
         functools.partial(last_kernel, y_own),
         out_shape=jax.ShapeDtypeStruct((blocks, rows, rank), jnp.float32),
@@ -284,72 +283,83 @@
         cost_estimate=pl.CostEstimate(flops=6 * 10**9, bytes_accessed=0, transcendentals=0),
         compiler_params=pltpu.CompilerParams(vmem_limit_bytes=VMEM_BYTES),
         name="solve_last",
-    )(system_shares, extra, kept, *terms)
-
-
-def sketch_kernel(order, left_at, y_own, pieces, packed, out, extra):
+    )(system_shares, kept, *terms)
+
+
+def packed_units(parts, unit):
+    return [(part, n * unit) for part in parts for n in range(part.shape[0] // unit)]
+
+
+def sketch_kernel(order, left_at, unit, pieces, mine, other, out):
     me = lax.axis_index("gx")
-    blocks, _, cols = pieces.shape
-    x_cells = packed.shape[1] - left_at
-    weights = jnp.concatenate([packed[k, left_at:] for k in range(blocks)], axis=0)
+    _, rows, cols = pieces.shape
+    x_cells = unit - left_at
+    weights = jnp.concatenate(
+        [part[at + left_at : at + unit] for part, at in packed_units((mine, other), unit)], axis=0
+    )
     weights = weights.astype(jnp.bfloat16)
-    for j in range(y_own):
-        column = jnp.concatenate(
-            [pieces[me ^ o, j * x_cells : (j + 1) * x_cells] for o in order], axis=0
+    columns = []
+    for j in range(rows // x_cells):
+        columns += two_terms(
+            jnp.concatenate(
+                [pieces[me ^ o, j * x_cells : (j + 1) * x_cells] for o in order], axis=0
+            )
         )
-        high = column.astype(jnp.bfloat16)
-        low = (column - high.astype(jnp.float32)).astype(jnp.bfloat16)
-        both = lax.dot_general(
-            weights,
-            jnp.concatenate([high, low], axis=1),
-            COL_COL,
-            preferred_element_type=jnp.float32,
-        )
-        both = both[:, :cols] + both[:, cols:]
-        out[:, j] = both.reshape(out.shape[0], out.shape[2], cols)
-    extra[...] = pieces[:, y_own * x_cells :]
-
-
-def sketch(order, left_at, y_own, own, pieces, packed):
-    blocks, rows, cols = pieces.shape
-    rank = packed.shape[2]
-    extra = rows - y_own * (packed.shape[1] - left_at)
+    sums = lax.dot_general(
+        weights,
+        jnp.concatenate(columns, axis=1),
+        COL_COL,
+        preferred_element_type=jnp.float32,
+    )
+    for j in range(rows // x_cells):
+        at = 2 * j * cols
+        core = sums[:, at : at + cols] + sums[:, at + cols : at + 2 * cols]
+        out[:, j] = core.reshape(out.shape[0], out.shape[2], cols)
+
+
+def sketch(order, left_at, unit, own, pieces, mine, other):
+    _, rows, cols = pieces.shape
+    rank = mine.shape[1]
+    y_own = rows // (unit - left_at)
     return pl.pallas_call(
-        functools.partial(sketch_kernel, order, left_at, y_own),
-        out_shape=(
-            jax.ShapeDtypeStruct((rank // own, y_own, own, cols), jnp.float32),
-            jax.ShapeDtypeStruct((blocks, extra, cols), jnp.float32),
-        ),
+        functools.partial(sketch_kernel, order, left_at, unit),
+        out_shape=jax.ShapeDtypeStruct((rank // own, y_own, own, cols), jnp.float32),
         compiler_params=pltpu.CompilerParams(vmem_limit_bytes=VMEM_BYTES),
         name="sketch",
-    )(pieces, packed)
-
-
-def first_sums_kernel(left_at, rows, packed, sums):
+    )(pieces, mine, other)
+
+
+def first_sums_kernel(left_at, unit, rows, mine, other, sums, extra):
     x_cells, cols = rows.shape
-    blocks = range(packed.shape[0])
-    left = jnp.concatenate([packed[k, left_at : left_at + x_cells] for k in blocks], axis=0)
+    units = packed_units((mine, other), unit)
+    left = jnp.concatenate([part[at + left_at : at + unit] for part, at in units], axis=0)
     sums[:x_cells] = rows[...]
     for c in range(cols // LANES):
-        at = c * x_cells
+        first = c * x_cells
         sums[x_cells:, c * LANES : (c + 1) * LANES] = lax.dot_general(
             left,
-            jnp.concatenate([packed[k, at : at + x_cells] for k in blocks], axis=0),
+            jnp.concatenate(
+                [part[at + first : at + first + x_cells] for part, at in units], axis=0
+            ),
             COL_COL,
             precision=HIGHEST,
             preferred_element_type=jnp.float32,
         )
-
-
-def first_sums(left_at, rows, packed):
+    extra[0] = mine[len(units) // 2 * unit :]
+    extra[1] = other[len(units) // 2 * unit :]
+
+
+def first_sums(left_at, unit, rows, mine, other):
+    height, rank = mine.shape
     return pl.pallas_call(
-        functools.partial(first_sums_kernel, left_at),
-        out_shape=jax.ShapeDtypeStruct(
-            (rows.shape[0] + packed.shape[2], rows.shape[1]), jnp.float32
+        functools.partial(first_sums_kernel, left_at, unit),
+        out_shape=(
+            jax.ShapeDtypeStruct((rows.shape[0] + rank, rows.shape[1]), jnp.float32),
+            jax.ShapeDtypeStruct((2, height % unit, rank), jnp.float32),
         ),
         compiler_params=pltpu.CompilerParams(vmem_limit_bytes=VMEM_BYTES),
         name="first_sums",
-    )(rows, packed)
+    )(rows, mine, other)
 
 
 def first_kernel(*refs):
@@ -377,22 +387,23 @@
     )(*sums)
 
 
-def place_kernel(own, inner_order, *refs):
+def place_kernel(own, outer_order, *refs):
     *parts, core_last = refs
-    inner = lax.axis_index("gy")
-    for part, i in zip(parts, inner_order):
-        for o in range(part.shape[0]):
-            at = pl.multiple_of((o * len(parts) + (inner ^ i)) * own, own)
+    outer, inner = lax.axis_index("gx"), lax.axis_index("gy")
+    for i, part in enumerate(parts):
+        for k, o in enumerate(outer_order):
+            at = ((outer ^ o) * len(parts) + (inner ^ i)) * own
+            at = pl.multiple_of(at, own)
             for c in range(part.shape[1] // own):
                 core_last[pl.ds(at, own), c * LANES : (c + 1) * LANES] = part[
-                    o, c * own : (c + 1) * own
+                    k, c * own : (c + 1) * own
                 ]
 
 
-def place(own, inner_order, parts):
+def place(own, outer_order, parts):
     outer, rows, lanes = parts[0].shape
     return pl.pallas_call(
-        functools.partial(place_kernel, own, inner_order),
+        functools.partial(place_kernel, own, outer_order),
         out_shape=jax.ShapeDtypeStruct(
             (len(parts) * outer * own, rows // own * lanes), jnp.float32
         ),
@@ -429,8 +440,9 @@
         axis=0,
     )[None]
     left_at = x_cells * cols // LANES
+    unit = left_at + x_cells
     first_bit, *bits = gather_bits("gx")
-    packed = swap_step(packed, "gx", first_bit)
+    packed = after(swap_step(packed, "gx", first_bit), *terms[::PARTS])
 
     group = ("gx", "gy")
     own = rank // lax.axis_size(group)
@@ -446,28 +458,34 @@
     if own % ROWS:
         system = jnp.sum(system, axis=1).reshape(-1, 1, ROWS, cols)
 
-    for bit in bits:
-        packed = swap_step(packed, "gx", bit)
-    sums = first_sums(left_at, first_part, packed)
     if own % ROWS:
         extra = jnp.zeros((ROWS, LANES), jnp.float32)
     else:
         extra = last_rows.reshape(own, -1, LANES).transpose(1, 0, 2).reshape(-1, LANES)
-    projected = solve_last(blocks, after(system, packed), extra, kept, terms)
+    *bits, last_bit = bits
+    for bit in bits:
+        packed = swap_step(packed, "gx", bit)
+    mine = jnp.concatenate([packed.reshape(-1, LANES), extra], axis=0)
+    other = swap(mine, "gx", last_bit)
+    projected = solve_last(blocks, after(system, other), kept, terms)
+    sums, extra = first_sums(left_at, unit, first_part, mine, other)
     sums = swap_sum(sums, "gz")
     sums = [swap(sums, "gy", y) if y else sums for y in range(lax.axis_size("gy"))]
 
     pieces = lax.all_to_all(projected, "gx", 0, 0, tiled=True)
-    core_first = solve_first(x_cells, after(sums[0], projected), *sums[1:])
     group = ("gx", "gz")
     devices = lax.axis_size(group)
     rank_own = rank // devices
     if rank_own % ROWS:
-        middle, extra = sketch(order, left_at, y_own, rank, pieces, packed)
+        middle = sketch(order, left_at, unit, rank, pieces, mine, other)
         middle = middle.reshape(y_own, devices, rank_own, rank).transpose(1, 0, 2, 3)
     else:
-        middle, extra = sketch(order, left_at, y_own, rank_own, pieces, packed)
-    middle, core_first = lax.optimization_barrier((middle, core_first))
+        middle = sketch(order, left_at, unit, rank_own, pieces, mine, other)
+    outer = [0, last_bit]
+    for bit in (*bits, first_bit):
+        extra = swap_step(extra, "gx", bit)
+        outer += [o ^ bit for o in outer]
+    middle = after(middle, extra, *sums)
     received = lax.all_to_all(middle, group, 0, 0, tiled=True)
     received = received.reshape(blocks, shares, y_own, rank_own, rank)
     core_middle = received.transpose(3, 1, 0, 2, 4).reshape(rank_own, y_cells, rank)
@@ -476,7 +494,8 @@
         core_last = gather_rows(last_rows, "gx", "gy")
     else:
         inner = range(lax.axis_size("gy"))
-        core_last = place(own, inner, [swap(extra, "gy", i) if i else extra for i in inner])
+        core_last = place(own, outer, [swap(extra, "gy", i) if i else extra for i in inner])
+    core_first = solve_first(x_cells, after(sums[0], middle), *sums[1:])
     return (core_first, core_middle, core_last)
 
 

time: 82.9 us -> 85.5 us (1.031)
  waiting for transfers between devices: 31.7 us -> 33.8 us
    ppermute x8 -> x10, waiting for transfers between devices: 18.7 us -> 29.4 us  [swap(): lax.ppermute(array, axis, [(s, s ^ bits) for s in range(lax.axis_size(axi...]
    all_to_all x1, waiting for transfers between devices: 7.91 us -> 1.77 us  [per_device(): received = lax.all_to_all(middle, group, 0, 0, tiled=True)]
    all_to_all x1, waiting for transfers between devices: 4.41 us -> 0.01 us  [per_device(): pieces = lax.all_to_all(projected, 'gx', 0, 0, tiled=True)]
    all_to_all x1, waiting for transfers between devices: 0.01 us -> 2.67 us  [per_device(): lax.all_to_all(last_part.reshape(-1, own, m_cells), group, 0, 0, tiled=True)]
    ppermute x8 -> x10, starting transfers between devices: 11.8 us -> 11.5 us  [swap(): lax.ppermute(array, axis, [(s, s ^ bits) for s in range(lax.axis_size(axi...]
  transfers between devices with their start and end apart: 12 -> 14, of which waited for: 9 -> 8; matrix products, arithmetic and copies ran while one was open for 4% -> 4% of each run, Pallas kernels for 7% -> 8%
where the time goes in v15:
time: 85.5 us; the launch traced here: 84.9 us
  waiting for transfers between devices  33.8 us (40%)
  starting transfers between devices  29.1 us (34%)
  Pallas kernels  17 us (20%)
  local copies, waits for them, and re-layouts  2.31 us (3%)
  matrix products  1.8 us (2%)
    ppermute x10, waiting for transfers between devices, swap(): lax.ppermute(array, axis, [(s, s ^ bits) for s in range(lax.axis_size(axi...  29.4 us
    ppermute x10, starting transfers between devices, swap(): lax.ppermute(array, axis, [(s, s ^ bits) for s in range(lax.axis_size(axi...  11.5 us
    all_to_all x1, starting transfers between devices, per_device(): lax.all_to_all(last_part.reshape(-1, own, m_cells), group, 0, 0, tiled=True)  5.91 us
    pallas_call x1, Pallas kernels, solve_last(): pl.pallas_call(functools.partial(last_kernel, y_own), out_shape=jax.Shape...  5.75 us
    pallas_call x1, Pallas kernels, solve_first(): pl.pallas_call(first_kernel, out_shape=jax.ShapeDtypeStruct((x_cells, sum...  4.98 us
    all_to_all x1, starting transfers between devices, per_device(): received = lax.all_to_all(middle, group, 0, 0, tiled=True)  4.91 us
    pallas_call x1, Pallas kernels, local_products(): pl.pallas_call(functools.partial(local_kernel, chunks, shares), in_specs=...  4.17 us
    all_to_all x1, starting transfers between devices, per_device(): pieces = lax.all_to_all(projected, 'gx', 0, 0, tiled=True)  3.87 us
  transfers between devices with their start and end apart: 14, of which 8 were waited for; matrix products, arithmetic and copies ran while one was open for 4% of the time, Pallas kernels for 8%

profile of v15, /device:TPU:0, one launch (start us, length us, event | category | flops | bytes accessed | tf_op | source)
XLA Modules:
  0.0 84.9 jit_solution(9888847928149148231)
XLA Ops:
  0.6 0.0 copy-start.1
  0.6 0.0 copy-start.2
  0.7 4.2 %local_products.1 = (f32[128,512]{1,0:T(8,128)}, f32[32,256]{1,0:T(8,128)}, f32[16,32,256]{2,1,0:T(8,128)}, f32[16,32,256]{2,1,0:T(8,128)}) custom-call(bf16[32,64,512]{2,1,0:T(8,128)(2,1)} %field_hbm.1, bf16[32,128]{1,0:T(8,128)(2,1)} %last_x_hbm.1, bf16[64,128]{1,0:T(8,128)(2,1)} %last_y_hbm.1, bf16[64,256]{1,0:T(8,128)(2,1)} %right_y_hbm.1, ...), custom_call_target="tpu_custom_call" | custom-call | tf_op jit(solution)/shard_map/local_products/pallas_call | solution.py:210
  4.8 3.0 %collective-permute-start.1 = (f32[16,32,256]{2,1,0:T(8,128)}, f32[16,32,256]{2,1,0:T(8,128)S(1)}, u32[]{:S(2)}, u32[]{:S(2)}) collective-permute-start(f32[16,32,256]{2,1,0:T(8,128)} %get-tuple-element.16), channel_id=1, source_target_pairs={{0,1},{1,0},{2,3},{3,2},{4,5},{5,4},{6,7},{7,6},{8,9},{9,8},{10,11... | collective-permute-start | bytes 1572872 | tf_op jit(solution)/shard_map/ppermute | solution.py:34
  7.9 5.9 %all-to-all-start = ((f32[16,8,512]{2,1,0:T(8,128)}), f32[16,8,512]{2,1,0:T(8,128)S(1)}, u32[]{:S(2)}, u32[]{:S(2)}) async-start(f32[16,8,512]{2,1,0:T(8,128)} %bitcast.30), calls=%async_computation | async-start | bytes 524288 | tf_op jit(solution)/shard_map/all_to_all | solution.py:449
  13.8 0.0 copy-done.2
  13.8 0.8 reshape.42
  14.6 2.0 %collective-permute-start = (f32[1,96,128]{2,1,0:T(8,128)S(1)}, f32[1,96,128]{2,1,0:T(8,128)S(1)}, u32[]{:S(2)}, u32[]{:S(2)}) collective-permute-start(f32[1,96,128]{2,1,0:T(8,128)S(1)} %maximum_bitcast_fusion), channel_id=1, source_target_pairs={{0,8},{4,12},{8,0},{12,4},{16,24},{20,28},{24,16},{28,20},{1,9},{5... | collective-permute-start | bytes 147464 | tf_op jit(solution)/shard_map/ppermute | solution.py:34
  16.6 0.5 collective-permute-start.5
  17.1 0.0 copy-done.1
  17.1 1.7 %fusion.kept = f32[32,32,256]{2,1,0:T(8,128)S(1)} fusion(bf16[32,2,32,512]{3,2,1,0:T(8,128)(2,1)} %bitcast.27, s32[]{:T(128)S(6)} %select_n.4, bf16[512,256]{1,0:T(8,128)(2,1)S(1)} %copy-done.1), kind=kOutput, calls=%fused_computation | convolution fusion | flops 268435456 | bytes 2359300 | tf_op jit(solution)/shard_map/dot_general | solution.py:431
  18.8 2.8 %collective-permute-done = f32[1,96,128]{2,1,0:T(8,128)S(1)} collective-permute-done((f32[1,96,128]{2,1,0:T(8,128)S(1)}, f32[1,96,128]{2,1,0:T(8,128)S(1)}, u32[]{:S(2)}, u32[]{:S(2)}) %collective-permute-start) | collective-permute-done | bytes 49184 | tf_op jit(solution)/shard_map/ppermute | solution.py:34
  21.6 2.7 %all-to-all-done = f32[16,8,512]{2,1,0:T(8,128)S(1)} async-done(((f32[16,8,512]{2,1,0:T(8,128)}), f32[16,8,512]{2,1,0:T(8,128)S(1)}, u32[]{:S(2)}, u32[]{:S(2)}) %all-to-all-start) | async-done | bytes 262176 | tf_op jit(solution)/shard_map/all_to_all | solution.py:449
  24.3 0.0 collective-permute-done.1.refs_0_
  24.3 0.6 collective-permute-start.2
  24.9 0.1 fusion.5
  25.1 0.7 broadcast_in_dim.10
  25.8 2.9 %all-to-all-start.1 = ((f32[32,8,256]{2,1,0:T(8,128)}), f32[32,8,256]{2,1,0:T(8,128)S(1)}, u32[]{:S(2)}, u32[]{:S(2)}) async-start(f32[32,8,256]{2,1,0:T(8,128)} %broadcast_in_dim.10), calls=%async_computation.1 | async-start | bytes 524288 | tf_op jit(solution)/shard_map/all_to_all | solution.py:457
  28.7 2.4 %collective-permute-done.2 = f32[2,96,128]{2,1,0:T(8,128)S(1)} collective-permute-done((f32[2,96,128]{2,1,0:T(8,128)S(1)}, f32[2,96,128]{2,1,0:T(8,128)S(1)}, u32[]{:S(2)}, u32[]{:S(2)}) %collective-permute-start.2) | collective-permute-done | bytes 98336 | tf_op jit(solution)/shard_map/ppermute | solution.py:34
  31.1 0.8 collective-permute-start.3
  31.9 7.8 %collective-permute-done.3.other = f32[416,128]{1,0:T(8,128)S(1)} collective-permute-done((f32[416,128]{1,0:T(8,128)S(1)}, f32[416,128]{1,0:T(8,128)S(1)}, u32[]{:S(2)}, u32[]{:S(2)}) %collective-permute-start.3) | collective-permute-done | bytes 213024 | tf_op jit(solution)/shard_map/ppermute | solution.py:34
  39.7 0.0 all-to-all-done.1
  39.7 0.0 copy-start
  39.7 0.0 collective-permute-done.5.refs_1_
  39.7 5.7 %solve_last.1 = f32[8,128,128]{2,1,0:T(8,128)} custom-call(f32[16,2,8,256]{3,2,1,0:T(8,128)S(1)} %bitcast.26, f32[32,32,256]{2,1,0:T(8,128)S(1)} %fusion.kept, f32[16,32,256]{2,1,0:T(8,128)S(1)} %collective-permute-done.1.refs_0_, f32[16,32,256]{2,1,0:T(8,128)S(1)} %collective-permute-done.5.refs_1_), custom_call_target="tpu_custom_call" | custom-call | flops 6000000000 | tf_op jit(solution)/shard_map/solve_last/pallas_call | solution.py:279
  45.4 3.9 %all-to-all-start.2 = ((f32[8,128,128]{2,1,0:T(8,128)}), f32[8,128,128]{2,1,0:T(8,128)S(1)}, u32[]{:S(2)}, u32[]{:S(2)}) async-start(f32[8,128,128]{2,1,0:T(8,128)} %solve_last.1), calls=%async_computation.2 | async-start | bytes 1048576 | tf_op jit(solution)/shard_map/all_to_all | solution.py:475
  49.3 0.0 copy-done
  49.3 0.4 first_sums.1
  49.7 1.6 %collective-permute-start.4 = (f32[160,256]{1,0:T(8,128)S(1)}, f32[160,256]{1,0:T(8,128)S(1)}, u32[]{:S(2)}, u32[]{:S(2)}) collective-permute-start(f32[160,256]{1,0:T(8,128)S(1)} %get-tuple-element.20), channel_id=1, source_target_pairs={{0,1},{1,0},{2,3},{3,2},{4,5},{5,4},{6,7},{7,6},{8,9},{9,8},{10,11... | collective-permute-start | bytes 491528 | tf_op jit(solution)/shard_map/ppermute | solution.py:34
  51.3 2.9 %collective-permute-start.6 = (f32[2,32,128]{2,1,0:T(8,128)S(1)}, f32[2,32,128]{2,1,0:T(8,128)S(1)}, u32[]{:S(2)}, u32[]{:S(2)}) collective-permute-start(f32[2,32,128]{2,1,0:T(8,128)S(1)} %get-tuple-element.24), channel_id=1, source_target_pairs={{0,16},{4,20},{8,24},{12,28},{16,0},{20,4},{24,8},{28,12},{1,17},{... | collective-permute-start | bytes 98312 | tf_op jit(solution)/shard_map/ppermute | solution.py:34
  54.2 10.9 %collective-permute-done.6 = f32[2,32,128]{2,1,0:T(8,128)S(1)} collective-permute-done((f32[2,32,128]{2,1,0:T(8,128)S(1)}, f32[2,32,128]{2,1,0:T(8,128)S(1)}, u32[]{:S(2)}, u32[]{:S(2)}) %collective-permute-start.6) | collective-permute-done | bytes 32800 | tf_op jit(solution)/shard_map/ppermute | solution.py:34
  65.1 0.0 collective-permute-start.7
  65.1 0.0 collective-permute-done.4
  65.1 0.1 collective-permute-start.8
  65.2 4.1 %collective-permute-done.7 = f32[4,32,128]{2,1,0:T(8,128)S(1)} collective-permute-done((f32[4,32,128]{2,1,0:T(8,128)S(1)}, f32[4,32,128]{2,1,0:T(8,128)S(1)}, u32[]{:S(2)}, u32[]{:S(2)}) %collective-permute-start.7) | collective-permute-done | bytes 65568 | tf_op jit(solution)/shard_map/ppermute | solution.py:34
  69.4 0.0 all-to-all-done.2.pieces
  69.4 1.0 %sketch.1 = f32[16,4,8,128]{3,2,1,0:T(8,128)} custom-call(f32[8,128,128]{2,1,0:T(8,128)S(1)} %all-to-all-done.2.pieces, f32[416,128]{1,0:T(8,128)S(1)} %pad_maximum_fusion.mine, f32[416,128]{1,0:T(8,128)S(1)} %collective-permute-done.3.other), custom_call_target="tpu_custom_call" | custom-call | tf_op jit(solution)/shard_map/sketch/pallas_call | solution.py:324
  70.3 0.0 collective-permute-done.8.refs_1_
  70.3 4.9 %all-to-all-start.3 = ((f32[16,4,8,128]{3,2,1,0:T(8,128)}), f32[16,4,8,128]{3,2,1,0:T(8,128)S(1)}, u32[]{:S(2)}, u32[]{:S(2)}) async-start(f32[16,4,8,128]{3,2,1,0:T(8,128)} %sketch.1), calls=%async_computation.3 | async-start | bytes 524288 | tf_op jit(solution)/shard_map/all_to_all | solution.py:489
  75.3 0.1 collective-permute-start.9
  75.3 1.3 %collective-permute-done.9.refs_1_ = f32[8,32,128]{2,1,0:T(8,128)S(1)} collective-permute-done((f32[8,32,128]{2,1,0:T(8,128)S(1)}, f32[8,32,128]{2,1,0:T(8,128)S(1)}, u32[]{:S(2)}, u32[]{:S(2)}) %collective-permute-start.9) | collective-permute-done | bytes 131104 | tf_op jit(solution)/shard_map/ppermute | solution.py:34
  76.7 0.7 place.1
  77.4 5.0 %solve_first.1 = f32[32,128]{1,0:T(8,128)} custom-call(f32[160,256]{1,0:T(8,128)S(1)} %add.10.refs_0_, f32[160,256]{1,0:T(8,128)S(1)} %collective-permute-done.8.refs_1_), custom_call_target="tpu_custom_call" | custom-call | tf_op jit(solution)/shard_map/solve_first/pallas_call | solution.py:382
  82.4 1.8 %all-to-all-done.3 = f32[16,4,8,128]{3,2,1,0:T(8,128)S(1)} async-done(((f32[16,4,8,128]{3,2,1,0:T(8,128)}), f32[16,4,8,128]{3,2,1,0:T(8,128)S(1)}, u32[]{:S(2)}, u32[]{:S(2)}) %all-to-all-start.3) | async-done | bytes 262176 | tf_op jit(solution)/shard_map/all_to_all | solution.py:489
  84.2 0.8 copy.12
  (14 shorter events, 0.1 us)
Async XLA Ops:
  0.6 16.5 %copy-start.1 = (bf16[512,256]{1,0:T(8,128)(2,1)S(1)}, bf16[512,256]{1,0:T(8,128)(2,1)}, u32[]{:S(2)}) copy-start(bf16[512,256]{1,0:T(8,128)(2,1)} %last_m_hbm.1) | copy-start | bytes 786436
  0.6 13.1 %copy-start.2 = (bf16[32,128]{1,0:T(8,128)(2,1)S(1)}, bf16[32,128]{1,0:T(8,128)(2,1)}, u32[]{:S(2)}) copy-start(bf16[32,128]{1,0:T(8,128)(2,1)} %param.8) | copy-start | bytes 24580
  4.8 19.5 %collective-permute-start.1 = (f32[16,32,256]{2,1,0:T(8,128)}, f32[16,32,256]{2,1,0:T(8,128)S(1)}, u32[]{:S(2)}, u32[]{:S(2)}) collective-permute-start(f32[16,32,256]{2,1,0:T(8,128)} %get-tuple-element.16), channel_id=1, source_target_pairs={{0,1},{1,0},{2,3},{3,2},{4,5},{5,4},{6,7},{7,6},{8,9},{9,8},{10,11... | collective-permute-start | bytes 1572872 | tf_op jit(solution)/shard_map/ppermute | solution.py:34
  7.9 16.4 %all-to-all-start = ((f32[16,8,512]{2,1,0:T(8,128)}), f32[16,8,512]{2,1,0:T(8,128)S(1)}, u32[]{:S(2)}, u32[]{:S(2)}) async-start(f32[16,8,512]{2,1,0:T(8,128)} %bitcast.30), calls=%async_computation | async-start | bytes 524288 | tf_op jit(solution)/shard_map/all_to_all | solution.py:449
  14.6 7.0 %collective-permute-start = (f32[1,96,128]{2,1,0:T(8,128)S(1)}, f32[1,96,128]{2,1,0:T(8,128)S(1)}, u32[]{:S(2)}, u32[]{:S(2)}) collective-permute-start(f32[1,96,128]{2,1,0:T(8,128)S(1)} %maximum_bitcast_fusion), channel_id=1, source_target_pairs={{0,8},{4,12},{8,0},{12,4},{16,24},{20,28},{24,16},{28,20},{1,9},{5... | collective-permute-start | bytes 147464 | tf_op jit(solution)/shard_map/ppermute | solution.py:34
  16.6 23.1 %collective-permute-start.5 = (f32[16,32,256]{2,1,0:T(8,128)}, f32[16,32,256]{2,1,0:T(8,128)S(1)}, u32[]{:S(2)}, u32[]{:S(2)}) collective-permute-start(f32[16,32,256]{2,1,0:T(8,128)} %get-tuple-element.23), channel_id=1, source_target_pairs={{0,1},{1,0},{2,3},{3,2},{4,5},{5,4},{6,7},{7,6},{8,9},{9,8},{10,11... | collective-permute-start | bytes 1572872 | tf_op jit(solution)/shard_map/ppermute | solution.py:34
  24.3 6.8 %collective-permute-start.2 = (f32[2,96,128]{2,1,0:T(8,128)S(1)}, f32[2,96,128]{2,1,0:T(8,128)S(1)}, u32[]{:S(2)}, u32[]{:S(2)}) collective-permute-start(f32[2,96,128]{2,1,0:T(8,128)S(1)} %pad_maximum_fusion.2), channel_id=1, source_target_pairs={{0,16},{4,20},{8,24},{12,28},{16,0},{20,4},{24,8},{28,12},{1,17},{... | collective-permute-start | bytes 294920 | tf_op jit(solution)/shard_map/ppermute | solution.py:34
  25.8 13.9 %all-to-all-start.1 = ((f32[32,8,256]{2,1,0:T(8,128)}), f32[32,8,256]{2,1,0:T(8,128)S(1)}, u32[]{:S(2)}, u32[]{:S(2)}) async-start(f32[32,8,256]{2,1,0:T(8,128)} %broadcast_in_dim.10), calls=%async_computation.1 | async-start | bytes 524288 | tf_op jit(solution)/shard_map/all_to_all | solution.py:457
  31.1 8.5 %collective-permute-start.3 = (f32[416,128]{1,0:T(8,128)S(1)}, f32[416,128]{1,0:T(8,128)S(1)}, u32[]{:S(2)}, u32[]{:S(2)}) collective-permute-start(f32[416,128]{1,0:T(8,128)S(1)} %pad_maximum_fusion.mine), channel_id=1, source_target_pairs={{0,4},{4,0},{8,12},{12,8},{16,20},{20,16},{24,28},{28,24},{1,5},{5... | collective-permute-start | bytes 638984 | tf_op jit(solution)/shard_map/ppermute | solution.py:34
  39.7 9.6 %copy-start = (f32[32,256]{1,0:T(8,128)S(1)}, f32[32,256]{1,0:T(8,128)}, u32[]{:S(2)}) copy-start(f32[32,256]{1,0:T(8,128)} %get-tuple-element.15.rows) | copy-start | bytes 98308
  45.4 23.9 %all-to-all-start.2 = ((f32[8,128,128]{2,1,0:T(8,128)}), f32[8,128,128]{2,1,0:T(8,128)S(1)}, u32[]{:S(2)}, u32[]{:S(2)}) async-start(f32[8,128,128]{2,1,0:T(8,128)} %solve_last.1), calls=%async_computation.2 | async-start | bytes 1048576 | tf_op jit(solution)/shard_map/all_to_all | solution.py:475
  49.7 15.4 %collective-permute-start.4 = (f32[160,256]{1,0:T(8,128)S(1)}, f32[160,256]{1,0:T(8,128)S(1)}, u32[]{:S(2)}, u32[]{:S(2)}) collective-permute-start(f32[160,256]{1,0:T(8,128)S(1)} %get-tuple-element.20), channel_id=1, source_target_pairs={{0,1},{1,0},{2,3},{3,2},{4,5},{5,4},{6,7},{7,6},{8,9},{9,8},{10,11... | collective-permute-start | bytes 491528 | tf_op jit(solution)/shard_map/ppermute | solution.py:34
  51.3 13.8 %collective-permute-start.6 = (f32[2,32,128]{2,1,0:T(8,128)S(1)}, f32[2,32,128]{2,1,0:T(8,128)S(1)}, u32[]{:S(2)}, u32[]{:S(2)}) collective-permute-start(f32[2,32,128]{2,1,0:T(8,128)S(1)} %get-tuple-element.24), channel_id=1, source_target_pairs={{0,16},{4,20},{8,24},{12,28},{16,0},{20,4},{24,8},{28,12},{1,17},{... | collective-permute-start | bytes 98312 | tf_op jit(solution)/shard_map/ppermute | solution.py:34
  65.1 4.3 %collective-permute-start.7 = (f32[4,32,128]{2,1,0:T(8,128)S(1)}, f32[4,32,128]{2,1,0:T(8,128)S(1)}, u32[]{:S(2)}, u32[]{:S(2)}) collective-permute-start(f32[4,32,128]{2,1,0:T(8,128)S(1)} %pad_maximum_fusion.3), channel_id=1, source_target_pairs={{0,8},{4,12},{8,0},{12,4},{16,24},{20,28},{24,16},{28,20},{1,9},{5... | collective-permute-start | bytes 196616 | tf_op jit(solution)/shard_map/ppermute | solution.py:34
  65.1 5.2 %collective-permute-start.8 = (f32[160,256]{1,0:T(8,128)S(1)}, f32[160,256]{1,0:T(8,128)S(1)}, u32[]{:S(2)}, u32[]{:S(2)}) collective-permute-start(f32[160,256]{1,0:T(8,128)S(1)} %add.10.refs_0_), channel_id=1, source_target_pairs={{0,2},{2,0},{1,3},{3,1},{4,6},{6,4},{5,7},{7,5},{8,10},{10,8},{9,1... | collective-permute-start | bytes 491528 | tf_op jit(solution)/shard_map/ppermute | solution.py:34
  70.3 13.8 %all-to-all-start.3 = ((f32[16,4,8,128]{3,2,1,0:T(8,128)}), f32[16,4,8,128]{3,2,1,0:T(8,128)S(1)}, u32[]{:S(2)}, u32[]{:S(2)}) async-start(f32[16,4,8,128]{3,2,1,0:T(8,128)} %sketch.1), calls=%async_computation.3 | async-start | bytes 524288 | tf_op jit(solution)/shard_map/all_to_all | solution.py:489
  75.3 1.4 %collective-permute-start.9 = (f32[8,32,128]{2,1,0:T(8,128)S(1)}, f32[8,32,128]{2,1,0:T(8,128)S(1)}, u32[]{:S(2)}, u32[]{:S(2)}) collective-permute-start(f32[8,32,128]{2,1,0:T(8,128)S(1)} %constant_dynamic-update-slice_fusion.refs_0_), channel_id=1, source_target_pairs={{0,2},{2,0},{1,3},{3,1},{4,6},{6,4},{5,7},{7,5},{8,10},{10,8},{9,1... | collective-permute-start | bytes 393224 | tf_op jit(solution)/shard_map/ppermute | solution.py:34

commit v16 on v14

--- a/solution.py
+++ b/solution.py
@@ -293,20 +293,23 @@
     x_cells = packed.shape[1] - left_at
     weights = jnp.concatenate([packed[k, left_at:] for k in range(blocks)], axis=0)
     weights = weights.astype(jnp.bfloat16)
+    columns = []
     for j in range(y_own):
-        column = jnp.concatenate(
-            [pieces[me ^ o, j * x_cells : (j + 1) * x_cells] for o in order], axis=0
+        columns += two_terms(
+            jnp.concatenate(
+                [pieces[me ^ o, j * x_cells : (j + 1) * x_cells] for o in order], axis=0
+            )
         )
-        high = column.astype(jnp.bfloat16)
-        low = (column - high.astype(jnp.float32)).astype(jnp.bfloat16)
-        both = lax.dot_general(
-            weights,
-            jnp.concatenate([high, low], axis=1),
-            COL_COL,
-            preferred_element_type=jnp.float32,
-        )
-        both = both[:, :cols] + both[:, cols:]
-        out[:, j] = both.reshape(out.shape[0], out.shape[2], cols)
+    sums = lax.dot_general(
+        weights,
+        jnp.concatenate(columns, axis=1),
+        COL_COL,
+        preferred_element_type=jnp.float32,
+    )
+    for j in range(y_own):
+        at = 2 * j * cols
+        core = sums[:, at : at + cols] + sums[:, at + cols : at + 2 * cols]
+        out[:, j] = core.reshape(out.shape[0], out.shape[2], cols)
     extra[...] = pieces[:, y_own * x_cells :]
 
 

time: 82.9 us -> 82.9 us (level)
  no operation moved by 1% of the time
where the time goes in v16:
time: 82.9 us; the launch traced here: 82.4 us
  waiting for transfers between devices  31.7 us (38%)
  starting transfers between devices  28.7 us (35%)
  Pallas kernels  17 us (21%)
  local copies, waits for them, and re-layouts  2.28 us (3%)
  matrix products  1.8 us (2%)
    ppermute x8, waiting for transfers between devices, swap(): lax.ppermute(array, axis, [(s, s ^ bits) for s in range(lax.axis_size(axi...  18.7 us
    ppermute x8, starting transfers between devices, swap(): lax.ppermute(array, axis, [(s, s ^ bits) for s in range(lax.axis_size(axi...  11.8 us
    all_to_all x1, waiting for transfers between devices, per_device(): received = lax.all_to_all(middle, group, 0, 0, tiled=True)  7.91 us
    all_to_all x1, starting transfers between devices, per_device(): lax.all_to_all(last_part.reshape(-1, own, m_cells), group, 0, 0, tiled=True)  5.91 us
    pallas_call x1, Pallas kernels, solve_last(): pl.pallas_call(functools.partial(last_kernel, y_own), out_shape=jax.Shape...  5.8 us
    pallas_call x1, Pallas kernels, solve_first(): pl.pallas_call(first_kernel, out_shape=jax.ShapeDtypeStruct((x_cells, sum...  4.98 us
    all_to_all x1, starting transfers between devices, per_device(): received = lax.all_to_all(middle, group, 0, 0, tiled=True)  4.63 us
    all_to_all x1, waiting for transfers between devices, per_device(): pieces = lax.all_to_all(projected, 'gx', 0, 0, tiled=True)  4.41 us
  transfers between devices with their start and end apart: 12, of which 9 were waited for; matrix products, arithmetic and copies ran while one was open for 4% of the time, Pallas kernels for 7%

profile of v16, /device:TPU:0, one launch (start us, length us, event | category | flops | bytes accessed | tf_op | source)
XLA Modules:
  0.0 82.4 jit_solution(6114580581446343839)
XLA Ops:
  0.6 0.0 copy-start.1
  0.6 0.0 copy-start.2
  0.7 4.2 %local_products.1 = (f32[128,512]{1,0:T(8,128)}, f32[32,256]{1,0:T(8,128)}, f32[16,32,256]{2,1,0:T(8,128)}, f32[16,32,256]{2,1,0:T(8,128)}) custom-call(bf16[32,64,512]{2,1,0:T(8,128)(2,1)} %field_hbm.1, bf16[32,128]{1,0:T(8,128)(2,1)} %last_x_hbm.1, bf16[64,128]{1,0:T(8,128)(2,1)} %last_y_hbm.1, bf16[64,256]{1,0:T(8,128)(2,1)} %right_y_hbm.1, ...), custom_call_target="tpu_custom_call" | custom-call | tf_op jit(solution)/shard_map/local_products/pallas_call | solution.py:210
  4.8 3.0 %collective-permute-start = (f32[16,32,256]{2,1,0:T(8,128)}, f32[16,32,256]{2,1,0:T(8,128)S(1)}, u32[]{:S(2)}, u32[]{:S(2)}) collective-permute-start(f32[16,32,256]{2,1,0:T(8,128)} %get-tuple-element.16), channel_id=1, source_target_pairs={{0,1},{1,0},{2,3},{3,2},{4,5},{5,4},{6,7},{7,6},{8,9},{9,8},{10,11... | collective-permute-start | bytes 1572872 | tf_op jit(solution)/shard_map/ppermute | solution.py:34
  7.9 5.9 %all-to-all-start = ((f32[16,8,512]{2,1,0:T(8,128)}), f32[16,8,512]{2,1,0:T(8,128)S(1)}, u32[]{:S(2)}, u32[]{:S(2)}) async-start(f32[16,8,512]{2,1,0:T(8,128)} %bitcast.35), calls=%async_computation | async-start | bytes 524288 | tf_op jit(solution)/shard_map/all_to_all | solution.py:440
  13.8 0.8 copy_bitcast_fusion
  14.5 0.0 copy-done.2
  14.6 2.0 %collective-permute-start.1 = (f32[1,96,128]{2,1,0:T(8,128)S(1)}, f32[1,96,128]{2,1,0:T(8,128)S(1)}, u32[]{:S(2)}, u32[]{:S(2)}) collective-permute-start(f32[1,96,128]{2,1,0:T(8,128)S(1)} %maximum_bitcast_fusion), channel_id=1, source_target_pairs={{0,8},{4,12},{8,0},{12,4},{16,24},{20,28},{24,16},{28,20},{1,9},{5... | collective-permute-start | bytes 147464 | tf_op jit(solution)/shard_map/ppermute | solution.py:34
  16.5 0.5 collective-permute-start.4
  17.1 0.0 copy-done.1
  17.1 1.7 %fusion.kept = f32[32,32,256]{2,1,0:T(8,128)S(1)} fusion(bf16[32,2,32,512]{3,2,1,0:T(8,128)(2,1)} %bitcast.33, s32[]{:T(128)S(6)} %select_n.4, bf16[512,256]{1,0:T(8,128)(2,1)S(1)} %copy-done.1), kind=kOutput, calls=%fused_computation | convolution fusion | flops 268435456 | bytes 2359300 | tf_op jit(solution)/shard_map/dot_general | solution.py:423
  18.7 2.9 %collective-permute-done.1 = f32[1,96,128]{2,1,0:T(8,128)S(1)} collective-permute-done((f32[1,96,128]{2,1,0:T(8,128)S(1)}, f32[1,96,128]{2,1,0:T(8,128)S(1)}, u32[]{:S(2)}, u32[]{:S(2)}) %collective-permute-start.1) | collective-permute-done | bytes 49184 | tf_op jit(solution)/shard_map/ppermute | solution.py:34
  21.6 3.0 %collective-permute-start.2 = (f32[2,96,128]{2,1,0:T(8,128)S(1)}, f32[2,96,128]{2,1,0:T(8,128)S(1)}, u32[]{:S(2)}, u32[]{:S(2)}) collective-permute-start(f32[2,96,128]{2,1,0:T(8,128)S(1)} %pad_maximum_fusion.2), channel_id=1, source_target_pairs={{0,16},{4,20},{8,24},{12,28},{16,0},{20,4},{24,8},{28,12},{1,17},{... | collective-permute-start | bytes 294920 | tf_op jit(solution)/shard_map/ppermute | solution.py:34
  24.6 0.0 all-to-all-done
  24.6 0.0 collective-permute-done.refs_0_
  24.7 0.1 fusion.5
  24.8 0.7 broadcast_in_dim.10
  25.6 2.6 %all-to-all-start.1 = ((f32[32,8,256]{2,1,0:T(8,128)}), f32[32,8,256]{2,1,0:T(8,128)S(1)}, u32[]{:S(2)}, u32[]{:S(2)}) async-start(f32[32,8,256]{2,1,0:T(8,128)} %broadcast_in_dim.10), calls=%async_computation.1 | async-start | bytes 524288 | tf_op jit(solution)/shard_map/all_to_all | solution.py:448
  28.2 1.2 %collective-permute-done.2 = f32[2,96,128]{2,1,0:T(8,128)S(1)} collective-permute-done((f32[2,96,128]{2,1,0:T(8,128)S(1)}, f32[2,96,128]{2,1,0:T(8,128)S(1)}, u32[]{:S(2)}, u32[]{:S(2)}) %collective-permute-start.2) | collective-permute-done | bytes 98336 | tf_op jit(solution)/shard_map/ppermute | solution.py:34
  29.3 1.5 %collective-permute-start.3 = (f32[4,96,128]{2,1,0:T(8,128)S(1)}, f32[4,96,128]{2,1,0:T(8,128)S(1)}, u32[]{:S(2)}, u32[]{:S(2)}) collective-permute-start(f32[4,96,128]{2,1,0:T(8,128)S(1)} %pad_maximum_fusion.1), channel_id=1, source_target_pairs={{0,4},{4,0},{8,12},{12,8},{16,20},{20,16},{24,28},{28,24},{1,5},{5... | collective-permute-start | bytes 589832 | tf_op jit(solution)/shard_map/ppermute | solution.py:34
  30.9 7.4 %collective-permute-done.3 = f32[4,96,128]{2,1,0:T(8,128)S(1)} collective-permute-done((f32[4,96,128]{2,1,0:T(8,128)S(1)}, f32[4,96,128]{2,1,0:T(8,128)S(1)}, u32[]{:S(2)}, u32[]{:S(2)}) %collective-permute-start.3) | collective-permute-done | bytes 196640 | tf_op jit(solution)/shard_map/ppermute | solution.py:34
  38.2 0.6 all-to-all-done.1
  38.8 0.0 collective-permute-done.4.refs_1_
  38.8 0.0 copy-start
  38.9 5.8 %solve_last.1 = f32[8,160,128]{2,1,0:T(8,128)} custom-call(f32[16,2,8,256]{3,2,1,0:T(8,128)S(1)} %bitcast.31, f32[32,128]{1,0:T(8,128)S(1)} %bitcast.32, f32[32,32,256]{2,1,0:T(8,128)S(1)} %fusion.kept, f32[16,32,256]{2,1,0:T(8,128)S(1)} %collective-permute-done.refs_0_, f32[16,32,256]{2,1,0:T(8,128)S(1)} %collective-permute-done.4.refs_1_), custom_call_target="tpu_custom_call" | custom-call | flops 6000000000 | tf_op jit(solution)/shard_map/solve_last/pallas_call | solution.py:280
  44.7 3.8 %all-to-all-start.2 = ((f32[8,160,128]{2,1,0:T(8,128)}), f32[8,160,128]{2,1,0:T(8,128)S(1)}, u32[]{:S(2)}, u32[]{:S(2)}) async-start(f32[8,160,128]{2,1,0:T(8,128)} %solve_last.1), calls=%async_computation.2 | async-start | bytes 1310720 | tf_op jit(solution)/shard_map/all_to_all | solution.py:463
  48.5 0.0 copy-done
  48.5 0.4 first_sums.1
  48.9 1.6 %collective-permute-start.5 = (f32[160,256]{1,0:T(8,128)S(1)}, f32[160,256]{1,0:T(8,128)S(1)}, u32[]{:S(2)}, u32[]{:S(2)}) collective-permute-start(f32[160,256]{1,0:T(8,128)S(1)} %first_sums.1), channel_id=1, source_target_pairs={{0,1},{1,0},{2,3},{3,2},{4,5},{5,4},{6,7},{7,6},{8,9},{9,8},{10,11... | collective-permute-start | bytes 491528 | tf_op jit(solution)/shard_map/ppermute | solution.py:34
  50.5 4.6 %collective-permute-done.5 = f32[160,256]{1,0:T(8,128)S(1)} collective-permute-done((f32[160,256]{1,0:T(8,128)S(1)}, f32[160,256]{1,0:T(8,128)S(1)}, u32[]{:S(2)}, u32[]{:S(2)}) %collective-permute-start.5) | collective-permute-done | bytes 163872 | tf_op jit(solution)/shard_map/ppermute | solution.py:34
  55.1 0.1 collective-permute-start.6
  55.2 1.4 %collective-permute-done.6.refs_1_ = f32[160,256]{1,0:T(8,128)S(1)} collective-permute-done((f32[160,256]{1,0:T(8,128)S(1)}, f32[160,256]{1,0:T(8,128)S(1)}, u32[]{:S(2)}, u32[]{:S(2)}) %collective-permute-start.6) | collective-permute-done | bytes 163872 | tf_op jit(solution)/shard_map/ppermute | solution.py:34
  56.6 5.0 %solve_first.1 = f32[32,128]{1,0:T(8,128)} custom-call(f32[160,256]{1,0:T(8,128)S(1)} %add.12.refs_0_, f32[160,256]{1,0:T(8,128)S(1)} %collective-permute-done.6.refs_1_), custom_call_target="tpu_custom_call" | custom-call | tf_op jit(solution)/shard_map/solve_first/pallas_call | solution.py:375
  61.6 4.4 %all-to-all-done.2.pieces = f32[8,160,128]{2,1,0:T(8,128)S(1)} async-done(((f32[8,160,128]{2,1,0:T(8,128)}), f32[8,160,128]{2,1,0:T(8,128)S(1)}, u32[]{:S(2)}, u32[]{:S(2)}) %all-to-all-start.2) | async-done | bytes 655392 | tf_op jit(solution)/shard_map/all_to_all | solution.py:463
  66.0 1.0 %sketch.1 = (f32[16,4,8,128]{3,2,1,0:T(8,128)}, f32[8,32,128]{2,1,0:T(8,128)S(1)}) custom-call(f32[8,160,128]{2,1,0:T(8,128)S(1)} %all-to-all-done.2.pieces, f32[8,96,128]{2,1,0:T(8,128)S(1)} %pad_maximum_fusion.packed), custom_call_target="tpu_custom_call" | custom-call | tf_op jit(solution)/shard_map/sketch/pallas_call | solution.py:320
  66.9 4.6 %all-to-all-start.3 = ((f32[16,4,8,128]{3,2,1,0:T(8,128)}), f32[16,4,8,128]{3,2,1,0:T(8,128)S(1)}, u32[]{:S(2)}, u32[]{:S(2)}) async-start(f32[16,4,8,128]{3,2,1,0:T(8,128)} %get-tuple-element.25), calls=%async_computation.3 | async-start | bytes 524288 | tf_op jit(solution)/shard_map/all_to_all | solution.py:474
  71.6 0.1 collective-permute-start.7
  71.6 1.3 %collective-permute-done.7.refs_1_ = f32[8,32,128]{2,1,0:T(8,128)S(1)} collective-permute-done((f32[8,32,128]{2,1,0:T(8,128)S(1)}, f32[8,32,128]{2,1,0:T(8,128)S(1)}, u32[]{:S(2)}, u32[]{:S(2)}) %collective-permute-start.7) | collective-permute-done | bytes 131104 | tf_op jit(solution)/shard_map/ppermute | solution.py:34
  73.0 0.7 place.1
  73.7 7.9 %all-to-all-done.3 = f32[16,4,8,128]{3,2,1,0:T(8,128)S(1)} async-done(((f32[16,4,8,128]{3,2,1,0:T(8,128)}), f32[16,4,8,128]{3,2,1,0:T(8,128)S(1)}, u32[]{:S(2)}, u32[]{:S(2)}) %all-to-all-start.3) | async-done | bytes 262176 | tf_op jit(solution)/shard_map/all_to_all | solution.py:474
  81.6 0.8 copy.12
  (9 shorter events, 0.1 us)
Async XLA Ops:
  0.6 16.4 %copy-start.1 = (bf16[512,256]{1,0:T(8,128)(2,1)S(1)}, bf16[512,256]{1,0:T(8,128)(2,1)}, u32[]{:S(2)}) copy-start(bf16[512,256]{1,0:T(8,128)(2,1)} %last_m_hbm.1) | copy-start | bytes 786436
  0.6 13.9 %copy-start.2 = (bf16[32,128]{1,0:T(8,128)(2,1)S(1)}, bf16[32,128]{1,0:T(8,128)(2,1)}, u32[]{:S(2)}) copy-start(bf16[32,128]{1,0:T(8,128)(2,1)} %param.8) | copy-start | bytes 24580
  4.8 19.8 %collective-permute-start = (f32[16,32,256]{2,1,0:T(8,128)}, f32[16,32,256]{2,1,0:T(8,128)S(1)}, u32[]{:S(2)}, u32[]{:S(2)}) collective-permute-start(f32[16,32,256]{2,1,0:T(8,128)} %get-tuple-element.16), channel_id=1, source_target_pairs={{0,1},{1,0},{2,3},{3,2},{4,5},{5,4},{6,7},{7,6},{8,9},{9,8},{10,11... | collective-permute-start | bytes 1572872 | tf_op jit(solution)/shard_map/ppermute | solution.py:34
  7.9 16.8 %all-to-all-start = ((f32[16,8,512]{2,1,0:T(8,128)}), f32[16,8,512]{2,1,0:T(8,128)S(1)}, u32[]{:S(2)}, u32[]{:S(2)}) async-start(f32[16,8,512]{2,1,0:T(8,128)} %bitcast.35), calls=%async_computation | async-start | bytes 524288 | tf_op jit(solution)/shard_map/all_to_all | solution.py:440
  14.6 7.1 %collective-permute-start.1 = (f32[1,96,128]{2,1,0:T(8,128)S(1)}, f32[1,96,128]{2,1,0:T(8,128)S(1)}, u32[]{:S(2)}, u32[]{:S(2)}) collective-permute-start(f32[1,96,128]{2,1,0:T(8,128)S(1)} %maximum_bitcast_fusion), channel_id=1, source_target_pairs={{0,8},{4,12},{8,0},{12,4},{16,24},{20,28},{24,16},{28,20},{1,9},{5... | collective-permute-start | bytes 147464 | tf_op jit(solution)/shard_map/ppermute | solution.py:34
  16.5 22.3 %collective-permute-start.4 = (f32[16,32,256]{2,1,0:T(8,128)}, f32[16,32,256]{2,1,0:T(8,128)S(1)}, u32[]{:S(2)}, u32[]{:S(2)}) collective-permute-start(f32[16,32,256]{2,1,0:T(8,128)} %get-tuple-element.21), channel_id=1, source_target_pairs={{0,1},{1,0},{2,3},{3,2},{4,5},{5,4},{6,7},{7,6},{8,9},{9,8},{10,11... | collective-permute-start | bytes 1572872 | tf_op jit(solution)/shard_map/ppermute | solution.py:34
  21.6 7.7 %collective-permute-start.2 = (f32[2,96,128]{2,1,0:T(8,128)S(1)}, f32[2,96,128]{2,1,0:T(8,128)S(1)}, u32[]{:S(2)}, u32[]{:S(2)}) collective-permute-start(f32[2,96,128]{2,1,0:T(8,128)S(1)} %pad_maximum_fusion.2), channel_id=1, source_target_pairs={{0,16},{4,20},{8,24},{12,28},{16,0},{20,4},{24,8},{28,12},{1,17},{... | collective-permute-start | bytes 294920 | tf_op jit(solution)/shard_map/ppermute | solution.py:34
  25.6 13.3 %all-to-all-start.1 = ((f32[32,8,256]{2,1,0:T(8,128)}), f32[32,8,256]{2,1,0:T(8,128)S(1)}, u32[]{:S(2)}, u32[]{:S(2)}) async-start(f32[32,8,256]{2,1,0:T(8,128)} %broadcast_in_dim.10), calls=%async_computation.1 | async-start | bytes 524288 | tf_op jit(solution)/shard_map/all_to_all | solution.py:448
  29.3 8.9 %collective-permute-start.3 = (f32[4,96,128]{2,1,0:T(8,128)S(1)}, f32[4,96,128]{2,1,0:T(8,128)S(1)}, u32[]{:S(2)}, u32[]{:S(2)}) collective-permute-start(f32[4,96,128]{2,1,0:T(8,128)S(1)} %pad_maximum_fusion.1), channel_id=1, source_target_pairs={{0,4},{4,0},{8,12},{12,8},{16,20},{20,16},{24,28},{28,24},{1,5},{5... | collective-permute-start | bytes 589832 | tf_op jit(solution)/shard_map/ppermute | solution.py:34
  38.8 9.7 %copy-start = (f32[32,256]{1,0:T(8,128)S(1)}, f32[32,256]{1,0:T(8,128)}, u32[]{:S(2)}) copy-start(f32[32,256]{1,0:T(8,128)} %get-tuple-element.18.rows) | copy-start | bytes 98308
  44.7 21.3 %all-to-all-start.2 = ((f32[8,160,128]{2,1,0:T(8,128)}), f32[8,160,128]{2,1,0:T(8,128)S(1)}, u32[]{:S(2)}, u32[]{:S(2)}) async-start(f32[8,160,128]{2,1,0:T(8,128)} %solve_last.1), calls=%async_computation.2 | async-start | bytes 1310720 | tf_op jit(solution)/shard_map/all_to_all | solution.py:463
  48.9 6.2 %collective-permute-start.5 = (f32[160,256]{1,0:T(8,128)S(1)}, f32[160,256]{1,0:T(8,128)S(1)}, u32[]{:S(2)}, u32[]{:S(2)}) collective-permute-start(f32[160,256]{1,0:T(8,128)S(1)} %first_sums.1), channel_id=1, source_target_pairs={{0,1},{1,0},{2,3},{3,2},{4,5},{5,4},{6,7},{7,6},{8,9},{9,8},{10,11... | collective-permute-start | bytes 491528 | tf_op jit(solution)/shard_map/ppermute | solution.py:34
  55.1 1.5 %collective-permute-start.6 = (f32[160,256]{1,0:T(8,128)S(1)}, f32[160,256]{1,0:T(8,128)S(1)}, u32[]{:S(2)}, u32[]{:S(2)}) collective-permute-start(f32[160,256]{1,0:T(8,128)S(1)} %add.12.refs_0_), channel_id=1, source_target_pairs={{0,2},{2,0},{1,3},{3,1},{4,6},{6,4},{5,7},{7,5},{8,10},{10,8},{9,1... | collective-permute-start | bytes 491528 | tf_op jit(solution)/shard_map/ppermute | solution.py:34
  66.9 14.7 %all-to-all-start.3 = ((f32[16,4,8,128]{3,2,1,0:T(8,128)}), f32[16,4,8,128]{3,2,1,0:T(8,128)S(1)}, u32[]{:S(2)}, u32[]{:S(2)}) async-start(f32[16,4,8,128]{3,2,1,0:T(8,128)} %get-tuple-element.25), calls=%async_computation.3 | async-start | bytes 524288 | tf_op jit(solution)/shard_map/all_to_all | solution.py:474
  71.6 1.4 %collective-permute-start.7 = (f32[8,32,128]{2,1,0:T(8,128)S(1)}, f32[8,32,128]{2,1,0:T(8,128)S(1)}, u32[]{:S(2)}, u32[]{:S(2)}) collective-permute-start(f32[8,32,128]{2,1,0:T(8,128)S(1)} %get-tuple-element.26.refs_0_), channel_id=1, source_target_pairs={{0,2},{2,0},{1,3},{3,1},{4,6},{6,4},{5,7},{7,5},{8,10},{10,8},{9,1... | collective-permute-start | bytes 393224 | tf_op jit(solution)/shard_map/ppermute | solution.py:34
